TPU v7x, 32 devices: a whole 2x2x4 slice. The times are simulated.
32 devices in a mesh: lat: 4 (over y, x), lon: 8 (over z, core).
Axes of the slice: x: 2, y: 2, z: 4, core: 2. Of those that a mesh axis runs over, the one named last changes fastest.
Arguments:
- queries: bfloat16 [32, 128, 1024], P('lat', 'lon'), may hold values from -108 to 108
- keys_values: bfloat16 [2, 32, 128, 1024], P(None, 'lat', 'lon'), may hold values from -6 to 6
- out_weight: bfloat16 [1024, 1024], replicated, may hold values from -0.1875 to 0.1875
Outputs:
- mixed: bfloat16 [32, 128, 1024], P('lat', 'lon')
All inputs are finite; a program needn't handle non-finite values.
Results may differ from a plain program's by a relative error of at most 0.0059.
Values may be sent and summed in bfloat16 or wider, within the bound.
No kernel may reach another device: no remote copies, remote signals or barrier semaphores. Data moves between devices by JAX's collectives and lax.ppermute only.
A program may use at most 64 MiB of HBM per device.

v0:
```python
import math

import jax
import jax.numpy as jnp
from jax import lax
from jax.sharding import PartitionSpec as P

HEADS = 8
HEAD_DIM = 128
TILE = 8
LEVELS = 2


def with_halo(block, sides, width):
    for axis, dim in sides:
        count = lax.axis_size(axis)
        forward = [(i, i + 1) for i in range(count - 1)]
        forward.append((count - 1, 0))
        backward = [(target, source) for source, target in forward]
        low = lax.ppermute(
            lax.slice_in_dim(block, block.shape[dim] - width, None, axis=dim), axis, forward
        )
        high = lax.ppermute(lax.slice_in_dim(block, 0, width, axis=dim), axis, backward)
        block = jnp.concatenate([low, block, high], axis=dim)
    return block


def from_partner(block, axis, stride):
    count = lax.axis_size(axis)
    route = []
    for low in range(count):
        high = low | 1 << stride
        if high != low and high < count:
            route += [(low, high), (high, low)]
    return lax.ppermute(block, axis, route)


def pool_pairs(grid, factor):
    two, rows, cols, width = grid.shape
    shaped = grid.reshape(two, rows // factor, factor, cols // factor, factor, width)
    return jnp.mean(shaped, axis=(2, 4), dtype=jnp.float32).astype(jnp.bfloat16)


def attend(queries, ext, valid, coarse_keys, coarse_vals, bias, out_weight):
    rows, cols, width = queries.shape
    tall, wide = (rows // TILE, cols // TILE)
    span = TILE * TILE
    q_tiles = queries.reshape(tall, TILE, wide, TILE, width).transpose(0, 2, 1, 3, 4)
    q_tiles = q_tiles.reshape(tall, wide, span, HEADS, HEAD_DIM)
    paired = ext.reshape(2, tall + 2, TILE, wide + 2, TILE, width)
    row_mask = valid.reshape(tall + 2, TILE)
    scale = 1.0 / math.sqrt(HEAD_DIM)
    near = []
    masks = []
    for da in range(3):
        for db in range(3):
            piece = paired[:, da : da + tall, :, db : db + wide].transpose(0, 1, 3, 2, 4, 5)
            near.append(piece.reshape(2, tall, wide, span, width))
            masks.append(jnp.repeat(row_mask[da : da + tall], TILE, axis=1))
    count = coarse_keys.shape[0]
    far = jnp.broadcast_to(
        jnp.stack([coarse_keys, coarse_vals])[:, None, None], (2, tall, wide, count, width)
    )
    stacked = jnp.concatenate(near + [far], axis=3)
    stacked = stacked.reshape(2, tall, wide, 9 * span + count, HEADS, HEAD_DIM)
    keep = jnp.concatenate(masks + [jnp.ones((tall, count), dtype=bool)], axis=1)
    full_bias = jnp.concatenate([jnp.zeros((9 * span,), jnp.float32), bias])
    scores = (
        jnp.einsum("abqhe,abkhe->abhqk", q_tiles, stacked[0], preferred_element_type=jnp.float32)
        * scale
        + full_bias
    )
    scores = jnp.where(keep[:, None, None, None, :], scores, jnp.float32(-1e30))
    top = jnp.max(scores, axis=-1, keepdims=True)
    expo = jnp.exp(scores - top)
    weights = (expo / jnp.sum(expo, axis=-1, keepdims=True)).astype(jnp.bfloat16)
    total = jnp.einsum(
        "abhqk,abkhe->abqhe", weights, stacked[1], preferred_element_type=jnp.float32
    )
    total = total.reshape(tall, wide, TILE, TILE, width).transpose(0, 2, 1, 3, 4)
    attended = total.reshape(rows * cols, width).astype(jnp.bfloat16)
    mixed = jnp.dot(attended, out_weight, preferred_element_type=jnp.float32)
    return mixed.astype(jnp.bfloat16).reshape(rows, cols, width)


def shards(queries, keys_values, out_weight):
    rows, cols = (queries.shape[0], queries.shape[1])
    tall, wide = (rows // TILE, cols // TILE)
    lat_pos = lax.axis_index("lat")
    lon_pos = lax.axis_index("lon")
    ext = with_halo(keys_values, (("lat", 1), ("lon", 2)), TILE)
    grid_rows = rows * lax.axis_size("lat")
    row_ids = lat_pos * rows - TILE + jnp.arange(rows + 2 * TILE, dtype=jnp.int32)
    valid = (row_ids >= 0) & (row_ids < grid_rows)
    level_sum = pool_pairs(keys_values, TILE)
    collected = []
    biases = []
    for level in range(LEVELS):
        across_lat = from_partner(level_sum, "lat", level)
        paired = from_partner(jnp.stack([level_sum, across_lat]), "lon", level)
        across_lon, diagonal = (paired[0], paired[1])
        for member in (across_lat, across_lon, diagonal):
            collected.append(member.reshape(2, tall * wide, member.shape[-1]))
        biases.append(jnp.full((3 * tall * wide,), math.log(TILE * TILE * 4**level), jnp.float32))
        if level + 1 < LEVELS:
            lat_bit = lat_pos >> level & 1
            lon_bit = lon_pos >> level & 1

            def member_at(lat_side, lon_side):
                same_lat = lat_bit == lat_side
                same_lon = lon_bit == lon_side
                return jnp.where(
                    same_lat,
                    jnp.where(same_lon, level_sum, across_lon),
                    jnp.where(same_lon, across_lat, diagonal),
                )

            upper = jnp.concatenate([member_at(0, 0), member_at(0, 1)], axis=2)
            lower = jnp.concatenate([member_at(1, 0), member_at(1, 1)], axis=2)
            level_sum = pool_pairs(jnp.concatenate([upper, lower], axis=1), 2)
    coarse = jnp.concatenate(collected, axis=1)
    bias = jnp.concatenate(biases)
    return attend(queries, ext, valid, coarse[0], coarse[1], bias, out_weight)


def solution(mesh):
    return jax.shard_map(
        shards,
        mesh=mesh,
        in_specs=(P("lat", "lon", None), P(None, "lat", "lon", None), P()),
        out_specs=P("lat", "lon", None),
        check_vma=False,
    )
```

profile of v0, /device:TPU:0, one launch (start us, length us, event | category | flops | bytes accessed | tf_op | source)
XLA Modules:
  0.0 74.2 jit_solution(6144668210680212162)
XLA Ops:
  0.0 1.3 %convert_reduce_fusion = f32[2,16,1024]{2,1,0:T(8,128)S(1)} fusion(bf16[2,8,16,1024]{3,2,1,0:T(8,128)(2,1)} %param.4), kind=kLoop, calls=%fused_computation.19 | loop fusion | flops 491520 | bytes 655360 | tf_op jit(solution)/shard_map/reduce_sum | solution.py:41
  1.4 3.0 %collective-permute-start.4 = (bf16[2,1,2,1024]{3,2,0,1:T(2,128)(2,1)S(1)}, bf16[2,1,2,1024]{3,2,0,1:T(2,128)(2,1)S(1)}, u32[]{:S(2)}, u32[]{:S(2)}) collective-permute-start(bf16[2,1,2,1024]{3,2,0,1:T(2,128)(2,1)S(1)} %get-tuple-element.29), channel_id=1, source_target_pairs={{0,8},{8,0},{16,24},{24,16},{1,9},{9,1},{17,25},{25,17},{2,10},{10... | collective-permute-start | bytes 24584 | tf_op jit(solution)/shard_map/ppermute | solution.py:35
  4.4 2.9 %collective-permute-start.1 = (bf16[2,8,16,1024]{3,2,1,0:T(8,128)(2,1)}, bf16[2,8,16,1024]{3,2,1,0:T(8,128)(2,1)S(1)}, u32[]{:S(2)}, u32[]{:S(2)}) collective-permute-start(bf16[2,8,16,1024]{3,2,1,0:T(8,128)(2,1)} %param.4), channel_id=1, source_target_pairs={{8,0},{16,8},{24,16},{0,24},{9,1},{17,9},{25,17},{1,25},{10,2},{18... | collective-permute-start | bytes 1572872 | tf_op jit(solution)/shard_map/ppermute | solution.py:23
  7.4 1.1 %collective-permute-done.5 = bf16[2,2,1,2,1024]{4,3,1,2,0:T(2,128)(2,1)S(1)} collective-permute-done((bf16[2,2,1,2,1024]{4,3,1,2,0:T(2,128)(2,1)S(1)}, bf16[2,2,1,2,1024]{4,3,1,2,0:T(2,128)(2,1)S(1)}, u32[]{:S(2)}, u32[]{:S(2)}) %collective-permute-start.5) | collective-permute-done | bytes 16416 | tf_op jit(solution)/shard_map/ppermute | solution.py:35
  8.8 1.6 %collective-permute-start.6 = (bf16[2,1,2,1024]{3,2,0,1:T(2,128)(2,1)S(1)}, bf16[2,1,2,1024]{3,2,0,1:T(2,128)(2,1)S(1)}, u32[]{:S(2)}, u32[]{:S(2)}) collective-permute-start(bf16[2,1,2,1024]{3,2,0,1:T(2,128)(2,1)S(1)} %get-tuple-element.25), channel_id=1, source_target_pairs={{0,16},{16,0},{8,24},{24,8},{1,17},{17,1},{9,25},{25,9},{2,18},{18... | collective-permute-start | bytes 24584 | tf_op jit(solution)/shard_map/ppermute | solution.py:35
  10.4 10.0 %collective-permute-done = bf16[2,8,16,1024]{3,2,1,0:T(8,128)(2,1)S(1)} collective-permute-done((bf16[2,8,16,1024]{3,2,1,0:T(8,128)(2,1)}, bf16[2,8,16,1024]{3,2,1,0:T(8,128)(2,1)S(1)}, u32[]{:S(2)}, u32[]{:S(2)}) %collective-permute-start) | collective-permute-done | bytes 524320 | tf_op jit(solution)/shard_map/ppermute | solution.py:20
  20.4 1.1 %constant_dynamic-update-slice_fusion.1 = bf16[2,24,16,1024]{3,2,1,0:T(8,128)(2,1)S(1)} fusion(bf16[2,24,16,1024]{3,2,1,0:T(8,128)(2,1)S(1)} %constant_dynamic-update-slice_fusion.2, bf16[2,8,16,1024]{3,2,1,0:T(8,128)(2,1)} %param.4), kind=kLoop, calls=%fused_computation.43 | loop fusion | bytes 1048576
  21.5 8.6 %collective-permute-done.1 = bf16[2,8,16,1024]{3,2,1,0:T(8,128)(2,1)S(1)} collective-permute-done((bf16[2,8,16,1024]{3,2,1,0:T(8,128)(2,1)}, bf16[2,8,16,1024]{3,2,1,0:T(8,128)(2,1)S(1)}, u32[]{:S(2)}, u32[]{:S(2)}) %collective-permute-start.1) | collective-permute-done | bytes 524320 | tf_op jit(solution)/shard_map/ppermute | solution.py:23
  30.2 1.2 %copy-done.1 = bf16[2,24,16,1024]{3,2,1,0:T(8,128)(2,1)} copy-done((bf16[2,24,16,1024]{3,2,1,0:T(8,128)(2,1)}, bf16[2,24,16,1024]{3,2,1,0:T(8,128)(2,1)S(1)}, u32[]{:S(2)}) %copy-start.1) | copy-done | bytes 1572888
  31.4 1.3 %fusion.27 = (bf16[2,24,8,1024]{3,2,1,0:T(8,128)(2,1)}, bf16[2,24,8,1024]{3,2,1,0:T(8,128)(2,1)}) fusion(bf16[2,24,16,1024]{3,2,1,0:T(8,128)(2,1)S(1)} %constant_dynamic-update-slice_fusion), kind=kLoop, calls=%fused_computation.69 | loop fusion | bytes 3145728 | tf_op jit(solution)/shard_map/slice | solution.py:21
  32.7 1.9 %collective-permute-start.3 = (bf16[2,24,8,1024]{3,2,1,0:T(8,128)(2,1)}, bf16[2,24,8,1024]{3,2,1,0:T(8,128)(2,1)S(1)}, u32[]{:S(2)}, u32[]{:S(2)}) collective-permute-start(bf16[2,24,8,1024]{3,2,1,0:T(8,128)(2,1)} %get-tuple-element.17), channel_id=1, source_target_pairs={{1,0},{2,1},{3,2},{4,3},{5,4},{6,5},{7,6},{0,7},{9,8},{10,9},{11,1... | collective-permute-start | bytes 2359304 | tf_op jit(solution)/shard_map/ppermute | solution.py:23
  34.5 0.1 fusion.28
  34.8 0.1 broadcast_in_dim.46
  34.9 0.1 broadcast_in_dim.48
  35.1 0.1 broadcast_in_dim.50
  35.2 0.1 concatenate.31
  35.4 0.3 collective-permute-start.7
  35.7 16.5 %collective-permute-done.7 = bf16[2,2,1,2,1024]{4,3,1,2,0:T(2,128)(2,1)S(1)} collective-permute-done((bf16[2,2,1,2,1024]{4,3,1,2,0:T(2,128)(2,1)S(1)}, bf16[2,2,1,2,1024]{4,3,1,2,0:T(2,128)(2,1)S(1)}, u32[]{:S(2)}, u32[]{:S(2)}) %collective-permute-start.7) | collective-permute-done | bytes 16416 | tf_op jit(solution)/shard_map/ppermute | solution.py:35
  52.2 0.1 concatenate.29
  52.3 2.9 %collective-permute-done.2 = bf16[2,24,8,1024]{3,2,1,0:T(8,128)(2,1)} collective-permute-done((bf16[2,24,8,1024]{3,2,1,0:T(8,128)(2,1)}, bf16[2,24,8,1024]{3,2,1,0:T(8,128)(2,1)}, u32[]{:S(2)}, u32[]{:S(2)}) %collective-permute-start.2) | collective-permute-done | bytes 786464 | tf_op jit(solution)/shard_map/ppermute | solution.py:20
  55.2 1.9 %pad_maximum_fusion = bf16[2,24,32,1024]{3,2,1,0:T(8,128)(2,1)S(1)} fusion(bf16[2,24,8,1024]{3,2,1,0:T(8,128)(2,1)S(1)} %collective-permute-done.3, bf16[2,24,16,1024]{3,2,1,0:T(8,128)(2,1)} %copy-done.1, bf16[2,24,8,1024]{3,2,1,0:T(8,128)(2,1)} %collective-permute-done.2), kind=kLoop, calls=%fused_computation.1 | loop fusion | flops 9437184 | bytes 6291456 | tf_op jit(solution)/shard_map/concatenate | solution.py:24
  57.1 0.5 slice_bitcast_fusion
  58.0 2.7 %fusion.26 = (bf16[1,1,2,588,1024]{4,3,2,0,1:T(8,128)(2,1)}, bf16[1,1,2,588,1024]{4,3,2,0,1:T(8,128)(2,1)}) fusion(bf16[2,1,2,588,1024]{4,3,2,0,1:T(8,128)(2,1)S(1)} %broadcast_dynamic-update-slice_fusion), kind=kLoop, calls=%fused_computation.68 | loop fusion | bytes 9633792 | tf_op jit(solution)/shard_map/slice | solution.py:78
  60.7 3.4 %reshape.229 = bf16[2,588,8,128]{3,2,1,0:T(8,128)(2,1)} reshape(bf16[1,1,2,588,1024]{4,3,2,0,1:T(8,128)(2,1)} %get-tuple-element.6) | data formatting | bytes 4816896 | tf_op jit(solution)/shard_map/reshape.10
  64.2 3.4 %reshape.228 = bf16[2,588,8,128]{3,2,1,0:T(8,128)(2,1)} reshape(bf16[1,1,2,588,1024]{4,3,2,0,1:T(8,128)(2,1)} %get-tuple-element.5) | data formatting | bytes 4816896 | tf_op jit(solution)/shard_map/reshape.15
  67.6 2.6 %fusion.5 = f32[2,8,588,64]{2,3,1,0:T(8,128)S(1)} fusion(bf16[2,588,8,128]{3,2,1,0:T(8,128)(2,1)} %reshape.229, bf16[2,64,8,128]{3,2,1,0:T(8,128)(2,1)S(1)} %bitcast.118), kind=kOutput, calls=%fused_computation.10 | convolution fusion | flops 154140672 | bytes 5079040 | tf_op jit(solution)/shard_map/abqhe,abkhe->abhqk/dot_general | solution.py:69
  70.2 1.1 %fusion.29 = (f32[2,8,64]{2,1,0:T(8,128)S(1)}, f32[2,8,64,588]{3,2,1,0:T(8,128)S(1)}) fusion(f32[2,8,588,64]{2,3,1,0:T(8,128)S(1)} %fusion.5, f32[588]{0:T(1024)S(1)} %copy-done.4, pred[588]{0:T(1024)(128)(4,1)S(1)} %reduce.10), kind=kOutput, calls=%fused_computation.71 | output fusion | flops 4817483 | bytes 4823932 | tf_op jit(solution)/shard_map/sub | solution.py:75
  71.3 0.6 copy-done.2
  71.9 0.8 %fusion.16 = bf16[1,2,64,8,128]{4,2,3,1,0:T(8,128)(2,1)S(1)} fusion(f32[2,8,64,588]{3,2,1,0:T(8,128)S(1)} %get-tuple-element.34, f32[2,8,64]{2,1,0:T(8,128)S(1)} %get-tuple-element.33, bf16[2,588,8,128]{3,2,1,0:T(8,128)(2,1)S(1)} %copy-done.2), kind=kOutput, calls=%fused_computation.18 | convolution fusion | flops 155475968 | bytes 5083136 | tf_op jit(solution)/shard_map/abhqk,abkhe->abqhe/dot_general | solution.py:77
  72.7 0.2 copy.38
  72.9 0.1 convert_element_type.98
  73.1 1.2 %convolution_convert_fusion = bf16[128,1024]{1,0:T(8,128)(2,1)} fusion(bf16[128,1024]{1,0:T(8,128)(2,1)S(1)} %bitcast.115, bf16[1024,1024]{1,0:T(8,128)(2,1)S(1)} %copy-done), kind=kOutput, calls=%fused_computation.17 | convolution fusion | flops 268566528 | bytes 2621440 | tf_op jit(solution)/shard_map/dot_general | solution.py:82
  (46 shorter events, 1.3 us)
Async XLA Ops:
  0.0 73.1 %copy-start = (bf16[1024,1024]{1,0:T(8,128)(2,1)S(1)}, bf16[1024,1024]{1,0:T(8,128)(2,1)}, u32[]{:S(2)}) copy-start(bf16[1024,1024]{1,0:T(8,128)(2,1)} %param.5) | copy-start | bytes 6291460
  1.4 5.9 %collective-permute-start.4 = (bf16[2,1,2,1024]{3,2,0,1:T(2,128)(2,1)S(1)}, bf16[2,1,2,1024]{3,2,0,1:T(2,128)(2,1)S(1)}, u32[]{:S(2)}, u32[]{:S(2)}) collective-permute-start(bf16[2,1,2,1024]{3,2,0,1:T(2,128)(2,1)S(1)} %get-tuple-element.29), channel_id=1, source_target_pairs={{0,8},{8,0},{16,24},{24,16},{1,9},{9,1},{17,25},{25,17},{2,10},{10... | collective-permute-start | bytes 24584 | tf_op jit(solution)/shard_map/ppermute | solution.py:35
  4.4 16.0 %collective-permute-start = (bf16[2,8,16,1024]{3,2,1,0:T(8,128)(2,1)}, bf16[2,8,16,1024]{3,2,1,0:T(8,128)(2,1)S(1)}, u32[]{:S(2)}, u32[]{:S(2)}) collective-permute-start(bf16[2,8,16,1024]{3,2,1,0:T(8,128)(2,1)} %param.4), channel_id=1, source_target_pairs={{0,8},{8,16},{16,24},{24,0},{1,9},{9,17},{17,25},{25,1},{2,10},{10... | collective-permute-start | bytes 1572872 | tf_op jit(solution)/shard_map/ppermute | solution.py:20
  4.4 25.8 %collective-permute-start.1 = (bf16[2,8,16,1024]{3,2,1,0:T(8,128)(2,1)}, bf16[2,8,16,1024]{3,2,1,0:T(8,128)(2,1)S(1)}, u32[]{:S(2)}, u32[]{:S(2)}) collective-permute-start(bf16[2,8,16,1024]{3,2,1,0:T(8,128)(2,1)} %param.4), channel_id=1, source_target_pairs={{8,0},{16,8},{24,16},{0,24},{9,1},{17,9},{25,17},{1,25},{10,2},{18... | collective-permute-start | bytes 1572872 | tf_op jit(solution)/shard_map/ppermute | solution.py:23
  7.3 1.2 %collective-permute-start.5 = (bf16[2,2,1,2,1024]{4,3,1,2,0:T(2,128)(2,1)S(1)}, bf16[2,2,1,2,1024]{4,3,1,2,0:T(2,128)(2,1)S(1)}, u32[]{:S(2)}, u32[]{:S(2)}) collective-permute-start(bf16[2,2,1,2,1024]{4,3,1,2,0:T(2,128)(2,1)S(1)} %pad_maximum_fusion.1), channel_id=1, source_target_pairs={{0,1},{1,0},{2,3},{3,2},{4,5},{5,4},{6,7},{7,6},{8,9},{9,8},{10,11... | collective-permute-start | bytes 49160 | tf_op jit(solution)/shard_map/ppermute | solution.py:35
  8.8 26.6 %collective-permute-start.6 = (bf16[2,1,2,1024]{3,2,0,1:T(2,128)(2,1)S(1)}, bf16[2,1,2,1024]{3,2,0,1:T(2,128)(2,1)S(1)}, u32[]{:S(2)}, u32[]{:S(2)}) collective-permute-start(bf16[2,1,2,1024]{3,2,0,1:T(2,128)(2,1)S(1)} %get-tuple-element.25), channel_id=1, source_target_pairs={{0,16},{16,0},{8,24},{24,8},{1,17},{17,1},{9,25},{25,9},{2,18},{18... | collective-permute-start | bytes 24584 | tf_op jit(solution)/shard_map/ppermute | solution.py:35
  20.4 14.2 %copy-start.3 = (bf16[8,16,1024]{2,1,0:T(8,128)(2,1)S(1)}, bf16[8,16,1024]{2,1,0:T(8,128)(2,1)}, u32[]{:S(2)}) copy-start(bf16[8,16,1024]{2,1,0:T(8,128)(2,1)} %param.3) | copy-start | bytes 786436
  30.2 1.2 %copy-start.1 = (bf16[2,24,16,1024]{3,2,1,0:T(8,128)(2,1)}, bf16[2,24,16,1024]{3,2,1,0:T(8,128)(2,1)S(1)}, u32[]{:S(2)}) copy-start(bf16[2,24,16,1024]{3,2,1,0:T(8,128)(2,1)S(1)} %constant_dynamic-update-slice_fusion) | copy-start | bytes 4718596
  32.7 19.6 %collective-permute-start.3 = (bf16[2,24,8,1024]{3,2,1,0:T(8,128)(2,1)}, bf16[2,24,8,1024]{3,2,1,0:T(8,128)(2,1)S(1)}, u32[]{:S(2)}, u32[]{:S(2)}) collective-permute-start(bf16[2,24,8,1024]{3,2,1,0:T(8,128)(2,1)} %get-tuple-element.17), channel_id=1, source_target_pairs={{1,0},{2,1},{3,2},{4,3},{5,4},{6,5},{7,6},{0,7},{9,8},{10,9},{11,1... | collective-permute-start | bytes 2359304 | tf_op jit(solution)/shard_map/ppermute | solution.py:23
  34.5 20.6 %collective-permute-start.2 = (bf16[2,24,8,1024]{3,2,1,0:T(8,128)(2,1)}, bf16[2,24,8,1024]{3,2,1,0:T(8,128)(2,1)}, u32[]{:S(2)}, u32[]{:S(2)}) collective-permute-start(bf16[2,24,8,1024]{3,2,1,0:T(8,128)(2,1)} %get-tuple-element.16), channel_id=1, source_target_pairs={{0,1},{1,2},{2,3},{3,4},{4,5},{5,6},{6,7},{7,0},{8,9},{9,10},{10,1... | collective-permute-start | bytes 2359304 | tf_op jit(solution)/shard_map/ppermute | solution.py:20
  35.4 16.8 %collective-permute-start.7 = (bf16[2,2,1,2,1024]{4,3,1,2,0:T(2,128)(2,1)S(1)}, bf16[2,2,1,2,1024]{4,3,1,2,0:T(2,128)(2,1)S(1)}, u32[]{:S(2)}, u32[]{:S(2)}) collective-permute-start(bf16[2,2,1,2,1024]{4,3,1,2,0:T(2,128)(2,1)S(1)} %pad_maximum_fusion.2), channel_id=1, source_target_pairs={{0,2},{2,0},{1,3},{3,1},{4,6},{6,4},{5,7},{7,5},{8,10},{10,8},{9,1... | collective-permute-start | bytes 49160 | tf_op jit(solution)/shard_map/ppermute | solution.py:35
  67.6 2.6 %copy-start.4 = (f32[588]{0:T(1024)S(1)}, f32[588]{0:T(1024)}, u32[]{:S(2)}) copy-start(f32[588]{0:T(1024)} %constant.35.clone.1) | copy-start | bytes 7060
  70.2 1.7 %copy-start.2 = (bf16[2,588,8,128]{3,2,1,0:T(8,128)(2,1)S(1)}, bf16[2,588,8,128]{3,2,1,0:T(8,128)(2,1)}, u32[]{:S(2)}) copy-start(bf16[2,588,8,128]{3,2,1,0:T(8,128)(2,1)} %reshape.228) | copy-start | bytes 7225348
where the time goes:
time: 74.5 us; the launch traced here: 74.2 us
  waiting for transfers between devices  39.1 us (52%)
  local copies, waits for them, and re-layouts  15.8 us (21%)
  starting transfers between devices  9.74 us (13%)
  other arithmetic  4.63 us (6%)
  matrix products  4.61 us (6%)
    ppermute x4, waiting for transfers between devices, from_partner(): return lax.ppermute(block, axis, route)  17.6 us
    ppermute x2, waiting for transfers between devices, with_halo(): lax.ppermute(lax.slice_in_dim(block, block.shape[dim] - width, None, axis...  12.9 us
    ppermute x2, waiting for transfers between devices, with_halo(): lax.ppermute(lax.slice_in_dim(block, 0, width, axis=dim), axis, backward)  8.64 us
    another operation x3, local copies, waits for them, and re-layouts  6.83 us
    ppermute x4, starting transfers between devices, from_partner(): return lax.ppermute(block, axis, route)  4.96 us
    ppermute x2, starting transfers between devices, with_halo(): lax.ppermute(lax.slice_in_dim(block, 0, width, axis=dim), axis, backward)  4.71 us
    unnamed x22, local copies, waits for them, and re-layouts  3.28 us
    slice x1, local copies, waits for them, and re-layouts, attend(): stacked[1]  2.71 us
  transfers between devices with their start and end apart: 8, of which 5 were waited for; matrix products, arithmetic and copies ran while one was open for 5% of the time, Pallas kernels for 0%

commit v1 on v0

v1 whole, which is shorter than its diff:
```python
import functools
import math

import jax
import jax.numpy as jnp
from jax import lax
from jax.experimental import pallas as pl
from jax.experimental.pallas import tpu as pltpu
from jax.sharding import PartitionSpec as P

HEADS = 8
HEAD_DIM = 128
TILE = 8
SPAN = TILE * TILE
SCALE = 1.0 / math.sqrt(HEAD_DIM)
NEG = -1e30
F32 = jnp.float32
BF16 = jnp.bfloat16
VMEM = pl.BlockSpec(memory_space=pltpu.VMEM)


def call(kernel, outs, name, flops, *args):
    moved = sum(a.size * a.dtype.itemsize for a in args)
    moved += sum(math.prod(o.shape) * o.dtype.itemsize for o in outs)
    return pl.pallas_call(
        kernel,
        out_shape=outs,
        in_specs=[VMEM] * len(args),
        out_specs=[VMEM] * len(outs),
        name=name,
        compiler_params=pltpu.CompilerParams(vmem_limit_bytes=16 * 1024 * 1024),
        cost_estimate=pl.CostEstimate(flops=flops, bytes_accessed=moved, transcendentals=0),
    )(*args)


def odd_column():
    return lax.rem(lax.axis_index("lon"), 2) == 1


def far_exists(n_lat):
    row = lax.axis_index("lat")
    return jnp.where(lax.rem(row, 2) == 1, row < n_lat - 1, row > 0)


def split_tiles(x, odd):
    cut = x.reshape(TILE, 2, TILE, x.shape[-1])
    left = cut[:, 0].reshape(SPAN, x.shape[-1])
    right = cut[:, 1].reshape(SPAN, x.shape[-1])
    return jnp.where(odd, right, left), jnp.where(odd, left, right)


def split_kernel(q_ref, kv_ref, qe_ref, qi_ref, kve_ref, kvi_ref, pool_ref):
    odd = odd_column()
    edge, inner = split_tiles(q_ref[...].astype(F32), odd)
    qe_ref[...] = edge.astype(BF16)
    qi_ref[...] = inner.astype(BF16)
    pooled = []
    for half in range(2):
        edge, inner = split_tiles(kv_ref[half].astype(F32), odd)
        kve_ref[half] = edge.astype(BF16)
        kvi_ref[half] = inner.astype(BF16)
        for tile in (edge, inner):
            pooled.append(jnp.sum(tile, axis=0, keepdims=True) * (1.0 / SPAN))
    pool_ref[...] = jnp.concatenate(pooled, axis=0).astype(BF16)


def logits(q, k):
    return lax.dot_general(q, k, (((1,), (1,)), ((), ())), preferred_element_type=F32) * SCALE


def partial_kernel(n_lat, q_ref, own_ref, pair_ref, far_ref, out_ref):
    far = far_exists(n_lat)
    lane = lax.broadcasted_iota(jnp.int32, (SPAN, 3 * SPAN), 1)
    keep = jnp.logical_or(lane < 2 * SPAN, far)
    column = lax.broadcasted_iota(jnp.int32, (SPAN, HEAD_DIM), 1)
    stats = jnp.zeros((SPAN, HEAD_DIM), F32)
    for h in range(HEADS):
        cols = slice(h * HEAD_DIM, (h + 1) * HEAD_DIM)
        k = jnp.concatenate([r[0, :, cols] for r in (own_ref, pair_ref, far_ref)], axis=0)
        v = jnp.concatenate([r[1, :, cols] for r in (own_ref, pair_ref, far_ref)], axis=0)
        s = jnp.where(keep, logits(q_ref[:, cols], k), NEG)
        top = jnp.max(s, axis=-1, keepdims=True)
        expo = jnp.exp(s - top)
        total = jnp.sum(expo, axis=-1, keepdims=True)
        part = jnp.dot(expo.astype(BF16), v, preferred_element_type=F32)
        out_ref[:, cols] = (part / total).astype(BF16)
        lse = top + jnp.log(total)
        high = lse.astype(BF16).astype(F32)
        mid = (lse - high).astype(BF16).astype(F32)
        low = lse - high - mid
        stats = jnp.where(column == h, high, stats)
        stats = jnp.where(column == HEADS + h, mid, stats)
        stats = jnp.where(column == 2 * HEADS + h, low, stats)
    out_ref[:, HEADS * HEAD_DIM :] = stats.astype(BF16)


def own_kernel(n_lat, count, qe_ref, qi_ref, *refs):
    tiles, (coarse_ref, out_ref, lse_ref) = refs[:6], refs[6:]
    rows = 2 * SPAN
    far = far_exists(n_lat)
    lane = lax.broadcasted_iota(jnp.int32, (rows, 6 * SPAN), 1)
    keep = jnp.logical_or(lane < 4 * SPAN, far)
    entry = lax.broadcasted_iota(jnp.int32, (rows, 2 * count), 1)
    bias = jnp.where(entry < count, math.log(SPAN), math.log(4 * SPAN)).astype(F32)
    column = lax.broadcasted_iota(jnp.int32, (rows, HEAD_DIM), 1)
    stats = jnp.zeros((rows, HEAD_DIM), F32)
    for h in range(HEADS):
        cols = slice(h * HEAD_DIM, (h + 1) * HEAD_DIM)
        q = jnp.concatenate([qe_ref[:, cols], qi_ref[:, cols]], axis=0)
        k = jnp.concatenate([r[0, :, cols] for r in tiles], axis=0)
        v = jnp.concatenate([r[1, :, cols] for r in tiles], axis=0)
        near = jnp.where(keep, logits(q, k), NEG)
        coarse = logits(q, coarse_ref[0, :, cols])[:, : 2 * count] + bias
        top = jnp.maximum(
            jnp.max(near, axis=-1, keepdims=True), jnp.max(coarse, axis=-1, keepdims=True)
        )
        near = jnp.exp(near - top)
        coarse = jnp.exp(coarse - top)
        total = jnp.sum(near, axis=-1, keepdims=True) + jnp.sum(coarse, axis=-1, keepdims=True)
        part = jnp.dot(near.astype(BF16), v, preferred_element_type=F32)
        part += jnp.dot(
            coarse.astype(BF16), coarse_ref[1, : 2 * count, cols], preferred_element_type=F32
        )
        out_ref[:, cols] = part / total
        stats = jnp.where(column == h, top + jnp.log(total), stats)
    lse_ref[...] = stats


def merge_kernel(own_ref, lse_ref, edge_ref, inner_ref, weight_ref, out_ref):
    width = HEADS * HEAD_DIM
    odd = odd_column()
    merged = []
    for index, back_ref in enumerate((edge_ref, inner_ref)):
        rows = slice(index * SPAN, (index + 1) * SPAN)
        stats = back_ref[:, width:].astype(F32)
        pieces = []
        for h in range(HEADS):
            cols = slice(h * HEAD_DIM, (h + 1) * HEAD_DIM)
            here = lse_ref[rows, h : h + 1]
            there = stats[:, h : h + 1] + stats[:, HEADS + h : HEADS + h + 1]
            there = there + stats[:, 2 * HEADS + h : 2 * HEADS + h + 1]
            share = 1.0 / (1.0 + jnp.exp(jnp.minimum(there - here, 80.0)))
            own = own_ref[rows, cols]
            pieces.append(own * share + back_ref[:, cols].astype(F32) * (1.0 - share))
        merged.append(jnp.concatenate(pieces, axis=1).reshape(TILE, TILE, width))
    edge, inner = merged
    left = jnp.where(odd, inner, edge)
    right = jnp.where(odd, edge, inner)
    attended = jnp.stack([left, right], axis=1).reshape(2 * SPAN, width).astype(BF16)
    mixed = jnp.dot(attended, weight_ref[...], preferred_element_type=F32)
    out_ref[...] = mixed.reshape(TILE, 2 * TILE, width).astype(BF16)


def swap(x, axis, distance):
    count = lax.axis_size(axis)
    return lax.ppermute(x, axis, [(i, i ^ distance) for i in range(count)])


def outward(x, axis):
    count = lax.axis_size(axis)
    return lax.ppermute(x, axis, [(i, (i + (1 if i % 2 else -1)) % count) for i in range(count)])


def onward(x, axis):
    count = lax.axis_size(axis)
    route = [(i, i + (-2 if i % 2 else 2)) for i in range(count)]
    return lax.ppermute(x, axis, [(s, t) for s, t in route if 0 <= t < count])


def mean_entries(*entries):
    total = sum(e.astype(F32) for e in entries)
    return (total * (1.0 / len(entries))).astype(BF16)


def shards(queries, keys_values, out_weight):
    n_lat = lax.axis_size("lat")
    width = queries.shape[-1]
    tile = jax.ShapeDtypeStruct((SPAN, width), BF16)
    pair = jax.ShapeDtypeStruct((2, SPAN, width), BF16)
    q_edge, q_inner, edge_own, inner_own, pooled = call(
        split_kernel,
        [tile, tile, pair, pair, jax.ShapeDtypeStruct((4, width), BF16)],
        "split",
        0,
        queries,
        keys_values,
    )
    edge_pair = swap(edge_own, "lat", 1)
    far_q_edge = outward(q_edge, "lon")
    far_q_inner = swap(q_inner, "lon", 1)
    level0 = pooled.reshape(2, 2, width)
    level0_lat = swap(level0, "lat", 1)
    inner_pair = swap(inner_own, "lat", 1)
    edge_far = onward(edge_pair, "lat")
    inner_far = onward(inner_pair, "lat")
    mine = mean_entries(level0[:, 0:1], level0[:, 1:2], level0_lat[:, 0:1], level0_lat[:, 1:2])
    beside = swap(jnp.concatenate([level0, level0_lat, mine], axis=1), "lon", 1)
    group = jnp.concatenate([mine, beside[:, 4:5]], axis=1)
    group_lon = swap(group, "lon", 2)
    group_lat = swap(jnp.concatenate([group, group_lon], axis=1), "lat", 2)
    coarse = jnp.concatenate([level0_lat, beside[:, 0:4], group_lon, group_lat], axis=1)
    count = coarse.shape[1] // 2
    coarse = jnp.pad(coarse, ((0, 0), (0, 16 - 2 * count), (0, 0)))

    back = jax.ShapeDtypeStruct((SPAN, width + HEAD_DIM), BF16)
    flops = 4 * SPAN * 3 * SPAN * width
    edge_part = call(
        functools.partial(partial_kernel, n_lat),
        [back],
        "edge_part",
        flops,
        far_q_edge,
        edge_own,
        edge_pair,
        edge_far,
    )[0]
    edge_back = outward(edge_part, "lon")
    inner_part = call(
        functools.partial(partial_kernel, n_lat),
        [back],
        "inner_part",
        flops,
        far_q_inner,
        inner_own,
        inner_pair,
        inner_far,
    )[0]
    inner_back = swap(inner_part, "lon", 1)
    own, lse = call(
        functools.partial(own_kernel, n_lat, count),
        [
            jax.ShapeDtypeStruct((2 * SPAN, width), F32),
            jax.ShapeDtypeStruct((2 * SPAN, HEAD_DIM), F32),
        ],
        "own_part",
        4 * flops,
        q_edge,
        q_inner,
        edge_own,
        inner_own,
        edge_pair,
        inner_pair,
        edge_far,
        inner_far,
        coarse,
    )
    return call(
        merge_kernel,
        [jax.ShapeDtypeStruct(queries.shape, BF16)],
        "merge",
        4 * SPAN * width * width,
        own,
        lse,
        edge_back,
        inner_back,
        out_weight,
    )[0]


def solution(mesh):
    return jax.shard_map(
        shards,
        mesh=mesh,
        in_specs=(P("lat", "lon", None), P(None, "lat", "lon", None), P()),
        out_specs=P("lat", "lon", None),
        check_vma=False,
    )
```

time: 74.5 us -> 45.3 us (0.61)
  waiting for transfers between devices: 39.1 us -> 16.1 us
  local copies, waits for them, and re-layouts: 15.8 us -> 2.03 us
  Pallas kernels: 0 us -> 8.73 us
  starting transfers between devices: 9.74 us -> 17.8 us
  matrix products: 4.61 us -> 0 us
  other arithmetic: 4.63 us -> 0.19 us
    ppermute x8 -> x12, waiting for transfers between devices: 39.1 us -> 16.1 us  [the longest x8 13.8 us: swap(): return lax.ppermute(x, axis, [(i, i ^ distance) for i in range(count)])]
    pallas_call x0 -> x5, Pallas kernels: none -> 8.73 us  [call(): pl.pallas_call(kernel, out_shape=outs, in_specs=[VMEM] * len(args), out_s...]
    ppermute x8 -> x12, starting transfers between devices: 9.74 us -> 17.8 us  [the longest x2 7.04 us: outward(): lax.ppermute(x, axis, [(i, (i + (1 if i % 2 else -1)) % count) for i in r...]
    another operation x5 -> x0, local copies, waits for them, and re-layouts: 6.85 us -> none
    dot_general x3 -> x0, matrix products: 4.61 us -> none  [the longest x1 2.62 us: attend(): jnp.einsum('abqhe,abkhe->abhqk', q_tiles, stacked[0], preferred_element_t...]
    slice x3 -> x2, local copies, waits for them, and re-layouts: 4.07 us -> 0.02 us  [the longest x1 0.01 us: shards(): group = jnp.concatenate([mine, beside[:, 4:5]], axis=1)]
    concatenate x2 -> x4, other arithmetic: 1.97 us -> 0.16 us  [the longest x1 0.06 us: shards(): jnp.concatenate([level0_lat, beside[:, 0:4], group_lon, group_lat], axis=1)]
    reduce_sum x4 -> x0, other arithmetic: 1.43 us -> none  [pool_pairs(): return jnp.mean(shaped, axis=(2, 4), dtype=jnp.float32).astype(jnp.bfloat16)]
  transfers between devices with their start and end apart: 8 -> 12, of which waited for: 5 -> 4; matrix products, arithmetic and copies ran while one was open for 5% -> 0% of each run, Pallas kernels for 0% -> 15%
where the time goes in v1:
time: 45.3 us; the launch traced here: 45 us
  starting transfers between devices  17.8 us (39%)
  waiting for transfers between devices  16.1 us (36%)
  Pallas kernels  8.73 us (19%)
  local copies, waits for them, and re-layouts  2.03 us (4%)
    ppermute x8, waiting for transfers between devices, swap(): return lax.ppermute(x, axis, [(i, i ^ distance) for i in range(count)])  13.8 us
    pallas_call x5, Pallas kernels, call(): pl.pallas_call(kernel, out_shape=outs, in_specs=[VMEM] * len(args), out_s...  8.73 us
    ppermute x2, starting transfers between devices, outward(): lax.ppermute(x, axis, [(i, (i + (1 if i % 2 else -1)) % count) for i in r...  7.04 us
    ppermute x8, starting transfers between devices, swap(): return lax.ppermute(x, axis, [(i, i ^ distance) for i in range(count)])  5.81 us
    ppermute x2, starting transfers between devices, onward(): return lax.ppermute(x, axis, [(s, t) for s, t in route if 0 <= t < count])  4.99 us
    unnamed x6, local copies, waits for them, and re-layouts  2 us
    ppermute x2, waiting for transfers between devices, onward(): return lax.ppermute(x, axis, [(s, t) for s, t in route if 0 <= t < count])  1.24 us
    ppermute x2, waiting for transfers between devices, outward(): lax.ppermute(x, axis, [(i, (i + (1 if i % 2 else -1)) % count) for i in r...  1.05 us
  transfers between devices with their start and end apart: 12, of which 4 were waited for; matrix products, arithmetic and copies ran while one was open for 0% of the time, Pallas kernels for 15%

profile of v1, /device:TPU:0, one launch (start us, length us, event | category | flops | bytes accessed | tf_op | source)
XLA Modules:
  0.0 45.0 jit_solution(16351966036124874470)
XLA Ops:
  0.0 1.0 %copy-done.1 = bf16[2,8,16,1024]{3,2,1,0:T(8,128)(2,1)S(1)} copy-done((bf16[2,8,16,1024]{3,2,1,0:T(8,128)(2,1)S(1)}, bf16[2,8,16,1024]{3,2,1,0:T(8,128)(2,1)}, u32[]{:S(2)}) %copy-start.1) | copy-done | bytes 524312
  1.0 0.9 %copy-done.2 = bf16[8,16,1024]{2,1,0:T(8,128)(2,1)S(1)} copy-done((bf16[8,16,1024]{2,1,0:T(8,128)(2,1)S(1)}, bf16[8,16,1024]{2,1,0:T(8,128)(2,1)}, u32[]{:S(2)}) %copy-start.2) | copy-done | bytes 262168
  2.0 0.3 split.1
  2.3 3.0 %collective-permute-start = (bf16[2,64,1024]{2,1,0:T(8,128)(2,1)S(1)}, bf16[2,64,1024]{2,1,0:T(8,128)(2,1)S(1)}, u32[]{:S(2)}, u32[]{:S(2)}) collective-permute-start(bf16[2,64,1024]{2,1,0:T(8,128)(2,1)S(1)} %get-tuple-element.14.refs_0_.own_ref), channel_id=1, source_target_pairs={{0,8},{8,0},{16,24},{24,16},{1,9},{9,1},{17,25},{25,17},{2,10},{10... | collective-permute-start | bytes 786440 | tf_op jit(solution)/shard_map/ppermute | solution.py:156
  5.3 0.1 collective-permute-start.1
  5.4 1.9 %collective-permute-start.4 = (bf16[2,2,1024]{2,1,0:T(2,128)(2,1)S(1)}, bf16[2,2,1024]{2,1,0:T(2,128)(2,1)S(1)}, u32[]{:S(2)}, u32[]{:S(2)}) collective-permute-start(bf16[2,2,1024]{2,1,0:T(2,128)(2,1)S(1)} %reshape.3), channel_id=1, source_target_pairs={{0,8},{8,0},{16,24},{24,16},{1,9},{9,1},{17,25},{25,17},{2,10},{10... | collective-permute-start | bytes 24584 | tf_op jit(solution)/shard_map/ppermute | solution.py:156
  7.3 10.1 %collective-permute-done.4 = bf16[2,2,1024]{2,1,0:T(2,128)(2,1)S(1)} collective-permute-done((bf16[2,2,1024]{2,1,0:T(2,128)(2,1)S(1)}, bf16[2,2,1024]{2,1,0:T(2,128)(2,1)S(1)}, u32[]{:S(2)}, u32[]{:S(2)}) %collective-permute-start.4) | collective-permute-done | bytes 8224 | tf_op jit(solution)/shard_map/ppermute | solution.py:156
  17.4 0.0 collective-permute-done.refs_2_.pair_ref
  17.4 3.7 %collective-permute-start.2 = (bf16[2,64,1024]{2,1,0:T(8,128)(2,1)S(1)}, bf16[2,64,1024]{2,1,0:T(8,128)(2,1)S(1)}, u32[]{:S(2)}, u32[]{:S(2)}) collective-permute-start(bf16[2,64,1024]{2,1,0:T(8,128)(2,1)S(1)} %collective-permute-done.refs_2_.pair_ref), channel_id=1, source_target_pairs={{0,16},{24,8},{1,17},{25,9},{2,18},{26,10},{3,19},{27,11},{4,20},{... | collective-permute-start | bytes 786440 | tf_op jit(solution)/shard_map/ppermute | solution.py:167
  21.1 0.0 collective-permute-done.1.refs_3_.pair_ref
  21.1 1.3 %collective-permute-start.3 = (bf16[2,64,1024]{2,1,0:T(8,128)(2,1)S(1)}, bf16[2,64,1024]{2,1,0:T(8,128)(2,1)S(1)}, u32[]{:S(2)}, u32[]{:S(2)}) collective-permute-start(bf16[2,64,1024]{2,1,0:T(8,128)(2,1)S(1)} %collective-permute-done.1.refs_3_.pair_ref), channel_id=1, source_target_pairs={{0,16},{24,8},{1,17},{25,9},{2,18},{26,10},{3,19},{27,11},{4,20},{... | collective-permute-start | bytes 786440 | tf_op jit(solution)/shard_map/ppermute | solution.py:167
  22.5 0.1 collective-permute-start.5
  22.6 0.5 %collective-permute-start.10 = (bf16[64,1024]{1,0:T(8,128)(2,1)S(1)}, bf16[64,1024]{1,0:T(8,128)(2,1)S(1)}, u32[]{:S(2)}, u32[]{:S(2)}) collective-permute-start(bf16[64,1024]{1,0:T(8,128)(2,1)S(1)} %get-tuple-element.13.qi_ref), channel_id=1, source_target_pairs={{0,1},{1,0},{2,3},{3,2},{4,5},{5,4},{6,7},{7,6},{8,9},{9,8},{10,11... | collective-permute-start | bytes 393224 | tf_op jit(solution)/shard_map/ppermute | solution.py:156
  23.0 3.3 %collective-permute-start.8 = (bf16[64,1024]{1,0:T(8,128)(2,1)S(1)}, bf16[64,1024]{1,0:T(8,128)(2,1)S(1)}, u32[]{:S(2)}, u32[]{:S(2)}) collective-permute-start(bf16[64,1024]{1,0:T(8,128)(2,1)S(1)} %get-tuple-element.12.qe_ref), channel_id=1, source_target_pairs={{0,7},{1,2},{2,1},{3,4},{4,3},{5,6},{6,5},{7,0},{8,15},{9,10},{10,... | collective-permute-start | bytes 393224 | tf_op jit(solution)/shard_map/ppermute | solution.py:161
  26.3 0.0 collective-permute-done.5
  26.4 0.1 collective-permute-start.6
  26.5 3.7 %collective-permute-done.6 = bf16[2,2,1024]{2,1,0:T(2,128)(2,1)S(1)} collective-permute-done((bf16[2,2,1024]{2,1,0:T(2,128)(2,1)S(1)}, bf16[2,2,1024]{2,1,0:T(2,128)(2,1)S(1)}, u32[]{:S(2)}, u32[]{:S(2)}) %collective-permute-start.6) | collective-permute-done | bytes 8224 | tf_op jit(solution)/shard_map/ppermute | solution.py:156
  30.2 0.0 copy-start
  30.2 0.1 collective-permute-start.7
  30.3 0.0 collective-permute-done.10.q_ref
  30.3 1.2 %collective-permute-done.3.refs_5_.far_ref = bf16[2,64,1024]{2,1,0:T(8,128)(2,1)S(1)} collective-permute-done((bf16[2,64,1024]{2,1,0:T(8,128)(2,1)S(1)}, bf16[2,64,1024]{2,1,0:T(8,128)(2,1)S(1)}, u32[]{:S(2)}, u32[]{:S(2)}) %collective-permute-start.3) | collective-permute-done | bytes 262176 | tf_op jit(solution)/shard_map/ppermute | solution.py:167
  31.6 2.2 %inner_part.1 = bf16[64,1152]{1,0:T(8,128)(2,1)S(1)} custom-call(bf16[64,1024]{1,0:T(8,128)(2,1)S(1)} %collective-permute-done.10.q_ref, bf16[2,64,1024]{2,1,0:T(8,128)(2,1)S(1)} %get-tuple-element.15.refs_1_.own_ref, bf16[2,64,1024]{2,1,0:T(8,128)(2,1)S(1)} %collective-permute-done.1.refs_3_.pair_ref, ...), custom_call_target="tpu_custom_call" | custom-call | flops 50331648 | bytes 1064960 | tf_op jit(solution)/shard_map/inner_part/pallas_call | solution.py:25
  33.8 0.1 collective-permute-start.11
  33.8 0.0 collective-permute-done.8.q_ref
  33.8 0.0 collective-permute-done.2.refs_4_.far_ref
  33.9 2.2 %edge_part.1 = bf16[64,1152]{1,0:T(8,128)(2,1)S(1)} custom-call(bf16[64,1024]{1,0:T(8,128)(2,1)S(1)} %collective-permute-done.8.q_ref, bf16[2,64,1024]{2,1,0:T(8,128)(2,1)S(1)} %get-tuple-element.14.refs_0_.own_ref, bf16[2,64,1024]{2,1,0:T(8,128)(2,1)S(1)} %collective-permute-done.refs_2_.pair_ref, ...), custom_call_target="tpu_custom_call" | custom-call | flops 50331648 | bytes 1064960 | tf_op jit(solution)/shard_map/edge_part/pallas_call | solution.py:25
  36.1 3.8 %collective-permute-start.9 = (bf16[64,1152]{1,0:T(8,128)(2,1)S(1)}, bf16[64,1152]{1,0:T(8,128)(2,1)S(1)}, u32[]{:S(2)}, u32[]{:S(2)}) collective-permute-start(bf16[64,1152]{1,0:T(8,128)(2,1)S(1)} %edge_part.1), channel_id=1, source_target_pairs={{0,7},{1,2},{2,1},{3,4},{4,3},{5,6},{6,5},{7,0},{8,15},{9,10},{10,... | collective-permute-start | bytes 442376 | tf_op jit(solution)/shard_map/ppermute | solution.py:161
  39.8 0.0 collective-permute-done.7
  39.8 0.1 fusion.6.refs_6_
  39.9 2.6 %own_part.1 = (f32[128,1024]{1,0:T(8,128)S(1)}, f32[128,128]{1,0:T(8,128)S(1)}) custom-call(bf16[64,1024]{1,0:T(8,128)(2,1)S(1)} %get-tuple-element.12.qe_ref, bf16[64,1024]{1,0:T(8,128)(2,1)S(1)} %get-tuple-element.13.qi_ref, bf16[2,64,1024]{2,1,0:T(8,128)(2,1)S(1)} %get-tuple-element.14.refs_0_.own_ref, ...), custom_call_target="tpu_custom_call" | custom-call | flops 201326592 | bytes 2490368 | tf_op jit(solution)/shard_map/own_part/pallas_call | solution.py:25
  42.5 1.0 %collective-permute-done.9.edge_ref = bf16[64,1152]{1,0:T(8,128)(2,1)S(1)} collective-permute-done((bf16[64,1152]{1,0:T(8,128)(2,1)S(1)}, bf16[64,1152]{1,0:T(8,128)(2,1)S(1)}, u32[]{:S(2)}, u32[]{:S(2)}) %collective-permute-start.9) | collective-permute-done | bytes 147488 | tf_op jit(solution)/shard_map/ppermute | solution.py:161
  43.5 1.5 %merge.1 = bf16[8,16,1024]{2,1,0:T(8,128)(2,1)} custom-call(f32[128,1024]{1,0:T(8,128)S(1)} %get-tuple-element.17.own_ref, f32[128,128]{1,0:T(8,128)S(1)} %get-tuple-element.18.lse_ref, bf16[64,1152]{1,0:T(8,128)(2,1)S(1)} %collective-permute-done.9.edge_ref, bf16[64,1152]{1,0:T(8,128)(2,1)S(1)} %collective-permute-done.11.inner_ref, ...), custom_call_target="tpu_custom_call" | custom-call | flops 268435456 | bytes 3244032 | tf_op jit(solution)/shard_map/merge/pallas_call | solution.py:25
  (11 shorter events, 0.2 us)
Async XLA Ops:
  0.0 1.0 %copy-start.1 = (bf16[2,8,16,1024]{3,2,1,0:T(8,128)(2,1)S(1)}, bf16[2,8,16,1024]{3,2,1,0:T(8,128)(2,1)}, u32[]{:S(2)}) copy-start(bf16[2,8,16,1024]{3,2,1,0:T(8,128)(2,1)} %kv_ref.1) | copy-start | bytes 1572868
  1.0 0.9 %copy-start.2 = (bf16[8,16,1024]{2,1,0:T(8,128)(2,1)S(1)}, bf16[8,16,1024]{2,1,0:T(8,128)(2,1)}, u32[]{:S(2)}) copy-start(bf16[8,16,1024]{2,1,0:T(8,128)(2,1)} %q_ref.1) | copy-start | bytes 786436
  2.3 15.1 %collective-permute-start = (bf16[2,64,1024]{2,1,0:T(8,128)(2,1)S(1)}, bf16[2,64,1024]{2,1,0:T(8,128)(2,1)S(1)}, u32[]{:S(2)}, u32[]{:S(2)}) collective-permute-start(bf16[2,64,1024]{2,1,0:T(8,128)(2,1)S(1)} %get-tuple-element.14.refs_0_.own_ref), channel_id=1, source_target_pairs={{0,8},{8,0},{16,24},{24,16},{1,9},{9,1},{17,25},{25,17},{2,10},{10... | collective-permute-start | bytes 786440 | tf_op jit(solution)/shard_map/ppermute | solution.py:156
  5.3 15.8 %collective-permute-start.1 = (bf16[2,64,1024]{2,1,0:T(8,128)(2,1)S(1)}, bf16[2,64,1024]{2,1,0:T(8,128)(2,1)S(1)}, u32[]{:S(2)}, u32[]{:S(2)}) collective-permute-start(bf16[2,64,1024]{2,1,0:T(8,128)(2,1)S(1)} %get-tuple-element.15.refs_1_.own_ref), channel_id=1, source_target_pairs={{0,8},{8,0},{16,24},{24,16},{1,9},{9,1},{17,25},{25,17},{2,10},{10... | collective-permute-start | bytes 786440 | tf_op jit(solution)/shard_map/ppermute | solution.py:156
  5.4 12.0 %collective-permute-start.4 = (bf16[2,2,1024]{2,1,0:T(2,128)(2,1)S(1)}, bf16[2,2,1024]{2,1,0:T(2,128)(2,1)S(1)}, u32[]{:S(2)}, u32[]{:S(2)}) collective-permute-start(bf16[2,2,1024]{2,1,0:T(2,128)(2,1)S(1)} %reshape.3), channel_id=1, source_target_pairs={{0,8},{8,0},{16,24},{24,16},{1,9},{9,1},{17,25},{25,17},{2,10},{10... | collective-permute-start | bytes 24584 | tf_op jit(solution)/shard_map/ppermute | solution.py:156
  17.4 16.4 %collective-permute-start.2 = (bf16[2,64,1024]{2,1,0:T(8,128)(2,1)S(1)}, bf16[2,64,1024]{2,1,0:T(8,128)(2,1)S(1)}, u32[]{:S(2)}, u32[]{:S(2)}) collective-permute-start(bf16[2,64,1024]{2,1,0:T(8,128)(2,1)S(1)} %collective-permute-done.refs_2_.pair_ref), channel_id=1, source_target_pairs={{0,16},{24,8},{1,17},{25,9},{2,18},{26,10},{3,19},{27,11},{4,20},{... | collective-permute-start | bytes 786440 | tf_op jit(solution)/shard_map/ppermute | solution.py:167
  21.1 10.4 %collective-permute-start.3 = (bf16[2,64,1024]{2,1,0:T(8,128)(2,1)S(1)}, bf16[2,64,1024]{2,1,0:T(8,128)(2,1)S(1)}, u32[]{:S(2)}, u32[]{:S(2)}) collective-permute-start(bf16[2,64,1024]{2,1,0:T(8,128)(2,1)S(1)} %collective-permute-done.1.refs_3_.pair_ref), channel_id=1, source_target_pairs={{0,16},{24,8},{1,17},{25,9},{2,18},{26,10},{3,19},{27,11},{4,20},{... | collective-permute-start | bytes 786440 | tf_op jit(solution)/shard_map/ppermute | solution.py:167
  22.5 3.9 %collective-permute-start.5 = (bf16[2,5,1024]{2,1,0:T(8,128)(2,1)S(1)}, bf16[2,5,1024]{2,1,0:T(8,128)(2,1)S(1)}, u32[]{:S(2)}, u32[]{:S(2)}) collective-permute-start(bf16[2,5,1024]{2,1,0:T(8,128)(2,1)S(1)} %pad_maximum_fusion), channel_id=1, source_target_pairs={{0,1},{1,0},{2,3},{3,2},{4,5},{5,4},{6,7},{7,6},{8,9},{9,8},{10,11... | collective-permute-start | bytes 61448 | tf_op jit(solution)/shard_map/ppermute | solution.py:156
  22.6 7.8 %collective-permute-start.10 = (bf16[64,1024]{1,0:T(8,128)(2,1)S(1)}, bf16[64,1024]{1,0:T(8,128)(2,1)S(1)}, u32[]{:S(2)}, u32[]{:S(2)}) collective-permute-start(bf16[64,1024]{1,0:T(8,128)(2,1)S(1)} %get-tuple-element.13.qi_ref), channel_id=1, source_target_pairs={{0,1},{1,0},{2,3},{3,2},{4,5},{5,4},{6,7},{7,6},{8,9},{9,8},{10,11... | collective-permute-start | bytes 393224 | tf_op jit(solution)/shard_map/ppermute | solution.py:156
  23.0 10.8 %collective-permute-start.8 = (bf16[64,1024]{1,0:T(8,128)(2,1)S(1)}, bf16[64,1024]{1,0:T(8,128)(2,1)S(1)}, u32[]{:S(2)}, u32[]{:S(2)}) collective-permute-start(bf16[64,1024]{1,0:T(8,128)(2,1)S(1)} %get-tuple-element.12.qe_ref), channel_id=1, source_target_pairs={{0,7},{1,2},{2,1},{3,4},{4,3},{5,6},{6,5},{7,0},{8,15},{9,10},{10,... | collective-permute-start | bytes 393224 | tf_op jit(solution)/shard_map/ppermute | solution.py:161
  26.4 3.8 %collective-permute-start.6 = (bf16[2,2,1024]{2,1,0:T(2,128)(2,1)S(1)}, bf16[2,2,1024]{2,1,0:T(2,128)(2,1)S(1)}, u32[]{:S(2)}, u32[]{:S(2)}) collective-permute-start(bf16[2,2,1024]{2,1,0:T(2,128)(2,1)S(1)} %pad_maximum_fusion.2), channel_id=1, source_target_pairs={{0,2},{1,3},{2,0},{3,1},{4,6},{5,7},{6,4},{7,5},{8,10},{9,11},{10,... | collective-permute-start | bytes 24584 | tf_op jit(solution)/shard_map/ppermute | solution.py:156
  30.2 13.3 %copy-start = (bf16[1024,1024]{1,0:T(8,128)(2,1)S(1)}, bf16[1024,1024]{1,0:T(8,128)(2,1)}, u32[]{:S(2)}) copy-start(bf16[1024,1024]{1,0:T(8,128)(2,1)} %weight_ref.1) | copy-start | bytes 6291460
  30.2 9.6 %collective-permute-start.7 = (bf16[2,4,1024]{2,1,0:T(4,128)(2,1)S(1)}, bf16[2,4,1024]{2,1,0:T(4,128)(2,1)S(1)}, u32[]{:S(2)}, u32[]{:S(2)}) collective-permute-start(bf16[2,4,1024]{2,1,0:T(4,128)(2,1)S(1)} %pad_maximum_fusion.1), channel_id=1, source_target_pairs={{0,16},{8,24},{16,0},{24,8},{1,17},{9,25},{17,1},{25,9},{2,18},{10... | collective-permute-start | bytes 49160 | tf_op jit(solution)/shard_map/ppermute | solution.py:156
  33.8 8.7 %collective-permute-start.11 = (bf16[64,1152]{1,0:T(8,128)(2,1)S(1)}, bf16[64,1152]{1,0:T(8,128)(2,1)S(1)}, u32[]{:S(2)}, u32[]{:S(2)}) collective-permute-start(bf16[64,1152]{1,0:T(8,128)(2,1)S(1)} %inner_part.1), channel_id=1, source_target_pairs={{0,1},{1,0},{2,3},{3,2},{4,5},{5,4},{6,7},{7,6},{8,9},{9,8},{10,11... | collective-permute-start | bytes 442376 | tf_op jit(solution)/shard_map/ppermute | solution.py:156
  36.1 7.5 %collective-permute-start.9 = (bf16[64,1152]{1,0:T(8,128)(2,1)S(1)}, bf16[64,1152]{1,0:T(8,128)(2,1)S(1)}, u32[]{:S(2)}, u32[]{:S(2)}) collective-permute-start(bf16[64,1152]{1,0:T(8,128)(2,1)S(1)} %edge_part.1), channel_id=1, source_target_pairs={{0,7},{1,2},{2,1},{3,4},{4,3},{5,6},{6,5},{7,0},{8,15},{9,10},{10,... | collective-permute-start | bytes 442376 | tf_op jit(solution)/shard_map/ppermute | solution.py:161

commit v2 on v1

--- a/solution.py
+++ b/solution.py
@@ -14,6 +14,7 @@
 SPAN = TILE * TILE
 SCALE = 1.0 / math.sqrt(HEAD_DIM)
 NEG = -1e30
+LIMIT = 16 * 1024 * 1024
 F32 = jnp.float32
 BF16 = jnp.bfloat16
 VMEM = pl.BlockSpec(memory_space=pltpu.VMEM)
@@ -28,7 +29,7 @@
         in_specs=[VMEM] * len(args),
         out_specs=[VMEM] * len(outs),
         name=name,
-        compiler_params=pltpu.CompilerParams(vmem_limit_bytes=16 * 1024 * 1024),
+        compiler_params=pltpu.CompilerParams(vmem_limit_bytes=LIMIT),
         cost_estimate=pl.CostEstimate(flops=flops, bytes_accessed=moved, transcendentals=0),
     )(*args)
 
@@ -49,48 +50,69 @@
     return jnp.where(odd, right, left), jnp.where(odd, left, right)
 
 
-def split_kernel(q_ref, kv_ref, qe_ref, qi_ref, kve_ref, kvi_ref, pool_ref):
+def split_kernel(q_hbm, kv_hbm, qe_ref, qi_ref, edge_ref, inner_ref, pool_ref, q_ref, kv_ref, sems):
+    copies = [pltpu.make_async_copy(kv_hbm.at[i], kv_ref.at[i], sems.at[i]) for i in range(2)]
+    copies.append(pltpu.make_async_copy(q_hbm, q_ref, sems.at[2]))
+    for copy in copies:
+        copy.start()
     odd = odd_column()
+    pooled = []
+    for half in range(2):
+        copies[half].wait()
+        edge, inner = split_tiles(kv_ref[half].astype(F32), odd)
+        rows = slice(half * SPAN, (half + 1) * SPAN)
+        edge_ref[rows] = edge.astype(BF16)
+        inner_ref[rows] = inner.astype(BF16)
+        for tile in (edge, inner):
+            pooled.append(jnp.sum(tile, axis=0, keepdims=True) * (1.0 / SPAN))
+    pooled = jnp.concatenate(pooled, axis=0).astype(BF16)
+    pool_ref[...] = pooled
+    edge_ref[2 * SPAN :] = pooled
+    copies[2].wait()
     edge, inner = split_tiles(q_ref[...].astype(F32), odd)
     qe_ref[...] = edge.astype(BF16)
     qi_ref[...] = inner.astype(BF16)
-    pooled = []
-    for half in range(2):
-        edge, inner = split_tiles(kv_ref[half].astype(F32), odd)
-        kve_ref[half] = edge.astype(BF16)
-        kvi_ref[half] = inner.astype(BF16)
-        for tile in (edge, inner):
-            pooled.append(jnp.sum(tile, axis=0, keepdims=True) * (1.0 / SPAN))
-    pool_ref[...] = jnp.concatenate(pooled, axis=0).astype(BF16)
 
 
 def logits(q, k):
     return lax.dot_general(q, k, (((1,), (1,)), ((), ())), preferred_element_type=F32) * SCALE
 
 
+def heads():
+    return [slice(h * HEAD_DIM, (h + 1) * HEAD_DIM) for h in range(HEADS)]
+
+
+def stacked(refs, half, cols):
+    return jnp.concatenate([r[half * SPAN : (half + 1) * SPAN, cols] for r in refs], axis=0)
+
+
 def partial_kernel(n_lat, q_ref, own_ref, pair_ref, far_ref, out_ref):
+    tiles = (own_ref, pair_ref, far_ref)
     far = far_exists(n_lat)
     lane = lax.broadcasted_iota(jnp.int32, (SPAN, 3 * SPAN), 1)
     keep = jnp.logical_or(lane < 2 * SPAN, far)
     column = lax.broadcasted_iota(jnp.int32, (SPAN, HEAD_DIM), 1)
+    scores = [
+        jnp.where(keep, logits(q_ref[:, cols], stacked(tiles, 0, cols)), NEG) for cols in heads()
+    ]
+    tops = [jnp.max(s, axis=-1, keepdims=True) for s in scores]
+    expos = [jnp.exp(s - top) for s, top in zip(scores, tops)]
+    totals = [jnp.sum(e, axis=-1, keepdims=True) for e in expos]
+    parts = [
+        jnp.dot(e.astype(BF16), stacked(tiles, 1, cols), preferred_element_type=F32)
+        for e, cols in zip(expos, heads())
+    ]
     stats = jnp.zeros((SPAN, HEAD_DIM), F32)
     for h in range(HEADS):
-        cols = slice(h * HEAD_DIM, (h + 1) * HEAD_DIM)
-        k = jnp.concatenate([r[0, :, cols] for r in (own_ref, pair_ref, far_ref)], axis=0)
-        v = jnp.concatenate([r[1, :, cols] for r in (own_ref, pair_ref, far_ref)], axis=0)
-        s = jnp.where(keep, logits(q_ref[:, cols], k), NEG)
-        top = jnp.max(s, axis=-1, keepdims=True)
-        expo = jnp.exp(s - top)
-        total = jnp.sum(expo, axis=-1, keepdims=True)
-        part = jnp.dot(expo.astype(BF16), v, preferred_element_type=F32)
-        out_ref[:, cols] = (part / total).astype(BF16)
-        lse = top + jnp.log(total)
+        lse = tops[h] + jnp.log(totals[h])
         high = lse.astype(BF16).astype(F32)
         mid = (lse - high).astype(BF16).astype(F32)
         low = lse - high - mid
         stats = jnp.where(column == h, high, stats)
         stats = jnp.where(column == HEADS + h, mid, stats)
         stats = jnp.where(column == 2 * HEADS + h, low, stats)
+    for h, cols in enumerate(heads()):
+        out_ref[:, cols] = (parts[h] * (1.0 / totals[h])).astype(BF16)
     out_ref[:, HEADS * HEAD_DIM :] = stats.astype(BF16)
 
 
@@ -104,25 +126,31 @@
     bias = jnp.where(entry < count, math.log(SPAN), math.log(4 * SPAN)).astype(F32)
     column = lax.broadcasted_iota(jnp.int32, (rows, HEAD_DIM), 1)
     stats = jnp.zeros((rows, HEAD_DIM), F32)
-    for h in range(HEADS):
-        cols = slice(h * HEAD_DIM, (h + 1) * HEAD_DIM)
-        q = jnp.concatenate([qe_ref[:, cols], qi_ref[:, cols]], axis=0)
-        k = jnp.concatenate([r[0, :, cols] for r in tiles], axis=0)
-        v = jnp.concatenate([r[1, :, cols] for r in tiles], axis=0)
-        near = jnp.where(keep, logits(q, k), NEG)
-        coarse = logits(q, coarse_ref[0, :, cols])[:, : 2 * count] + bias
-        top = jnp.maximum(
-            jnp.max(near, axis=-1, keepdims=True), jnp.max(coarse, axis=-1, keepdims=True)
-        )
-        near = jnp.exp(near - top)
-        coarse = jnp.exp(coarse - top)
-        total = jnp.sum(near, axis=-1, keepdims=True) + jnp.sum(coarse, axis=-1, keepdims=True)
-        part = jnp.dot(near.astype(BF16), v, preferred_element_type=F32)
-        part += jnp.dot(
-            coarse.astype(BF16), coarse_ref[1, : 2 * count, cols], preferred_element_type=F32
-        )
-        out_ref[:, cols] = part / total
-        stats = jnp.where(column == h, top + jnp.log(total), stats)
+    for group in range(0, HEADS, 4):
+        near, coarse = [], []
+        for cols in heads()[group : group + 4]:
+            q = jnp.concatenate([qe_ref[:, cols], qi_ref[:, cols]], axis=0)
+            near.append(jnp.where(keep, logits(q, stacked(tiles, 0, cols)), NEG))
+            coarse.append(logits(q, coarse_ref[0, :, cols])[:, : 2 * count] + bias)
+        tops = [
+            jnp.maximum(jnp.max(n, axis=-1, keepdims=True), jnp.max(c, axis=-1, keepdims=True))
+            for n, c in zip(near, coarse)
+        ]
+        near = [jnp.exp(n - top) for n, top in zip(near, tops)]
+        coarse = [jnp.exp(c - top) for c, top in zip(coarse, tops)]
+        totals = [
+            jnp.sum(n, axis=-1, keepdims=True) + jnp.sum(c, axis=-1, keepdims=True)
+            for n, c in zip(near, coarse)
+        ]
+        for i, cols in enumerate(heads()[group : group + 4]):
+            part = jnp.dot(
+                near[i].astype(BF16), stacked(tiles, 1, cols), preferred_element_type=F32
+            )
+            part += jnp.dot(
+                coarse[i].astype(BF16), coarse_ref[1, : 2 * count, cols], preferred_element_type=F32
+            )
+            out_ref[:, cols] = part * (1.0 / totals[i])
+            stats = jnp.where(column == group + i, tops[i] + jnp.log(totals[i]), stats)
     lse_ref[...] = stats
 
 
@@ -161,10 +189,25 @@
     return lax.ppermute(x, axis, [(i, (i + (1 if i % 2 else -1)) % count) for i in range(count)])
 
 
-def onward(x, axis):
+def stride(x, axis, step):
     count = lax.axis_size(axis)
-    route = [(i, i + (-2 if i % 2 else 2)) for i in range(count)]
-    return lax.ppermute(x, axis, [(s, t) for s, t in route if 0 <= t < count])
+    route = [(i, (i + (-step if i % 2 else step)) % count) for i in range(count)]
+    return lax.ppermute(x, axis, route)
+
+
+def after_kernel(*refs):
+    pass
+
+
+def after(x, *tokens):
+    return pl.pallas_call(
+        after_kernel,
+        out_shape=jax.ShapeDtypeStruct(x.shape, x.dtype),
+        in_specs=[pl.BlockSpec(memory_space=pl.ANY)] * (1 + len(tokens)),
+        out_specs=pl.BlockSpec(memory_space=pl.ANY),
+        input_output_aliases={0: 0},
+        name="after",
+    )(x, *tokens)
 
 
 def mean_entries(*entries):
@@ -175,28 +218,44 @@
 def shards(queries, keys_values, out_weight):
     n_lat = lax.axis_size("lat")
     width = queries.shape[-1]
-    tile = jax.ShapeDtypeStruct((SPAN, width), BF16)
-    pair = jax.ShapeDtypeStruct((2, SPAN, width), BF16)
-    q_edge, q_inner, edge_own, inner_own, pooled = call(
+    def like(*shape):
+        return jax.ShapeDtypeStruct(shape, BF16)
+
+    pack = 2 * SPAN + 4
+    q_edge, q_inner, edge_own, inner_own, pooled = pl.pallas_call(
         split_kernel,
-        [tile, tile, pair, pair, jax.ShapeDtypeStruct((4, width), BF16)],
-        "split",
-        0,
-        queries,
-        keys_values,
-    )
+        out_shape=[
+            like(SPAN, width),
+            like(SPAN, width),
+            like(pack, width),
+            like(2 * SPAN, width),
+            like(4, width),
+        ],
+        in_specs=[pl.BlockSpec(memory_space=pltpu.HBM)] * 2,
+        out_specs=[VMEM] * 5,
+        scratch_shapes=[
+            pltpu.VMEM(queries.shape, BF16),
+            pltpu.VMEM(keys_values.shape, BF16),
+            pltpu.SemaphoreType.DMA((3,)),
+        ],
+        name="split",
+        compiler_params=pltpu.CompilerParams(vmem_limit_bytes=LIMIT),
+        cost_estimate=pl.CostEstimate(flops=0, bytes_accessed=2 << 20, transcendentals=0),
+    )(*(pltpu.with_memory_space_constraint(x, pltpu.HBM) for x in (queries, keys_values)))
     edge_pair = swap(edge_own, "lat", 1)
     far_q_edge = outward(q_edge, "lon")
     far_q_inner = swap(q_inner, "lon", 1)
+    inner_pair = swap(inner_own, "lat", 1)
+    edge_pair = after(edge_pair, far_q_edge, far_q_inner)
+    edge_far = stride(edge_pair, "lat", 2)
     level0 = pooled.reshape(2, 2, width)
-    level0_lat = swap(level0, "lat", 1)
-    inner_pair = swap(inner_own, "lat", 1)
-    edge_far = onward(edge_pair, "lat")
-    inner_far = onward(inner_pair, "lat")
+    level0_lat = edge_pair[2 * SPAN :].reshape(2, 2, width)
     mine = mean_entries(level0[:, 0:1], level0[:, 1:2], level0_lat[:, 0:1], level0_lat[:, 1:2])
     beside = swap(jnp.concatenate([level0, level0_lat, mine], axis=1), "lon", 1)
     group = jnp.concatenate([mine, beside[:, 4:5]], axis=1)
     group_lon = swap(group, "lon", 2)
+    inner_pair = after(inner_pair, group_lon)
+    inner_far = stride(inner_pair, "lat", 2)
     group_lat = swap(jnp.concatenate([group, group_lon], axis=1), "lat", 2)
     coarse = jnp.concatenate([level0_lat, beside[:, 0:4], group_lon, group_lat], axis=1)
     count = coarse.shape[1] // 2
@@ -215,6 +274,7 @@
         edge_far,
     )[0]
     edge_back = outward(edge_part, "lon")
+    inner_far = after(inner_far, edge_part)
     inner_part = call(
         functools.partial(partial_kernel, n_lat),
         [back],
@@ -226,6 +286,7 @@
         inner_far,
     )[0]
     inner_back = swap(inner_part, "lon", 1)
+    coarse = after(coarse, inner_part)
     own, lse = call(
         functools.partial(own_kernel, n_lat, count),
         [

time: 45.3 us -> 44.1 us (0.974)
  local copies, waits for them, and re-layouts: 2.03 us -> 12.6 us
  waiting for transfers between devices: 16.1 us -> 6.77 us
  starting transfers between devices: 17.8 us -> 13.8 us
  other arithmetic: 0.19 us -> 1.51 us
    ppermute x8 -> x7, waiting for transfers between devices: 13.8 us -> 2.27 us  [swap(): return lax.ppermute(x, axis, [(i, i ^ distance) for i in range(count)])]
    unnamed x6 -> x42, local copies, waits for them, and re-layouts: 2 us -> 11.8 us
    ppermute x2, waiting for transfers between devices: 1.05 us -> 3.53 us  [outward(): lax.ppermute(x, axis, [(i, (i + (1 if i % 2 else -1)) % count) for i in r...]
    ppermute x2, starting transfers between devices: 4.99 us -> 2.71 us  [stride(): return lax.ppermute(x, axis, route)]
    pallas_call x5 -> x4, Pallas kernels: 8.73 us -> 6.64 us  [call(): pl.pallas_call(kernel, out_shape=outs, in_specs=[VMEM] * len(args), out_s...]
    pallas_call x0 -> x5, Pallas kernels: none -> 2.06 us  [the longest x1 2.06 us: shards(): pl.pallas_call(split_kernel, out_shape=[like(SPAN, width), like(SPAN, wid...]
    ppermute x2, starting transfers between devices: 7.04 us -> 4.99 us  [outward(): lax.ppermute(x, axis, [(i, (i + (1 if i % 2 else -1)) % count) for i in r...]
    slice x0 -> x1, local copies, waits for them, and re-layouts: none -> 0.79 us  [shards(): level0_lat = edge_pair[2 * SPAN:].reshape(2, 2, width)]
  transfers between devices with their start and end apart: 12 -> 11, of which waited for: 4 -> 3; matrix products, arithmetic and copies ran while one was open for 0% -> 5% of each run, Pallas kernels for 15% -> 10%
where the time goes in v2:
time: 44.1 us; the launch traced here: 43.5 us
  starting transfers between devices  13.8 us (31%)
  local copies, waits for them, and re-layouts  12.6 us (29%)
  Pallas kernels  8.7 us (20%)
  waiting for transfers between devices  6.77 us (15%)
  other arithmetic  1.51 us (3%)
    unnamed x42, local copies, waits for them, and re-layouts  11.8 us
    pallas_call x4, Pallas kernels, call(): pl.pallas_call(kernel, out_shape=outs, in_specs=[VMEM] * len(args), out_s...  6.64 us
    ppermute x7, starting transfers between devices, swap(): return lax.ppermute(x, axis, [(i, i ^ distance) for i in range(count)])  6.1 us
    ppermute x2, starting transfers between devices, outward(): lax.ppermute(x, axis, [(i, (i + (1 if i % 2 else -1)) % count) for i in r...  4.99 us
    ppermute x2, waiting for transfers between devices, outward(): lax.ppermute(x, axis, [(i, (i + (1 if i % 2 else -1)) % count) for i in r...  3.53 us
    ppermute x2, starting transfers between devices, stride(): return lax.ppermute(x, axis, route)  2.71 us
    ppermute x7, waiting for transfers between devices, swap(): return lax.ppermute(x, axis, [(i, i ^ distance) for i in range(count)])  2.27 us
    pallas_call x1, Pallas kernels, shards(): pl.pallas_call(split_kernel, out_shape=[like(SPAN, width), like(SPAN, wid...  2.06 us
  transfers between devices with their start and end apart: 11, of which 3 were waited for; matrix products, arithmetic and copies ran while one was open for 5% of the time, Pallas kernels for 10%

profile of v2, /device:TPU:0, one launch (start us, length us, event | category | flops | bytes accessed | tf_op | source)
XLA Modules:
  0.0 43.5 jit_solution(12986236256160802432)
XLA Ops:
  0.0 2.1 %split.1 = (bf16[64,1024]{1,0:T(8,128)(2,1)}, bf16[64,1024]{1,0:T(8,128)(2,1)}, bf16[132,1024]{1,0:T(8,128)(2,1)S(1)}, bf16[128,1024]{1,0:T(8,128)(2,1)S(1)}, bf16[4,1024]{1,0:T(4,128)(2,1)S(1)}) custom-call(bf16[8,16,1024]{2,1,0:T(8,128)(2,1)} %q_hbm.1, bf16[2,8,16,1024]{3,2,1,0:T(8,128)(2,1)} %kv_hbm.1), custom_call_target="tpu_custom_call" | custom-call | bytes 2097152 | tf_op jit(solution)/shard_map/split/pallas_call | solution.py:225
  2.1 3.0 %collective-permute-start = (bf16[132,1024]{1,0:T(8,128)(2,1)S(1)}, bf16[132,1024]{1,0:T(8,128)(2,1)S(1)}, u32[]{:S(2)}, u32[]{:S(2)}) collective-permute-start(bf16[132,1024]{1,0:T(8,128)(2,1)S(1)} %get-tuple-element.14.own_ref.refs_0_), channel_id=1, source_target_pairs={{0,8},{8,0},{16,24},{24,16},{1,9},{9,1},{17,25},{25,17},{2,10},{10... | collective-permute-start | bytes 811016 | tf_op jit(solution)/shard_map/ppermute | solution.py:184
  5.1 2.8 %collective-permute-start.1 = (bf16[64,1024]{1,0:T(8,128)(2,1)}, bf16[64,1024]{1,0:T(8,128)(2,1)S(1)}, u32[]{:S(2)}, u32[]{:S(2)}) collective-permute-start(bf16[64,1024]{1,0:T(8,128)(2,1)} %get-tuple-element.12.qe_ref), channel_id=1, source_target_pairs={{0,7},{1,2},{2,1},{3,4},{4,3},{5,6},{6,5},{7,0},{8,15},{9,10},{10,... | collective-permute-start | bytes 393224 | tf_op jit(solution)/shard_map/ppermute | solution.py:189
  8.4 0.7 %copy-done.10 = bf16[128,1024]{1,0:T(8,128)(2,1)} copy-done((bf16[128,1024]{1,0:T(8,128)(2,1)}, bf16[128,1024]{1,0:T(8,128)(2,1)S(1)}, u32[]{:S(2)}) %copy-start.10) | copy-done | bytes 262168
  9.1 3.5 %collective-permute-done.1.refs_1_.q_ref = bf16[64,1024]{1,0:T(8,128)(2,1)S(1)} collective-permute-done((bf16[64,1024]{1,0:T(8,128)(2,1)}, bf16[64,1024]{1,0:T(8,128)(2,1)S(1)}, u32[]{:S(2)}, u32[]{:S(2)}) %collective-permute-start.1) | collective-permute-done | bytes 131104 | tf_op jit(solution)/shard_map/ppermute | solution.py:189
  12.6 0.6 %copy-done.15 = bf16[64,1024]{1,0:T(8,128)(2,1)} copy-done((bf16[64,1024]{1,0:T(8,128)(2,1)}, bf16[64,1024]{1,0:T(8,128)(2,1)S(1)}, u32[]{:S(2)}) %copy-start.15) | copy-done | bytes 131096
  13.3 0.7 %copy-done = bf16[132,1024]{1,0:T(8,128)(2,1)} copy-done((bf16[132,1024]{1,0:T(8,128)(2,1)}, bf16[132,1024]{1,0:T(8,128)(2,1)S(1)}, u32[]{:S(2)}) %copy-start) | copy-done | bytes 270360
  14.0 0.8 %slice.30 = bf16[4,1024]{1,0:T(4,128)(2,1)S(1)} slice(bf16[132,1024]{1,0:T(8,128)(2,1)} %after.4.pair_ref.refs_2_), slice={[128:132], [0:1024]} | slice | bytes 16384 | tf_op jit(solution)/shard_map/slice | solution.py:252
  15.0 1.6 %collective-permute-start.6 = (bf16[132,1024]{1,0:T(8,128)(2,1)}, bf16[132,1024]{1,0:T(8,128)(2,1)S(1)}, u32[]{:S(2)}, u32[]{:S(2)}) collective-permute-start(bf16[132,1024]{1,0:T(8,128)(2,1)} %after.4.pair_ref.refs_2_), channel_id=1, source_target_pairs={{0,16},{8,24},{16,0},{24,8},{1,17},{9,25},{17,1},{25,9},{2,18},{10... | collective-permute-start | bytes 811016 | tf_op jit(solution)/shard_map/ppermute | solution.py:195
  16.6 1.5 %collective-permute-start.5 = (bf16[2,2,1024]{2,1,0:T(2,128)(2,1)S(1)}, bf16[2,2,1024]{2,1,0:T(2,128)(2,1)S(1)}, u32[]{:S(2)}, u32[]{:S(2)}) collective-permute-start(bf16[2,2,1024]{2,1,0:T(2,128)(2,1)S(1)} %pad_maximum_fusion.2), channel_id=1, source_target_pairs={{0,2},{1,3},{2,0},{3,1},{4,6},{5,7},{6,4},{7,5},{8,10},{9,11},{10,... | collective-permute-start | bytes 24584 | tf_op jit(solution)/shard_map/ppermute | solution.py:184
  18.1 2.3 %collective-permute-done.5.refs_1_ = bf16[2,2,1024]{2,1,0:T(2,128)(2,1)S(1)} collective-permute-done((bf16[2,2,1024]{2,1,0:T(2,128)(2,1)S(1)}, bf16[2,2,1024]{2,1,0:T(2,128)(2,1)S(1)}, u32[]{:S(2)}, u32[]{:S(2)}) %collective-permute-start.5) | collective-permute-done | bytes 8224 | tf_op jit(solution)/shard_map/ppermute | solution.py:184
  20.4 0.6 %copy-done.19 = bf16[2,2,1024]{2,1,0:T(2,128)(2,1)} copy-done((bf16[2,2,1024]{2,1,0:T(2,128)(2,1)}, bf16[2,2,1024]{2,1,0:T(2,128)(2,1)S(1)}, u32[]{:S(2)}) %copy-start.19) | copy-done | bytes 8216
  20.9 1.1 %collective-permute-start.7 = (bf16[128,1024]{1,0:T(8,128)(2,1)}, bf16[128,1024]{1,0:T(8,128)(2,1)S(1)}, u32[]{:S(2)}, u32[]{:S(2)}) collective-permute-start(bf16[128,1024]{1,0:T(8,128)(2,1)} %after.5.pair_ref.refs_3_), channel_id=1, source_target_pairs={{0,16},{8,24},{16,0},{24,8},{1,17},{9,25},{17,1},{25,9},{2,18},{10... | collective-permute-start | bytes 786440 | tf_op jit(solution)/shard_map/ppermute | solution.py:195
  22.1 0.7 %pad_maximum_fusion.1 = bf16[2,4,1024]{2,1,0:T(4,128)(2,1)S(1)} fusion(bf16[2,2,1024]{2,1,0:T(2,128)(2,1)} %copy-done.19, bf16[2,1,1024]{2,1,0:T(2,128)(2,1)S(1)} %slice.33, bf16[2,1,1024]{2,1,0:T(2,128)(2,1)S(1)} %fusion.11), kind=kLoop, calls=%fused_computation.9 | loop fusion | flops 49152 | bytes 32768 | tf_op jit(solution)/shard_map/concatenate | solution.py:259
  22.8 1.0 %collective-permute-start.8 = (bf16[2,4,1024]{2,1,0:T(4,128)(2,1)S(1)}, bf16[2,4,1024]{2,1,0:T(4,128)(2,1)S(1)}, u32[]{:S(2)}, u32[]{:S(2)}) collective-permute-start(bf16[2,4,1024]{2,1,0:T(4,128)(2,1)S(1)} %pad_maximum_fusion.1), channel_id=1, source_target_pairs={{0,16},{8,24},{16,0},{24,8},{1,17},{9,25},{17,1},{25,9},{2,18},{10... | collective-permute-start | bytes 49160 | tf_op jit(solution)/shard_map/ppermute | solution.py:184
  23.8 1.0 %collective-permute-done.6.far_ref.refs_4_ = bf16[132,1024]{1,0:T(8,128)(2,1)S(1)} collective-permute-done((bf16[132,1024]{1,0:T(8,128)(2,1)}, bf16[132,1024]{1,0:T(8,128)(2,1)S(1)}, u32[]{:S(2)}, u32[]{:S(2)}) %collective-permute-start.6) | collective-permute-done | bytes 270368 | tf_op jit(solution)/shard_map/ppermute | solution.py:195
  24.7 1.0 %copy-done.1 = bf16[132,1024]{1,0:T(8,128)(2,1)S(1)} copy-done((bf16[132,1024]{1,0:T(8,128)(2,1)S(1)}, bf16[132,1024]{1,0:T(8,128)(2,1)}, u32[]{:S(2)}) %copy-start.1) | copy-done | bytes 270360
  25.7 0.9 %copy-done.16 = bf16[64,1024]{1,0:T(8,128)(2,1)S(1)} copy-done((bf16[64,1024]{1,0:T(8,128)(2,1)S(1)}, bf16[64,1024]{1,0:T(8,128)(2,1)}, u32[]{:S(2)}) %copy-start.16) | copy-done | bytes 131096
  26.6 1.3 %edge_part.1.refs_1_ = bf16[64,1152]{1,0:T(8,128)(2,1)} custom-call(bf16[64,1024]{1,0:T(8,128)(2,1)S(1)} %copy-done.16, bf16[132,1024]{1,0:T(8,128)(2,1)S(1)} %get-tuple-element.14.own_ref.refs_0_, bf16[132,1024]{1,0:T(8,128)(2,1)S(1)} %copy-done.1, bf16[132,1024]{1,0:T(8,128)(2,1)S(1)} %collective-permute-done.6.far_ref.refs_4_), custom_call_target="tpu_custom_call" | custom-call | flops 50331648 | bytes 1089536 | tf_op jit(solution)/shard_map/edge_part/pallas_call | solution.py:26
  27.9 2.2 %collective-permute-start.9 = (bf16[64,1152]{1,0:T(8,128)(2,1)}, bf16[64,1152]{1,0:T(8,128)(2,1)}, u32[]{:S(2)}, u32[]{:S(2)}) collective-permute-start(bf16[64,1152]{1,0:T(8,128)(2,1)} %edge_part.1.refs_1_), channel_id=1, source_target_pairs={{0,7},{1,2},{2,1},{3,4},{4,3},{5,6},{6,5},{7,0},{8,15},{9,10},{10,... | collective-permute-start | bytes 442376 | tf_op jit(solution)/shard_map/ppermute | solution.py:189
  30.1 0.7 %copy-done.6 = bf16[128,1024]{1,0:T(8,128)(2,1)} copy-done((bf16[128,1024]{1,0:T(8,128)(2,1)}, bf16[128,1024]{1,0:T(8,128)(2,1)S(1)}, u32[]{:S(2)}) %copy-start.6) | copy-done | bytes 262168
  30.8 0.9 %copy-done.4 = bf16[128,1024]{1,0:T(8,128)(2,1)S(1)} copy-done((bf16[128,1024]{1,0:T(8,128)(2,1)S(1)}, bf16[128,1024]{1,0:T(8,128)(2,1)}, u32[]{:S(2)}) %copy-start.4) | copy-done | bytes 262168
  31.8 0.9 %copy-done.7 = bf16[128,1024]{1,0:T(8,128)(2,1)S(1)} copy-done((bf16[128,1024]{1,0:T(8,128)(2,1)S(1)}, bf16[128,1024]{1,0:T(8,128)(2,1)}, u32[]{:S(2)}) %copy-start.7) | copy-done | bytes 262168
  32.7 0.9 %copy-done.11 = bf16[128,1024]{1,0:T(8,128)(2,1)S(1)} copy-done((bf16[128,1024]{1,0:T(8,128)(2,1)S(1)}, bf16[128,1024]{1,0:T(8,128)(2,1)}, u32[]{:S(2)}) %copy-start.11) | copy-done | bytes 262168
  33.7 0.9 %copy-done.18 = bf16[64,1024]{1,0:T(8,128)(2,1)S(1)} copy-done((bf16[64,1024]{1,0:T(8,128)(2,1)S(1)}, bf16[64,1024]{1,0:T(8,128)(2,1)}, u32[]{:S(2)}) %copy-start.18) | copy-done | bytes 131096
  34.6 0.6 %inner_part.1.refs_1_ = bf16[64,1152]{1,0:T(8,128)(2,1)S(1)} custom-call(bf16[64,1024]{1,0:T(8,128)(2,1)S(1)} %copy-done.18, bf16[128,1024]{1,0:T(8,128)(2,1)S(1)} %copy-done.11, bf16[128,1024]{1,0:T(8,128)(2,1)S(1)} %copy-done.4, bf16[128,1024]{1,0:T(8,128)(2,1)S(1)} %copy-done.7), custom_call_target="tpu_custom_call" | custom-call | flops 50331648 | bytes 1064960 | tf_op jit(solution)/shard_map/inner_part/pallas_call | solution.py:26
  35.4 0.7 %fusion.6.refs_0_ = bf16[2,16,1024]{2,1,0:T(8,128)(2,1)} fusion(bf16[2,4,1024]{2,1,0:T(4,128)(2,1)S(1)} %collective-permute-done.8, bf16[2,2,1024]{2,1,0:T(2,128)(2,1)S(1)} %copy-done.20, bf16[2,4,1024]{2,1,0:T(4,128)(2,1)S(1)} %slice.34, bf16[2,2,1024]{2,1,0:T(2,128)(2,1)S(1)} %reshape.7), kind=kLoop, calls=%fused_computation.7 | loop fusion | flops 425984 | bytes 114688 | tf_op jit(solution)/shard_map/concatenate | solution.py:260
  36.1 0.9 %copy-done.8 = bf16[128,1024]{1,0:T(8,128)(2,1)S(1)} copy-done((bf16[128,1024]{1,0:T(8,128)(2,1)S(1)}, bf16[128,1024]{1,0:T(8,128)(2,1)}, u32[]{:S(2)}) %copy-start.8) | copy-done | bytes 262168
  37.0 0.9 %copy-done.12 = bf16[128,1024]{1,0:T(8,128)(2,1)S(1)} copy-done((bf16[128,1024]{1,0:T(8,128)(2,1)S(1)}, bf16[128,1024]{1,0:T(8,128)(2,1)}, u32[]{:S(2)}) %copy-start.12) | copy-done | bytes 262168
  38.0 0.8 %copy-done.14 = bf16[2,16,1024]{2,1,0:T(8,128)(2,1)S(1)} copy-done((bf16[2,16,1024]{2,1,0:T(8,128)(2,1)S(1)}, bf16[2,16,1024]{2,1,0:T(8,128)(2,1)}, u32[]{:S(2)}) %copy-start.14) | copy-done | bytes 65560
  38.8 2.2 %own_part.1 = (f32[128,1024]{1,0:T(8,128)S(1)}, f32[128,128]{1,0:T(8,128)S(1)}) custom-call(bf16[64,1024]{1,0:T(8,128)(2,1)} %get-tuple-element.12.qe_ref, bf16[64,1024]{1,0:T(8,128)(2,1)} %get-tuple-element.13.qi_ref, bf16[132,1024]{1,0:T(8,128)(2,1)S(1)} %get-tuple-element.14.own_ref.refs_0_, bf16[128,1024]{1,0:T(8,128)(2,1)S(1)} %copy-done.12, ...), custom_call_target="tpu_custom_call" | custom-call | flops 201326592 | bytes 2514944 | tf_op jit(solution)/shard_map/own_part/pallas_call | solution.py:26
  41.0 2.5 %merge.1 = bf16[8,16,1024]{2,1,0:T(8,128)(2,1)} custom-call(f32[128,1024]{1,0:T(8,128)S(1)} %get-tuple-element.17.own_ref, f32[128,128]{1,0:T(8,128)S(1)} %get-tuple-element.18.lse_ref, bf16[64,1152]{1,0:T(8,128)(2,1)} %collective-permute-done.9.edge_ref, bf16[64,1152]{1,0:T(8,128)(2,1)} %collective-permute-done.10.inner_ref, bf16[1024,1024]{1,0:T(8,128)(2,1)S(1)} %copy-done.9), custom_call_target="tpu_custom_call" | custom-call | flops 268435456 | bytes 3244032 | tf_op jit(solution)/shard_map/merge/pallas_call | solution.py:26
  (51 shorter events, 0.9 us)
Async XLA Ops:
  0.0 41.0 %copy-start.9 = (bf16[1024,1024]{1,0:T(8,128)(2,1)S(1)}, bf16[1024,1024]{1,0:T(8,128)(2,1)}, u32[]{:S(2)}) copy-start(bf16[1024,1024]{1,0:T(8,128)(2,1)} %weight_ref.1) | copy-start | bytes 6291460
  2.1 10.6 %collective-permute-start = (bf16[132,1024]{1,0:T(8,128)(2,1)S(1)}, bf16[132,1024]{1,0:T(8,128)(2,1)S(1)}, u32[]{:S(2)}, u32[]{:S(2)}) collective-permute-start(bf16[132,1024]{1,0:T(8,128)(2,1)S(1)} %get-tuple-element.14.own_ref.refs_0_), channel_id=1, source_target_pairs={{0,8},{8,0},{16,24},{24,16},{1,9},{9,1},{17,25},{25,17},{2,10},{10... | collective-permute-start | bytes 811016 | tf_op jit(solution)/shard_map/ppermute | solution.py:184
  5.1 7.5 %collective-permute-start.1 = (bf16[64,1024]{1,0:T(8,128)(2,1)}, bf16[64,1024]{1,0:T(8,128)(2,1)S(1)}, u32[]{:S(2)}, u32[]{:S(2)}) collective-permute-start(bf16[64,1024]{1,0:T(8,128)(2,1)} %get-tuple-element.12.qe_ref), channel_id=1, source_target_pairs={{0,7},{1,2},{2,1},{3,4},{4,3},{5,6},{6,5},{7,0},{8,15},{9,10},{10,... | collective-permute-start | bytes 393224 | tf_op jit(solution)/shard_map/ppermute | solution.py:189
  7.8 4.8 %collective-permute-start.2 = (bf16[64,1024]{1,0:T(8,128)(2,1)}, bf16[64,1024]{1,0:T(8,128)(2,1)S(1)}, u32[]{:S(2)}, u32[]{:S(2)}) collective-permute-start(bf16[64,1024]{1,0:T(8,128)(2,1)} %get-tuple-element.13.qi_ref), channel_id=1, source_target_pairs={{0,1},{1,0},{2,3},{3,2},{4,5},{5,4},{6,7},{7,6},{8,9},{9,8},{10,11... | collective-permute-start | bytes 393224 | tf_op jit(solution)/shard_map/ppermute | solution.py:184
  7.8 10.2 %collective-permute-start.3 = (bf16[128,1024]{1,0:T(8,128)(2,1)S(1)}, bf16[128,1024]{1,0:T(8,128)(2,1)S(1)}, u32[]{:S(2)}, u32[]{:S(2)}) collective-permute-start(bf16[128,1024]{1,0:T(8,128)(2,1)S(1)} %get-tuple-element.15.own_ref.refs_1_), channel_id=1, source_target_pairs={{0,8},{8,0},{16,24},{24,16},{1,9},{9,1},{17,25},{25,17},{2,10},{10... | collective-permute-start | bytes 786440 | tf_op jit(solution)/shard_map/ppermute | solution.py:184
  8.4 0.7 %copy-start.10 = (bf16[128,1024]{1,0:T(8,128)(2,1)}, bf16[128,1024]{1,0:T(8,128)(2,1)S(1)}, u32[]{:S(2)}) copy-start(bf16[128,1024]{1,0:T(8,128)(2,1)S(1)} %get-tuple-element.15.own_ref.refs_1_) | copy-start | bytes 786436
  12.6 0.6 %copy-start.15 = (bf16[64,1024]{1,0:T(8,128)(2,1)}, bf16[64,1024]{1,0:T(8,128)(2,1)S(1)}, u32[]{:S(2)}) copy-start(bf16[64,1024]{1,0:T(8,128)(2,1)S(1)} %collective-permute-done.1.refs_1_.q_ref) | copy-start | bytes 393220
  12.6 0.7 %copy-start.17 = (bf16[64,1024]{1,0:T(8,128)(2,1)}, bf16[64,1024]{1,0:T(8,128)(2,1)S(1)}, u32[]{:S(2)}) copy-start(bf16[64,1024]{1,0:T(8,128)(2,1)S(1)} %collective-permute-done.2.refs_2_.q_ref) | copy-start | bytes 393220
  13.3 0.7 %copy-start = (bf16[132,1024]{1,0:T(8,128)(2,1)}, bf16[132,1024]{1,0:T(8,128)(2,1)S(1)}, u32[]{:S(2)}) copy-start(bf16[132,1024]{1,0:T(8,128)(2,1)S(1)} %collective-permute-done.refs_0_) | copy-start | bytes 811012
  14.0 22.0 %copy-start.2 = (bf16[132,1024]{1,0:T(8,128)(2,1)S(1)}, bf16[132,1024]{1,0:T(8,128)(2,1)}, u32[]{:S(2)}) copy-start(bf16[132,1024]{1,0:T(8,128)(2,1)} %after.4.pair_ref.refs_2_) | copy-start | bytes 811012
  14.9 1.7 %collective-permute-start.4 = (bf16[2,5,1024]{2,1,0:T(8,128)(2,1)S(1)}, bf16[2,5,1024]{2,1,0:T(8,128)(2,1)S(1)}, u32[]{:S(2)}, u32[]{:S(2)}) collective-permute-start(bf16[2,5,1024]{2,1,0:T(8,128)(2,1)S(1)} %pad_maximum_fusion), channel_id=1, source_target_pairs={{0,1},{1,0},{2,3},{3,2},{4,5},{5,4},{6,7},{7,6},{8,9},{9,8},{10,11... | collective-permute-start | bytes 61448 | tf_op jit(solution)/shard_map/ppermute | solution.py:184
  15.0 9.7 %collective-permute-start.6 = (bf16[132,1024]{1,0:T(8,128)(2,1)}, bf16[132,1024]{1,0:T(8,128)(2,1)S(1)}, u32[]{:S(2)}, u32[]{:S(2)}) collective-permute-start(bf16[132,1024]{1,0:T(8,128)(2,1)} %after.4.pair_ref.refs_2_), channel_id=1, source_target_pairs={{0,16},{8,24},{16,0},{24,8},{1,17},{9,25},{17,1},{25,9},{2,18},{10... | collective-permute-start | bytes 811016 | tf_op jit(solution)/shard_map/ppermute | solution.py:195
  16.6 3.7 %collective-permute-start.5 = (bf16[2,2,1024]{2,1,0:T(2,128)(2,1)S(1)}, bf16[2,2,1024]{2,1,0:T(2,128)(2,1)S(1)}, u32[]{:S(2)}, u32[]{:S(2)}) collective-permute-start(bf16[2,2,1024]{2,1,0:T(2,128)(2,1)S(1)} %pad_maximum_fusion.2), channel_id=1, source_target_pairs={{0,2},{1,3},{2,0},{3,1},{4,6},{5,7},{6,4},{7,5},{8,10},{9,11},{10,... | collective-permute-start | bytes 24584 | tf_op jit(solution)/shard_map/ppermute | solution.py:184
  18.1 2.3 %copy-start.3 = (bf16[128,1024]{1,0:T(8,128)(2,1)}, bf16[128,1024]{1,0:T(8,128)(2,1)S(1)}, u32[]{:S(2)}) copy-start(bf16[128,1024]{1,0:T(8,128)(2,1)S(1)} %collective-permute-done.3.refs_0_) | copy-start | bytes 786436
  20.4 0.6 %copy-start.19 = (bf16[2,2,1024]{2,1,0:T(2,128)(2,1)}, bf16[2,2,1024]{2,1,0:T(2,128)(2,1)S(1)}, u32[]{:S(2)}) copy-start(bf16[2,2,1024]{2,1,0:T(2,128)(2,1)S(1)} %collective-permute-done.5.refs_1_) | copy-start | bytes 24580
  20.9 9.2 %collective-permute-start.7 = (bf16[128,1024]{1,0:T(8,128)(2,1)}, bf16[128,1024]{1,0:T(8,128)(2,1)S(1)}, u32[]{:S(2)}, u32[]{:S(2)}) collective-permute-start(bf16[128,1024]{1,0:T(8,128)(2,1)} %after.5.pair_ref.refs_3_), channel_id=1, source_target_pairs={{0,16},{8,24},{16,0},{24,8},{1,17},{9,25},{17,1},{25,9},{2,18},{10... | collective-permute-start | bytes 786440 | tf_op jit(solution)/shard_map/ppermute | solution.py:195
  22.8 12.5 %collective-permute-start.8 = (bf16[2,4,1024]{2,1,0:T(4,128)(2,1)S(1)}, bf16[2,4,1024]{2,1,0:T(4,128)(2,1)S(1)}, u32[]{:S(2)}, u32[]{:S(2)}) collective-permute-start(bf16[2,4,1024]{2,1,0:T(4,128)(2,1)S(1)} %pad_maximum_fusion.1), channel_id=1, source_target_pairs={{0,16},{8,24},{16,0},{24,8},{1,17},{9,25},{17,1},{25,9},{2,18},{10... | collective-permute-start | bytes 49160 | tf_op jit(solution)/shard_map/ppermute | solution.py:184
  24.7 1.0 %copy-start.1 = (bf16[132,1024]{1,0:T(8,128)(2,1)S(1)}, bf16[132,1024]{1,0:T(8,128)(2,1)}, u32[]{:S(2)}) copy-start(bf16[132,1024]{1,0:T(8,128)(2,1)} %after.4.pair_ref.refs_2_) | copy-start | bytes 811012
  25.7 0.9 %copy-start.16 = (bf16[64,1024]{1,0:T(8,128)(2,1)S(1)}, bf16[64,1024]{1,0:T(8,128)(2,1)}, u32[]{:S(2)}) copy-start(bf16[64,1024]{1,0:T(8,128)(2,1)} %copy-done.15) | copy-start | bytes 393220
  26.6 8.8 %copy-start.20 = (bf16[2,2,1024]{2,1,0:T(2,128)(2,1)S(1)}, bf16[2,2,1024]{2,1,0:T(2,128)(2,1)}, u32[]{:S(2)}) copy-start(bf16[2,2,1024]{2,1,0:T(2,128)(2,1)} %copy-done.19) | copy-start | bytes 24580
  26.6 9.5 %copy-start.5 = (bf16[128,1024]{1,0:T(8,128)(2,1)S(1)}, bf16[128,1024]{1,0:T(8,128)(2,1)}, u32[]{:S(2)}) copy-start(bf16[128,1024]{1,0:T(8,128)(2,1)} %after.5.pair_ref.refs_3_) | copy-start | bytes 786436
  27.9 13.1 %collective-permute-start.9 = (bf16[64,1152]{1,0:T(8,128)(2,1)}, bf16[64,1152]{1,0:T(8,128)(2,1)}, u32[]{:S(2)}, u32[]{:S(2)}) collective-permute-start(bf16[64,1152]{1,0:T(8,128)(2,1)} %edge_part.1.refs_1_), channel_id=1, source_target_pairs={{0,7},{1,2},{2,1},{3,4},{4,3},{5,6},{6,5},{7,0},{8,15},{9,10},{10,... | collective-permute-start | bytes 442376 | tf_op jit(solution)/shard_map/ppermute | solution.py:189
  30.1 0.7 %copy-start.6 = (bf16[128,1024]{1,0:T(8,128)(2,1)}, bf16[128,1024]{1,0:T(8,128)(2,1)S(1)}, u32[]{:S(2)}) copy-start(bf16[128,1024]{1,0:T(8,128)(2,1)S(1)} %collective-permute-done.7.refs_0_) | copy-start | bytes 786436
  30.8 0.9 %copy-start.4 = (bf16[128,1024]{1,0:T(8,128)(2,1)S(1)}, bf16[128,1024]{1,0:T(8,128)(2,1)}, u32[]{:S(2)}) copy-start(bf16[128,1024]{1,0:T(8,128)(2,1)} %after.5.pair_ref.refs_3_) | copy-start | bytes 786436
  31.8 0.9 %copy-start.7 = (bf16[128,1024]{1,0:T(8,128)(2,1)S(1)}, bf16[128,1024]{1,0:T(8,128)(2,1)}, u32[]{:S(2)}) copy-start(bf16[128,1024]{1,0:T(8,128)(2,1)} %after.6.far_ref.refs_5_) | copy-start | bytes 786436
  32.7 0.9 %copy-start.11 = (bf16[128,1024]{1,0:T(8,128)(2,1)S(1)}, bf16[128,1024]{1,0:T(8,128)(2,1)}, u32[]{:S(2)}) copy-start(bf16[128,1024]{1,0:T(8,128)(2,1)} %copy-done.10) | copy-start | bytes 786436
  33.7 0.9 %copy-start.18 = (bf16[64,1024]{1,0:T(8,128)(2,1)S(1)}, bf16[64,1024]{1,0:T(8,128)(2,1)}, u32[]{:S(2)}) copy-start(bf16[64,1024]{1,0:T(8,128)(2,1)} %copy-done.17) | copy-start | bytes 393220
  35.2 0.8 %copy-start.13 = (bf16[64,1152]{1,0:T(8,128)(2,1)}, bf16[64,1152]{1,0:T(8,128)(2,1)S(1)}, u32[]{:S(2)}) copy-start(bf16[64,1152]{1,0:T(8,128)(2,1)S(1)} %inner_part.1.refs_1_) | copy-start | bytes 442372
  35.2 5.8 %collective-permute-start.10 = (bf16[64,1152]{1,0:T(8,128)(2,1)S(1)}, bf16[64,1152]{1,0:T(8,128)(2,1)}, u32[]{:S(2)}, u32[]{:S(2)}) collective-permute-start(bf16[64,1152]{1,0:T(8,128)(2,1)S(1)} %inner_part.1.refs_1_), channel_id=1, source_target_pairs={{0,1},{1,0},{2,3},{3,2},{4,5},{5,4},{6,7},{7,6},{8,9},{9,8},{10,11... | collective-permute-start | bytes 442376 | tf_op jit(solution)/shard_map/ppermute | solution.py:184
  36.0 1.0 %copy-start.8 = (bf16[128,1024]{1,0:T(8,128)(2,1)S(1)}, bf16[128,1024]{1,0:T(8,128)(2,1)}, u32[]{:S(2)}) copy-start(bf16[128,1024]{1,0:T(8,128)(2,1)} %after.6.far_ref.refs_5_) | copy-start | bytes 786436
  37.0 0.9 %copy-start.12 = (bf16[128,1024]{1,0:T(8,128)(2,1)S(1)}, bf16[128,1024]{1,0:T(8,128)(2,1)}, u32[]{:S(2)}) copy-start(bf16[128,1024]{1,0:T(8,128)(2,1)} %copy-done.10) | copy-start | bytes 786436
  38.0 0.8 %copy-start.14 = (bf16[2,16,1024]{2,1,0:T(8,128)(2,1)S(1)}, bf16[2,16,1024]{2,1,0:T(8,128)(2,1)}, u32[]{:S(2)}) copy-start(bf16[2,16,1024]{2,1,0:T(8,128)(2,1)} %after.7.refs_6_) | copy-start | bytes 196612

commit v3 on v2

--- a/solution.py
+++ b/solution.py
@@ -207,6 +207,7 @@
         out_specs=pl.BlockSpec(memory_space=pl.ANY),
         input_output_aliases={0: 0},
         name="after",
+        compiler_params=pltpu.CompilerParams(vmem_limit_bytes=1024 * 1024),
     )(x, *tokens)
 
 

time: 44.1 us -> 30.8 us (0.70)
  local copies, waits for them, and re-layouts: 12.6 us -> 0.06 us
  Pallas kernels: 8.7 us -> 5.27 us
  waiting for transfers between devices: 6.77 us -> 9.51 us
  starting transfers between devices: 13.8 us -> 15.5 us
  other arithmetic: 1.51 us -> 0.19 us
    unnamed x42 -> x2, local copies, waits for them, and re-layouts: 11.8 us -> 0.01 us
    pallas_call x4, Pallas kernels: 6.64 us -> 4.03 us  [call(): pl.pallas_call(kernel, out_shape=outs, in_specs=[VMEM] * len(args), out_s...]
    ppermute x2, waiting for transfers between devices: 0.97 us -> 3.42 us  [stride(): return lax.ppermute(x, axis, route)]
    ppermute x2, starting transfers between devices: 4.99 us -> 5.84 us  [outward(): lax.ppermute(x, axis, [(i, (i + (1 if i % 2 else -1)) % count) for i in r...]
    pallas_call x1, Pallas kernels: 2.06 us -> 1.23 us  [shards(): pl.pallas_call(split_kernel, out_shape=[like(SPAN, width), like(SPAN, wid...]
    slice x1, local copies, waits for them, and re-layouts: 0.79 us -> 0.01 us  [shards(): level0_lat = edge_pair[2 * SPAN:].reshape(2, 2, width)]
    concatenate x1, other arithmetic: 0.73 us -> 0.03 us  [shards(): group_lat = swap(jnp.concatenate([group, group_lon], axis=1), 'lat', 2)]
    concatenate x1, other arithmetic: 0.68 us -> 0.06 us  [shards(): jnp.concatenate([level0_lat, beside[:, 0:4], group_lon, group_lat], axis=1)]
  transfers between devices with their start and end apart: 11 -> 11, of which waited for: 3 -> 6; matrix products, arithmetic and copies ran while one was open for 5% -> 1% of each run, Pallas kernels for 10% -> 8%
where the time goes in v3:
time: 30.8 us; the launch traced here: 30.7 us
  starting transfers between devices  15.5 us (50%)
  waiting for transfers between devices  9.51 us (31%)
  Pallas kernels  5.27 us (17%)
    ppermute x7, starting transfers between devices, swap(): return lax.ppermute(x, axis, [(i, i ^ distance) for i in range(count)])  6.47 us
    ppermute x2, starting transfers between devices, outward(): lax.ppermute(x, axis, [(i, (i + (1 if i % 2 else -1)) % count) for i in r...  5.84 us
    ppermute x2, waiting for transfers between devices, outward(): lax.ppermute(x, axis, [(i, (i + (1 if i % 2 else -1)) % count) for i in r...  4.14 us
    pallas_call x4, Pallas kernels, call(): pl.pallas_call(kernel, out_shape=outs, in_specs=[VMEM] * len(args), out_s...  4.03 us
    ppermute x2, waiting for transfers between devices, stride(): return lax.ppermute(x, axis, route)  3.42 us
    ppermute x2, starting transfers between devices, stride(): return lax.ppermute(x, axis, route)  3.21 us
    ppermute x7, waiting for transfers between devices, swap(): return lax.ppermute(x, axis, [(i, i ^ distance) for i in range(count)])  1.95 us
    pallas_call x1, Pallas kernels, shards(): pl.pallas_call(split_kernel, out_shape=[like(SPAN, width), like(SPAN, wid...  1.23 us
  transfers between devices with their start and end apart: 11, of which 6 were waited for; matrix products, arithmetic and copies ran while one was open for 1% of the time, Pallas kernels for 8%

profile of v3, /device:TPU:0, one launch (start us, length us, event | category | flops | bytes accessed | tf_op | source)
XLA Modules:
  0.0 30.7 jit_solution(1355454740167172951)
XLA Ops:
  0.0 1.2 %split.1 = (bf16[64,1024]{1,0:T(8,128)(2,1)S(1)}, bf16[64,1024]{1,0:T(8,128)(2,1)S(1)}, bf16[132,1024]{1,0:T(8,128)(2,1)S(1)}, bf16[128,1024]{1,0:T(8,128)(2,1)S(1)}, bf16[4,1024]{1,0:T(4,128)(2,1)S(1)}) custom-call(bf16[8,16,1024]{2,1,0:T(8,128)(2,1)} %q_hbm.1, bf16[2,8,16,1024]{3,2,1,0:T(8,128)(2,1)} %kv_hbm.1), custom_call_target="tpu_custom_call" | custom-call | bytes 2097152 | tf_op jit(solution)/shard_map/split/pallas_call | solution.py:226
  1.2 3.0 %collective-permute-start = (bf16[132,1024]{1,0:T(8,128)(2,1)S(1)}, bf16[132,1024]{1,0:T(8,128)(2,1)S(1)}, u32[]{:S(2)}, u32[]{:S(2)}) collective-permute-start(bf16[132,1024]{1,0:T(8,128)(2,1)S(1)} %get-tuple-element.14.own_ref.refs_0_), channel_id=1, source_target_pairs={{0,8},{8,0},{16,24},{24,16},{1,9},{9,1},{17,25},{25,17},{2,10},{10... | collective-permute-start | bytes 811016 | tf_op jit(solution)/shard_map/ppermute | solution.py:184
  4.2 2.8 %collective-permute-start.1 = (bf16[64,1024]{1,0:T(8,128)(2,1)S(1)}, bf16[64,1024]{1,0:T(8,128)(2,1)S(1)}, u32[]{:S(2)}, u32[]{:S(2)}) collective-permute-start(bf16[64,1024]{1,0:T(8,128)(2,1)S(1)} %get-tuple-element.12.qe_ref), channel_id=1, source_target_pairs={{0,7},{1,2},{2,1},{3,4},{4,3},{5,6},{6,5},{7,0},{8,15},{9,10},{10,... | collective-permute-start | bytes 393224 | tf_op jit(solution)/shard_map/ppermute | solution.py:189
  7.0 0.0 collective-permute-start.2
  7.0 0.5 %collective-permute-start.3 = (bf16[128,1024]{1,0:T(8,128)(2,1)S(1)}, bf16[128,1024]{1,0:T(8,128)(2,1)S(1)}, u32[]{:S(2)}, u32[]{:S(2)}) collective-permute-start(bf16[128,1024]{1,0:T(8,128)(2,1)S(1)} %get-tuple-element.15.own_ref.refs_1_), channel_id=1, source_target_pairs={{0,8},{8,0},{16,24},{24,16},{1,9},{9,1},{17,25},{25,17},{2,10},{10... | collective-permute-start | bytes 786440 | tf_op jit(solution)/shard_map/ppermute | solution.py:184
  7.6 4.0 %collective-permute-done.1.refs_1_.q_ref = bf16[64,1024]{1,0:T(8,128)(2,1)S(1)} collective-permute-done((bf16[64,1024]{1,0:T(8,128)(2,1)S(1)}, bf16[64,1024]{1,0:T(8,128)(2,1)S(1)}, u32[]{:S(2)}, u32[]{:S(2)}) %collective-permute-start.1) | collective-permute-done | bytes 131104 | tf_op jit(solution)/shard_map/ppermute | solution.py:189
  11.6 0.0 collective-permute-done.2.refs_2_.q_ref
  11.6 0.0 collective-permute-done.refs_0_
  11.7 0.1 collective-permute-start.4
  11.8 2.1 %collective-permute-start.6 = (bf16[132,1024]{1,0:T(8,128)(2,1)S(1)}, bf16[132,1024]{1,0:T(8,128)(2,1)S(1)}, u32[]{:S(2)}, u32[]{:S(2)}) collective-permute-start(bf16[132,1024]{1,0:T(8,128)(2,1)S(1)} %after.4.pair_ref.refs_2_), channel_id=1, source_target_pairs={{0,16},{8,24},{16,0},{24,8},{1,17},{9,25},{17,1},{25,9},{2,18},{10... | collective-permute-start | bytes 811016 | tf_op jit(solution)/shard_map/ppermute | solution.py:195
  13.9 0.0 collective-permute-done.4
  13.9 1.8 %collective-permute-start.5 = (bf16[2,2,1024]{2,1,0:T(2,128)(2,1)S(1)}, bf16[2,2,1024]{2,1,0:T(2,128)(2,1)S(1)}, u32[]{:S(2)}, u32[]{:S(2)}) collective-permute-start(bf16[2,2,1024]{2,1,0:T(2,128)(2,1)S(1)} %pad_maximum_fusion.2), channel_id=1, source_target_pairs={{0,2},{1,3},{2,0},{3,1},{4,6},{5,7},{6,4},{7,5},{8,10},{9,11},{10,... | collective-permute-start | bytes 24584 | tf_op jit(solution)/shard_map/ppermute | solution.py:184
  15.8 0.8 %collective-permute-done.3.refs_0_ = bf16[128,1024]{1,0:T(8,128)(2,1)S(1)} collective-permute-done((bf16[128,1024]{1,0:T(8,128)(2,1)S(1)}, bf16[128,1024]{1,0:T(8,128)(2,1)S(1)}, u32[]{:S(2)}, u32[]{:S(2)}) %collective-permute-start.3) | collective-permute-done | bytes 262176 | tf_op jit(solution)/shard_map/ppermute | solution.py:184
  16.5 1.1 %collective-permute-done.5.refs_1_ = bf16[2,2,1024]{2,1,0:T(2,128)(2,1)S(1)} collective-permute-done((bf16[2,2,1024]{2,1,0:T(2,128)(2,1)S(1)}, bf16[2,2,1024]{2,1,0:T(2,128)(2,1)S(1)}, u32[]{:S(2)}, u32[]{:S(2)}) %collective-permute-start.5) | collective-permute-done | bytes 8224 | tf_op jit(solution)/shard_map/ppermute | solution.py:184
  17.7 1.1 %collective-permute-start.7 = (bf16[128,1024]{1,0:T(8,128)(2,1)S(1)}, bf16[128,1024]{1,0:T(8,128)(2,1)S(1)}, u32[]{:S(2)}, u32[]{:S(2)}) collective-permute-start(bf16[128,1024]{1,0:T(8,128)(2,1)S(1)} %after.5.pair_ref.refs_3_), channel_id=1, source_target_pairs={{0,16},{8,24},{16,0},{24,8},{1,17},{9,25},{17,1},{25,9},{2,18},{10... | collective-permute-start | bytes 786440 | tf_op jit(solution)/shard_map/ppermute | solution.py:195
  18.8 1.0 %collective-permute-start.8 = (bf16[2,4,1024]{2,1,0:T(4,128)(2,1)S(1)}, bf16[2,4,1024]{2,1,0:T(4,128)(2,1)S(1)}, u32[]{:S(2)}, u32[]{:S(2)}) collective-permute-start(bf16[2,4,1024]{2,1,0:T(4,128)(2,1)S(1)} %pad_maximum_fusion.1), channel_id=1, source_target_pairs={{0,16},{8,24},{16,0},{24,8},{1,17},{9,25},{17,1},{25,9},{2,18},{10... | collective-permute-start | bytes 49160 | tf_op jit(solution)/shard_map/ppermute | solution.py:184
  19.8 1.6 %collective-permute-done.6.far_ref.refs_4_ = bf16[132,1024]{1,0:T(8,128)(2,1)S(1)} collective-permute-done((bf16[132,1024]{1,0:T(8,128)(2,1)S(1)}, bf16[132,1024]{1,0:T(8,128)(2,1)S(1)}, u32[]{:S(2)}, u32[]{:S(2)}) %collective-permute-start.6) | collective-permute-done | bytes 270368 | tf_op jit(solution)/shard_map/ppermute | solution.py:195
  21.4 0.6 %edge_part.1.refs_1_ = bf16[64,1152]{1,0:T(8,128)(2,1)S(1)} custom-call(bf16[64,1024]{1,0:T(8,128)(2,1)S(1)} %collective-permute-done.1.refs_1_.q_ref, bf16[132,1024]{1,0:T(8,128)(2,1)S(1)} %get-tuple-element.14.own_ref.refs_0_, bf16[132,1024]{1,0:T(8,128)(2,1)S(1)} %after.4.pair_ref.refs_2_, bf16[132,1024]{1,0:T(8,128)(2,1)S(1)} %collective-permute-done.6.far_ref.refs_4_), custom_call_target="tpu_custom_call" | custom-call | flops 50331648 | bytes 1089536 | tf_op jit(solution)/shard_map/edge_part/pallas_call | solution.py:26
  22.0 0.0 copy-start
  22.0 3.1 %collective-permute-start.9 = (bf16[64,1152]{1,0:T(8,128)(2,1)S(1)}, bf16[64,1152]{1,0:T(8,128)(2,1)S(1)}, u32[]{:S(2)}, u32[]{:S(2)}) collective-permute-start(bf16[64,1152]{1,0:T(8,128)(2,1)S(1)} %edge_part.1.refs_1_), channel_id=1, source_target_pairs={{0,7},{1,2},{2,1},{3,4},{4,3},{5,6},{6,5},{7,0},{8,15},{9,10},{10,... | collective-permute-start | bytes 442376 | tf_op jit(solution)/shard_map/ppermute | solution.py:189
  25.1 1.8 %collective-permute-done.7.refs_0_ = bf16[128,1024]{1,0:T(8,128)(2,1)S(1)} collective-permute-done((bf16[128,1024]{1,0:T(8,128)(2,1)S(1)}, bf16[128,1024]{1,0:T(8,128)(2,1)S(1)}, u32[]{:S(2)}, u32[]{:S(2)}) %collective-permute-start.7) | collective-permute-done | bytes 262176 | tf_op jit(solution)/shard_map/ppermute | solution.py:195
  26.9 0.6 %inner_part.1.refs_1_ = bf16[64,1152]{1,0:T(8,128)(2,1)S(1)} custom-call(bf16[64,1024]{1,0:T(8,128)(2,1)S(1)} %collective-permute-done.2.refs_2_.q_ref, bf16[128,1024]{1,0:T(8,128)(2,1)S(1)} %get-tuple-element.15.own_ref.refs_1_, bf16[128,1024]{1,0:T(8,128)(2,1)S(1)} %after.5.pair_ref.refs_3_, bf16[128,1024]{1,0:T(8,128)(2,1)S(1)} %after.6.far_ref.refs_5_), custom_call_target="tpu_custom_call" | custom-call | flops 50331648 | bytes 1064960 | tf_op jit(solution)/shard_map/inner_part/pallas_call | solution.py:26
  27.6 0.1 collective-permute-start.10
  27.7 0.0 collective-permute-done.8
  27.7 0.1 fusion.6.refs_0_
  27.7 1.3 %own_part.1 = (f32[128,1024]{1,0:T(8,128)S(1)}, f32[128,128]{1,0:T(8,128)S(1)}) custom-call(bf16[64,1024]{1,0:T(8,128)(2,1)S(1)} %get-tuple-element.12.qe_ref, bf16[64,1024]{1,0:T(8,128)(2,1)S(1)} %get-tuple-element.13.qi_ref, bf16[132,1024]{1,0:T(8,128)(2,1)S(1)} %get-tuple-element.14.own_ref.refs_0_, ...), custom_call_target="tpu_custom_call" | custom-call | flops 201326592 | bytes 2514944 | tf_op jit(solution)/shard_map/own_part/pallas_call | solution.py:26
  29.0 0.1 collective-permute-done.9.edge_ref
  29.1 0.0 collective-permute-done.10.inner_ref
  29.1 0.0 copy-done
  29.1 1.5 %merge.1 = bf16[8,16,1024]{2,1,0:T(8,128)(2,1)} custom-call(f32[128,1024]{1,0:T(8,128)S(1)} %get-tuple-element.17.own_ref, f32[128,128]{1,0:T(8,128)S(1)} %get-tuple-element.18.lse_ref, bf16[64,1152]{1,0:T(8,128)(2,1)S(1)} %collective-permute-done.9.edge_ref, bf16[64,1152]{1,0:T(8,128)(2,1)S(1)} %collective-permute-done.10.inner_ref, ...), custom_call_target="tpu_custom_call" | custom-call | flops 268435456 | bytes 3244032 | tf_op jit(solution)/shard_map/merge/pallas_call | solution.py:26
  (13 shorter events, 0.2 us)
Async XLA Ops:
  1.2 10.4 %collective-permute-start = (bf16[132,1024]{1,0:T(8,128)(2,1)S(1)}, bf16[132,1024]{1,0:T(8,128)(2,1)S(1)}, u32[]{:S(2)}, u32[]{:S(2)}) collective-permute-start(bf16[132,1024]{1,0:T(8,128)(2,1)S(1)} %get-tuple-element.14.own_ref.refs_0_), channel_id=1, source_target_pairs={{0,8},{8,0},{16,24},{24,16},{1,9},{9,1},{17,25},{25,17},{2,10},{10... | collective-permute-start | bytes 811016 | tf_op jit(solution)/shard_map/ppermute | solution.py:184
  4.2 7.3 %collective-permute-start.1 = (bf16[64,1024]{1,0:T(8,128)(2,1)S(1)}, bf16[64,1024]{1,0:T(8,128)(2,1)S(1)}, u32[]{:S(2)}, u32[]{:S(2)}) collective-permute-start(bf16[64,1024]{1,0:T(8,128)(2,1)S(1)} %get-tuple-element.12.qe_ref), channel_id=1, source_target_pairs={{0,7},{1,2},{2,1},{3,4},{4,3},{5,6},{6,5},{7,0},{8,15},{9,10},{10,... | collective-permute-start | bytes 393224 | tf_op jit(solution)/shard_map/ppermute | solution.py:189
  7.0 4.6 %collective-permute-start.2 = (bf16[64,1024]{1,0:T(8,128)(2,1)S(1)}, bf16[64,1024]{1,0:T(8,128)(2,1)S(1)}, u32[]{:S(2)}, u32[]{:S(2)}) collective-permute-start(bf16[64,1024]{1,0:T(8,128)(2,1)S(1)} %get-tuple-element.13.qi_ref), channel_id=1, source_target_pairs={{0,1},{1,0},{2,3},{3,2},{4,5},{5,4},{6,7},{7,6},{8,9},{9,8},{10,11... | collective-permute-start | bytes 393224 | tf_op jit(solution)/shard_map/ppermute | solution.py:184
  7.0 9.5 %collective-permute-start.3 = (bf16[128,1024]{1,0:T(8,128)(2,1)S(1)}, bf16[128,1024]{1,0:T(8,128)(2,1)S(1)}, u32[]{:S(2)}, u32[]{:S(2)}) collective-permute-start(bf16[128,1024]{1,0:T(8,128)(2,1)S(1)} %get-tuple-element.15.own_ref.refs_1_), channel_id=1, source_target_pairs={{0,8},{8,0},{16,24},{24,16},{1,9},{9,1},{17,25},{25,17},{2,10},{10... | collective-permute-start | bytes 786440 | tf_op jit(solution)/shard_map/ppermute | solution.py:184
  11.7 2.2 %collective-permute-start.4 = (bf16[2,5,1024]{2,1,0:T(8,128)(2,1)S(1)}, bf16[2,5,1024]{2,1,0:T(8,128)(2,1)S(1)}, u32[]{:S(2)}, u32[]{:S(2)}) collective-permute-start(bf16[2,5,1024]{2,1,0:T(8,128)(2,1)S(1)} %pad_maximum_fusion), channel_id=1, source_target_pairs={{0,1},{1,0},{2,3},{3,2},{4,5},{5,4},{6,7},{7,6},{8,9},{9,8},{10,11... | collective-permute-start | bytes 61448 | tf_op jit(solution)/shard_map/ppermute | solution.py:184
  11.8 9.6 %collective-permute-start.6 = (bf16[132,1024]{1,0:T(8,128)(2,1)S(1)}, bf16[132,1024]{1,0:T(8,128)(2,1)S(1)}, u32[]{:S(2)}, u32[]{:S(2)}) collective-permute-start(bf16[132,1024]{1,0:T(8,128)(2,1)S(1)} %after.4.pair_ref.refs_2_), channel_id=1, source_target_pairs={{0,16},{8,24},{16,0},{24,8},{1,17},{9,25},{17,1},{25,9},{2,18},{10... | collective-permute-start | bytes 811016 | tf_op jit(solution)/shard_map/ppermute | solution.py:195
  13.9 3.7 %collective-permute-start.5 = (bf16[2,2,1024]{2,1,0:T(2,128)(2,1)S(1)}, bf16[2,2,1024]{2,1,0:T(2,128)(2,1)S(1)}, u32[]{:S(2)}, u32[]{:S(2)}) collective-permute-start(bf16[2,2,1024]{2,1,0:T(2,128)(2,1)S(1)} %pad_maximum_fusion.2), channel_id=1, source_target_pairs={{0,2},{1,3},{2,0},{3,1},{4,6},{5,7},{6,4},{7,5},{8,10},{9,11},{10,... | collective-permute-start | bytes 24584 | tf_op jit(solution)/shard_map/ppermute | solution.py:184
  17.7 9.3 %collective-permute-start.7 = (bf16[128,1024]{1,0:T(8,128)(2,1)S(1)}, bf16[128,1024]{1,0:T(8,128)(2,1)S(1)}, u32[]{:S(2)}, u32[]{:S(2)}) collective-permute-start(bf16[128,1024]{1,0:T(8,128)(2,1)S(1)} %after.5.pair_ref.refs_3_), channel_id=1, source_target_pairs={{0,16},{8,24},{16,0},{24,8},{1,17},{9,25},{17,1},{25,9},{2,18},{10... | collective-permute-start | bytes 786440 | tf_op jit(solution)/shard_map/ppermute | solution.py:195
  18.8 8.8 %collective-permute-start.8 = (bf16[2,4,1024]{2,1,0:T(4,128)(2,1)S(1)}, bf16[2,4,1024]{2,1,0:T(4,128)(2,1)S(1)}, u32[]{:S(2)}, u32[]{:S(2)}) collective-permute-start(bf16[2,4,1024]{2,1,0:T(4,128)(2,1)S(1)} %pad_maximum_fusion.1), channel_id=1, source_target_pairs={{0,16},{8,24},{16,0},{24,8},{1,17},{9,25},{17,1},{25,9},{2,18},{10... | collective-permute-start | bytes 49160 | tf_op jit(solution)/shard_map/ppermute | solution.py:184
  22.0 7.1 %copy-start = (bf16[1024,1024]{1,0:T(8,128)(2,1)S(1)}, bf16[1024,1024]{1,0:T(8,128)(2,1)}, u32[]{:S(2)}) copy-start(bf16[1024,1024]{1,0:T(8,128)(2,1)} %weight_ref.1) | copy-start | bytes 6291460
  22.0 7.1 %collective-permute-start.9 = (bf16[64,1152]{1,0:T(8,128)(2,1)S(1)}, bf16[64,1152]{1,0:T(8,128)(2,1)S(1)}, u32[]{:S(2)}, u32[]{:S(2)}) collective-permute-start(bf16[64,1152]{1,0:T(8,128)(2,1)S(1)} %edge_part.1.refs_1_), channel_id=1, source_target_pairs={{0,7},{1,2},{2,1},{3,4},{4,3},{5,6},{6,5},{7,0},{8,15},{9,10},{10,... | collective-permute-start | bytes 442376 | tf_op jit(solution)/shard_map/ppermute | solution.py:189
  27.6 1.6 %collective-permute-start.10 = (bf16[64,1152]{1,0:T(8,128)(2,1)S(1)}, bf16[64,1152]{1,0:T(8,128)(2,1)S(1)}, u32[]{:S(2)}, u32[]{:S(2)}) collective-permute-start(bf16[64,1152]{1,0:T(8,128)(2,1)S(1)} %inner_part.1.refs_1_), channel_id=1, source_target_pairs={{0,1},{1,0},{2,3},{3,2},{4,5},{5,4},{6,7},{7,6},{8,9},{9,8},{10,11... | collective-permute-start | bytes 442376 | tf_op jit(solution)/shard_map/ppermute | solution.py:184

commit v4 on v3

--- a/solution.py
+++ b/solution.py
@@ -14,6 +14,7 @@
 SPAN = TILE * TILE
 SCALE = 1.0 / math.sqrt(HEAD_DIM)
 NEG = -1e30
+WEIGHT = 2 * 10**8
 LIMIT = 16 * 1024 * 1024
 F32 = jnp.float32
 BF16 = jnp.bfloat16
@@ -116,8 +117,8 @@
     out_ref[:, HEADS * HEAD_DIM :] = stats.astype(BF16)
 
 
-def own_kernel(n_lat, count, qe_ref, qi_ref, *refs):
-    tiles, (coarse_ref, out_ref, lse_ref) = refs[:6], refs[6:]
+def own_kernel(n_lat, count, *refs):
+    tiles, (qi_ref, qe_ref, coarse_ref, out_ref, lse_ref) = refs[:6], refs[6:]
     rows = 2 * SPAN
     far = far_exists(n_lat)
     lane = lax.broadcasted_iota(jnp.int32, (rows, 6 * SPAN), 1)
@@ -199,7 +200,7 @@
     pass
 
 
-def after(x, *tokens):
+def after(x, *tokens, weight=0):
     return pl.pallas_call(
         after_kernel,
         out_shape=jax.ShapeDtypeStruct(x.shape, x.dtype),
@@ -208,6 +209,7 @@
         input_output_aliases={0: 0},
         name="after",
         compiler_params=pltpu.CompilerParams(vmem_limit_bytes=1024 * 1024),
+        cost_estimate=pl.CostEstimate(flops=weight, bytes_accessed=0, transcendentals=0),
     )(x, *tokens)
 
 
@@ -247,17 +249,19 @@
     far_q_edge = outward(q_edge, "lon")
     far_q_inner = swap(q_inner, "lon", 1)
     inner_pair = swap(inner_own, "lat", 1)
-    edge_pair = after(edge_pair, far_q_edge, far_q_inner)
+    inner_hop = stride(inner_own, "lat", -2)
+    pooled = after(pooled, weight=4 * WEIGHT)
+    edge_pair = after(edge_pair, pooled, far_q_edge, far_q_inner, inner_hop)
     edge_far = stride(edge_pair, "lat", 2)
+    inner_far = swap(inner_hop, "lat", 1)
     level0 = pooled.reshape(2, 2, width)
     level0_lat = edge_pair[2 * SPAN :].reshape(2, 2, width)
     mine = mean_entries(level0[:, 0:1], level0[:, 1:2], level0_lat[:, 0:1], level0_lat[:, 1:2])
     beside = swap(jnp.concatenate([level0, level0_lat, mine], axis=1), "lon", 1)
     group = jnp.concatenate([mine, beside[:, 4:5]], axis=1)
     group_lon = swap(group, "lon", 2)
-    inner_pair = after(inner_pair, group_lon)
-    inner_far = stride(inner_pair, "lat", 2)
-    group_lat = swap(jnp.concatenate([group, group_lon], axis=1), "lat", 2)
+    group_both = jnp.concatenate([group, group_lon], axis=1)
+    group_lat = swap(after(group_both, inner_pair), "lat", 2)
     coarse = jnp.concatenate([level0_lat, beside[:, 0:4], group_lon, group_lat], axis=1)
     count = coarse.shape[1] // 2
     coarse = jnp.pad(coarse, ((0, 0), (0, 16 - 2 * count), (0, 0)))
@@ -296,16 +300,17 @@
         ],
         "own_part",
         4 * flops,
-        q_edge,
-        q_inner,
         edge_own,
         inner_own,
         edge_pair,
         inner_pair,
         edge_far,
         inner_far,
+        q_inner,
+        q_edge,
         coarse,
     )
+    edge_back = after(edge_back, own, weight=WEIGHT)
     return call(
         merge_kernel,
         [jax.ShapeDtypeStruct(queries.shape, BF16)],

time: 30.8 us -> 30.7 us (level)
  starting transfers between devices: 15.5 us -> 14.5 us
  waiting for transfers between devices: 9.51 us -> 10.4 us
    ppermute x2, waiting for transfers between devices: 4.14 us -> 8.26 us  [outward(): lax.ppermute(x, axis, [(i, (i + (1 if i % 2 else -1)) % count) for i in r...]
    ppermute x2, waiting for transfers between devices: 3.42 us -> 0.01 us  [stride(): return lax.ppermute(x, axis, route)]
    ppermute x7 -> x8, starting transfers between devices: 6.47 us -> 8.1 us  [swap(): return lax.ppermute(x, axis, [(i, i ^ distance) for i in range(count)])]
    ppermute x2, starting transfers between devices: 5.84 us -> 4.32 us  [outward(): lax.ppermute(x, axis, [(i, (i + (1 if i % 2 else -1)) % count) for i in r...]
    ppermute x2, starting transfers between devices: 3.21 us -> 2.09 us  [stride(): return lax.ppermute(x, axis, route)]
    ppermute x7 -> x8, waiting for transfers between devices: 1.95 us -> 2.09 us  [swap(): return lax.ppermute(x, axis, [(i, i ^ distance) for i in range(count)])]
  transfers between devices with their start and end apart: 11 -> 12, of which waited for: 6 -> 3; matrix products, arithmetic and copies ran while one was open for 1% -> 1% of each run, Pallas kernels for 8% -> 8%
where the time goes in v4:
time: 30.7 us; the launch traced here: 30.5 us
  starting transfers between devices  14.5 us (47%)
  waiting for transfers between devices  10.4 us (34%)
  Pallas kernels  5.28 us (17%)
    ppermute x2, waiting for transfers between devices, outward(): lax.ppermute(x, axis, [(i, (i + (1 if i % 2 else -1)) % count) for i in r...  8.26 us
    ppermute x8, starting transfers between devices, swap(): return lax.ppermute(x, axis, [(i, i ^ distance) for i in range(count)])  8.1 us
    ppermute x2, starting transfers between devices, outward(): lax.ppermute(x, axis, [(i, (i + (1 if i % 2 else -1)) % count) for i in r...  4.32 us
    pallas_call x4, Pallas kernels, call(): pl.pallas_call(kernel, out_shape=outs, in_specs=[VMEM] * len(args), out_s...  4.04 us
    ppermute x8, waiting for transfers between devices, swap(): return lax.ppermute(x, axis, [(i, i ^ distance) for i in range(count)])  2.09 us
    ppermute x2, starting transfers between devices, stride(): return lax.ppermute(x, axis, route)  2.09 us
    pallas_call x1, Pallas kernels, shards(): pl.pallas_call(split_kernel, out_shape=[like(SPAN, width), like(SPAN, wid...  1.23 us
  transfers between devices with their start and end apart: 12, of which 3 were waited for; matrix products, arithmetic and copies ran while one was open for 1% of the time, Pallas kernels for 8%

profile of v4, /device:TPU:0, one launch (start us, length us, event | category | flops | bytes accessed | tf_op | source)
XLA Modules:
  0.0 30.5 jit_solution(3495937248882691247)
XLA Ops:
  0.0 1.2 %split.1 = (bf16[64,1024]{1,0:T(8,128)(2,1)S(1)}, bf16[64,1024]{1,0:T(8,128)(2,1)S(1)}, bf16[132,1024]{1,0:T(8,128)(2,1)S(1)}, bf16[128,1024]{1,0:T(8,128)(2,1)S(1)}, bf16[4,1024]{1,0:T(4,128)(2,1)S(1)}) custom-call(bf16[8,16,1024]{2,1,0:T(8,128)(2,1)} %q_hbm.1, bf16[2,8,16,1024]{3,2,1,0:T(8,128)(2,1)} %kv_hbm.1), custom_call_target="tpu_custom_call" | custom-call | bytes 2097152 | tf_op jit(solution)/shard_map/split/pallas_call | solution.py:228
  1.2 3.0 %collective-permute-start = (bf16[132,1024]{1,0:T(8,128)(2,1)S(1)}, bf16[132,1024]{1,0:T(8,128)(2,1)S(1)}, u32[]{:S(2)}, u32[]{:S(2)}) collective-permute-start(bf16[132,1024]{1,0:T(8,128)(2,1)S(1)} %get-tuple-element.12.own_ref.refs_0_), channel_id=1, source_target_pairs={{0,8},{8,0},{16,24},{24,16},{1,9},{9,1},{17,25},{25,17},{2,10},{10... | collective-permute-start | bytes 811016 | tf_op jit(solution)/shard_map/ppermute | solution.py:185
  4.2 1.5 %collective-permute-start.3 = (bf16[128,1024]{1,0:T(8,128)(2,1)S(1)}, bf16[128,1024]{1,0:T(8,128)(2,1)S(1)}, u32[]{:S(2)}, u32[]{:S(2)}) collective-permute-start(bf16[128,1024]{1,0:T(8,128)(2,1)S(1)} %get-tuple-element.13.own_ref.refs_1_), channel_id=1, source_target_pairs={{0,16},{8,24},{16,0},{24,8},{1,17},{9,25},{17,1},{25,9},{2,18},{10... | collective-permute-start | bytes 786440 | tf_op jit(solution)/shard_map/ppermute | solution.py:196
  5.8 2.5 %collective-permute-start.1 = (bf16[64,1024]{1,0:T(8,128)(2,1)S(1)}, bf16[64,1024]{1,0:T(8,128)(2,1)S(1)}, u32[]{:S(2)}, u32[]{:S(2)}) collective-permute-start(bf16[64,1024]{1,0:T(8,128)(2,1)S(1)} %get-tuple-element.15.refs_7_), channel_id=1, source_target_pairs={{0,7},{1,2},{2,1},{3,4},{4,3},{5,6},{6,5},{7,0},{8,15},{9,10},{10,... | collective-permute-start | bytes 393224 | tf_op jit(solution)/shard_map/ppermute | solution.py:190
  8.2 0.0 collective-permute-start.2
  8.2 0.5 %collective-permute-start.4 = (bf16[128,1024]{1,0:T(8,128)(2,1)S(1)}, bf16[128,1024]{1,0:T(8,128)(2,1)S(1)}, u32[]{:S(2)}, u32[]{:S(2)}) collective-permute-start(bf16[128,1024]{1,0:T(8,128)(2,1)S(1)} %get-tuple-element.13.own_ref.refs_1_), channel_id=1, source_target_pairs={{0,8},{8,0},{16,24},{24,16},{1,9},{9,1},{17,25},{25,17},{2,10},{10... | collective-permute-start | bytes 786440 | tf_op jit(solution)/shard_map/ppermute | solution.py:185
  8.8 4.3 %collective-permute-done.1.refs_2_.q_ref = bf16[64,1024]{1,0:T(8,128)(2,1)S(1)} collective-permute-done((bf16[64,1024]{1,0:T(8,128)(2,1)S(1)}, bf16[64,1024]{1,0:T(8,128)(2,1)S(1)}, u32[]{:S(2)}, u32[]{:S(2)}) %collective-permute-start.1) | collective-permute-done | bytes 131104 | tf_op jit(solution)/shard_map/ppermute | solution.py:190
  13.1 0.0 collective-permute-done.2.refs_3_.q_ref
  13.1 0.0 collective-permute-done.3.refs_4_
  13.1 0.0 collective-permute-done.refs_0_
  13.1 0.6 %collective-permute-start.5 = (bf16[132,1024]{1,0:T(8,128)(2,1)S(1)}, bf16[132,1024]{1,0:T(8,128)(2,1)S(1)}, u32[]{:S(2)}, u32[]{:S(2)}) collective-permute-start(bf16[132,1024]{1,0:T(8,128)(2,1)S(1)} %after.7.pair_ref.refs_2_), channel_id=1, source_target_pairs={{0,16},{8,24},{16,0},{24,8},{1,17},{9,25},{17,1},{25,9},{2,18},{10... | collective-permute-start | bytes 811016 | tf_op jit(solution)/shard_map/ppermute | solution.py:196
  13.8 0.1 collective-permute-start.7
  13.9 1.7 %collective-permute-start.6 = (bf16[128,1024]{1,0:T(8,128)(2,1)S(1)}, bf16[128,1024]{1,0:T(8,128)(2,1)S(1)}, u32[]{:S(2)}, u32[]{:S(2)}) collective-permute-start(bf16[128,1024]{1,0:T(8,128)(2,1)S(1)} %collective-permute-done.3.refs_4_), channel_id=1, source_target_pairs={{0,8},{8,0},{16,24},{24,16},{1,9},{9,1},{17,25},{25,17},{2,10},{10... | collective-permute-start | bytes 786440 | tf_op jit(solution)/shard_map/ppermute | solution.py:185
  15.6 0.0 collective-permute-done.7
  15.7 1.6 %collective-permute-start.8 = (bf16[2,2,1024]{2,1,0:T(2,128)(2,1)S(1)}, bf16[2,2,1024]{2,1,0:T(2,128)(2,1)S(1)}, u32[]{:S(2)}, u32[]{:S(2)}) collective-permute-start(bf16[2,2,1024]{2,1,0:T(2,128)(2,1)S(1)} %pad_maximum_fusion.2), channel_id=1, source_target_pairs={{0,2},{1,3},{2,0},{3,1},{4,6},{5,7},{6,4},{7,5},{8,10},{9,11},{10,... | collective-permute-start | bytes 24584 | tf_op jit(solution)/shard_map/ppermute | solution.py:185
  17.3 2.1 %collective-permute-done.8 = bf16[2,2,1024]{2,1,0:T(2,128)(2,1)S(1)} collective-permute-done((bf16[2,2,1024]{2,1,0:T(2,128)(2,1)S(1)}, bf16[2,2,1024]{2,1,0:T(2,128)(2,1)S(1)}, u32[]{:S(2)}, u32[]{:S(2)}) %collective-permute-start.8) | collective-permute-done | bytes 8224 | tf_op jit(solution)/shard_map/ppermute | solution.py:185
  19.4 0.0 collective-permute-done.4.refs_1_.pair_ref.refs_3_
  19.4 1.0 %collective-permute-start.9 = (bf16[2,4,1024]{2,1,0:T(4,128)(2,1)S(1)}, bf16[2,4,1024]{2,1,0:T(4,128)(2,1)S(1)}, u32[]{:S(2)}, u32[]{:S(2)}) collective-permute-start(bf16[2,4,1024]{2,1,0:T(4,128)(2,1)S(1)} %after.9), channel_id=1, source_target_pairs={{0,16},{8,24},{16,0},{24,8},{1,17},{9,25},{17,1},{25,9},{2,18},{10... | collective-permute-start | bytes 49160 | tf_op jit(solution)/shard_map/ppermute | solution.py:185
  20.5 0.0 collective-permute-done.5.far_ref.refs_4_
  20.5 0.6 %edge_part.1.refs_1_ = bf16[64,1152]{1,0:T(8,128)(2,1)S(1)} custom-call(bf16[64,1024]{1,0:T(8,128)(2,1)S(1)} %collective-permute-done.1.refs_2_.q_ref, bf16[132,1024]{1,0:T(8,128)(2,1)S(1)} %get-tuple-element.12.own_ref.refs_0_, bf16[132,1024]{1,0:T(8,128)(2,1)S(1)} %after.7.pair_ref.refs_2_, bf16[132,1024]{1,0:T(8,128)(2,1)S(1)} %collective-permute-done.5.far_ref.refs_4_), custom_call_target="tpu_custom_call" | custom-call | flops 50331648 | bytes 1089536 | tf_op jit(solution)/shard_map/edge_part/pallas_call | solution.py:27
  21.1 1.8 %collective-permute-start.10 = (bf16[64,1152]{1,0:T(8,128)(2,1)S(1)}, bf16[64,1152]{1,0:T(8,128)(2,1)S(1)}, u32[]{:S(2)}, u32[]{:S(2)}) collective-permute-start(bf16[64,1152]{1,0:T(8,128)(2,1)S(1)} %edge_part.1.refs_1_), channel_id=1, source_target_pairs={{0,7},{1,2},{2,1},{3,4},{4,3},{5,6},{6,5},{7,0},{8,15},{9,10},{10,... | collective-permute-start | bytes 442376 | tf_op jit(solution)/shard_map/ppermute | solution.py:190
  23.0 0.0 collective-permute-done.6.refs_0_
  23.0 0.0 copy-start
  23.0 0.6 %inner_part.1.refs_1_ = bf16[64,1152]{1,0:T(8,128)(2,1)S(1)} custom-call(bf16[64,1024]{1,0:T(8,128)(2,1)S(1)} %collective-permute-done.2.refs_3_.q_ref, bf16[128,1024]{1,0:T(8,128)(2,1)S(1)} %get-tuple-element.13.own_ref.refs_1_, bf16[128,1024]{1,0:T(8,128)(2,1)S(1)} %collective-permute-done.4.refs_1_.pair_ref.refs_3_, ...), custom_call_target="tpu_custom_call" | custom-call | flops 50331648 | bytes 1064960 | tf_op jit(solution)/shard_map/inner_part/pallas_call | solution.py:27
  23.6 0.1 collective-permute-start.11
  23.7 0.0 collective-permute-done.9
  23.7 0.1 fusion.6.refs_0_
  23.8 1.3 %own_part.1 = (f32[128,1024]{1,0:T(8,128)S(1)}, f32[128,128]{1,0:T(8,128)S(1)}) custom-call(bf16[132,1024]{1,0:T(8,128)(2,1)S(1)} %get-tuple-element.12.own_ref.refs_0_, bf16[128,1024]{1,0:T(8,128)(2,1)S(1)} %get-tuple-element.13.own_ref.refs_1_, bf16[132,1024]{1,0:T(8,128)(2,1)S(1)} %after.7.pair_ref.refs_2_, ...), custom_call_target="tpu_custom_call" | custom-call | flops 201326592 | bytes 2514944 | tf_op jit(solution)/shard_map/own_part/pallas_call | solution.py:27
  25.1 4.0 %collective-permute-done.10.refs_0_ = bf16[64,1152]{1,0:T(8,128)(2,1)S(1)} collective-permute-done((bf16[64,1152]{1,0:T(8,128)(2,1)S(1)}, bf16[64,1152]{1,0:T(8,128)(2,1)S(1)}, u32[]{:S(2)}, u32[]{:S(2)}) %collective-permute-start.10) | collective-permute-done | bytes 147488 | tf_op jit(solution)/shard_map/ppermute | solution.py:190
  29.0 0.0 collective-permute-done.11.inner_ref
  29.0 0.0 copy-done
  29.0 1.5 %merge.1 = bf16[8,16,1024]{2,1,0:T(8,128)(2,1)} custom-call(f32[128,1024]{1,0:T(8,128)S(1)} %get-tuple-element.17.refs_1_.own_ref, f32[128,128]{1,0:T(8,128)S(1)} %get-tuple-element.18.lse_ref, bf16[64,1152]{1,0:T(8,128)(2,1)S(1)} %after.11.edge_ref, bf16[64,1152]{1,0:T(8,128)(2,1)S(1)} %collective-permute-done.11.inner_ref, bf16[1024,1024]{1,0:T(8,128)(2,1)S(1)} %copy-done), custom_call_target="tpu_custom_call" | custom-call | flops 268435456 | bytes 3244032 | tf_op jit(solution)/shard_map/merge/pallas_call | solution.py:27
  (15 shorter events, 0.2 us)
Async XLA Ops:
  1.2 11.9 %collective-permute-start = (bf16[132,1024]{1,0:T(8,128)(2,1)S(1)}, bf16[132,1024]{1,0:T(8,128)(2,1)S(1)}, u32[]{:S(2)}, u32[]{:S(2)}) collective-permute-start(bf16[132,1024]{1,0:T(8,128)(2,1)S(1)} %get-tuple-element.12.own_ref.refs_0_), channel_id=1, source_target_pairs={{0,8},{8,0},{16,24},{24,16},{1,9},{9,1},{17,25},{25,17},{2,10},{10... | collective-permute-start | bytes 811016 | tf_op jit(solution)/shard_map/ppermute | solution.py:185
  4.2 8.9 %collective-permute-start.3 = (bf16[128,1024]{1,0:T(8,128)(2,1)S(1)}, bf16[128,1024]{1,0:T(8,128)(2,1)S(1)}, u32[]{:S(2)}, u32[]{:S(2)}) collective-permute-start(bf16[128,1024]{1,0:T(8,128)(2,1)S(1)} %get-tuple-element.13.own_ref.refs_1_), channel_id=1, source_target_pairs={{0,16},{8,24},{16,0},{24,8},{1,17},{9,25},{17,1},{25,9},{2,18},{10... | collective-permute-start | bytes 786440 | tf_op jit(solution)/shard_map/ppermute | solution.py:196
  5.8 7.3 %collective-permute-start.1 = (bf16[64,1024]{1,0:T(8,128)(2,1)S(1)}, bf16[64,1024]{1,0:T(8,128)(2,1)S(1)}, u32[]{:S(2)}, u32[]{:S(2)}) collective-permute-start(bf16[64,1024]{1,0:T(8,128)(2,1)S(1)} %get-tuple-element.15.refs_7_), channel_id=1, source_target_pairs={{0,7},{1,2},{2,1},{3,4},{4,3},{5,6},{6,5},{7,0},{8,15},{9,10},{10,... | collective-permute-start | bytes 393224 | tf_op jit(solution)/shard_map/ppermute | solution.py:190
  8.2 4.9 %collective-permute-start.2 = (bf16[64,1024]{1,0:T(8,128)(2,1)S(1)}, bf16[64,1024]{1,0:T(8,128)(2,1)S(1)}, u32[]{:S(2)}, u32[]{:S(2)}) collective-permute-start(bf16[64,1024]{1,0:T(8,128)(2,1)S(1)} %get-tuple-element.16.refs_6_), channel_id=1, source_target_pairs={{0,1},{1,0},{2,3},{3,2},{4,5},{5,4},{6,7},{7,6},{8,9},{9,8},{10,11... | collective-permute-start | bytes 393224 | tf_op jit(solution)/shard_map/ppermute | solution.py:185
  8.2 11.2 %collective-permute-start.4 = (bf16[128,1024]{1,0:T(8,128)(2,1)S(1)}, bf16[128,1024]{1,0:T(8,128)(2,1)S(1)}, u32[]{:S(2)}, u32[]{:S(2)}) collective-permute-start(bf16[128,1024]{1,0:T(8,128)(2,1)S(1)} %get-tuple-element.13.own_ref.refs_1_), channel_id=1, source_target_pairs={{0,8},{8,0},{16,24},{24,16},{1,9},{9,1},{17,25},{25,17},{2,10},{10... | collective-permute-start | bytes 786440 | tf_op jit(solution)/shard_map/ppermute | solution.py:185
  13.1 7.3 %collective-permute-start.5 = (bf16[132,1024]{1,0:T(8,128)(2,1)S(1)}, bf16[132,1024]{1,0:T(8,128)(2,1)S(1)}, u32[]{:S(2)}, u32[]{:S(2)}) collective-permute-start(bf16[132,1024]{1,0:T(8,128)(2,1)S(1)} %after.7.pair_ref.refs_2_), channel_id=1, source_target_pairs={{0,16},{8,24},{16,0},{24,8},{1,17},{9,25},{17,1},{25,9},{2,18},{10... | collective-permute-start | bytes 811016 | tf_op jit(solution)/shard_map/ppermute | solution.py:196
  13.8 1.8 %collective-permute-start.7 = (bf16[2,5,1024]{2,1,0:T(8,128)(2,1)S(1)}, bf16[2,5,1024]{2,1,0:T(8,128)(2,1)S(1)}, u32[]{:S(2)}, u32[]{:S(2)}) collective-permute-start(bf16[2,5,1024]{2,1,0:T(8,128)(2,1)S(1)} %pad_maximum_fusion), channel_id=1, source_target_pairs={{0,1},{1,0},{2,3},{3,2},{4,5},{5,4},{6,7},{7,6},{8,9},{9,8},{10,11... | collective-permute-start | bytes 61448 | tf_op jit(solution)/shard_map/ppermute | solution.py:185
  13.9 9.1 %collective-permute-start.6 = (bf16[128,1024]{1,0:T(8,128)(2,1)S(1)}, bf16[128,1024]{1,0:T(8,128)(2,1)S(1)}, u32[]{:S(2)}, u32[]{:S(2)}) collective-permute-start(bf16[128,1024]{1,0:T(8,128)(2,1)S(1)} %collective-permute-done.3.refs_4_), channel_id=1, source_target_pairs={{0,8},{8,0},{16,24},{24,16},{1,9},{9,1},{17,25},{25,17},{2,10},{10... | collective-permute-start | bytes 786440 | tf_op jit(solution)/shard_map/ppermute | solution.py:185
  15.7 3.7 %collective-permute-start.8 = (bf16[2,2,1024]{2,1,0:T(2,128)(2,1)S(1)}, bf16[2,2,1024]{2,1,0:T(2,128)(2,1)S(1)}, u32[]{:S(2)}, u32[]{:S(2)}) collective-permute-start(bf16[2,2,1024]{2,1,0:T(2,128)(2,1)S(1)} %pad_maximum_fusion.2), channel_id=1, source_target_pairs={{0,2},{1,3},{2,0},{3,1},{4,6},{5,7},{6,4},{7,5},{8,10},{9,11},{10,... | collective-permute-start | bytes 24584 | tf_op jit(solution)/shard_map/ppermute | solution.py:185
  19.4 4.3 %collective-permute-start.9 = (bf16[2,4,1024]{2,1,0:T(4,128)(2,1)S(1)}, bf16[2,4,1024]{2,1,0:T(4,128)(2,1)S(1)}, u32[]{:S(2)}, u32[]{:S(2)}) collective-permute-start(bf16[2,4,1024]{2,1,0:T(4,128)(2,1)S(1)} %after.9), channel_id=1, source_target_pairs={{0,16},{8,24},{16,0},{24,8},{1,17},{9,25},{17,1},{25,9},{2,18},{10... | collective-permute-start | bytes 49160 | tf_op jit(solution)/shard_map/ppermute | solution.py:185
  21.1 7.9 %collective-permute-start.10 = (bf16[64,1152]{1,0:T(8,128)(2,1)S(1)}, bf16[64,1152]{1,0:T(8,128)(2,1)S(1)}, u32[]{:S(2)}, u32[]{:S(2)}) collective-permute-start(bf16[64,1152]{1,0:T(8,128)(2,1)S(1)} %edge_part.1.refs_1_), channel_id=1, source_target_pairs={{0,7},{1,2},{2,1},{3,4},{4,3},{5,6},{6,5},{7,0},{8,15},{9,10},{10,... | collective-permute-start | bytes 442376 | tf_op jit(solution)/shard_map/ppermute | solution.py:190
  23.0 6.0 %copy-start = (bf16[1024,1024]{1,0:T(8,128)(2,1)S(1)}, bf16[1024,1024]{1,0:T(8,128)(2,1)}, u32[]{:S(2)}) copy-start(bf16[1024,1024]{1,0:T(8,128)(2,1)} %weight_ref.1) | copy-start | bytes 6291460
  23.6 5.4 %collective-permute-start.11 = (bf16[64,1152]{1,0:T(8,128)(2,1)S(1)}, bf16[64,1152]{1,0:T(8,128)(2,1)S(1)}, u32[]{:S(2)}, u32[]{:S(2)}) collective-permute-start(bf16[64,1152]{1,0:T(8,128)(2,1)S(1)} %inner_part.1.refs_1_), channel_id=1, source_target_pairs={{0,1},{1,0},{2,3},{3,2},{4,5},{5,4},{6,7},{7,6},{8,9},{9,8},{10,11... | collective-permute-start | bytes 442376 | tf_op jit(solution)/shard_map/ppermute | solution.py:185

commit v5 on v4

--- a/solution.py
+++ b/solution.py
@@ -51,24 +51,24 @@
     return jnp.where(odd, right, left), jnp.where(odd, left, right)
 
 
-def split_kernel(q_hbm, kv_hbm, qe_ref, qi_ref, edge_ref, inner_ref, pool_ref, q_ref, kv_ref, sems):
+def split_kernel(q_hbm, kv_hbm, *refs):
+    ke_ref, ve_ref, ki_ref, vi_ref, qi_ref, qe_ref, pool_ref, q_ref, kv_ref, sems = refs
     copies = [pltpu.make_async_copy(kv_hbm.at[i], kv_ref.at[i], sems.at[i]) for i in range(2)]
     copies.append(pltpu.make_async_copy(q_hbm, q_ref, sems.at[2]))
     for copy in copies:
         copy.start()
     odd = odd_column()
     pooled = []
-    for half in range(2):
+    for half, edge_ref, inner_ref in ((0, ke_ref, ki_ref), (1, ve_ref, vi_ref)):
         copies[half].wait()
         edge, inner = split_tiles(kv_ref[half].astype(F32), odd)
-        rows = slice(half * SPAN, (half + 1) * SPAN)
-        edge_ref[rows] = edge.astype(BF16)
-        inner_ref[rows] = inner.astype(BF16)
+        edge_ref[:SPAN] = edge.astype(BF16)
+        inner_ref[...] = inner.astype(BF16)
         for tile in (edge, inner):
             pooled.append(jnp.sum(tile, axis=0, keepdims=True) * (1.0 / SPAN))
     pooled = jnp.concatenate(pooled, axis=0).astype(BF16)
     pool_ref[...] = pooled
-    edge_ref[2 * SPAN :] = pooled
+    ke_ref[SPAN:] = pooled
     copies[2].wait()
     edge, inner = split_tiles(q_ref[...].astype(F32), odd)
     qe_ref[...] = edge.astype(BF16)
@@ -83,24 +83,24 @@
     return [slice(h * HEAD_DIM, (h + 1) * HEAD_DIM) for h in range(HEADS)]
 
 
-def stacked(refs, half, cols):
-    return jnp.concatenate([r[half * SPAN : (half + 1) * SPAN, cols] for r in refs], axis=0)
-
-
-def partial_kernel(n_lat, q_ref, own_ref, pair_ref, far_ref, out_ref):
-    tiles = (own_ref, pair_ref, far_ref)
+def stacked(refs, cols):
+    return jnp.concatenate([r[:SPAN, cols] for r in refs], axis=0)
+
+
+def partial_kernel(n_lat, q_ref, *refs):
+    keys, values, out_ref = refs[:3], refs[3:6], refs[6]
     far = far_exists(n_lat)
     lane = lax.broadcasted_iota(jnp.int32, (SPAN, 3 * SPAN), 1)
     keep = jnp.logical_or(lane < 2 * SPAN, far)
     column = lax.broadcasted_iota(jnp.int32, (SPAN, HEAD_DIM), 1)
     scores = [
-        jnp.where(keep, logits(q_ref[:, cols], stacked(tiles, 0, cols)), NEG) for cols in heads()
+        jnp.where(keep, logits(q_ref[:, cols], stacked(keys, cols)), NEG) for cols in heads()
     ]
     tops = [jnp.max(s, axis=-1, keepdims=True) for s in scores]
     expos = [jnp.exp(s - top) for s, top in zip(scores, tops)]
     totals = [jnp.sum(e, axis=-1, keepdims=True) for e in expos]
     parts = [
-        jnp.dot(e.astype(BF16), stacked(tiles, 1, cols), preferred_element_type=F32)
+        jnp.dot(e.astype(BF16), stacked(values, cols), preferred_element_type=F32)
         for e, cols in zip(expos, heads())
     ]
     stats = jnp.zeros((SPAN, HEAD_DIM), F32)
@@ -118,7 +118,8 @@
 
 
 def own_kernel(n_lat, count, *refs):
-    tiles, (qi_ref, qe_ref, coarse_ref, out_ref, lse_ref) = refs[:6], refs[6:]
+    keys, values = refs[0:12:2], refs[1:12:2]
+    qi_ref, qe_ref, coarse_ref, out_ref, lse_ref = refs[12:]
     rows = 2 * SPAN
     far = far_exists(n_lat)
     lane = lax.broadcasted_iota(jnp.int32, (rows, 6 * SPAN), 1)
@@ -131,7 +132,7 @@
         near, coarse = [], []
         for cols in heads()[group : group + 4]:
             q = jnp.concatenate([qe_ref[:, cols], qi_ref[:, cols]], axis=0)
-            near.append(jnp.where(keep, logits(q, stacked(tiles, 0, cols)), NEG))
+            near.append(jnp.where(keep, logits(q, stacked(keys, cols)), NEG))
             coarse.append(logits(q, coarse_ref[0, :, cols])[:, : 2 * count] + bias)
         tops = [
             jnp.maximum(jnp.max(n, axis=-1, keepdims=True), jnp.max(c, axis=-1, keepdims=True))
@@ -145,7 +146,7 @@
         ]
         for i, cols in enumerate(heads()[group : group + 4]):
             part = jnp.dot(
-                near[i].astype(BF16), stacked(tiles, 1, cols), preferred_element_type=F32
+                near[i].astype(BF16), stacked(values, cols), preferred_element_type=F32
             )
             part += jnp.dot(
                 coarse[i].astype(BF16), coarse_ref[1, : 2 * count, cols], preferred_element_type=F32
@@ -224,18 +225,12 @@
     def like(*shape):
         return jax.ShapeDtypeStruct(shape, BF16)
 
-    pack = 2 * SPAN + 4
-    q_edge, q_inner, edge_own, inner_own, pooled = pl.pallas_call(
+    tile = like(SPAN, width)
+    ke_own, ve_own, ki_own, vi_own, q_inner, q_edge, pooled = pl.pallas_call(
         split_kernel,
-        out_shape=[
-            like(SPAN, width),
-            like(SPAN, width),
-            like(pack, width),
-            like(2 * SPAN, width),
-            like(4, width),
-        ],
+        out_shape=[like(SPAN + 4, width), *[tile] * 5, like(4, width)],
         in_specs=[pl.BlockSpec(memory_space=pltpu.HBM)] * 2,
-        out_specs=[VMEM] * 5,
+        out_specs=[VMEM] * 7,
         scratch_shapes=[
             pltpu.VMEM(queries.shape, BF16),
             pltpu.VMEM(keys_values.shape, BF16),
@@ -245,53 +240,48 @@
         compiler_params=pltpu.CompilerParams(vmem_limit_bytes=LIMIT),
         cost_estimate=pl.CostEstimate(flops=0, bytes_accessed=2 << 20, transcendentals=0),
     )(*(pltpu.with_memory_space_constraint(x, pltpu.HBM) for x in (queries, keys_values)))
-    edge_pair = swap(edge_own, "lat", 1)
+    ke_pair = swap(ke_own, "lat", 1)
+    ve_pair = swap(ve_own, "lat", 1)
+    vi_hop = stride(vi_own, "lat", -2)
+    ki_pair = swap(ki_own, "lat", 1)
+    vi_pair = swap(vi_own, "lat", 1)
     far_q_edge = outward(q_edge, "lon")
     far_q_inner = swap(q_inner, "lon", 1)
-    inner_pair = swap(inner_own, "lat", 1)
-    inner_hop = stride(inner_own, "lat", -2)
     pooled = after(pooled, weight=4 * WEIGHT)
-    edge_pair = after(edge_pair, pooled, far_q_edge, far_q_inner, inner_hop)
-    edge_far = stride(edge_pair, "lat", 2)
-    inner_far = swap(inner_hop, "lat", 1)
+    ke_pair = after(ke_pair, pooled, far_q_inner, vi_hop)
+    ke_far = stride(ke_pair, "lat", 2)
+    ki_far = stride(ki_pair, "lat", 2)
+    vi_far = swap(vi_hop, "lat", 1)
     level0 = pooled.reshape(2, 2, width)
-    level0_lat = edge_pair[2 * SPAN :].reshape(2, 2, width)
+    level0_lat = ke_pair[SPAN:].reshape(2, 2, width)
     mine = mean_entries(level0[:, 0:1], level0[:, 1:2], level0_lat[:, 0:1], level0_lat[:, 1:2])
-    beside = swap(jnp.concatenate([level0, level0_lat, mine], axis=1), "lon", 1)
+    three = jnp.concatenate([level0, level0_lat, mine], axis=1)
+    beside = swap(three, "lon", 1)
+    ve_pair = after(ve_pair, far_q_edge, beside)
+    ve_far = stride(ve_pair, "lat", 2)
     group = jnp.concatenate([mine, beside[:, 4:5]], axis=1)
     group_lon = swap(group, "lon", 2)
-    group_both = jnp.concatenate([group, group_lon], axis=1)
-    group_lat = swap(after(group_both, inner_pair), "lat", 2)
+    both = jnp.concatenate([group, group_lon], axis=1)
+    both = after(both, ki_pair)
+    group_lat = swap(both, "lat", 2)
     coarse = jnp.concatenate([level0_lat, beside[:, 0:4], group_lon, group_lat], axis=1)
     count = coarse.shape[1] // 2
     coarse = jnp.pad(coarse, ((0, 0), (0, 16 - 2 * count), (0, 0)))
 
-    back = jax.ShapeDtypeStruct((SPAN, width + HEAD_DIM), BF16)
+    back = like(SPAN, width + HEAD_DIM)
     flops = 4 * SPAN * 3 * SPAN * width
-    edge_part = call(
-        functools.partial(partial_kernel, n_lat),
-        [back],
-        "edge_part",
-        flops,
-        far_q_edge,
-        edge_own,
-        edge_pair,
-        edge_far,
-    )[0]
+    part = functools.partial(partial_kernel, n_lat)
+    edge = (ke_own, ke_pair, ke_far, ve_own, ve_pair, ve_far)
+    edge_part = call(part, [back], "edge_part", flops, far_q_edge, *edge)[0]
     edge_back = outward(edge_part, "lon")
-    inner_far = after(inner_far, edge_part)
-    inner_part = call(
-        functools.partial(partial_kernel, n_lat),
-        [back],
-        "inner_part",
-        flops,
-        far_q_inner,
-        inner_own,
-        inner_pair,
-        inner_far,
-    )[0]
+    vi_far = after(vi_far, edge_part)
+    inner = (ki_own, ki_pair, ki_far, vi_own, vi_pair, vi_far)
+    inner_part = call(part, [back], "inner_part", flops, far_q_inner, *inner)[0]
     inner_back = swap(inner_part, "lon", 1)
     coarse = after(coarse, inner_part)
+    own_tiles = (ke_own, ve_own, ki_own, vi_own)
+    pair_tiles = (ke_pair, ve_pair, ki_pair, vi_pair)
+    far_tiles = (ke_far, ve_far, ki_far, vi_far)
     own, lse = call(
         functools.partial(own_kernel, n_lat, count),
         [
@@ -300,12 +290,9 @@
         ],
         "own_part",
         4 * flops,
-        edge_own,
-        inner_own,
-        edge_pair,
-        inner_pair,
-        edge_far,
-        inner_far,
+        *own_tiles,
+        *pair_tiles,
+        *far_tiles,
         q_inner,
         q_edge,
         coarse,

time: 30.7 us -> 31.1 us (1.013)
  starting transfers between devices: 14.5 us -> 16.1 us
  waiting for transfers between devices: 10.4 us -> 9.14 us
    ppermute x2, waiting for transfers between devices: 8.26 us -> 3.83 us  [outward(): lax.ppermute(x, axis, [(i, (i + (1 if i % 2 else -1)) % count) for i in r...]
    ppermute x2 -> x4, starting transfers between devices: 2.09 us -> 4.48 us  [stride(): return lax.ppermute(x, axis, route)]
    ppermute x8 -> x10, waiting for transfers between devices: 2.09 us -> 4.31 us  [swap(): return lax.ppermute(x, axis, [(i, i ^ distance) for i in range(count)])]
    ppermute x8 -> x10, starting transfers between devices: 8.1 us -> 6.71 us  [swap(): return lax.ppermute(x, axis, [(i, i ^ distance) for i in range(count)])]
    ppermute x2 -> x4, waiting for transfers between devices: 0.01 us -> 1 us  [stride(): return lax.ppermute(x, axis, route)]
    ppermute x2, starting transfers between devices: 4.32 us -> 4.95 us  [outward(): lax.ppermute(x, axis, [(i, (i + (1 if i % 2 else -1)) % count) for i in r...]
  transfers between devices with their start and end apart: 12 -> 16, of which waited for: 3 -> 8; matrix products, arithmetic and copies ran while one was open for 1% -> 1% of each run, Pallas kernels for 8% -> 8%
where the time goes in v5:
time: 31.1 us; the launch traced here: 31 us
  starting transfers between devices  16.1 us (52%)
  waiting for transfers between devices  9.14 us (29%)
  Pallas kernels  5.27 us (17%)
    ppermute x10, starting transfers between devices, swap(): return lax.ppermute(x, axis, [(i, i ^ distance) for i in range(count)])  6.71 us
    ppermute x2, starting transfers between devices, outward(): lax.ppermute(x, axis, [(i, (i + (1 if i % 2 else -1)) % count) for i in r...  4.95 us
    ppermute x4, starting transfers between devices, stride(): return lax.ppermute(x, axis, route)  4.48 us
    ppermute x10, waiting for transfers between devices, swap(): return lax.ppermute(x, axis, [(i, i ^ distance) for i in range(count)])  4.31 us
    pallas_call x4, Pallas kernels, call(): pl.pallas_call(kernel, out_shape=outs, in_specs=[VMEM] * len(args), out_s...  4.03 us
    ppermute x2, waiting for transfers between devices, outward(): lax.ppermute(x, axis, [(i, (i + (1 if i % 2 else -1)) % count) for i in r...  3.83 us
    pallas_call x1, Pallas kernels, shards(): pl.pallas_call(split_kernel, out_shape=[like(SPAN + 4, width), *[tile] *...  1.23 us
    ppermute x4, waiting for transfers between devices, stride(): return lax.ppermute(x, axis, route)  1 us
  transfers between devices with their start and end apart: 16, of which 8 were waited for; matrix products, arithmetic and copies ran while one was open for 1% of the time, Pallas kernels for 8%

profile of v5, /device:TPU:0, one launch (start us, length us, event | category | flops | bytes accessed | tf_op | source)
XLA Modules:
  0.0 31.0 jit_solution(3482304020032138496)
XLA Ops:
  0.0 1.2 %split.1 = (bf16[68,1024]{1,0:T(8,128)(2,1)S(1)}, bf16[64,1024]{1,0:T(8,128)(2,1)S(1)}, bf16[64,1024]{1,0:T(8,128)(2,1)S(1)}, bf16[64,1024]{1,0:T(8,128)(2,1)S(1...) custom-call(bf16[8,16,1024]{2,1,0:T(8,128)(2,1)} %q_hbm.1, ...), custom_call_target="tpu_custom_call" | custom-call | bytes 2097152 | tf_op jit(solution)/shard_map/split/pallas_call | solution.py:229
  1.2 3.0 %collective-permute-start = (bf16[68,1024]{1,0:T(8,128)(2,1)S(1)}, bf16[68,1024]{1,0:T(8,128)(2,1)S(1)}, u32[]{:S(2)}, u32[]{:S(2)}) collective-permute-start(bf16[68,1024]{1,0:T(8,128)(2,1)S(1)} %get-tuple-element.14.refs_0_), channel_id=1, source_target_pairs={{0,8},{8,0},{16,24},{24,16},{1,9},{9,1},{17,25},{25,17},{2,10},{10... | collective-permute-start | bytes 417800 | tf_op jit(solution)/shard_map/ppermute | solution.py:186
  4.2 1.5 %collective-permute-start.2 = (bf16[64,1024]{1,0:T(8,128)(2,1)S(1)}, bf16[64,1024]{1,0:T(8,128)(2,1)S(1)}, u32[]{:S(2)}, u32[]{:S(2)}) collective-permute-start(bf16[64,1024]{1,0:T(8,128)(2,1)S(1)} %get-tuple-element.17.refs_3_), channel_id=1, source_target_pairs={{0,16},{8,24},{16,0},{24,8},{1,17},{9,25},{17,1},{25,9},{2,18},{10... | collective-permute-start | bytes 393224 | tf_op jit(solution)/shard_map/ppermute | solution.py:197
  5.8 3.4 %collective-permute-start.4 = (bf16[64,1024]{1,0:T(8,128)(2,1)S(1)}, bf16[64,1024]{1,0:T(8,128)(2,1)S(1)}, u32[]{:S(2)}, u32[]{:S(2)}) collective-permute-start(bf16[64,1024]{1,0:T(8,128)(2,1)S(1)} %get-tuple-element.20.refs_13_), channel_id=1, source_target_pairs={{0,7},{1,2},{2,1},{3,4},{4,3},{5,6},{6,5},{7,0},{8,15},{9,10},{10,... | collective-permute-start | bytes 393224 | tf_op jit(solution)/shard_map/ppermute | solution.py:191
  9.2 0.5 %collective-permute-start.3 = (bf16[64,1024]{1,0:T(8,128)(2,1)S(1)}, bf16[64,1024]{1,0:T(8,128)(2,1)S(1)}, u32[]{:S(2)}, u32[]{:S(2)}) collective-permute-start(bf16[64,1024]{1,0:T(8,128)(2,1)S(1)} %get-tuple-element.15.refs_3_.refs_1_), channel_id=1, source_target_pairs={{0,8},{8,0},{16,24},{24,16},{1,9},{9,1},{17,25},{25,17},{2,10},{10... | collective-permute-start | bytes 393224 | tf_op jit(solution)/shard_map/ppermute | solution.py:186
  9.8 0.4 %collective-permute-done.2.refs_3_ = bf16[64,1024]{1,0:T(8,128)(2,1)S(1)} collective-permute-done((bf16[64,1024]{1,0:T(8,128)(2,1)S(1)}, bf16[64,1024]{1,0:T(8,128)(2,1)S(1)}, u32[]{:S(2)}, u32[]{:S(2)}) %collective-permute-start.2) | collective-permute-done | bytes 131104 | tf_op jit(solution)/shard_map/ppermute | solution.py:197
  10.2 0.0 collective-permute-done.refs_0_
  10.3 0.1 collective-permute-start.5
  10.3 1.2 %collective-permute-start.6 = (bf16[64,1024]{1,0:T(8,128)(2,1)S(1)}, bf16[64,1024]{1,0:T(8,128)(2,1)S(1)}, u32[]{:S(2)}, u32[]{:S(2)}) collective-permute-start(bf16[64,1024]{1,0:T(8,128)(2,1)S(1)} %get-tuple-element.16.refs_0_.refs_2_), channel_id=1, source_target_pairs={{0,8},{8,0},{16,24},{24,16},{1,9},{9,1},{17,25},{25,17},{2,10},{10... | collective-permute-start | bytes 393224 | tf_op jit(solution)/shard_map/ppermute | solution.py:186
  11.5 0.9 %collective-permute-start.8 = (bf16[68,1024]{1,0:T(8,128)(2,1)S(1)}, bf16[68,1024]{1,0:T(8,128)(2,1)S(1)}, u32[]{:S(2)}, u32[]{:S(2)}) collective-permute-start(bf16[68,1024]{1,0:T(8,128)(2,1)S(1)} %after.8.refs_1_.refs_4_), channel_id=1, source_target_pairs={{0,16},{8,24},{16,0},{24,8},{1,17},{9,25},{17,1},{25,9},{2,18},{10... | collective-permute-start | bytes 417800 | tf_op jit(solution)/shard_map/ppermute | solution.py:197
  12.5 0.3 %collective-permute-done.4.refs_1_.q_ref = bf16[64,1024]{1,0:T(8,128)(2,1)S(1)} collective-permute-done((bf16[64,1024]{1,0:T(8,128)(2,1)S(1)}, bf16[64,1024]{1,0:T(8,128)(2,1)S(1)}, u32[]{:S(2)}, u32[]{:S(2)}) %collective-permute-start.4) | collective-permute-done | bytes 131104 | tf_op jit(solution)/shard_map/ppermute | solution.py:191
  12.8 2.2 %collective-permute-done.3.refs_0_ = bf16[64,1024]{1,0:T(8,128)(2,1)S(1)} collective-permute-done((bf16[64,1024]{1,0:T(8,128)(2,1)S(1)}, bf16[64,1024]{1,0:T(8,128)(2,1)S(1)}, u32[]{:S(2)}, u32[]{:S(2)}) %collective-permute-start.3) | collective-permute-done | bytes 131104 | tf_op jit(solution)/shard_map/ppermute | solution.py:186
  14.9 0.0 collective-permute-start.9
  15.0 0.1 collective-permute-start.12
  15.1 1.2 %collective-permute-start.11 = (bf16[64,1024]{1,0:T(8,128)(2,1)S(1)}, bf16[64,1024]{1,0:T(8,128)(2,1)S(1)}, u32[]{:S(2)}, u32[]{:S(2)}) collective-permute-start(bf16[64,1024]{1,0:T(8,128)(2,1)S(1)} %collective-permute-done.2.refs_3_), channel_id=1, source_target_pairs={{0,8},{8,0},{16,24},{24,16},{1,9},{9,1},{17,25},{25,17},{2,10},{10... | collective-permute-start | bytes 393224 | tf_op jit(solution)/shard_map/ppermute | solution.py:186
  16.2 0.7 %collective-permute-done.6.refs_1_.refs_6_ = bf16[64,1024]{1,0:T(8,128)(2,1)S(1)} collective-permute-done((bf16[64,1024]{1,0:T(8,128)(2,1)S(1)}, bf16[64,1024]{1,0:T(8,128)(2,1)S(1)}, u32[]{:S(2)}, u32[]{:S(2)}) %collective-permute-start.6) | collective-permute-done | bytes 131104 | tf_op jit(solution)/shard_map/ppermute | solution.py:186
  17.0 0.5 %collective-permute-start.7 = (bf16[64,1024]{1,0:T(8,128)(2,1)S(1)}, bf16[64,1024]{1,0:T(8,128)(2,1)S(1)}, u32[]{:S(2)}, u32[]{:S(2)}) collective-permute-start(bf16[64,1024]{1,0:T(8,128)(2,1)S(1)} %get-tuple-element.17.refs_3_), channel_id=1, source_target_pairs={{0,8},{8,0},{16,24},{24,16},{1,9},{9,1},{17,25},{25,17},{2,10},{10... | collective-permute-start | bytes 393224 | tf_op jit(solution)/shard_map/ppermute | solution.py:186
  17.5 1.2 %collective-permute-done.12 = bf16[2,2,1024]{2,1,0:T(2,128)(2,1)S(1)} collective-permute-done((bf16[2,2,1024]{2,1,0:T(2,128)(2,1)S(1)}, bf16[2,2,1024]{2,1,0:T(2,128)(2,1)S(1)}, u32[]{:S(2)}, u32[]{:S(2)}) %collective-permute-start.12) | collective-permute-done | bytes 8224 | tf_op jit(solution)/shard_map/ppermute | solution.py:186
  18.7 2.0 %collective-permute-start.10 = (bf16[64,1024]{1,0:T(8,128)(2,1)S(1)}, bf16[64,1024]{1,0:T(8,128)(2,1)S(1)}, u32[]{:S(2)}, u32[]{:S(2)}) collective-permute-start(bf16[64,1024]{1,0:T(8,128)(2,1)S(1)} %collective-permute-done.6.refs_1_.refs_6_), channel_id=1, source_target_pairs={{0,16},{8,24},{16,0},{24,8},{1,17},{9,25},{17,1},{25,9},{2,18},{10... | collective-permute-start | bytes 393224 | tf_op jit(solution)/shard_map/ppermute | solution.py:197
  20.8 0.0 collective-permute-done.8.refs_2_.refs_8_
  20.8 0.1 collective-permute-start.13
  20.9 0.6 %edge_part.1.refs_1_ = bf16[64,1152]{1,0:T(8,128)(2,1)S(1)} custom-call(bf16[64,1024]{1,0:T(8,128)(2,1)S(1)} %collective-permute-done.4.refs_1_.q_ref, bf16[68,1024]{1,0:T(8,128)(2,1)S(1)} %get-tuple-element.14.refs_0_, bf16[68,1024]{1,0:T(8,128)(2,1)S(1)} %after.8.refs_1_.refs_4_, bf16[68,1024]{1,0:T(8,128)(2,1)S(1)} %collective-permute-done.8.refs_2_.refs_8_, ...), custom_call_target="tpu_custom_call" | custom-call | flops 50331648 | bytes 1089536 | tf_op jit(solution)/shard_map/edge_part/pallas_call | solution.py:27
  21.5 1.5 %collective-permute-start.14 = (bf16[64,1152]{1,0:T(8,128)(2,1)S(1)}, bf16[64,1152]{1,0:T(8,128)(2,1)S(1)}, u32[]{:S(2)}, u32[]{:S(2)}) collective-permute-start(bf16[64,1152]{1,0:T(8,128)(2,1)S(1)} %edge_part.1.refs_1_), channel_id=1, source_target_pairs={{0,7},{1,2},{2,1},{3,4},{4,3},{5,6},{6,5},{7,0},{8,15},{9,10},{10,... | collective-permute-start | bytes 442376 | tf_op jit(solution)/shard_map/ppermute | solution.py:191
  23.1 0.0 copy-start
  23.1 0.6 %collective-permute-done.10.refs_2_.refs_10_ = bf16[64,1024]{1,0:T(8,128)(2,1)S(1)} collective-permute-done((bf16[64,1024]{1,0:T(8,128)(2,1)S(1)}, bf16[64,1024]{1,0:T(8,128)(2,1)S(1)}, u32[]{:S(2)}, u32[]{:S(2)}) %collective-permute-start.10) | collective-permute-done | bytes 131104 | tf_op jit(solution)/shard_map/ppermute | solution.py:197
  23.7 0.6 %inner_part.1.refs_1_ = bf16[64,1152]{1,0:T(8,128)(2,1)S(1)} custom-call(bf16[64,1024]{1,0:T(8,128)(2,1)S(1)} %collective-permute-done.1.refs_2_.q_ref, bf16[64,1024]{1,0:T(8,128)(2,1)S(1)} %get-tuple-element.16.refs_0_.refs_2_, bf16[64,1024]{1,0:T(8,128)(2,1)S(1)} %collective-permute-done.6.refs_1_.refs_6_, ...), custom_call_target="tpu_custom_call" | custom-call | flops 50331648 | bytes 1064960 | tf_op jit(solution)/shard_map/inner_part/pallas_call | solution.py:27
  24.3 0.1 collective-permute-start.15
  24.4 0.2 collective-permute-done.13
  24.6 0.1 fusion.6.refs_0_
  24.7 1.3 %own_part.1 = (f32[128,1024]{1,0:T(8,128)S(1)}, f32[128,128]{1,0:T(8,128)S(1)}) custom-call(bf16[68,1024]{1,0:T(8,128)(2,1)S(1)} %get-tuple-element.14.refs_0_, bf16[64,1024]{1,0:T(8,128)(2,1)S(1)} %get-tuple-element.15.refs_3_.refs_1_, bf16[64,1024]{1,0:T(8,128)(2,1)S(1)} %get-tuple-element.16.refs_0_.refs_2_, ...), custom_call_target="tpu_custom_call" | custom-call | flops 201326592 | bytes 2514944 | tf_op jit(solution)/shard_map/own_part/pallas_call | solution.py:27
  25.9 3.5 %collective-permute-done.14.refs_0_ = bf16[64,1152]{1,0:T(8,128)(2,1)S(1)} collective-permute-done((bf16[64,1152]{1,0:T(8,128)(2,1)S(1)}, bf16[64,1152]{1,0:T(8,128)(2,1)S(1)}, u32[]{:S(2)}, u32[]{:S(2)}) %collective-permute-start.14) | collective-permute-done | bytes 147488 | tf_op jit(solution)/shard_map/ppermute | solution.py:191
  29.4 1.5 %merge.1 = bf16[8,16,1024]{2,1,0:T(8,128)(2,1)} custom-call(f32[128,1024]{1,0:T(8,128)S(1)} %get-tuple-element.21.refs_1_.own_ref, f32[128,128]{1,0:T(8,128)S(1)} %get-tuple-element.22.lse_ref, bf16[64,1152]{1,0:T(8,128)(2,1)S(1)} %after.13.edge_ref, bf16[64,1152]{1,0:T(8,128)(2,1)S(1)} %collective-permute-done.15.inner_ref, bf16[1024,1024]{1,0:T(8,128)(2,1)S(1)} %copy-done), custom_call_target="tpu_custom_call" | custom-call | flops 268435456 | bytes 3244032 | tf_op jit(solution)/shard_map/merge/pallas_call | solution.py:27
  (24 shorter events, 0.2 us)
Async XLA Ops:
  1.2 8.9 %collective-permute-start = (bf16[68,1024]{1,0:T(8,128)(2,1)S(1)}, bf16[68,1024]{1,0:T(8,128)(2,1)S(1)}, u32[]{:S(2)}, u32[]{:S(2)}) collective-permute-start(bf16[68,1024]{1,0:T(8,128)(2,1)S(1)} %get-tuple-element.14.refs_0_), channel_id=1, source_target_pairs={{0,8},{8,0},{16,24},{24,16},{1,9},{9,1},{17,25},{25,17},{2,10},{10... | collective-permute-start | bytes 417800 | tf_op jit(solution)/shard_map/ppermute | solution.py:186
  4.2 5.5 %collective-permute-start.1 = (bf16[64,1024]{1,0:T(8,128)(2,1)S(1)}, bf16[64,1024]{1,0:T(8,128)(2,1)S(1)}, u32[]{:S(2)}, u32[]{:S(2)}) collective-permute-start(bf16[64,1024]{1,0:T(8,128)(2,1)S(1)} %get-tuple-element.19.refs_12_), channel_id=1, source_target_pairs={{0,1},{1,0},{2,3},{3,2},{4,5},{5,4},{6,7},{7,6},{8,9},{9,8},{10,11... | collective-permute-start | bytes 393224 | tf_op jit(solution)/shard_map/ppermute | solution.py:186
  4.2 5.9 %collective-permute-start.2 = (bf16[64,1024]{1,0:T(8,128)(2,1)S(1)}, bf16[64,1024]{1,0:T(8,128)(2,1)S(1)}, u32[]{:S(2)}, u32[]{:S(2)}) collective-permute-start(bf16[64,1024]{1,0:T(8,128)(2,1)S(1)} %get-tuple-element.17.refs_3_), channel_id=1, source_target_pairs={{0,16},{8,24},{16,0},{24,8},{1,17},{9,25},{17,1},{25,9},{2,18},{10... | collective-permute-start | bytes 393224 | tf_op jit(solution)/shard_map/ppermute | solution.py:197
  5.8 7.0 %collective-permute-start.4 = (bf16[64,1024]{1,0:T(8,128)(2,1)S(1)}, bf16[64,1024]{1,0:T(8,128)(2,1)S(1)}, u32[]{:S(2)}, u32[]{:S(2)}) collective-permute-start(bf16[64,1024]{1,0:T(8,128)(2,1)S(1)} %get-tuple-element.20.refs_13_), channel_id=1, source_target_pairs={{0,7},{1,2},{2,1},{3,4},{4,3},{5,6},{6,5},{7,0},{8,15},{9,10},{10,... | collective-permute-start | bytes 393224 | tf_op jit(solution)/shard_map/ppermute | solution.py:191
  9.2 5.7 %collective-permute-start.3 = (bf16[64,1024]{1,0:T(8,128)(2,1)S(1)}, bf16[64,1024]{1,0:T(8,128)(2,1)S(1)}, u32[]{:S(2)}, u32[]{:S(2)}) collective-permute-start(bf16[64,1024]{1,0:T(8,128)(2,1)S(1)} %get-tuple-element.15.refs_3_.refs_1_), channel_id=1, source_target_pairs={{0,8},{8,0},{16,24},{24,16},{1,9},{9,1},{17,25},{25,17},{2,10},{10... | collective-permute-start | bytes 393224 | tf_op jit(solution)/shard_map/ppermute | solution.py:186
  10.3 4.7 %collective-permute-start.5 = (bf16[2,5,1024]{2,1,0:T(8,128)(2,1)S(1)}, bf16[2,5,1024]{2,1,0:T(8,128)(2,1)S(1)}, u32[]{:S(2)}, u32[]{:S(2)}) collective-permute-start(bf16[2,5,1024]{2,1,0:T(8,128)(2,1)S(1)} %pad_maximum_fusion), channel_id=1, source_target_pairs={{0,1},{1,0},{2,3},{3,2},{4,5},{5,4},{6,7},{7,6},{8,9},{9,8},{10,11... | collective-permute-start | bytes 61448 | tf_op jit(solution)/shard_map/ppermute | solution.py:186
  10.3 6.6 %collective-permute-start.6 = (bf16[64,1024]{1,0:T(8,128)(2,1)S(1)}, bf16[64,1024]{1,0:T(8,128)(2,1)S(1)}, u32[]{:S(2)}, u32[]{:S(2)}) collective-permute-start(bf16[64,1024]{1,0:T(8,128)(2,1)S(1)} %get-tuple-element.16.refs_0_.refs_2_), channel_id=1, source_target_pairs={{0,8},{8,0},{16,24},{24,16},{1,9},{9,1},{17,25},{25,17},{2,10},{10... | collective-permute-start | bytes 393224 | tf_op jit(solution)/shard_map/ppermute | solution.py:186
  11.5 9.3 %collective-permute-start.8 = (bf16[68,1024]{1,0:T(8,128)(2,1)S(1)}, bf16[68,1024]{1,0:T(8,128)(2,1)S(1)}, u32[]{:S(2)}, u32[]{:S(2)}) collective-permute-start(bf16[68,1024]{1,0:T(8,128)(2,1)S(1)} %after.8.refs_1_.refs_4_), channel_id=1, source_target_pairs={{0,16},{8,24},{16,0},{24,8},{1,17},{9,25},{17,1},{25,9},{2,18},{10... | collective-permute-start | bytes 417800 | tf_op jit(solution)/shard_map/ppermute | solution.py:197
  14.9 5.9 %collective-permute-start.9 = (bf16[64,1024]{1,0:T(8,128)(2,1)S(1)}, bf16[64,1024]{1,0:T(8,128)(2,1)S(1)}, u32[]{:S(2)}, u32[]{:S(2)}) collective-permute-start(bf16[64,1024]{1,0:T(8,128)(2,1)S(1)} %after.9.refs_4_.refs_5_), channel_id=1, source_target_pairs={{0,16},{8,24},{16,0},{24,8},{1,17},{9,25},{17,1},{25,9},{2,18},{10... | collective-permute-start | bytes 393224 | tf_op jit(solution)/shard_map/ppermute | solution.py:197
  15.0 3.7 %collective-permute-start.12 = (bf16[2,2,1024]{2,1,0:T(2,128)(2,1)S(1)}, bf16[2,2,1024]{2,1,0:T(2,128)(2,1)S(1)}, u32[]{:S(2)}, u32[]{:S(2)}) collective-permute-start(bf16[2,2,1024]{2,1,0:T(2,128)(2,1)S(1)} %pad_maximum_fusion.2), channel_id=1, source_target_pairs={{0,2},{1,3},{2,0},{3,1},{4,6},{5,7},{6,4},{7,5},{8,10},{9,11},{10,... | collective-permute-start | bytes 24584 | tf_op jit(solution)/shard_map/ppermute | solution.py:186
  15.1 8.0 %collective-permute-start.11 = (bf16[64,1024]{1,0:T(8,128)(2,1)S(1)}, bf16[64,1024]{1,0:T(8,128)(2,1)S(1)}, u32[]{:S(2)}, u32[]{:S(2)}) collective-permute-start(bf16[64,1024]{1,0:T(8,128)(2,1)S(1)} %collective-permute-done.2.refs_3_), channel_id=1, source_target_pairs={{0,8},{8,0},{16,24},{24,16},{1,9},{9,1},{17,25},{25,17},{2,10},{10... | collective-permute-start | bytes 393224 | tf_op jit(solution)/shard_map/ppermute | solution.py:186
  17.0 6.1 %collective-permute-start.7 = (bf16[64,1024]{1,0:T(8,128)(2,1)S(1)}, bf16[64,1024]{1,0:T(8,128)(2,1)S(1)}, u32[]{:S(2)}, u32[]{:S(2)}) collective-permute-start(bf16[64,1024]{1,0:T(8,128)(2,1)S(1)} %get-tuple-element.17.refs_3_), channel_id=1, source_target_pairs={{0,8},{8,0},{16,24},{24,16},{1,9},{9,1},{17,25},{25,17},{2,10},{10... | collective-permute-start | bytes 393224 | tf_op jit(solution)/shard_map/ppermute | solution.py:186
  18.7 5.0 %collective-permute-start.10 = (bf16[64,1024]{1,0:T(8,128)(2,1)S(1)}, bf16[64,1024]{1,0:T(8,128)(2,1)S(1)}, u32[]{:S(2)}, u32[]{:S(2)}) collective-permute-start(bf16[64,1024]{1,0:T(8,128)(2,1)S(1)} %collective-permute-done.6.refs_1_.refs_6_), channel_id=1, source_target_pairs={{0,16},{8,24},{16,0},{24,8},{1,17},{9,25},{17,1},{25,9},{2,18},{10... | collective-permute-start | bytes 393224 | tf_op jit(solution)/shard_map/ppermute | solution.py:197
  20.8 3.8 %collective-permute-start.13 = (bf16[2,4,1024]{2,1,0:T(4,128)(2,1)S(1)}, bf16[2,4,1024]{2,1,0:T(4,128)(2,1)S(1)}, u32[]{:S(2)}, u32[]{:S(2)}) collective-permute-start(bf16[2,4,1024]{2,1,0:T(4,128)(2,1)S(1)} %after.11), channel_id=1, source_target_pairs={{0,16},{8,24},{16,0},{24,8},{1,17},{9,25},{17,1},{25,9},{2,18},{10... | collective-permute-start | bytes 49160 | tf_op jit(solution)/shard_map/ppermute | solution.py:186
  21.5 7.9 %collective-permute-start.14 = (bf16[64,1152]{1,0:T(8,128)(2,1)S(1)}, bf16[64,1152]{1,0:T(8,128)(2,1)S(1)}, u32[]{:S(2)}, u32[]{:S(2)}) collective-permute-start(bf16[64,1152]{1,0:T(8,128)(2,1)S(1)} %edge_part.1.refs_1_), channel_id=1, source_target_pairs={{0,7},{1,2},{2,1},{3,4},{4,3},{5,6},{6,5},{7,0},{8,15},{9,10},{10,... | collective-permute-start | bytes 442376 | tf_op jit(solution)/shard_map/ppermute | solution.py:191
  23.1 6.4 %copy-start = (bf16[1024,1024]{1,0:T(8,128)(2,1)S(1)}, bf16[1024,1024]{1,0:T(8,128)(2,1)}, u32[]{:S(2)}) copy-start(bf16[1024,1024]{1,0:T(8,128)(2,1)} %weight_ref.1) | copy-start | bytes 6291460
  24.3 5.1 %collective-permute-start.15 = (bf16[64,1152]{1,0:T(8,128)(2,1)S(1)}, bf16[64,1152]{1,0:T(8,128)(2,1)S(1)}, u32[]{:S(2)}, u32[]{:S(2)}) collective-permute-start(bf16[64,1152]{1,0:T(8,128)(2,1)S(1)} %inner_part.1.refs_1_), channel_id=1, source_target_pairs={{0,1},{1,0},{2,3},{3,2},{4,5},{5,4},{6,7},{7,6},{8,9},{9,8},{10,11... | collective-permute-start | bytes 442376 | tf_op jit(solution)/shard_map/ppermute | solution.py:186

commit v6 on v5

--- a/solution.py
+++ b/solution.py
@@ -242,16 +242,16 @@
     )(*(pltpu.with_memory_space_constraint(x, pltpu.HBM) for x in (queries, keys_values)))
     ke_pair = swap(ke_own, "lat", 1)
     ve_pair = swap(ve_own, "lat", 1)
-    vi_hop = stride(vi_own, "lat", -2)
     ki_pair = swap(ki_own, "lat", 1)
     vi_pair = swap(vi_own, "lat", 1)
     far_q_edge = outward(q_edge, "lon")
     far_q_inner = swap(q_inner, "lon", 1)
     pooled = after(pooled, weight=4 * WEIGHT)
-    ke_pair = after(ke_pair, pooled, far_q_inner, vi_hop)
+    ke_pair = after(ke_pair, pooled, far_q_inner)
     ke_far = stride(ke_pair, "lat", 2)
     ki_far = stride(ki_pair, "lat", 2)
-    vi_far = swap(vi_hop, "lat", 1)
+    vi_pair = after(vi_pair, ke_far)
+    vi_far = stride(vi_pair, "lat", 2)
     level0 = pooled.reshape(2, 2, width)
     level0_lat = ke_pair[SPAN:].reshape(2, 2, width)
     mine = mean_entries(level0[:, 0:1], level0[:, 1:2], level0_lat[:, 0:1], level0_lat[:, 1:2])
@@ -262,7 +262,6 @@
     group = jnp.concatenate([mine, beside[:, 4:5]], axis=1)
     group_lon = swap(group, "lon", 2)
     both = jnp.concatenate([group, group_lon], axis=1)
-    both = after(both, ki_pair)
     group_lat = swap(both, "lat", 2)
     coarse = jnp.concatenate([level0_lat, beside[:, 0:4], group_lon, group_lat], axis=1)
     count = coarse.shape[1] // 2

time: 31.1 us -> 30.9 us (level)
  waiting for transfers between devices: 9.14 us -> 6.24 us
  starting transfers between devices: 16.1 us -> 18.8 us
    ppermute x2, waiting for transfers between devices: 3.83 us -> 2.13 us  [outward(): lax.ppermute(x, axis, [(i, (i + (1 if i % 2 else -1)) % count) for i in r...]
    ppermute x2, starting transfers between devices: 4.95 us -> 6.61 us  [outward(): lax.ppermute(x, axis, [(i, (i + (1 if i % 2 else -1)) % count) for i in r...]
    ppermute x4, waiting for transfers between devices: 1 us -> 0.01 us  [stride(): return lax.ppermute(x, axis, route)]
    ppermute x10 -> x9, starting transfers between devices: 6.71 us -> 7.24 us  [swap(): return lax.ppermute(x, axis, [(i, i ^ distance) for i in range(count)])]
    ppermute x4, starting transfers between devices: 4.48 us -> 4.95 us  [stride(): return lax.ppermute(x, axis, route)]
    ppermute x10 -> x9, waiting for transfers between devices: 4.31 us -> 4.1 us  [swap(): return lax.ppermute(x, axis, [(i, i ^ distance) for i in range(count)])]
  transfers between devices with their start and end apart: 16 -> 15, of which waited for: 8 -> 4; matrix products, arithmetic and copies ran while one was open for 1% -> 1% of each run, Pallas kernels for 8% -> 8%
where the time goes in v6:
time: 30.9 us; the launch traced here: 30.7 us
  starting transfers between devices  18.8 us (61%)
  waiting for transfers between devices  6.24 us (20%)
  Pallas kernels  5.27 us (17%)
    ppermute x9, starting transfers between devices, swap(): return lax.ppermute(x, axis, [(i, i ^ distance) for i in range(count)])  7.24 us
    ppermute x2, starting transfers between devices, outward(): lax.ppermute(x, axis, [(i, (i + (1 if i % 2 else -1)) % count) for i in r...  6.61 us
    ppermute x4, starting transfers between devices, stride(): return lax.ppermute(x, axis, route)  4.95 us
    ppermute x9, waiting for transfers between devices, swap(): return lax.ppermute(x, axis, [(i, i ^ distance) for i in range(count)])  4.1 us
    pallas_call x4, Pallas kernels, call(): pl.pallas_call(kernel, out_shape=outs, in_specs=[VMEM] * len(args), out_s...  4.04 us
    ppermute x2, waiting for transfers between devices, outward(): lax.ppermute(x, axis, [(i, (i + (1 if i % 2 else -1)) % count) for i in r...  2.13 us
    pallas_call x1, Pallas kernels, shards(): pl.pallas_call(split_kernel, out_shape=[like(SPAN + 4, width), *[tile] *...  1.23 us
  transfers between devices with their start and end apart: 15, of which 4 were waited for; matrix products, arithmetic and copies ran while one was open for 1% of the time, Pallas kernels for 8%

profile of v6, /device:TPU:0, one launch (start us, length us, event | category | flops | bytes accessed | tf_op | source)
XLA Modules:
  0.0 30.7 jit_solution(17073694508667825599)
XLA Ops:
  0.0 1.2 %split.1 = (bf16[68,1024]{1,0:T(8,128)(2,1)S(1)}, bf16[64,1024]{1,0:T(8,128)(2,1)S(1)}, bf16[64,1024]{1,0:T(8,128)(2,1)S(1)}, bf16[64,1024]{1,0:T(8,128)(2,1)S(1...) custom-call(bf16[8,16,1024]{2,1,0:T(8,128)(2,1)} %q_hbm.1, ...), custom_call_target="tpu_custom_call" | custom-call | bytes 2097152 | tf_op jit(solution)/shard_map/split/pallas_call | solution.py:229
  1.2 3.0 %collective-permute-start = (bf16[68,1024]{1,0:T(8,128)(2,1)S(1)}, bf16[68,1024]{1,0:T(8,128)(2,1)S(1)}, u32[]{:S(2)}, u32[]{:S(2)}) collective-permute-start(bf16[68,1024]{1,0:T(8,128)(2,1)S(1)} %get-tuple-element.14.refs_0_), channel_id=1, source_target_pairs={{0,8},{8,0},{16,24},{24,16},{1,9},{9,1},{17,25},{25,17},{2,10},{10... | collective-permute-start | bytes 417800 | tf_op jit(solution)/shard_map/ppermute | solution.py:186
  4.2 3.7 %collective-permute-start.3 = (bf16[64,1024]{1,0:T(8,128)(2,1)S(1)}, bf16[64,1024]{1,0:T(8,128)(2,1)S(1)}, u32[]{:S(2)}, u32[]{:S(2)}) collective-permute-start(bf16[64,1024]{1,0:T(8,128)(2,1)S(1)} %get-tuple-element.20.refs_13_), channel_id=1, source_target_pairs={{0,7},{1,2},{2,1},{3,4},{4,3},{5,6},{6,5},{7,0},{8,15},{9,10},{10,... | collective-permute-start | bytes 393224 | tf_op jit(solution)/shard_map/ppermute | solution.py:191
  8.0 0.5 %collective-permute-start.2 = (bf16[64,1024]{1,0:T(8,128)(2,1)S(1)}, bf16[64,1024]{1,0:T(8,128)(2,1)S(1)}, u32[]{:S(2)}, u32[]{:S(2)}) collective-permute-start(bf16[64,1024]{1,0:T(8,128)(2,1)S(1)} %get-tuple-element.15.refs_3_.refs_1_), channel_id=1, source_target_pairs={{0,8},{8,0},{16,24},{24,16},{1,9},{9,1},{17,25},{25,17},{2,10},{10... | collective-permute-start | bytes 393224 | tf_op jit(solution)/shard_map/ppermute | solution.py:186
  8.5 0.0 collective-permute-done.1.refs_2_.q_ref
  8.5 1.6 %collective-permute-start.7 = (bf16[68,1024]{1,0:T(8,128)(2,1)S(1)}, bf16[68,1024]{1,0:T(8,128)(2,1)S(1)}, u32[]{:S(2)}, u32[]{:S(2)}) collective-permute-start(bf16[68,1024]{1,0:T(8,128)(2,1)S(1)} %after.8.refs_1_.refs_4_), channel_id=1, source_target_pairs={{0,16},{8,24},{16,0},{24,8},{1,17},{9,25},{17,1},{25,9},{2,18},{10... | collective-permute-start | bytes 417800 | tf_op jit(solution)/shard_map/ppermute | solution.py:197
  10.2 0.1 collective-permute-start.4
  10.3 2.1 %collective-permute-start.6 = (bf16[64,1024]{1,0:T(8,128)(2,1)S(1)}, bf16[64,1024]{1,0:T(8,128)(2,1)S(1)}, u32[]{:S(2)}, u32[]{:S(2)}) collective-permute-start(bf16[64,1024]{1,0:T(8,128)(2,1)S(1)} %get-tuple-element.17.refs_3_), channel_id=1, source_target_pairs={{0,8},{8,0},{16,24},{24,16},{1,9},{9,1},{17,25},{25,17},{2,10},{10... | collective-permute-start | bytes 393224 | tf_op jit(solution)/shard_map/ppermute | solution.py:186
  12.4 0.0 collective-permute-done.3.refs_1_.q_ref
  12.4 0.1 collective-permute-start.5
  12.5 0.4 %collective-permute-done.2.refs_0_ = bf16[64,1024]{1,0:T(8,128)(2,1)S(1)} collective-permute-done((bf16[64,1024]{1,0:T(8,128)(2,1)S(1)}, bf16[64,1024]{1,0:T(8,128)(2,1)S(1)}, u32[]{:S(2)}, u32[]{:S(2)}) %collective-permute-start.2) | collective-permute-done | bytes 131104 | tf_op jit(solution)/shard_map/ppermute | solution.py:186
  12.9 0.0 collective-permute-done.4.refs_2_
  12.9 1.8 %collective-permute-start.8 = (bf16[64,1024]{1,0:T(8,128)(2,1)S(1)}, bf16[64,1024]{1,0:T(8,128)(2,1)S(1)}, u32[]{:S(2)}, u32[]{:S(2)}) collective-permute-start(bf16[64,1024]{1,0:T(8,128)(2,1)S(1)} %after.9.refs_4_.refs_5_), channel_id=1, source_target_pairs={{0,16},{8,24},{16,0},{24,8},{1,17},{9,25},{17,1},{25,9},{2,18},{10... | collective-permute-start | bytes 393224 | tf_op jit(solution)/shard_map/ppermute | solution.py:197
  14.8 0.1 collective-permute-start.11
  14.8 1.9 %collective-permute-done.6.refs_0_ = bf16[64,1024]{1,0:T(8,128)(2,1)S(1)} collective-permute-done((bf16[64,1024]{1,0:T(8,128)(2,1)S(1)}, bf16[64,1024]{1,0:T(8,128)(2,1)S(1)}, u32[]{:S(2)}, u32[]{:S(2)}) %collective-permute-start.6) | collective-permute-done | bytes 131104 | tf_op jit(solution)/shard_map/ppermute | solution.py:186
  16.7 0.0 collective-permute-done.7.refs_1_.refs_2_.refs_8_
  16.7 0.8 %collective-permute-start.10 = (bf16[64,1024]{1,0:T(8,128)(2,1)S(1)}, bf16[64,1024]{1,0:T(8,128)(2,1)S(1)}, u32[]{:S(2)}, u32[]{:S(2)}) collective-permute-start(bf16[64,1024]{1,0:T(8,128)(2,1)S(1)} %after.10.refs_4_.refs_7_), channel_id=1, source_target_pairs={{0,16},{8,24},{16,0},{24,8},{1,17},{9,25},{17,1},{25,9},{2,18},{10... | collective-permute-start | bytes 393224 | tf_op jit(solution)/shard_map/ppermute | solution.py:197
  17.5 1.8 %collective-permute-done.5.refs_1_.refs_6_ = bf16[64,1024]{1,0:T(8,128)(2,1)S(1)} collective-permute-done((bf16[64,1024]{1,0:T(8,128)(2,1)S(1)}, bf16[64,1024]{1,0:T(8,128)(2,1)S(1)}, u32[]{:S(2)}, u32[]{:S(2)}) %collective-permute-start.5) | collective-permute-done | bytes 131104 | tf_op jit(solution)/shard_map/ppermute | solution.py:186
  19.3 0.8 %collective-permute-start.9 = (bf16[64,1024]{1,0:T(8,128)(2,1)S(1)}, bf16[64,1024]{1,0:T(8,128)(2,1)S(1)}, u32[]{:S(2)}, u32[]{:S(2)}) collective-permute-start(bf16[64,1024]{1,0:T(8,128)(2,1)S(1)} %collective-permute-done.5.refs_1_.refs_6_), channel_id=1, source_target_pairs={{0,16},{8,24},{16,0},{24,8},{1,17},{9,25},{17,1},{25,9},{2,18},{10... | collective-permute-start | bytes 393224 | tf_op jit(solution)/shard_map/ppermute | solution.py:197
  20.1 0.0 collective-permute-done.11
  20.1 1.3 %collective-permute-start.12 = (bf16[2,4,1024]{2,1,0:T(4,128)(2,1)S(1)}, bf16[2,4,1024]{2,1,0:T(4,128)(2,1)S(1)}, u32[]{:S(2)}, u32[]{:S(2)}) collective-permute-start(bf16[2,4,1024]{2,1,0:T(4,128)(2,1)S(1)} %pad_maximum_fusion.1), channel_id=1, source_target_pairs={{0,16},{8,24},{16,0},{24,8},{1,17},{9,25},{17,1},{25,9},{2,18},{10... | collective-permute-start | bytes 49160 | tf_op jit(solution)/shard_map/ppermute | solution.py:186
  21.4 0.6 %edge_part.1.refs_1_ = bf16[64,1152]{1,0:T(8,128)(2,1)S(1)} custom-call(bf16[64,1024]{1,0:T(8,128)(2,1)S(1)} %collective-permute-done.3.refs_1_.q_ref, bf16[68,1024]{1,0:T(8,128)(2,1)S(1)} %get-tuple-element.14.refs_0_, bf16[68,1024]{1,0:T(8,128)(2,1)S(1)} %after.8.refs_1_.refs_4_, bf16[68,1024]{1,0:T(8,128)(2,1)S(1)} %collective-permute-done.7.refs_1_.refs_2_.refs_8_, ...), custom_call_target="tpu_custom_call" | custom-call | flops 50331648 | bytes 1089536 | tf_op jit(solution)/shard_map/edge_part/pallas_call | solution.py:27
  22.0 2.9 %collective-permute-start.13 = (bf16[64,1152]{1,0:T(8,128)(2,1)S(1)}, bf16[64,1152]{1,0:T(8,128)(2,1)S(1)}, u32[]{:S(2)}, u32[]{:S(2)}) collective-permute-start(bf16[64,1152]{1,0:T(8,128)(2,1)S(1)} %edge_part.1.refs_1_), channel_id=1, source_target_pairs={{0,7},{1,2},{2,1},{3,4},{4,3},{5,6},{6,5},{7,0},{8,15},{9,10},{10,... | collective-permute-start | bytes 442376 | tf_op jit(solution)/shard_map/ppermute | solution.py:191
  25.0 0.0 collective-permute-done.10.refs_0_
  25.0 0.0 copy-start
  25.0 0.6 %inner_part.1.refs_1_ = bf16[64,1152]{1,0:T(8,128)(2,1)S(1)} custom-call(bf16[64,1024]{1,0:T(8,128)(2,1)S(1)} %collective-permute-done.1.refs_2_.q_ref, bf16[64,1024]{1,0:T(8,128)(2,1)S(1)} %get-tuple-element.16.refs_0_.refs_2_, bf16[64,1024]{1,0:T(8,128)(2,1)S(1)} %collective-permute-done.5.refs_1_.refs_6_, ...), custom_call_target="tpu_custom_call" | custom-call | flops 50331648 | bytes 1064960 | tf_op jit(solution)/shard_map/inner_part/pallas_call | solution.py:27
  25.6 0.1 collective-permute-start.14
  25.7 0.0 collective-permute-done.12
  25.7 0.1 fusion.6.refs_0_
  25.8 1.3 %own_part.1 = (f32[128,1024]{1,0:T(8,128)S(1)}, f32[128,128]{1,0:T(8,128)S(1)}) custom-call(bf16[68,1024]{1,0:T(8,128)(2,1)S(1)} %get-tuple-element.14.refs_0_, bf16[64,1024]{1,0:T(8,128)(2,1)S(1)} %get-tuple-element.15.refs_3_.refs_1_, bf16[64,1024]{1,0:T(8,128)(2,1)S(1)} %get-tuple-element.16.refs_0_.refs_2_, ...), custom_call_target="tpu_custom_call" | custom-call | flops 201326592 | bytes 2514944 | tf_op jit(solution)/shard_map/own_part/pallas_call | solution.py:27
  27.1 2.1 %collective-permute-done.13.refs_0_ = bf16[64,1152]{1,0:T(8,128)(2,1)S(1)} collective-permute-done((bf16[64,1152]{1,0:T(8,128)(2,1)S(1)}, bf16[64,1152]{1,0:T(8,128)(2,1)S(1)}, u32[]{:S(2)}, u32[]{:S(2)}) %collective-permute-start.13) | collective-permute-done | bytes 147488 | tf_op jit(solution)/shard_map/ppermute | solution.py:191
  29.2 1.5 %merge.1 = bf16[8,16,1024]{2,1,0:T(8,128)(2,1)} custom-call(f32[128,1024]{1,0:T(8,128)S(1)} %get-tuple-element.21.refs_1_.own_ref, f32[128,128]{1,0:T(8,128)S(1)} %get-tuple-element.22.lse_ref, bf16[64,1152]{1,0:T(8,128)(2,1)S(1)} %after.13.edge_ref, bf16[64,1152]{1,0:T(8,128)(2,1)S(1)} %collective-permute-done.14.inner_ref, bf16[1024,1024]{1,0:T(8,128)(2,1)S(1)} %copy-done), custom_call_target="tpu_custom_call" | custom-call | flops 268435456 | bytes 3244032 | tf_op jit(solution)/shard_map/merge/pallas_call | solution.py:27
  (22 shorter events, 0.2 us)
Async XLA Ops:
  1.2 7.3 %collective-permute-start = (bf16[68,1024]{1,0:T(8,128)(2,1)S(1)}, bf16[68,1024]{1,0:T(8,128)(2,1)S(1)}, u32[]{:S(2)}, u32[]{:S(2)}) collective-permute-start(bf16[68,1024]{1,0:T(8,128)(2,1)S(1)} %get-tuple-element.14.refs_0_), channel_id=1, source_target_pairs={{0,8},{8,0},{16,24},{24,16},{1,9},{9,1},{17,25},{25,17},{2,10},{10... | collective-permute-start | bytes 417800 | tf_op jit(solution)/shard_map/ppermute | solution.py:186
  4.2 4.3 %collective-permute-start.1 = (bf16[64,1024]{1,0:T(8,128)(2,1)S(1)}, bf16[64,1024]{1,0:T(8,128)(2,1)S(1)}, u32[]{:S(2)}, u32[]{:S(2)}) collective-permute-start(bf16[64,1024]{1,0:T(8,128)(2,1)S(1)} %get-tuple-element.19.refs_12_), channel_id=1, source_target_pairs={{0,1},{1,0},{2,3},{3,2},{4,5},{5,4},{6,7},{7,6},{8,9},{9,8},{10,11... | collective-permute-start | bytes 393224 | tf_op jit(solution)/shard_map/ppermute | solution.py:186
  4.2 8.1 %collective-permute-start.3 = (bf16[64,1024]{1,0:T(8,128)(2,1)S(1)}, bf16[64,1024]{1,0:T(8,128)(2,1)S(1)}, u32[]{:S(2)}, u32[]{:S(2)}) collective-permute-start(bf16[64,1024]{1,0:T(8,128)(2,1)S(1)} %get-tuple-element.20.refs_13_), channel_id=1, source_target_pairs={{0,7},{1,2},{2,1},{3,4},{4,3},{5,6},{6,5},{7,0},{8,15},{9,10},{10,... | collective-permute-start | bytes 393224 | tf_op jit(solution)/shard_map/ppermute | solution.py:191
  8.0 5.0 %collective-permute-start.2 = (bf16[64,1024]{1,0:T(8,128)(2,1)S(1)}, bf16[64,1024]{1,0:T(8,128)(2,1)S(1)}, u32[]{:S(2)}, u32[]{:S(2)}) collective-permute-start(bf16[64,1024]{1,0:T(8,128)(2,1)S(1)} %get-tuple-element.15.refs_3_.refs_1_), channel_id=1, source_target_pairs={{0,8},{8,0},{16,24},{24,16},{1,9},{9,1},{17,25},{25,17},{2,10},{10... | collective-permute-start | bytes 393224 | tf_op jit(solution)/shard_map/ppermute | solution.py:186
  8.5 8.2 %collective-permute-start.7 = (bf16[68,1024]{1,0:T(8,128)(2,1)S(1)}, bf16[68,1024]{1,0:T(8,128)(2,1)S(1)}, u32[]{:S(2)}, u32[]{:S(2)}) collective-permute-start(bf16[68,1024]{1,0:T(8,128)(2,1)S(1)} %after.8.refs_1_.refs_4_), channel_id=1, source_target_pairs={{0,16},{8,24},{16,0},{24,8},{1,17},{9,25},{17,1},{25,9},{2,18},{10... | collective-permute-start | bytes 417800 | tf_op jit(solution)/shard_map/ppermute | solution.py:197
  10.2 2.7 %collective-permute-start.4 = (bf16[2,5,1024]{2,1,0:T(8,128)(2,1)S(1)}, bf16[2,5,1024]{2,1,0:T(8,128)(2,1)S(1)}, u32[]{:S(2)}, u32[]{:S(2)}) collective-permute-start(bf16[2,5,1024]{2,1,0:T(8,128)(2,1)S(1)} %pad_maximum_fusion), channel_id=1, source_target_pairs={{0,1},{1,0},{2,3},{3,2},{4,5},{5,4},{6,7},{7,6},{8,9},{9,8},{10,11... | collective-permute-start | bytes 61448 | tf_op jit(solution)/shard_map/ppermute | solution.py:186
  10.3 6.4 %collective-permute-start.6 = (bf16[64,1024]{1,0:T(8,128)(2,1)S(1)}, bf16[64,1024]{1,0:T(8,128)(2,1)S(1)}, u32[]{:S(2)}, u32[]{:S(2)}) collective-permute-start(bf16[64,1024]{1,0:T(8,128)(2,1)S(1)} %get-tuple-element.17.refs_3_), channel_id=1, source_target_pairs={{0,8},{8,0},{16,24},{24,16},{1,9},{9,1},{17,25},{25,17},{2,10},{10... | collective-permute-start | bytes 393224 | tf_op jit(solution)/shard_map/ppermute | solution.py:186
  12.4 6.9 %collective-permute-start.5 = (bf16[64,1024]{1,0:T(8,128)(2,1)S(1)}, bf16[64,1024]{1,0:T(8,128)(2,1)S(1)}, u32[]{:S(2)}, u32[]{:S(2)}) collective-permute-start(bf16[64,1024]{1,0:T(8,128)(2,1)S(1)} %get-tuple-element.16.refs_0_.refs_2_), channel_id=1, source_target_pairs={{0,8},{8,0},{16,24},{24,16},{1,9},{9,1},{17,25},{25,17},{2,10},{10... | collective-permute-start | bytes 393224 | tf_op jit(solution)/shard_map/ppermute | solution.py:186
  12.9 8.5 %collective-permute-start.8 = (bf16[64,1024]{1,0:T(8,128)(2,1)S(1)}, bf16[64,1024]{1,0:T(8,128)(2,1)S(1)}, u32[]{:S(2)}, u32[]{:S(2)}) collective-permute-start(bf16[64,1024]{1,0:T(8,128)(2,1)S(1)} %after.9.refs_4_.refs_5_), channel_id=1, source_target_pairs={{0,16},{8,24},{16,0},{24,8},{1,17},{9,25},{17,1},{25,9},{2,18},{10... | collective-permute-start | bytes 393224 | tf_op jit(solution)/shard_map/ppermute | solution.py:197
  14.8 5.3 %collective-permute-start.11 = (bf16[2,2,1024]{2,1,0:T(2,128)(2,1)S(1)}, bf16[2,2,1024]{2,1,0:T(2,128)(2,1)S(1)}, u32[]{:S(2)}, u32[]{:S(2)}) collective-permute-start(bf16[2,2,1024]{2,1,0:T(2,128)(2,1)S(1)} %pad_maximum_fusion.2), channel_id=1, source_target_pairs={{0,2},{1,3},{2,0},{3,1},{4,6},{5,7},{6,4},{7,5},{8,10},{9,11},{10,... | collective-permute-start | bytes 24584 | tf_op jit(solution)/shard_map/ppermute | solution.py:186
  16.7 8.2 %collective-permute-start.10 = (bf16[64,1024]{1,0:T(8,128)(2,1)S(1)}, bf16[64,1024]{1,0:T(8,128)(2,1)S(1)}, u32[]{:S(2)}, u32[]{:S(2)}) collective-permute-start(bf16[64,1024]{1,0:T(8,128)(2,1)S(1)} %after.10.refs_4_.refs_7_), channel_id=1, source_target_pairs={{0,16},{8,24},{16,0},{24,8},{1,17},{9,25},{17,1},{25,9},{2,18},{10... | collective-permute-start | bytes 393224 | tf_op jit(solution)/shard_map/ppermute | solution.py:197
  19.3 5.7 %collective-permute-start.9 = (bf16[64,1024]{1,0:T(8,128)(2,1)S(1)}, bf16[64,1024]{1,0:T(8,128)(2,1)S(1)}, u32[]{:S(2)}, u32[]{:S(2)}) collective-permute-start(bf16[64,1024]{1,0:T(8,128)(2,1)S(1)} %collective-permute-done.5.refs_1_.refs_6_), channel_id=1, source_target_pairs={{0,16},{8,24},{16,0},{24,8},{1,17},{9,25},{17,1},{25,9},{2,18},{10... | collective-permute-start | bytes 393224 | tf_op jit(solution)/shard_map/ppermute | solution.py:197
  20.1 5.6 %collective-permute-start.12 = (bf16[2,4,1024]{2,1,0:T(4,128)(2,1)S(1)}, bf16[2,4,1024]{2,1,0:T(4,128)(2,1)S(1)}, u32[]{:S(2)}, u32[]{:S(2)}) collective-permute-start(bf16[2,4,1024]{2,1,0:T(4,128)(2,1)S(1)} %pad_maximum_fusion.1), channel_id=1, source_target_pairs={{0,16},{8,24},{16,0},{24,8},{1,17},{9,25},{17,1},{25,9},{2,18},{10... | collective-permute-start | bytes 49160 | tf_op jit(solution)/shard_map/ppermute | solution.py:186
  22.0 7.1 %collective-permute-start.13 = (bf16[64,1152]{1,0:T(8,128)(2,1)S(1)}, bf16[64,1152]{1,0:T(8,128)(2,1)S(1)}, u32[]{:S(2)}, u32[]{:S(2)}) collective-permute-start(bf16[64,1152]{1,0:T(8,128)(2,1)S(1)} %edge_part.1.refs_1_), channel_id=1, source_target_pairs={{0,7},{1,2},{2,1},{3,4},{4,3},{5,6},{6,5},{7,0},{8,15},{9,10},{10,... | collective-permute-start | bytes 442376 | tf_op jit(solution)/shard_map/ppermute | solution.py:191
  25.0 4.2 %copy-start = (bf16[1024,1024]{1,0:T(8,128)(2,1)S(1)}, bf16[1024,1024]{1,0:T(8,128)(2,1)}, u32[]{:S(2)}) copy-start(bf16[1024,1024]{1,0:T(8,128)(2,1)} %weight_ref.1) | copy-start | bytes 6291460
  25.6 3.6 %collective-permute-start.14 = (bf16[64,1152]{1,0:T(8,128)(2,1)S(1)}, bf16[64,1152]{1,0:T(8,128)(2,1)S(1)}, u32[]{:S(2)}, u32[]{:S(2)}) collective-permute-start(bf16[64,1152]{1,0:T(8,128)(2,1)S(1)} %inner_part.1.refs_1_), channel_id=1, source_target_pairs={{0,1},{1,0},{2,3},{3,2},{4,5},{5,4},{6,7},{7,6},{8,9},{9,8},{10,11... | collective-permute-start | bytes 442376 | tf_op jit(solution)/shard_map/ppermute | solution.py:186

commit v7 on v4

--- a/solution.py
+++ b/solution.py
@@ -192,8 +192,8 @@
 
 def stride(x, axis, step):
     count = lax.axis_size(axis)
-    route = [(i, (i + (-step if i % 2 else step)) % count) for i in range(count)]
-    return lax.ppermute(x, axis, route)
+    route = [(i, i + (-step if i % 2 else step)) for i in range(count)]
+    return lax.ppermute(x, axis, [(s, t) for s, t in route if 0 <= t < count])
 
 
 def after_kernel(*refs):

time: 30.7 us -> 32.9 us (1.072)
  waiting for transfers between devices: 10.4 us -> 11.9 us
  starting transfers between devices: 14.5 us -> 15.2 us
    ppermute x8, waiting for transfers between devices: 2.09 us -> 6.05 us  [swap(): return lax.ppermute(x, axis, [(i, i ^ distance) for i in range(count)])]
    ppermute x2, waiting for transfers between devices: 8.26 us -> 4.86 us  [outward(): lax.ppermute(x, axis, [(i, (i + (1 if i % 2 else -1)) % count) for i in r...]
    ppermute x2, starting transfers between devices: 2.09 us -> 4.91 us  [stride(): return lax.ppermute(x, axis, [(s, t) for s, t in route if 0 <= t < count])]
    ppermute x8, starting transfers between devices: 8.1 us -> 6.69 us  [swap(): return lax.ppermute(x, axis, [(i, i ^ distance) for i in range(count)])]
    ppermute x2, waiting for transfers between devices: 0.01 us -> 0.97 us  [stride(): return lax.ppermute(x, axis, [(s, t) for s, t in route if 0 <= t < count])]
    ppermute x2, starting transfers between devices: 4.32 us -> 3.6 us  [outward(): lax.ppermute(x, axis, [(i, (i + (1 if i % 2 else -1)) % count) for i in r...]
  transfers between devices with their start and end apart: 12 -> 12, of which waited for: 3 -> 6; matrix products, arithmetic and copies ran while one was open for 1% -> 1% of each run, Pallas kernels for 8% -> 8%
where the time goes in v7:
time: 32.9 us; the launch traced here: 32.7 us
  starting transfers between devices  15.2 us (46%)
  waiting for transfers between devices  11.9 us (36%)
  Pallas kernels  5.26 us (16%)
    ppermute x8, starting transfers between devices, swap(): return lax.ppermute(x, axis, [(i, i ^ distance) for i in range(count)])  6.69 us
    ppermute x8, waiting for transfers between devices, swap(): return lax.ppermute(x, axis, [(i, i ^ distance) for i in range(count)])  6.05 us
    ppermute x2, starting transfers between devices, stride(): return lax.ppermute(x, axis, [(s, t) for s, t in route if 0 <= t < count])  4.91 us
    ppermute x2, waiting for transfers between devices, outward(): lax.ppermute(x, axis, [(i, (i + (1 if i % 2 else -1)) % count) for i in r...  4.86 us
    pallas_call x4, Pallas kernels, call(): pl.pallas_call(kernel, out_shape=outs, in_specs=[VMEM] * len(args), out_s...  4.03 us
    ppermute x2, starting transfers between devices, outward(): lax.ppermute(x, axis, [(i, (i + (1 if i % 2 else -1)) % count) for i in r...  3.6 us
    pallas_call x1, Pallas kernels, shards(): pl.pallas_call(split_kernel, out_shape=[like(SPAN, width), like(SPAN, wid...  1.23 us
    ppermute x2, waiting for transfers between devices, stride(): return lax.ppermute(x, axis, [(s, t) for s, t in route if 0 <= t < count])  0.97 us
  transfers between devices with their start and end apart: 12, of which 6 were waited for; matrix products, arithmetic and copies ran while one was open for 1% of the time, Pallas kernels for 8%

profile of v7, /device:TPU:0, one launch (start us, length us, event | category | flops | bytes accessed | tf_op | source)
XLA Modules:
  0.0 32.7 jit_solution(7442802986095906183)
XLA Ops:
  0.0 1.2 %split.1 = (bf16[64,1024]{1,0:T(8,128)(2,1)S(1)}, bf16[64,1024]{1,0:T(8,128)(2,1)S(1)}, bf16[132,1024]{1,0:T(8,128)(2,1)S(1)}, bf16[128,1024]{1,0:T(8,128)(2,1)S(1)}, bf16[4,1024]{1,0:T(4,128)(2,1)S(1)}) custom-call(bf16[8,16,1024]{2,1,0:T(8,128)(2,1)} %q_hbm.1, bf16[2,8,16,1024]{3,2,1,0:T(8,128)(2,1)} %kv_hbm.1), custom_call_target="tpu_custom_call" | custom-call | bytes 2097152 | tf_op jit(solution)/shard_map/split/pallas_call | solution.py:228
  1.2 3.0 %collective-permute-start = (bf16[132,1024]{1,0:T(8,128)(2,1)S(1)}, bf16[132,1024]{1,0:T(8,128)(2,1)S(1)}, u32[]{:S(2)}, u32[]{:S(2)}) collective-permute-start(bf16[132,1024]{1,0:T(8,128)(2,1)S(1)} %get-tuple-element.12.own_ref.refs_0_), channel_id=1, source_target_pairs={{0,8},{8,0},{16,24},{24,16},{1,9},{9,1},{17,25},{25,17},{2,10},{10... | collective-permute-start | bytes 811016 | tf_op jit(solution)/shard_map/ppermute | solution.py:185
  4.2 1.3 %collective-permute-start.3 = (bf16[128,1024]{1,0:T(8,128)(2,1)S(1)}, bf16[128,1024]{1,0:T(8,128)(2,1)S(1)}, u32[]{:S(2)}, u32[]{:S(2)}) collective-permute-start(bf16[128,1024]{1,0:T(8,128)(2,1)S(1)} %get-tuple-element.13.own_ref.refs_1_), channel_id=1, source_target_pairs={{8,24},{16,0},{9,25},{17,1},{10,26},{18,2},{11,27},{19,3},{12,28},... | collective-permute-start | bytes 786440 | tf_op jit(solution)/shard_map/ppermute | solution.py:196
  5.5 2.8 %collective-permute-start.1 = (bf16[64,1024]{1,0:T(8,128)(2,1)S(1)}, bf16[64,1024]{1,0:T(8,128)(2,1)S(1)}, u32[]{:S(2)}, u32[]{:S(2)}) collective-permute-start(bf16[64,1024]{1,0:T(8,128)(2,1)S(1)} %get-tuple-element.15.refs_7_), channel_id=1, source_target_pairs={{0,7},{1,2},{2,1},{3,4},{4,3},{5,6},{6,5},{7,0},{8,15},{9,10},{10,... | collective-permute-start | bytes 393224 | tf_op jit(solution)/shard_map/ppermute | solution.py:190
  8.4 0.0 collective-permute-start.2
  8.4 2.4 %collective-permute-start.4 = (bf16[128,1024]{1,0:T(8,128)(2,1)S(1)}, bf16[128,1024]{1,0:T(8,128)(2,1)S(1)}, u32[]{:S(2)}, u32[]{:S(2)}) collective-permute-start(bf16[128,1024]{1,0:T(8,128)(2,1)S(1)} %get-tuple-element.13.own_ref.refs_1_), channel_id=1, source_target_pairs={{0,8},{8,0},{16,24},{24,16},{1,9},{9,1},{17,25},{25,17},{2,10},{10... | collective-permute-start | bytes 786440 | tf_op jit(solution)/shard_map/ppermute | solution.py:185
  10.8 2.1 %collective-permute-done.1.refs_2_.q_ref = bf16[64,1024]{1,0:T(8,128)(2,1)S(1)} collective-permute-done((bf16[64,1024]{1,0:T(8,128)(2,1)S(1)}, bf16[64,1024]{1,0:T(8,128)(2,1)S(1)}, u32[]{:S(2)}, u32[]{:S(2)}) %collective-permute-start.1) | collective-permute-done | bytes 131104 | tf_op jit(solution)/shard_map/ppermute | solution.py:190
  12.9 0.0 collective-permute-done.2.refs_3_.q_ref
  12.9 1.0 %collective-permute-done.3.refs_4_ = bf16[128,1024]{1,0:T(8,128)(2,1)S(1)} collective-permute-done((bf16[128,1024]{1,0:T(8,128)(2,1)S(1)}, bf16[128,1024]{1,0:T(8,128)(2,1)S(1)}, u32[]{:S(2)}, u32[]{:S(2)}) %collective-permute-start.3) | collective-permute-done | bytes 262176 | tf_op jit(solution)/shard_map/ppermute | solution.py:196
  13.9 0.0 collective-permute-done.refs_0_
  13.9 3.6 %collective-permute-start.5 = (bf16[132,1024]{1,0:T(8,128)(2,1)S(1)}, bf16[132,1024]{1,0:T(8,128)(2,1)S(1)}, u32[]{:S(2)}, u32[]{:S(2)}) collective-permute-start(bf16[132,1024]{1,0:T(8,128)(2,1)S(1)} %after.7.pair_ref.refs_2_), channel_id=1, source_target_pairs={{0,16},{24,8},{1,17},{25,9},{2,18},{26,10},{3,19},{27,11},{4,20},{... | collective-permute-start | bytes 811016 | tf_op jit(solution)/shard_map/ppermute | solution.py:196
  17.6 0.1 collective-permute-start.7
  17.7 0.1 collective-permute-start.6
  17.8 1.1 %collective-permute-done.7 = bf16[2,5,1024]{2,1,0:T(8,128)(2,1)S(1)} collective-permute-done((bf16[2,5,1024]{2,1,0:T(8,128)(2,1)S(1)}, bf16[2,5,1024]{2,1,0:T(8,128)(2,1)S(1)}, u32[]{:S(2)}, u32[]{:S(2)}) %collective-permute-start.7) | collective-permute-done | bytes 20512 | tf_op jit(solution)/shard_map/ppermute | solution.py:185
  19.0 0.1 collective-permute-start.8
  19.0 3.6 %collective-permute-done.8 = bf16[2,2,1024]{2,1,0:T(2,128)(2,1)S(1)} collective-permute-done((bf16[2,2,1024]{2,1,0:T(2,128)(2,1)S(1)}, bf16[2,2,1024]{2,1,0:T(2,128)(2,1)S(1)}, u32[]{:S(2)}, u32[]{:S(2)}) %collective-permute-start.8) | collective-permute-done | bytes 8224 | tf_op jit(solution)/shard_map/ppermute | solution.py:185
  22.7 0.0 collective-permute-done.4.refs_1_.pair_ref.refs_3_
  22.7 1.0 %collective-permute-start.9 = (bf16[2,4,1024]{2,1,0:T(4,128)(2,1)S(1)}, bf16[2,4,1024]{2,1,0:T(4,128)(2,1)S(1)}, u32[]{:S(2)}, u32[]{:S(2)}) collective-permute-start(bf16[2,4,1024]{2,1,0:T(4,128)(2,1)S(1)} %after.9), channel_id=1, source_target_pairs={{0,16},{8,24},{16,0},{24,8},{1,17},{9,25},{17,1},{25,9},{2,18},{10... | collective-permute-start | bytes 49160 | tf_op jit(solution)/shard_map/ppermute | solution.py:185
  23.7 0.0 collective-permute-done.5.far_ref.refs_4_
  23.7 0.6 %edge_part.1.refs_1_ = bf16[64,1152]{1,0:T(8,128)(2,1)S(1)} custom-call(bf16[64,1024]{1,0:T(8,128)(2,1)S(1)} %collective-permute-done.1.refs_2_.q_ref, bf16[132,1024]{1,0:T(8,128)(2,1)S(1)} %get-tuple-element.12.own_ref.refs_0_, bf16[132,1024]{1,0:T(8,128)(2,1)S(1)} %after.7.pair_ref.refs_2_, bf16[132,1024]{1,0:T(8,128)(2,1)S(1)} %collective-permute-done.5.far_ref.refs_4_), custom_call_target="tpu_custom_call" | custom-call | flops 50331648 | bytes 1089536 | tf_op jit(solution)/shard_map/edge_part/pallas_call | solution.py:27
  24.4 0.8 %collective-permute-start.10 = (bf16[64,1152]{1,0:T(8,128)(2,1)S(1)}, bf16[64,1152]{1,0:T(8,128)(2,1)S(1)}, u32[]{:S(2)}, u32[]{:S(2)}) collective-permute-start(bf16[64,1152]{1,0:T(8,128)(2,1)S(1)} %edge_part.1.refs_1_), channel_id=1, source_target_pairs={{0,7},{1,2},{2,1},{3,4},{4,3},{5,6},{6,5},{7,0},{8,15},{9,10},{10,... | collective-permute-start | bytes 442376 | tf_op jit(solution)/shard_map/ppermute | solution.py:190
  25.1 1.3 %collective-permute-done.6.refs_0_ = bf16[128,1024]{1,0:T(8,128)(2,1)S(1)} collective-permute-done((bf16[128,1024]{1,0:T(8,128)(2,1)S(1)}, bf16[128,1024]{1,0:T(8,128)(2,1)S(1)}, u32[]{:S(2)}, u32[]{:S(2)}) %collective-permute-start.6) | collective-permute-done | bytes 262176 | tf_op jit(solution)/shard_map/ppermute | solution.py:185
  26.4 0.0 copy-start
  26.4 0.6 %inner_part.1.refs_1_ = bf16[64,1152]{1,0:T(8,128)(2,1)S(1)} custom-call(bf16[64,1024]{1,0:T(8,128)(2,1)S(1)} %collective-permute-done.2.refs_3_.q_ref, bf16[128,1024]{1,0:T(8,128)(2,1)S(1)} %get-tuple-element.13.own_ref.refs_1_, bf16[128,1024]{1,0:T(8,128)(2,1)S(1)} %collective-permute-done.4.refs_1_.pair_ref.refs_3_, ...), custom_call_target="tpu_custom_call" | custom-call | flops 50331648 | bytes 1064960 | tf_op jit(solution)/shard_map/inner_part/pallas_call | solution.py:27
  27.1 0.1 collective-permute-start.11
  27.2 0.0 collective-permute-done.9
  27.2 0.1 fusion.6.refs_0_
  27.2 1.2 %own_part.1 = (f32[128,1024]{1,0:T(8,128)S(1)}, f32[128,128]{1,0:T(8,128)S(1)}) custom-call(bf16[132,1024]{1,0:T(8,128)(2,1)S(1)} %get-tuple-element.12.own_ref.refs_0_, bf16[128,1024]{1,0:T(8,128)(2,1)S(1)} %get-tuple-element.13.own_ref.refs_1_, bf16[132,1024]{1,0:T(8,128)(2,1)S(1)} %after.7.pair_ref.refs_2_, ...), custom_call_target="tpu_custom_call" | custom-call | flops 201326592 | bytes 2514944 | tf_op jit(solution)/shard_map/own_part/pallas_call | solution.py:27
  28.5 2.7 %collective-permute-done.10.refs_0_ = bf16[64,1152]{1,0:T(8,128)(2,1)S(1)} collective-permute-done((bf16[64,1152]{1,0:T(8,128)(2,1)S(1)}, bf16[64,1152]{1,0:T(8,128)(2,1)S(1)}, u32[]{:S(2)}, u32[]{:S(2)}) %collective-permute-start.10) | collective-permute-done | bytes 147488 | tf_op jit(solution)/shard_map/ppermute | solution.py:190
  31.2 0.0 collective-permute-done.11.inner_ref
  31.2 0.0 copy-done
  31.2 1.5 %merge.1 = bf16[8,16,1024]{2,1,0:T(8,128)(2,1)} custom-call(f32[128,1024]{1,0:T(8,128)S(1)} %get-tuple-element.17.refs_1_.own_ref, f32[128,128]{1,0:T(8,128)S(1)} %get-tuple-element.18.lse_ref, bf16[64,1152]{1,0:T(8,128)(2,1)S(1)} %after.11.edge_ref, bf16[64,1152]{1,0:T(8,128)(2,1)S(1)} %collective-permute-done.11.inner_ref, bf16[1024,1024]{1,0:T(8,128)(2,1)S(1)} %copy-done), custom_call_target="tpu_custom_call" | custom-call | flops 268435456 | bytes 3244032 | tf_op jit(solution)/shard_map/merge/pallas_call | solution.py:27
  (15 shorter events, 0.2 us)
Async XLA Ops:
  1.2 12.7 %collective-permute-start = (bf16[132,1024]{1,0:T(8,128)(2,1)S(1)}, bf16[132,1024]{1,0:T(8,128)(2,1)S(1)}, u32[]{:S(2)}, u32[]{:S(2)}) collective-permute-start(bf16[132,1024]{1,0:T(8,128)(2,1)S(1)} %get-tuple-element.12.own_ref.refs_0_), channel_id=1, source_target_pairs={{0,8},{8,0},{16,24},{24,16},{1,9},{9,1},{17,25},{25,17},{2,10},{10... | collective-permute-start | bytes 811016 | tf_op jit(solution)/shard_map/ppermute | solution.py:185
  4.2 9.6 %collective-permute-start.3 = (bf16[128,1024]{1,0:T(8,128)(2,1)S(1)}, bf16[128,1024]{1,0:T(8,128)(2,1)S(1)}, u32[]{:S(2)}, u32[]{:S(2)}) collective-permute-start(bf16[128,1024]{1,0:T(8,128)(2,1)S(1)} %get-tuple-element.13.own_ref.refs_1_), channel_id=1, source_target_pairs={{8,24},{16,0},{9,25},{17,1},{10,26},{18,2},{11,27},{19,3},{12,28},... | collective-permute-start | bytes 786440 | tf_op jit(solution)/shard_map/ppermute | solution.py:196
  5.5 7.4 %collective-permute-start.1 = (bf16[64,1024]{1,0:T(8,128)(2,1)S(1)}, bf16[64,1024]{1,0:T(8,128)(2,1)S(1)}, u32[]{:S(2)}, u32[]{:S(2)}) collective-permute-start(bf16[64,1024]{1,0:T(8,128)(2,1)S(1)} %get-tuple-element.15.refs_7_), channel_id=1, source_target_pairs={{0,7},{1,2},{2,1},{3,4},{4,3},{5,6},{6,5},{7,0},{8,15},{9,10},{10,... | collective-permute-start | bytes 393224 | tf_op jit(solution)/shard_map/ppermute | solution.py:190
  8.4 4.6 %collective-permute-start.2 = (bf16[64,1024]{1,0:T(8,128)(2,1)S(1)}, bf16[64,1024]{1,0:T(8,128)(2,1)S(1)}, u32[]{:S(2)}, u32[]{:S(2)}) collective-permute-start(bf16[64,1024]{1,0:T(8,128)(2,1)S(1)} %get-tuple-element.16.refs_6_), channel_id=1, source_target_pairs={{0,1},{1,0},{2,3},{3,2},{4,5},{5,4},{6,7},{7,6},{8,9},{9,8},{10,11... | collective-permute-start | bytes 393224 | tf_op jit(solution)/shard_map/ppermute | solution.py:185
  8.4 14.4 %collective-permute-start.4 = (bf16[128,1024]{1,0:T(8,128)(2,1)S(1)}, bf16[128,1024]{1,0:T(8,128)(2,1)S(1)}, u32[]{:S(2)}, u32[]{:S(2)}) collective-permute-start(bf16[128,1024]{1,0:T(8,128)(2,1)S(1)} %get-tuple-element.13.own_ref.refs_1_), channel_id=1, source_target_pairs={{0,8},{8,0},{16,24},{24,16},{1,9},{9,1},{17,25},{25,17},{2,10},{10... | collective-permute-start | bytes 786440 | tf_op jit(solution)/shard_map/ppermute | solution.py:185
  13.9 9.8 %collective-permute-start.5 = (bf16[132,1024]{1,0:T(8,128)(2,1)S(1)}, bf16[132,1024]{1,0:T(8,128)(2,1)S(1)}, u32[]{:S(2)}, u32[]{:S(2)}) collective-permute-start(bf16[132,1024]{1,0:T(8,128)(2,1)S(1)} %after.7.pair_ref.refs_2_), channel_id=1, source_target_pairs={{0,16},{24,8},{1,17},{25,9},{2,18},{26,10},{3,19},{27,11},{4,20},{... | collective-permute-start | bytes 811016 | tf_op jit(solution)/shard_map/ppermute | solution.py:196
  17.6 1.3 %collective-permute-start.7 = (bf16[2,5,1024]{2,1,0:T(8,128)(2,1)S(1)}, bf16[2,5,1024]{2,1,0:T(8,128)(2,1)S(1)}, u32[]{:S(2)}, u32[]{:S(2)}) collective-permute-start(bf16[2,5,1024]{2,1,0:T(8,128)(2,1)S(1)} %pad_maximum_fusion), channel_id=1, source_target_pairs={{0,1},{1,0},{2,3},{3,2},{4,5},{5,4},{6,7},{7,6},{8,9},{9,8},{10,11... | collective-permute-start | bytes 61448 | tf_op jit(solution)/shard_map/ppermute | solution.py:185
  17.7 8.7 %collective-permute-start.6 = (bf16[128,1024]{1,0:T(8,128)(2,1)S(1)}, bf16[128,1024]{1,0:T(8,128)(2,1)S(1)}, u32[]{:S(2)}, u32[]{:S(2)}) collective-permute-start(bf16[128,1024]{1,0:T(8,128)(2,1)S(1)} %collective-permute-done.3.refs_4_), channel_id=1, source_target_pairs={{0,8},{8,0},{16,24},{24,16},{1,9},{9,1},{17,25},{25,17},{2,10},{10... | collective-permute-start | bytes 786440 | tf_op jit(solution)/shard_map/ppermute | solution.py:185
  19.0 3.7 %collective-permute-start.8 = (bf16[2,2,1024]{2,1,0:T(2,128)(2,1)S(1)}, bf16[2,2,1024]{2,1,0:T(2,128)(2,1)S(1)}, u32[]{:S(2)}, u32[]{:S(2)}) collective-permute-start(bf16[2,2,1024]{2,1,0:T(2,128)(2,1)S(1)} %pad_maximum_fusion.2), channel_id=1, source_target_pairs={{0,2},{1,3},{2,0},{3,1},{4,6},{5,7},{6,4},{7,5},{8,10},{9,11},{10,... | collective-permute-start | bytes 24584 | tf_op jit(solution)/shard_map/ppermute | solution.py:185
  22.7 4.4 %collective-permute-start.9 = (bf16[2,4,1024]{2,1,0:T(4,128)(2,1)S(1)}, bf16[2,4,1024]{2,1,0:T(4,128)(2,1)S(1)}, u32[]{:S(2)}, u32[]{:S(2)}) collective-permute-start(bf16[2,4,1024]{2,1,0:T(4,128)(2,1)S(1)} %after.9), channel_id=1, source_target_pairs={{0,16},{8,24},{16,0},{24,8},{1,17},{9,25},{17,1},{25,9},{2,18},{10... | collective-permute-start | bytes 49160 | tf_op jit(solution)/shard_map/ppermute | solution.py:185
  24.4 6.8 %collective-permute-start.10 = (bf16[64,1152]{1,0:T(8,128)(2,1)S(1)}, bf16[64,1152]{1,0:T(8,128)(2,1)S(1)}, u32[]{:S(2)}, u32[]{:S(2)}) collective-permute-start(bf16[64,1152]{1,0:T(8,128)(2,1)S(1)} %edge_part.1.refs_1_), channel_id=1, source_target_pairs={{0,7},{1,2},{2,1},{3,4},{4,3},{5,6},{6,5},{7,0},{8,15},{9,10},{10,... | collective-permute-start | bytes 442376 | tf_op jit(solution)/shard_map/ppermute | solution.py:190
  26.4 4.8 %copy-start = (bf16[1024,1024]{1,0:T(8,128)(2,1)S(1)}, bf16[1024,1024]{1,0:T(8,128)(2,1)}, u32[]{:S(2)}) copy-start(bf16[1024,1024]{1,0:T(8,128)(2,1)} %weight_ref.1) | copy-start | bytes 6291460
  27.1 4.1 %collective-permute-start.11 = (bf16[64,1152]{1,0:T(8,128)(2,1)S(1)}, bf16[64,1152]{1,0:T(8,128)(2,1)S(1)}, u32[]{:S(2)}, u32[]{:S(2)}) collective-permute-start(bf16[64,1152]{1,0:T(8,128)(2,1)S(1)} %inner_part.1.refs_1_), channel_id=1, source_target_pairs={{0,1},{1,0},{2,3},{3,2},{4,5},{5,4},{6,7},{7,6},{8,9},{9,8},{10,11... | collective-permute-start | bytes 442376 | tf_op jit(solution)/shard_map/ppermute | solution.py:185

commit v8 on v6

--- a/solution.py
+++ b/solution.py
@@ -52,18 +52,18 @@
 
 
 def split_kernel(q_hbm, kv_hbm, *refs):
-    ke_ref, ve_ref, ki_ref, vi_ref, qi_ref, qe_ref, pool_ref, q_ref, kv_ref, sems = refs
+    ke_ref, ve_ref, inner_ref, qi_ref, qe_ref, pool_ref, q_ref, kv_ref, sems = refs
     copies = [pltpu.make_async_copy(kv_hbm.at[i], kv_ref.at[i], sems.at[i]) for i in range(2)]
     copies.append(pltpu.make_async_copy(q_hbm, q_ref, sems.at[2]))
     for copy in copies:
         copy.start()
     odd = odd_column()
     pooled = []
-    for half, edge_ref, inner_ref in ((0, ke_ref, ki_ref), (1, ve_ref, vi_ref)):
+    for half, edge_ref in enumerate((ke_ref, ve_ref)):
         copies[half].wait()
         edge, inner = split_tiles(kv_ref[half].astype(F32), odd)
         edge_ref[:SPAN] = edge.astype(BF16)
-        inner_ref[...] = inner.astype(BF16)
+        inner_ref[half * SPAN : (half + 1) * SPAN] = inner.astype(BF16)
         for tile in (edge, inner):
             pooled.append(jnp.sum(tile, axis=0, keepdims=True) * (1.0 / SPAN))
     pooled = jnp.concatenate(pooled, axis=0).astype(BF16)
@@ -83,12 +83,19 @@
     return [slice(h * HEAD_DIM, (h + 1) * HEAD_DIM) for h in range(HEADS)]
 
 
-def stacked(refs, cols):
-    return jnp.concatenate([r[:SPAN, cols] for r in refs], axis=0)
-
-
-def partial_kernel(n_lat, q_ref, *refs):
-    keys, values, out_ref = refs[:3], refs[3:6], refs[6]
+def stacked(places, cols):
+    return jnp.concatenate([r[row : row + SPAN, cols] for r, row in places], axis=0)
+
+
+def halves(refs, apart):
+    if apart:
+        return [(r, 0) for r in refs[0::2]], [(r, 0) for r in refs[1::2]]
+    return [(r, 0) for r in refs], [(r, SPAN) for r in refs]
+
+
+def partial_kernel(n_lat, apart, q_ref, *refs):
+    keys, values = halves(refs[:-1], apart)
+    out_ref = refs[-1]
     far = far_exists(n_lat)
     lane = lax.broadcasted_iota(jnp.int32, (SPAN, 3 * SPAN), 1)
     keep = jnp.logical_or(lane < 2 * SPAN, far)
@@ -118,8 +125,11 @@
 
 
 def own_kernel(n_lat, count, *refs):
-    keys, values = refs[0:12:2], refs[1:12:2]
-    qi_ref, qe_ref, coarse_ref, out_ref, lse_ref = refs[12:]
+    edge_keys, edge_values = halves(refs[:6], True)
+    inner_keys, inner_values = halves(refs[6:9], False)
+    keys = [k for pair in zip(edge_keys, inner_keys) for k in pair]
+    values = [v for pair in zip(edge_values, inner_values) for v in pair]
+    qi_ref, qe_ref, coarse_ref, out_ref, lse_ref = refs[9:]
     rows = 2 * SPAN
     far = far_exists(n_lat)
     lane = lax.broadcasted_iota(jnp.int32, (rows, 6 * SPAN), 1)
@@ -226,11 +236,18 @@
         return jax.ShapeDtypeStruct(shape, BF16)
 
     tile = like(SPAN, width)
-    ke_own, ve_own, ki_own, vi_own, q_inner, q_edge, pooled = pl.pallas_call(
+    ke_own, ve_own, inner_own, q_inner, q_edge, pooled = pl.pallas_call(
         split_kernel,
-        out_shape=[like(SPAN + 4, width), *[tile] * 5, like(4, width)],
+        out_shape=[
+            like(SPAN + 4, width),
+            tile,
+            like(2 * SPAN, width),
+            tile,
+            tile,
+            like(4, width),
+        ],
         in_specs=[pl.BlockSpec(memory_space=pltpu.HBM)] * 2,
-        out_specs=[VMEM] * 7,
+        out_specs=[VMEM] * 6,
         scratch_shapes=[
             pltpu.VMEM(queries.shape, BF16),
             pltpu.VMEM(keys_values.shape, BF16),
@@ -242,16 +259,12 @@
     )(*(pltpu.with_memory_space_constraint(x, pltpu.HBM) for x in (queries, keys_values)))
     ke_pair = swap(ke_own, "lat", 1)
     ve_pair = swap(ve_own, "lat", 1)
-    ki_pair = swap(ki_own, "lat", 1)
-    vi_pair = swap(vi_own, "lat", 1)
+    inner_pair = swap(inner_own, "lat", 1)
     far_q_edge = outward(q_edge, "lon")
     far_q_inner = swap(q_inner, "lon", 1)
     pooled = after(pooled, weight=4 * WEIGHT)
     ke_pair = after(ke_pair, pooled, far_q_inner)
     ke_far = stride(ke_pair, "lat", 2)
-    ki_far = stride(ki_pair, "lat", 2)
-    vi_pair = after(vi_pair, ke_far)
-    vi_far = stride(vi_pair, "lat", 2)
     level0 = pooled.reshape(2, 2, width)
     level0_lat = ke_pair[SPAN:].reshape(2, 2, width)
     mine = mean_entries(level0[:, 0:1], level0[:, 1:2], level0_lat[:, 0:1], level0_lat[:, 1:2])
@@ -263,24 +276,24 @@
     group_lon = swap(group, "lon", 2)
     both = jnp.concatenate([group, group_lon], axis=1)
     group_lat = swap(both, "lat", 2)
+    inner_pair = after(inner_pair, ke_far, ve_far, group_lon)
+    inner_far = stride(inner_pair, "lat", 2)
     coarse = jnp.concatenate([level0_lat, beside[:, 0:4], group_lon, group_lat], axis=1)
     count = coarse.shape[1] // 2
     coarse = jnp.pad(coarse, ((0, 0), (0, 16 - 2 * count), (0, 0)))
 
     back = like(SPAN, width + HEAD_DIM)
     flops = 4 * SPAN * 3 * SPAN * width
-    part = functools.partial(partial_kernel, n_lat)
-    edge = (ke_own, ke_pair, ke_far, ve_own, ve_pair, ve_far)
+    edge = (ke_own, ve_own, ke_pair, ve_pair, ke_far, ve_far)
+    part = functools.partial(partial_kernel, n_lat, True)
     edge_part = call(part, [back], "edge_part", flops, far_q_edge, *edge)[0]
     edge_back = outward(edge_part, "lon")
-    vi_far = after(vi_far, edge_part)
-    inner = (ki_own, ki_pair, ki_far, vi_own, vi_pair, vi_far)
+    inner_far = after(inner_far, edge_part)
+    inner = (inner_own, inner_pair, inner_far)
+    part = functools.partial(partial_kernel, n_lat, False)
     inner_part = call(part, [back], "inner_part", flops, far_q_inner, *inner)[0]
     inner_back = swap(inner_part, "lon", 1)
     coarse = after(coarse, inner_part)
-    own_tiles = (ke_own, ve_own, ki_own, vi_own)
-    pair_tiles = (ke_pair, ve_pair, ki_pair, vi_pair)
-    far_tiles = (ke_far, ve_far, ki_far, vi_far)
     own, lse = call(
         functools.partial(own_kernel, n_lat, count),
         [
@@ -289,9 +302,8 @@
         ],
         "own_part",
         4 * flops,
-        *own_tiles,
-        *pair_tiles,
-        *far_tiles,
+        *edge,
+        *inner,
         q_inner,
         q_edge,
         coarse,

time: 30.9 us -> 31.4 us (1.016)
  waiting for transfers between devices: 6.24 us -> 9.93 us
  starting transfers between devices: 18.8 us -> 15.6 us
    ppermute x4 -> x3, waiting for transfers between devices: 0.01 us -> 2.75 us  [stride(): return lax.ppermute(x, axis, route)]
    ppermute x9 -> x8, waiting for transfers between devices: 4.1 us -> 6.01 us  [swap(): return lax.ppermute(x, axis, [(i, i ^ distance) for i in range(count)])]
    ppermute x2, starting transfers between devices: 6.61 us -> 5.14 us  [outward(): lax.ppermute(x, axis, [(i, (i + (1 if i % 2 else -1)) % count) for i in r...]
    ppermute x9 -> x8, starting transfers between devices: 7.24 us -> 6.06 us  [swap(): return lax.ppermute(x, axis, [(i, i ^ distance) for i in range(count)])]
    ppermute x2, waiting for transfers between devices: 2.13 us -> 1.18 us  [outward(): lax.ppermute(x, axis, [(i, (i + (1 if i % 2 else -1)) % count) for i in r...]
    ppermute x4 -> x3, starting transfers between devices: 4.95 us -> 4.44 us  [stride(): return lax.ppermute(x, axis, route)]
  transfers between devices with their start and end apart: 15 -> 13, of which waited for: 4 -> 4; matrix products, arithmetic and copies ran while one was open for 1% -> 1% of each run, Pallas kernels for 8% -> 8%
where the time goes in v8:
time: 31.4 us; the launch traced here: 31.2 us
  starting transfers between devices  15.6 us (50%)
  waiting for transfers between devices  9.93 us (32%)
  Pallas kernels  5.27 us (17%)
    ppermute x8, starting transfers between devices, swap(): return lax.ppermute(x, axis, [(i, i ^ distance) for i in range(count)])  6.06 us
    ppermute x8, waiting for transfers between devices, swap(): return lax.ppermute(x, axis, [(i, i ^ distance) for i in range(count)])  6.01 us
    ppermute x2, starting transfers between devices, outward(): lax.ppermute(x, axis, [(i, (i + (1 if i % 2 else -1)) % count) for i in r...  5.14 us
    ppermute x3, starting transfers between devices, stride(): return lax.ppermute(x, axis, route)  4.44 us
    pallas_call x4, Pallas kernels, call(): pl.pallas_call(kernel, out_shape=outs, in_specs=[VMEM] * len(args), out_s...  4.04 us
    ppermute x3, waiting for transfers between devices, stride(): return lax.ppermute(x, axis, route)  2.75 us
    pallas_call x1, Pallas kernels, shards(): pl.pallas_call(split_kernel, out_shape=[like(SPAN + 4, width), tile, like...  1.23 us
    ppermute x2, waiting for transfers between devices, outward(): lax.ppermute(x, axis, [(i, (i + (1 if i % 2 else -1)) % count) for i in r...  1.18 us
  transfers between devices with their start and end apart: 13, of which 4 were waited for; matrix products, arithmetic and copies ran while one was open for 1% of the time, Pallas kernels for 8%

profile of v8, /device:TPU:0, one launch (start us, length us, event | category | flops | bytes accessed | tf_op | source)
XLA Modules:
  0.0 31.2 jit_solution(7667679779659559083)
XLA Ops:
  0.0 1.2 %split.1 = (bf16[68,1024]{1,0:T(8,128)(2,1)S(1)}, bf16[64,1024]{1,0:T(8,128)(2,1)S(1)}, bf16[128,1024]{1,0:T(8,128)(2,1)S(1)}, bf16[64,1024]{1,0:T(8,128)(2,1)S(...) custom-call(bf16[8,16,1024]{2,1,0:T(8,128)(2,1)} %q_hbm.1, bf16[2,8,16,1024]{3,2,1,0:T(8,128)(2,1)} %kv_hbm.1), custom_call_target="tpu_custom_call" | custom-call | bytes 2097152 | tf_op jit(solution)/shard_map/split/pallas_call | solution.py:239
  1.2 3.0 %collective-permute-start = (bf16[68,1024]{1,0:T(8,128)(2,1)S(1)}, bf16[68,1024]{1,0:T(8,128)(2,1)S(1)}, u32[]{:S(2)}, u32[]{:S(2)}) collective-permute-start(bf16[68,1024]{1,0:T(8,128)(2,1)S(1)} %get-tuple-element.13.refs_0_), channel_id=1, source_target_pairs={{0,8},{8,0},{16,24},{24,16},{1,9},{9,1},{17,25},{25,17},{2,10},{10... | collective-permute-start | bytes 417800 | tf_op jit(solution)/shard_map/ppermute | solution.py:196
  4.2 0.0 collective-permute-start.1
  4.2 3.7 %collective-permute-start.3 = (bf16[64,1024]{1,0:T(8,128)(2,1)S(1)}, bf16[64,1024]{1,0:T(8,128)(2,1)S(1)}, u32[]{:S(2)}, u32[]{:S(2)}) collective-permute-start(bf16[64,1024]{1,0:T(8,128)(2,1)S(1)} %get-tuple-element.17.refs_10_), channel_id=1, source_target_pairs={{0,7},{1,2},{2,1},{3,4},{4,3},{5,6},{6,5},{7,0},{8,15},{9,10},{10,... | collective-permute-start | bytes 393224 | tf_op jit(solution)/shard_map/ppermute | solution.py:201
  8.0 0.5 %collective-permute-start.2 = (bf16[64,1024]{1,0:T(8,128)(2,1)S(1)}, bf16[64,1024]{1,0:T(8,128)(2,1)S(1)}, u32[]{:S(2)}, u32[]{:S(2)}) collective-permute-start(bf16[64,1024]{1,0:T(8,128)(2,1)S(1)} %get-tuple-element.14.refs_1_), channel_id=1, source_target_pairs={{0,8},{8,0},{16,24},{24,16},{1,9},{9,1},{17,25},{25,17},{2,10},{10... | collective-permute-start | bytes 393224 | tf_op jit(solution)/shard_map/ppermute | solution.py:196
  8.5 1.5 %collective-permute-start.7 = (bf16[128,1024]{1,0:T(8,128)(2,1)S(1)}, bf16[128,1024]{1,0:T(8,128)(2,1)S(1)}, u32[]{:S(2)}, u32[]{:S(2)}) collective-permute-start(bf16[128,1024]{1,0:T(8,128)(2,1)S(1)} %get-tuple-element.18.refs_0_.refs_6_), channel_id=1, source_target_pairs={{0,8},{8,0},{16,24},{24,16},{1,9},{9,1},{17,25},{25,17},{2,10},{10... | collective-permute-start | bytes 786440 | tf_op jit(solution)/shard_map/ppermute | solution.py:196
  10.0 0.0 collective-permute-done.1.refs_2_.q_ref
  10.0 0.0 collective-permute-done.refs_0_
  10.1 0.1 collective-permute-start.4
  10.2 1.6 %collective-permute-start.5 = (bf16[68,1024]{1,0:T(8,128)(2,1)S(1)}, bf16[68,1024]{1,0:T(8,128)(2,1)S(1)}, u32[]{:S(2)}, u32[]{:S(2)}) collective-permute-start(bf16[68,1024]{1,0:T(8,128)(2,1)S(1)} %after.8.refs_2_), channel_id=1, source_target_pairs={{0,16},{8,24},{16,0},{24,8},{1,17},{9,25},{17,1},{25,9},{2,18},{10... | collective-permute-start | bytes 417800 | tf_op jit(solution)/shard_map/ppermute | solution.py:207
  11.8 0.0 collective-permute-done.3.refs_1_.q_ref
  11.8 2.4 %collective-permute-done.2.refs_0_ = bf16[64,1024]{1,0:T(8,128)(2,1)S(1)} collective-permute-done((bf16[64,1024]{1,0:T(8,128)(2,1)S(1)}, bf16[64,1024]{1,0:T(8,128)(2,1)S(1)}, u32[]{:S(2)}, u32[]{:S(2)}) %collective-permute-start.2) | collective-permute-done | bytes 131104 | tf_op jit(solution)/shard_map/ppermute | solution.py:196
  14.1 0.0 collective-permute-done.4.refs_2_
  14.2 1.5 %collective-permute-start.6 = (bf16[64,1024]{1,0:T(8,128)(2,1)S(1)}, bf16[64,1024]{1,0:T(8,128)(2,1)S(1)}, u32[]{:S(2)}, u32[]{:S(2)}) collective-permute-start(bf16[64,1024]{1,0:T(8,128)(2,1)S(1)} %after.9.refs_3_), channel_id=1, source_target_pairs={{0,16},{8,24},{16,0},{24,8},{1,17},{9,25},{17,1},{25,9},{2,18},{10... | collective-permute-start | bytes 393224 | tf_op jit(solution)/shard_map/ppermute | solution.py:207
  15.7 0.1 collective-permute-start.8
  15.8 3.6 %collective-permute-done.8.refs_3_ = bf16[2,2,1024]{2,1,0:T(2,128)(2,1)S(1)} collective-permute-done((bf16[2,2,1024]{2,1,0:T(2,128)(2,1)S(1)}, bf16[2,2,1024]{2,1,0:T(2,128)(2,1)S(1)}, u32[]{:S(2)}, u32[]{:S(2)}) %collective-permute-start.8) | collective-permute-done | bytes 8224 | tf_op jit(solution)/shard_map/ppermute | solution.py:196
  19.4 0.0 collective-permute-done.7.refs_0_
  19.4 0.0 collective-permute-done.5.refs_1_.refs_4_
  19.4 0.0 collective-permute-done.6.refs_2_.refs_5_
  19.5 1.3 %collective-permute-start.9 = (bf16[128,1024]{1,0:T(8,128)(2,1)S(1)}, bf16[128,1024]{1,0:T(8,128)(2,1)S(1)}, u32[]{:S(2)}, u32[]{:S(2)}) collective-permute-start(bf16[128,1024]{1,0:T(8,128)(2,1)S(1)} %after.10.refs_1_.refs_7_), channel_id=1, source_target_pairs={{0,16},{8,24},{16,0},{24,8},{1,17},{9,25},{17,1},{25,9},{2,18},{10... | collective-permute-start | bytes 786440 | tf_op jit(solution)/shard_map/ppermute | solution.py:207
  20.8 0.8 %collective-permute-start.10 = (bf16[2,4,1024]{2,1,0:T(4,128)(2,1)S(1)}, bf16[2,4,1024]{2,1,0:T(4,128)(2,1)S(1)}, u32[]{:S(2)}, u32[]{:S(2)}) collective-permute-start(bf16[2,4,1024]{2,1,0:T(4,128)(2,1)S(1)} %pad_maximum_fusion.1), channel_id=1, source_target_pairs={{0,16},{8,24},{16,0},{24,8},{1,17},{9,25},{17,1},{25,9},{2,18},{10... | collective-permute-start | bytes 49160 | tf_op jit(solution)/shard_map/ppermute | solution.py:196
  21.7 0.6 %edge_part.1.refs_1_ = bf16[64,1152]{1,0:T(8,128)(2,1)S(1)} custom-call(bf16[64,1024]{1,0:T(8,128)(2,1)S(1)} %collective-permute-done.3.refs_1_.q_ref, bf16[68,1024]{1,0:T(8,128)(2,1)S(1)} %get-tuple-element.13.refs_0_, bf16[64,1024]{1,0:T(8,128)(2,1)S(1)} %get-tuple-element.14.refs_1_, bf16[68,1024]{1,0:T(8,128)(2,1)S(1)} %after.8.refs_2_, ...), custom_call_target="tpu_custom_call" | custom-call | flops 50331648 | bytes 1089536 | tf_op jit(solution)/shard_map/edge_part/pallas_call | solution.py:27
  22.3 1.4 %collective-permute-start.11 = (bf16[64,1152]{1,0:T(8,128)(2,1)S(1)}, bf16[64,1152]{1,0:T(8,128)(2,1)S(1)}, u32[]{:S(2)}, u32[]{:S(2)}) collective-permute-start(bf16[64,1152]{1,0:T(8,128)(2,1)S(1)} %edge_part.1.refs_1_), channel_id=1, source_target_pairs={{0,7},{1,2},{2,1},{3,4},{4,3},{5,6},{6,5},{7,0},{8,15},{9,10},{10,... | collective-permute-start | bytes 442376 | tf_op jit(solution)/shard_map/ppermute | solution.py:201
  23.7 2.7 %collective-permute-done.9.refs_0_ = bf16[128,1024]{1,0:T(8,128)(2,1)S(1)} collective-permute-done((bf16[128,1024]{1,0:T(8,128)(2,1)S(1)}, bf16[128,1024]{1,0:T(8,128)(2,1)S(1)}, u32[]{:S(2)}, u32[]{:S(2)}) %collective-permute-start.9) | collective-permute-done | bytes 262176 | tf_op jit(solution)/shard_map/ppermute | solution.py:207
  26.5 0.6 %inner_part.1.refs_1_ = bf16[64,1152]{1,0:T(8,128)(2,1)S(1)} custom-call(bf16[64,1024]{1,0:T(8,128)(2,1)S(1)} %collective-permute-done.1.refs_2_.q_ref, bf16[128,1024]{1,0:T(8,128)(2,1)S(1)} %get-tuple-element.18.refs_0_.refs_6_, bf16[128,1024]{1,0:T(8,128)(2,1)S(1)} %after.10.refs_1_.refs_7_, bf16[128,1024]{1,0:T(8,128)(2,1)S(1)} %after.11.refs_2_.refs_8_), custom_call_target="tpu_custom_call" | custom-call | flops 50331648 | bytes 1064960 | tf_op jit(solution)/shard_map/inner_part/pallas_call | solution.py:27
  27.1 0.1 collective-permute-start.12
  27.2 0.0 collective-permute-done.10
  27.2 0.1 fusion.6.refs_0_
  27.3 1.3 %own_part.1 = (f32[128,1024]{1,0:T(8,128)S(1)}, f32[128,128]{1,0:T(8,128)S(1)}) custom-call(bf16[68,1024]{1,0:T(8,128)(2,1)S(1)} %get-tuple-element.13.refs_0_, bf16[64,1024]{1,0:T(8,128)(2,1)S(1)} %get-tuple-element.14.refs_1_, bf16[68,1024]{1,0:T(8,128)(2,1)S(1)} %after.8.refs_2_, bf16[64,1024]{1,0:T(8,128)(2,1)S(1)} %after.9.refs_3_, ...), custom_call_target="tpu_custom_call" | custom-call | flops 201326592 | bytes 2514944 | tf_op jit(solution)/shard_map/own_part/pallas_call | solution.py:27
  28.5 1.2 %collective-permute-done.11.refs_0_ = bf16[64,1152]{1,0:T(8,128)(2,1)S(1)} collective-permute-done((bf16[64,1152]{1,0:T(8,128)(2,1)S(1)}, bf16[64,1152]{1,0:T(8,128)(2,1)S(1)}, u32[]{:S(2)}, u32[]{:S(2)}) %collective-permute-start.11) | collective-permute-done | bytes 147488 | tf_op jit(solution)/shard_map/ppermute | solution.py:201
  29.7 0.0 collective-permute-done.12.inner_ref
  29.7 1.5 %merge.1 = bf16[8,16,1024]{2,1,0:T(8,128)(2,1)} custom-call(f32[128,1024]{1,0:T(8,128)S(1)} %get-tuple-element.19.refs_1_.own_ref, f32[128,128]{1,0:T(8,128)S(1)} %get-tuple-element.20.lse_ref, bf16[64,1152]{1,0:T(8,128)(2,1)S(1)} %after.13.edge_ref, bf16[64,1152]{1,0:T(8,128)(2,1)S(1)} %collective-permute-done.12.inner_ref, bf16[1024,1024]{1,0:T(8,128)(2,1)S(1)} %copy-done), custom_call_target="tpu_custom_call" | custom-call | flops 268435456 | bytes 3244032 | tf_op jit(solution)/shard_map/merge/pallas_call | solution.py:27
  (18 shorter events, 0.2 us)
Async XLA Ops:
  1.2 8.8 %collective-permute-start = (bf16[68,1024]{1,0:T(8,128)(2,1)S(1)}, bf16[68,1024]{1,0:T(8,128)(2,1)S(1)}, u32[]{:S(2)}, u32[]{:S(2)}) collective-permute-start(bf16[68,1024]{1,0:T(8,128)(2,1)S(1)} %get-tuple-element.13.refs_0_), channel_id=1, source_target_pairs={{0,8},{8,0},{16,24},{24,16},{1,9},{9,1},{17,25},{25,17},{2,10},{10... | collective-permute-start | bytes 417800 | tf_op jit(solution)/shard_map/ppermute | solution.py:196
  4.2 5.8 %collective-permute-start.1 = (bf16[64,1024]{1,0:T(8,128)(2,1)S(1)}, bf16[64,1024]{1,0:T(8,128)(2,1)S(1)}, u32[]{:S(2)}, u32[]{:S(2)}) collective-permute-start(bf16[64,1024]{1,0:T(8,128)(2,1)S(1)} %get-tuple-element.16.refs_9_), channel_id=1, source_target_pairs={{0,1},{1,0},{2,3},{3,2},{4,5},{5,4},{6,7},{7,6},{8,9},{9,8},{10,11... | collective-permute-start | bytes 393224 | tf_op jit(solution)/shard_map/ppermute | solution.py:196
  4.2 7.5 %collective-permute-start.3 = (bf16[64,1024]{1,0:T(8,128)(2,1)S(1)}, bf16[64,1024]{1,0:T(8,128)(2,1)S(1)}, u32[]{:S(2)}, u32[]{:S(2)}) collective-permute-start(bf16[64,1024]{1,0:T(8,128)(2,1)S(1)} %get-tuple-element.17.refs_10_), channel_id=1, source_target_pairs={{0,7},{1,2},{2,1},{3,4},{4,3},{5,6},{6,5},{7,0},{8,15},{9,10},{10,... | collective-permute-start | bytes 393224 | tf_op jit(solution)/shard_map/ppermute | solution.py:201
  8.0 6.2 %collective-permute-start.2 = (bf16[64,1024]{1,0:T(8,128)(2,1)S(1)}, bf16[64,1024]{1,0:T(8,128)(2,1)S(1)}, u32[]{:S(2)}, u32[]{:S(2)}) collective-permute-start(bf16[64,1024]{1,0:T(8,128)(2,1)S(1)} %get-tuple-element.14.refs_1_), channel_id=1, source_target_pairs={{0,8},{8,0},{16,24},{24,16},{1,9},{9,1},{17,25},{25,17},{2,10},{10... | collective-permute-start | bytes 393224 | tf_op jit(solution)/shard_map/ppermute | solution.py:196
  8.5 10.9 %collective-permute-start.7 = (bf16[128,1024]{1,0:T(8,128)(2,1)S(1)}, bf16[128,1024]{1,0:T(8,128)(2,1)S(1)}, u32[]{:S(2)}, u32[]{:S(2)}) collective-permute-start(bf16[128,1024]{1,0:T(8,128)(2,1)S(1)} %get-tuple-element.18.refs_0_.refs_6_), channel_id=1, source_target_pairs={{0,8},{8,0},{16,24},{24,16},{1,9},{9,1},{17,25},{25,17},{2,10},{10... | collective-permute-start | bytes 786440 | tf_op jit(solution)/shard_map/ppermute | solution.py:196
  10.1 4.0 %collective-permute-start.4 = (bf16[2,5,1024]{2,1,0:T(8,128)(2,1)S(1)}, bf16[2,5,1024]{2,1,0:T(8,128)(2,1)S(1)}, u32[]{:S(2)}, u32[]{:S(2)}) collective-permute-start(bf16[2,5,1024]{2,1,0:T(8,128)(2,1)S(1)} %pad_maximum_fusion), channel_id=1, source_target_pairs={{0,1},{1,0},{2,3},{3,2},{4,5},{5,4},{6,7},{7,6},{8,9},{9,8},{10,11... | collective-permute-start | bytes 61448 | tf_op jit(solution)/shard_map/ppermute | solution.py:196
  10.2 9.2 %collective-permute-start.5 = (bf16[68,1024]{1,0:T(8,128)(2,1)S(1)}, bf16[68,1024]{1,0:T(8,128)(2,1)S(1)}, u32[]{:S(2)}, u32[]{:S(2)}) collective-permute-start(bf16[68,1024]{1,0:T(8,128)(2,1)S(1)} %after.8.refs_2_), channel_id=1, source_target_pairs={{0,16},{8,24},{16,0},{24,8},{1,17},{9,25},{17,1},{25,9},{2,18},{10... | collective-permute-start | bytes 417800 | tf_op jit(solution)/shard_map/ppermute | solution.py:207
  14.2 5.3 %collective-permute-start.6 = (bf16[64,1024]{1,0:T(8,128)(2,1)S(1)}, bf16[64,1024]{1,0:T(8,128)(2,1)S(1)}, u32[]{:S(2)}, u32[]{:S(2)}) collective-permute-start(bf16[64,1024]{1,0:T(8,128)(2,1)S(1)} %after.9.refs_3_), channel_id=1, source_target_pairs={{0,16},{8,24},{16,0},{24,8},{1,17},{9,25},{17,1},{25,9},{2,18},{10... | collective-permute-start | bytes 393224 | tf_op jit(solution)/shard_map/ppermute | solution.py:207
  15.7 3.7 %collective-permute-start.8 = (bf16[2,2,1024]{2,1,0:T(2,128)(2,1)S(1)}, bf16[2,2,1024]{2,1,0:T(2,128)(2,1)S(1)}, u32[]{:S(2)}, u32[]{:S(2)}) collective-permute-start(bf16[2,2,1024]{2,1,0:T(2,128)(2,1)S(1)} %pad_maximum_fusion.2), channel_id=1, source_target_pairs={{0,2},{1,3},{2,0},{3,1},{4,6},{5,7},{6,4},{7,5},{8,10},{9,11},{10,... | collective-permute-start | bytes 24584 | tf_op jit(solution)/shard_map/ppermute | solution.py:196
  19.5 7.0 %collective-permute-start.9 = (bf16[128,1024]{1,0:T(8,128)(2,1)S(1)}, bf16[128,1024]{1,0:T(8,128)(2,1)S(1)}, u32[]{:S(2)}, u32[]{:S(2)}) collective-permute-start(bf16[128,1024]{1,0:T(8,128)(2,1)S(1)} %after.10.refs_1_.refs_7_), channel_id=1, source_target_pairs={{0,16},{8,24},{16,0},{24,8},{1,17},{9,25},{17,1},{25,9},{2,18},{10... | collective-permute-start | bytes 786440 | tf_op jit(solution)/shard_map/ppermute | solution.py:207
  20.8 6.3 %collective-permute-start.10 = (bf16[2,4,1024]{2,1,0:T(4,128)(2,1)S(1)}, bf16[2,4,1024]{2,1,0:T(4,128)(2,1)S(1)}, u32[]{:S(2)}, u32[]{:S(2)}) collective-permute-start(bf16[2,4,1024]{2,1,0:T(4,128)(2,1)S(1)} %pad_maximum_fusion.1), channel_id=1, source_target_pairs={{0,16},{8,24},{16,0},{24,8},{1,17},{9,25},{17,1},{25,9},{2,18},{10... | collective-permute-start | bytes 49160 | tf_op jit(solution)/shard_map/ppermute | solution.py:196
  22.3 7.4 %collective-permute-start.11 = (bf16[64,1152]{1,0:T(8,128)(2,1)S(1)}, bf16[64,1152]{1,0:T(8,128)(2,1)S(1)}, u32[]{:S(2)}, u32[]{:S(2)}) collective-permute-start(bf16[64,1152]{1,0:T(8,128)(2,1)S(1)} %edge_part.1.refs_1_), channel_id=1, source_target_pairs={{0,7},{1,2},{2,1},{3,4},{4,3},{5,6},{6,5},{7,0},{8,15},{9,10},{10,... | collective-permute-start | bytes 442376 | tf_op jit(solution)/shard_map/ppermute | solution.py:201
  26.5 3.2 %copy-start = (bf16[1024,1024]{1,0:T(8,128)(2,1)S(1)}, bf16[1024,1024]{1,0:T(8,128)(2,1)}, u32[]{:S(2)}) copy-start(bf16[1024,1024]{1,0:T(8,128)(2,1)} %weight_ref.1) | copy-start | bytes 6291460
  27.1 2.6 %collective-permute-start.12 = (bf16[64,1152]{1,0:T(8,128)(2,1)S(1)}, bf16[64,1152]{1,0:T(8,128)(2,1)S(1)}, u32[]{:S(2)}, u32[]{:S(2)}) collective-permute-start(bf16[64,1152]{1,0:T(8,128)(2,1)S(1)} %inner_part.1.refs_1_), channel_id=1, source_target_pairs={{0,1},{1,0},{2,3},{3,2},{4,5},{5,4},{6,7},{7,6},{8,9},{9,8},{10,11... | collective-permute-start | bytes 442376 | tf_op jit(solution)/shard_map/ppermute | solution.py:196

commit v9 on v8

--- a/solution.py
+++ b/solution.py
@@ -275,19 +275,20 @@
     group = jnp.concatenate([mine, beside[:, 4:5]], axis=1)
     group_lon = swap(group, "lon", 2)
     both = jnp.concatenate([group, group_lon], axis=1)
-    group_lat = swap(both, "lat", 2)
-    inner_pair = after(inner_pair, ke_far, ve_far, group_lon)
+    inner_pair = after(inner_pair, ve_pair, ke_far)
     inner_far = stride(inner_pair, "lat", 2)
-    coarse = jnp.concatenate([level0_lat, beside[:, 0:4], group_lon, group_lat], axis=1)
-    count = coarse.shape[1] // 2
-    coarse = jnp.pad(coarse, ((0, 0), (0, 16 - 2 * count), (0, 0)))
-
     back = like(SPAN, width + HEAD_DIM)
     flops = 4 * SPAN * 3 * SPAN * width
+    ve_far = after(ve_far, weight=WEIGHT)
     edge = (ke_own, ve_own, ke_pair, ve_pair, ke_far, ve_far)
     part = functools.partial(partial_kernel, n_lat, True)
     edge_part = call(part, [back], "edge_part", flops, far_q_edge, *edge)[0]
     edge_back = outward(edge_part, "lon")
+    both = after(both, edge_part)
+    group_lat = swap(both, "lat", 2)
+    coarse = jnp.concatenate([level0_lat, beside[:, 0:4], group_lon, group_lat], axis=1)
+    count = coarse.shape[1] // 2
+    coarse = jnp.pad(coarse, ((0, 0), (0, 16 - 2 * count), (0, 0)))
     inner_far = after(inner_far, edge_part)
     inner = (inner_own, inner_pair, inner_far)
     part = functools.partial(partial_kernel, n_lat, False)

time: 31.4 us -> 33 us (1.051)
  starting transfers between devices: 15.6 us -> 16.6 us
  waiting for transfers between devices: 9.93 us -> 10.6 us
    ppermute x3, waiting for transfers between devices: 2.75 us -> 0.23 us  [stride(): return lax.ppermute(x, axis, route)]
    ppermute x2, waiting for transfers between devices: 1.18 us -> 3.22 us  [outward(): lax.ppermute(x, axis, [(i, (i + (1 if i % 2 else -1)) % count) for i in r...]
    ppermute x8, starting transfers between devices: 6.06 us -> 7.81 us  [swap(): return lax.ppermute(x, axis, [(i, i ^ distance) for i in range(count)])]
    ppermute x8, waiting for transfers between devices: 6.01 us -> 7.15 us  [swap(): return lax.ppermute(x, axis, [(i, i ^ distance) for i in range(count)])]
    ppermute x2, starting transfers between devices: 5.14 us -> 4.14 us  [outward(): lax.ppermute(x, axis, [(i, (i + (1 if i % 2 else -1)) % count) for i in r...]
  transfers between devices with their start and end apart: 13 -> 13, of which waited for: 4 -> 6; matrix products, arithmetic and copies ran while one was open for 1% -> 1% of each run, Pallas kernels for 8% -> 8%
where the time goes in v9:
time: 33 us; the launch traced here: 32.8 us
  starting transfers between devices  16.6 us (50%)
  waiting for transfers between devices  10.6 us (32%)
  Pallas kernels  5.28 us (16%)
    ppermute x8, starting transfers between devices, swap(): return lax.ppermute(x, axis, [(i, i ^ distance) for i in range(count)])  7.81 us
    ppermute x8, waiting for transfers between devices, swap(): return lax.ppermute(x, axis, [(i, i ^ distance) for i in range(count)])  7.15 us
    ppermute x3, starting transfers between devices, stride(): return lax.ppermute(x, axis, route)  4.63 us
    ppermute x2, starting transfers between devices, outward(): lax.ppermute(x, axis, [(i, (i + (1 if i % 2 else -1)) % count) for i in r...  4.14 us
    pallas_call x4, Pallas kernels, call(): pl.pallas_call(kernel, out_shape=outs, in_specs=[VMEM] * len(args), out_s...  4.04 us
    ppermute x2, waiting for transfers between devices, outward(): lax.ppermute(x, axis, [(i, (i + (1 if i % 2 else -1)) % count) for i in r...  3.22 us
    pallas_call x1, Pallas kernels, shards(): pl.pallas_call(split_kernel, out_shape=[like(SPAN + 4, width), tile, like...  1.23 us
  transfers between devices with their start and end apart: 13, of which 6 were waited for; matrix products, arithmetic and copies ran while one was open for 1% of the time, Pallas kernels for 8%

profile of v9, /device:TPU:0, one launch (start us, length us, event | category | flops | bytes accessed | tf_op | source)
XLA Modules:
  0.0 32.8 jit_solution(14964226463989075081)
XLA Ops:
  0.0 1.2 %split.1 = (bf16[68,1024]{1,0:T(8,128)(2,1)S(1)}, bf16[64,1024]{1,0:T(8,128)(2,1)S(1)}, bf16[128,1024]{1,0:T(8,128)(2,1)S(1)}, bf16[64,1024]{1,0:T(8,128)(2,1)S(...) custom-call(bf16[8,16,1024]{2,1,0:T(8,128)(2,1)} %q_hbm.1, bf16[2,8,16,1024]{3,2,1,0:T(8,128)(2,1)} %kv_hbm.1), custom_call_target="tpu_custom_call" | custom-call | bytes 2097152 | tf_op jit(solution)/shard_map/split/pallas_call | solution.py:239
  1.2 3.0 %collective-permute-start = (bf16[68,1024]{1,0:T(8,128)(2,1)S(1)}, bf16[68,1024]{1,0:T(8,128)(2,1)S(1)}, u32[]{:S(2)}, u32[]{:S(2)}) collective-permute-start(bf16[68,1024]{1,0:T(8,128)(2,1)S(1)} %get-tuple-element.13.refs_0_), channel_id=1, source_target_pairs={{0,8},{8,0},{16,24},{24,16},{1,9},{9,1},{17,25},{25,17},{2,10},{10... | collective-permute-start | bytes 417800 | tf_op jit(solution)/shard_map/ppermute | solution.py:196
  4.2 0.0 collective-permute-start.1
  4.2 3.7 %collective-permute-start.3 = (bf16[64,1024]{1,0:T(8,128)(2,1)S(1)}, bf16[64,1024]{1,0:T(8,128)(2,1)S(1)}, u32[]{:S(2)}, u32[]{:S(2)}) collective-permute-start(bf16[64,1024]{1,0:T(8,128)(2,1)S(1)} %get-tuple-element.17.refs_10_), channel_id=1, source_target_pairs={{0,7},{1,2},{2,1},{3,4},{4,3},{5,6},{6,5},{7,0},{8,15},{9,10},{10,... | collective-permute-start | bytes 393224 | tf_op jit(solution)/shard_map/ppermute | solution.py:201
  8.0 0.5 %collective-permute-start.2 = (bf16[64,1024]{1,0:T(8,128)(2,1)S(1)}, bf16[64,1024]{1,0:T(8,128)(2,1)S(1)}, u32[]{:S(2)}, u32[]{:S(2)}) collective-permute-start(bf16[64,1024]{1,0:T(8,128)(2,1)S(1)} %get-tuple-element.14.refs_1_), channel_id=1, source_target_pairs={{0,8},{8,0},{16,24},{24,16},{1,9},{9,1},{17,25},{25,17},{2,10},{10... | collective-permute-start | bytes 393224 | tf_op jit(solution)/shard_map/ppermute | solution.py:196
  8.5 1.5 %collective-permute-start.7 = (bf16[128,1024]{1,0:T(8,128)(2,1)S(1)}, bf16[128,1024]{1,0:T(8,128)(2,1)S(1)}, u32[]{:S(2)}, u32[]{:S(2)}) collective-permute-start(bf16[128,1024]{1,0:T(8,128)(2,1)S(1)} %get-tuple-element.18.refs_0_.refs_6_), channel_id=1, source_target_pairs={{0,8},{8,0},{16,24},{24,16},{1,9},{9,1},{17,25},{25,17},{2,10},{10... | collective-permute-start | bytes 786440 | tf_op jit(solution)/shard_map/ppermute | solution.py:196
  10.0 0.0 collective-permute-done.1.refs_2_.q_ref
  10.0 0.0 collective-permute-done.refs_0_
  10.0 1.6 %collective-permute-start.5 = (bf16[68,1024]{1,0:T(8,128)(2,1)S(1)}, bf16[68,1024]{1,0:T(8,128)(2,1)S(1)}, u32[]{:S(2)}, u32[]{:S(2)}) collective-permute-start(bf16[68,1024]{1,0:T(8,128)(2,1)S(1)} %after.10.refs_2_), channel_id=1, source_target_pairs={{0,16},{8,24},{16,0},{24,8},{1,17},{9,25},{17,1},{25,9},{2,18},{10... | collective-permute-start | bytes 417800 | tf_op jit(solution)/shard_map/ppermute | solution.py:207
  11.7 0.1 collective-permute-start.4
  11.8 0.0 collective-permute-done.3.refs_1_.q_ref
  11.8 2.4 %collective-permute-done.2.refs_0_ = bf16[64,1024]{1,0:T(8,128)(2,1)S(1)} collective-permute-done((bf16[64,1024]{1,0:T(8,128)(2,1)S(1)}, bf16[64,1024]{1,0:T(8,128)(2,1)S(1)}, u32[]{:S(2)}, u32[]{:S(2)}) %collective-permute-start.2) | collective-permute-done | bytes 131104 | tf_op jit(solution)/shard_map/ppermute | solution.py:196
  14.1 0.0 collective-permute-done.4.refs_2_
  14.2 1.5 %collective-permute-start.6 = (bf16[64,1024]{1,0:T(8,128)(2,1)S(1)}, bf16[64,1024]{1,0:T(8,128)(2,1)S(1)}, u32[]{:S(2)}, u32[]{:S(2)}) collective-permute-start(bf16[64,1024]{1,0:T(8,128)(2,1)S(1)} %after.11.refs_1_.refs_3_), channel_id=1, source_target_pairs={{0,16},{8,24},{16,0},{24,8},{1,17},{9,25},{17,1},{25,9},{2,18},{10... | collective-permute-start | bytes 393224 | tf_op jit(solution)/shard_map/ppermute | solution.py:207
  15.7 1.3 %collective-permute-done.7.refs_0_ = bf16[128,1024]{1,0:T(8,128)(2,1)S(1)} collective-permute-done((bf16[128,1024]{1,0:T(8,128)(2,1)S(1)}, bf16[128,1024]{1,0:T(8,128)(2,1)S(1)}, u32[]{:S(2)}, u32[]{:S(2)}) %collective-permute-start.7) | collective-permute-done | bytes 262176 | tf_op jit(solution)/shard_map/ppermute | solution.py:196
  17.0 0.0 collective-permute-done.5.refs_2_.refs_4_
  17.0 1.5 %collective-permute-start.8 = (bf16[128,1024]{1,0:T(8,128)(2,1)S(1)}, bf16[128,1024]{1,0:T(8,128)(2,1)S(1)}, u32[]{:S(2)}, u32[]{:S(2)}) collective-permute-start(bf16[128,1024]{1,0:T(8,128)(2,1)S(1)} %after.13.refs_1_.refs_7_), channel_id=1, source_target_pairs={{0,16},{8,24},{16,0},{24,8},{1,17},{9,25},{17,1},{25,9},{2,18},{10... | collective-permute-start | bytes 786440 | tf_op jit(solution)/shard_map/ppermute | solution.py:207
  18.5 1.3 %collective-permute-start.9 = (bf16[2,2,1024]{2,1,0:T(2,128)(2,1)S(1)}, bf16[2,2,1024]{2,1,0:T(2,128)(2,1)S(1)}, u32[]{:S(2)}, u32[]{:S(2)}) collective-permute-start(bf16[2,2,1024]{2,1,0:T(2,128)(2,1)S(1)} %pad_maximum_fusion.2), channel_id=1, source_target_pairs={{0,2},{1,3},{2,0},{3,1},{4,6},{5,7},{6,4},{7,5},{8,10},{9,11},{10,... | collective-permute-start | bytes 24584 | tf_op jit(solution)/shard_map/ppermute | solution.py:196
  19.8 2.4 %collective-permute-done.9 = bf16[2,2,1024]{2,1,0:T(2,128)(2,1)S(1)} collective-permute-done((bf16[2,2,1024]{2,1,0:T(2,128)(2,1)S(1)}, bf16[2,2,1024]{2,1,0:T(2,128)(2,1)S(1)}, u32[]{:S(2)}, u32[]{:S(2)}) %collective-permute-start.9) | collective-permute-done | bytes 8224 | tf_op jit(solution)/shard_map/ppermute | solution.py:196
  22.3 0.0 collective-permute-done.6.refs_0_
  22.3 0.6 %edge_part.1.refs_1_ = bf16[64,1152]{1,0:T(8,128)(2,1)S(1)} custom-call(bf16[64,1024]{1,0:T(8,128)(2,1)S(1)} %collective-permute-done.3.refs_1_.q_ref, bf16[68,1024]{1,0:T(8,128)(2,1)S(1)} %get-tuple-element.13.refs_0_, bf16[64,1024]{1,0:T(8,128)(2,1)S(1)} %get-tuple-element.14.refs_1_, bf16[68,1024]{1,0:T(8,128)(2,1)S(1)} %after.10.refs_2_, ...), custom_call_target="tpu_custom_call" | custom-call | flops 50331648 | bytes 1089536 | tf_op jit(solution)/shard_map/edge_part/pallas_call | solution.py:27
  22.9 0.6 %collective-permute-start.10 = (bf16[2,4,1024]{2,1,0:T(4,128)(2,1)S(1)}, bf16[2,4,1024]{2,1,0:T(4,128)(2,1)S(1)}, u32[]{:S(2)}, u32[]{:S(2)}) collective-permute-start(bf16[2,4,1024]{2,1,0:T(4,128)(2,1)S(1)} %after.15), channel_id=1, source_target_pairs={{0,16},{8,24},{16,0},{24,8},{1,17},{9,25},{17,1},{25,9},{2,18},{10... | collective-permute-start | bytes 49160 | tf_op jit(solution)/shard_map/ppermute | solution.py:196
  23.5 0.4 %collective-permute-start.11 = (bf16[64,1152]{1,0:T(8,128)(2,1)S(1)}, bf16[64,1152]{1,0:T(8,128)(2,1)S(1)}, u32[]{:S(2)}, u32[]{:S(2)}) collective-permute-start(bf16[64,1152]{1,0:T(8,128)(2,1)S(1)} %edge_part.1.refs_1_), channel_id=1, source_target_pairs={{0,7},{1,2},{2,1},{3,4},{4,3},{5,6},{6,5},{7,0},{8,15},{9,10},{10,... | collective-permute-start | bytes 442376 | tf_op jit(solution)/shard_map/ppermute | solution.py:201
  23.9 0.2 collective-permute-done.8.refs_0_
  24.2 0.6 %inner_part.1.refs_1_ = bf16[64,1152]{1,0:T(8,128)(2,1)S(1)} custom-call(bf16[64,1024]{1,0:T(8,128)(2,1)S(1)} %collective-permute-done.1.refs_2_.q_ref, bf16[128,1024]{1,0:T(8,128)(2,1)S(1)} %get-tuple-element.18.refs_0_.refs_6_, bf16[128,1024]{1,0:T(8,128)(2,1)S(1)} %after.13.refs_1_.refs_7_, bf16[128,1024]{1,0:T(8,128)(2,1)S(1)} %after.14.refs_2_.refs_8_), custom_call_target="tpu_custom_call" | custom-call | flops 50331648 | bytes 1064960 | tf_op jit(solution)/shard_map/inner_part/pallas_call | solution.py:27
  24.8 0.8 %collective-permute-start.12 = (bf16[64,1152]{1,0:T(8,128)(2,1)S(1)}, bf16[64,1152]{1,0:T(8,128)(2,1)S(1)}, u32[]{:S(2)}, u32[]{:S(2)}) collective-permute-start(bf16[64,1152]{1,0:T(8,128)(2,1)S(1)} %inner_part.1.refs_1_), channel_id=1, source_target_pairs={{0,1},{1,0},{2,3},{3,2},{4,5},{5,4},{6,7},{7,6},{8,9},{9,8},{10,11... | collective-permute-start | bytes 442376 | tf_op jit(solution)/shard_map/ppermute | solution.py:196
  25.6 1.1 %collective-permute-done.10 = bf16[2,4,1024]{2,1,0:T(4,128)(2,1)S(1)} collective-permute-done((bf16[2,4,1024]{2,1,0:T(4,128)(2,1)S(1)}, bf16[2,4,1024]{2,1,0:T(4,128)(2,1)S(1)}, u32[]{:S(2)}, u32[]{:S(2)}) %collective-permute-start.10) | collective-permute-done | bytes 16416 | tf_op jit(solution)/shard_map/ppermute | solution.py:196
  26.7 0.1 fusion.6.refs_0_
  26.8 1.3 %own_part.1 = (f32[128,1024]{1,0:T(8,128)S(1)}, f32[128,128]{1,0:T(8,128)S(1)}) custom-call(bf16[68,1024]{1,0:T(8,128)(2,1)S(1)} %get-tuple-element.13.refs_0_, bf16[64,1024]{1,0:T(8,128)(2,1)S(1)} %get-tuple-element.14.refs_1_, bf16[68,1024]{1,0:T(8,128)(2,1)S(1)} %after.10.refs_2_, bf16[64,1024]{1,0:T(8,128)(2,1)S(1)} %after.11.refs_1_.refs_3_, ...), custom_call_target="tpu_custom_call" | custom-call | flops 201326592 | bytes 2514944 | tf_op jit(solution)/shard_map/own_part/pallas_call | solution.py:27
  28.1 3.2 %collective-permute-done.11.refs_0_ = bf16[64,1152]{1,0:T(8,128)(2,1)S(1)} collective-permute-done((bf16[64,1152]{1,0:T(8,128)(2,1)S(1)}, bf16[64,1152]{1,0:T(8,128)(2,1)S(1)}, u32[]{:S(2)}, u32[]{:S(2)}) %collective-permute-start.11) | collective-permute-done | bytes 147488 | tf_op jit(solution)/shard_map/ppermute | solution.py:201
  31.3 0.0 collective-permute-done.12.inner_ref
  31.3 1.5 %merge.1 = bf16[8,16,1024]{2,1,0:T(8,128)(2,1)} custom-call(f32[128,1024]{1,0:T(8,128)S(1)} %get-tuple-element.19.refs_1_.own_ref, f32[128,128]{1,0:T(8,128)S(1)} %get-tuple-element.20.lse_ref, bf16[64,1152]{1,0:T(8,128)(2,1)S(1)} %after.17.edge_ref, bf16[64,1152]{1,0:T(8,128)(2,1)S(1)} %collective-permute-done.12.inner_ref, bf16[1024,1024]{1,0:T(8,128)(2,1)S(1)} %copy-done), custom_call_target="tpu_custom_call" | custom-call | flops 268435456 | bytes 3244032 | tf_op jit(solution)/shard_map/merge/pallas_call | solution.py:27
  (20 shorter events, 0.2 us)
Async XLA Ops:
  1.2 8.8 %collective-permute-start = (bf16[68,1024]{1,0:T(8,128)(2,1)S(1)}, bf16[68,1024]{1,0:T(8,128)(2,1)S(1)}, u32[]{:S(2)}, u32[]{:S(2)}) collective-permute-start(bf16[68,1024]{1,0:T(8,128)(2,1)S(1)} %get-tuple-element.13.refs_0_), channel_id=1, source_target_pairs={{0,8},{8,0},{16,24},{24,16},{1,9},{9,1},{17,25},{25,17},{2,10},{10... | collective-permute-start | bytes 417800 | tf_op jit(solution)/shard_map/ppermute | solution.py:196
  4.2 5.8 %collective-permute-start.1 = (bf16[64,1024]{1,0:T(8,128)(2,1)S(1)}, bf16[64,1024]{1,0:T(8,128)(2,1)S(1)}, u32[]{:S(2)}, u32[]{:S(2)}) collective-permute-start(bf16[64,1024]{1,0:T(8,128)(2,1)S(1)} %get-tuple-element.16.refs_9_), channel_id=1, source_target_pairs={{0,1},{1,0},{2,3},{3,2},{4,5},{5,4},{6,7},{7,6},{8,9},{9,8},{10,11... | collective-permute-start | bytes 393224 | tf_op jit(solution)/shard_map/ppermute | solution.py:196
  4.2 7.5 %collective-permute-start.3 = (bf16[64,1024]{1,0:T(8,128)(2,1)S(1)}, bf16[64,1024]{1,0:T(8,128)(2,1)S(1)}, u32[]{:S(2)}, u32[]{:S(2)}) collective-permute-start(bf16[64,1024]{1,0:T(8,128)(2,1)S(1)} %get-tuple-element.17.refs_10_), channel_id=1, source_target_pairs={{0,7},{1,2},{2,1},{3,4},{4,3},{5,6},{6,5},{7,0},{8,15},{9,10},{10,... | collective-permute-start | bytes 393224 | tf_op jit(solution)/shard_map/ppermute | solution.py:201
  8.0 6.2 %collective-permute-start.2 = (bf16[64,1024]{1,0:T(8,128)(2,1)S(1)}, bf16[64,1024]{1,0:T(8,128)(2,1)S(1)}, u32[]{:S(2)}, u32[]{:S(2)}) collective-permute-start(bf16[64,1024]{1,0:T(8,128)(2,1)S(1)} %get-tuple-element.14.refs_1_), channel_id=1, source_target_pairs={{0,8},{8,0},{16,24},{24,16},{1,9},{9,1},{17,25},{25,17},{2,10},{10... | collective-permute-start | bytes 393224 | tf_op jit(solution)/shard_map/ppermute | solution.py:196
  8.5 8.5 %collective-permute-start.7 = (bf16[128,1024]{1,0:T(8,128)(2,1)S(1)}, bf16[128,1024]{1,0:T(8,128)(2,1)S(1)}, u32[]{:S(2)}, u32[]{:S(2)}) collective-permute-start(bf16[128,1024]{1,0:T(8,128)(2,1)S(1)} %get-tuple-element.18.refs_0_.refs_6_), channel_id=1, source_target_pairs={{0,8},{8,0},{16,24},{24,16},{1,9},{9,1},{17,25},{25,17},{2,10},{10... | collective-permute-start | bytes 786440 | tf_op jit(solution)/shard_map/ppermute | solution.py:196
  10.0 6.9 %collective-permute-start.5 = (bf16[68,1024]{1,0:T(8,128)(2,1)S(1)}, bf16[68,1024]{1,0:T(8,128)(2,1)S(1)}, u32[]{:S(2)}, u32[]{:S(2)}) collective-permute-start(bf16[68,1024]{1,0:T(8,128)(2,1)S(1)} %after.10.refs_2_), channel_id=1, source_target_pairs={{0,16},{8,24},{16,0},{24,8},{1,17},{9,25},{17,1},{25,9},{2,18},{10... | collective-permute-start | bytes 417800 | tf_op jit(solution)/shard_map/ppermute | solution.py:207
  11.7 2.4 %collective-permute-start.4 = (bf16[2,5,1024]{2,1,0:T(8,128)(2,1)S(1)}, bf16[2,5,1024]{2,1,0:T(8,128)(2,1)S(1)}, u32[]{:S(2)}, u32[]{:S(2)}) collective-permute-start(bf16[2,5,1024]{2,1,0:T(8,128)(2,1)S(1)} %pad_maximum_fusion), channel_id=1, source_target_pairs={{0,1},{1,0},{2,3},{3,2},{4,5},{5,4},{6,7},{7,6},{8,9},{9,8},{10,11... | collective-permute-start | bytes 61448 | tf_op jit(solution)/shard_map/ppermute | solution.py:196
  14.2 8.1 %collective-permute-start.6 = (bf16[64,1024]{1,0:T(8,128)(2,1)S(1)}, bf16[64,1024]{1,0:T(8,128)(2,1)S(1)}, u32[]{:S(2)}, u32[]{:S(2)}) collective-permute-start(bf16[64,1024]{1,0:T(8,128)(2,1)S(1)} %after.11.refs_1_.refs_3_), channel_id=1, source_target_pairs={{0,16},{8,24},{16,0},{24,8},{1,17},{9,25},{17,1},{25,9},{2,18},{10... | collective-permute-start | bytes 393224 | tf_op jit(solution)/shard_map/ppermute | solution.py:207
  17.0 7.2 %collective-permute-start.8 = (bf16[128,1024]{1,0:T(8,128)(2,1)S(1)}, bf16[128,1024]{1,0:T(8,128)(2,1)S(1)}, u32[]{:S(2)}, u32[]{:S(2)}) collective-permute-start(bf16[128,1024]{1,0:T(8,128)(2,1)S(1)} %after.13.refs_1_.refs_7_), channel_id=1, source_target_pairs={{0,16},{8,24},{16,0},{24,8},{1,17},{9,25},{17,1},{25,9},{2,18},{10... | collective-permute-start | bytes 786440 | tf_op jit(solution)/shard_map/ppermute | solution.py:207
  18.5 3.7 %collective-permute-start.9 = (bf16[2,2,1024]{2,1,0:T(2,128)(2,1)S(1)}, bf16[2,2,1024]{2,1,0:T(2,128)(2,1)S(1)}, u32[]{:S(2)}, u32[]{:S(2)}) collective-permute-start(bf16[2,2,1024]{2,1,0:T(2,128)(2,1)S(1)} %pad_maximum_fusion.2), channel_id=1, source_target_pairs={{0,2},{1,3},{2,0},{3,1},{4,6},{5,7},{6,4},{7,5},{8,10},{9,11},{10,... | collective-permute-start | bytes 24584 | tf_op jit(solution)/shard_map/ppermute | solution.py:196
  22.9 3.8 %collective-permute-start.10 = (bf16[2,4,1024]{2,1,0:T(4,128)(2,1)S(1)}, bf16[2,4,1024]{2,1,0:T(4,128)(2,1)S(1)}, u32[]{:S(2)}, u32[]{:S(2)}) collective-permute-start(bf16[2,4,1024]{2,1,0:T(4,128)(2,1)S(1)} %after.15), channel_id=1, source_target_pairs={{0,16},{8,24},{16,0},{24,8},{1,17},{9,25},{17,1},{25,9},{2,18},{10... | collective-permute-start | bytes 49160 | tf_op jit(solution)/shard_map/ppermute | solution.py:196
  23.5 7.8 %collective-permute-start.11 = (bf16[64,1152]{1,0:T(8,128)(2,1)S(1)}, bf16[64,1152]{1,0:T(8,128)(2,1)S(1)}, u32[]{:S(2)}, u32[]{:S(2)}) collective-permute-start(bf16[64,1152]{1,0:T(8,128)(2,1)S(1)} %edge_part.1.refs_1_), channel_id=1, source_target_pairs={{0,7},{1,2},{2,1},{3,4},{4,3},{5,6},{6,5},{7,0},{8,15},{9,10},{10,... | collective-permute-start | bytes 442376 | tf_op jit(solution)/shard_map/ppermute | solution.py:201
  24.2 7.1 %copy-start = (bf16[1024,1024]{1,0:T(8,128)(2,1)S(1)}, bf16[1024,1024]{1,0:T(8,128)(2,1)}, u32[]{:S(2)}) copy-start(bf16[1024,1024]{1,0:T(8,128)(2,1)} %weight_ref.1) | copy-start | bytes 6291460
  24.8 6.5 %collective-permute-start.12 = (bf16[64,1152]{1,0:T(8,128)(2,1)S(1)}, bf16[64,1152]{1,0:T(8,128)(2,1)S(1)}, u32[]{:S(2)}, u32[]{:S(2)}) collective-permute-start(bf16[64,1152]{1,0:T(8,128)(2,1)S(1)} %inner_part.1.refs_1_), channel_id=1, source_target_pairs={{0,1},{1,0},{2,3},{3,2},{4,5},{5,4},{6,7},{7,6},{8,9},{9,8},{10,11... | collective-permute-start | bytes 442376 | tf_op jit(solution)/shard_map/ppermute | solution.py:196

commit v10 on v4

--- a/solution.py
+++ b/solution.py
@@ -260,8 +260,7 @@
     beside = swap(jnp.concatenate([level0, level0_lat, mine], axis=1), "lon", 1)
     group = jnp.concatenate([mine, beside[:, 4:5]], axis=1)
     group_lon = swap(group, "lon", 2)
-    group_both = jnp.concatenate([group, group_lon], axis=1)
-    group_lat = swap(after(group_both, inner_pair), "lat", 2)
+    group_lat = swap(jnp.concatenate([group, group_lon], axis=1), "lat", 2)
     coarse = jnp.concatenate([level0_lat, beside[:, 0:4], group_lon, group_lat], axis=1)
     count = coarse.shape[1] // 2
     coarse = jnp.pad(coarse, ((0, 0), (0, 16 - 2 * count), (0, 0)))

time: 30.7 us -> 32 us (1.042)
  waiting for transfers between devices: 10.4 us -> 12.3 us
  starting transfers between devices: 14.5 us -> 13.9 us
    ppermute x8, waiting for transfers between devices: 2.09 us -> 7.47 us  [swap(): return lax.ppermute(x, axis, [(i, i ^ distance) for i in range(count)])]
    ppermute x2, waiting for transfers between devices: 8.26 us -> 4.84 us  [outward(): lax.ppermute(x, axis, [(i, (i + (1 if i % 2 else -1)) % count) for i in r...]
    ppermute x2, starting transfers between devices: 4.32 us -> 3.39 us  [outward(): lax.ppermute(x, axis, [(i, (i + (1 if i % 2 else -1)) % count) for i in r...]
  transfers between devices with their start and end apart: 12 -> 12, of which waited for: 3 -> 4; matrix products, arithmetic and copies ran while one was open for 1% -> 1% of each run, Pallas kernels for 8% -> 8%
where the time goes in v10:
time: 32 us; the launch traced here: 31.8 us
  starting transfers between devices  13.9 us (43%)
  waiting for transfers between devices  12.3 us (38%)
  Pallas kernels  5.28 us (16%)
    ppermute x8, starting transfers between devices, swap(): return lax.ppermute(x, axis, [(i, i ^ distance) for i in range(count)])  8.37 us
    ppermute x8, waiting for transfers between devices, swap(): return lax.ppermute(x, axis, [(i, i ^ distance) for i in range(count)])  7.47 us
    ppermute x2, waiting for transfers between devices, outward(): lax.ppermute(x, axis, [(i, (i + (1 if i % 2 else -1)) % count) for i in r...  4.84 us
    pallas_call x4, Pallas kernels, call(): pl.pallas_call(kernel, out_shape=outs, in_specs=[VMEM] * len(args), out_s...  4.04 us
    ppermute x2, starting transfers between devices, outward(): lax.ppermute(x, axis, [(i, (i + (1 if i % 2 else -1)) % count) for i in r...  3.39 us
    ppermute x2, starting transfers between devices, stride(): return lax.ppermute(x, axis, route)  2.09 us
    pallas_call x1, Pallas kernels, shards(): pl.pallas_call(split_kernel, out_shape=[like(SPAN, width), like(SPAN, wid...  1.23 us
  transfers between devices with their start and end apart: 12, of which 4 were waited for; matrix products, arithmetic and copies ran while one was open for 1% of the time, Pallas kernels for 8%

profile of v10, /device:TPU:0, one launch (start us, length us, event | category | flops | bytes accessed | tf_op | source)
XLA Modules:
  0.0 31.8 jit_solution(10211456453181118645)
XLA Ops:
  0.0 1.2 %split.1 = (bf16[64,1024]{1,0:T(8,128)(2,1)S(1)}, bf16[64,1024]{1,0:T(8,128)(2,1)S(1)}, bf16[132,1024]{1,0:T(8,128)(2,1)S(1)}, bf16[128,1024]{1,0:T(8,128)(2,1)S(1)}, bf16[4,1024]{1,0:T(4,128)(2,1)S(1)}) custom-call(bf16[8,16,1024]{2,1,0:T(8,128)(2,1)} %q_hbm.1, bf16[2,8,16,1024]{3,2,1,0:T(8,128)(2,1)} %kv_hbm.1), custom_call_target="tpu_custom_call" | custom-call | bytes 2097152 | tf_op jit(solution)/shard_map/split/pallas_call | solution.py:228
  1.2 3.0 %collective-permute-start = (bf16[132,1024]{1,0:T(8,128)(2,1)S(1)}, bf16[132,1024]{1,0:T(8,128)(2,1)S(1)}, u32[]{:S(2)}, u32[]{:S(2)}) collective-permute-start(bf16[132,1024]{1,0:T(8,128)(2,1)S(1)} %get-tuple-element.12.own_ref.refs_0_), channel_id=1, source_target_pairs={{0,8},{8,0},{16,24},{24,16},{1,9},{9,1},{17,25},{25,17},{2,10},{10... | collective-permute-start | bytes 811016 | tf_op jit(solution)/shard_map/ppermute | solution.py:185
  4.2 1.5 %collective-permute-start.3 = (bf16[128,1024]{1,0:T(8,128)(2,1)S(1)}, bf16[128,1024]{1,0:T(8,128)(2,1)S(1)}, u32[]{:S(2)}, u32[]{:S(2)}) collective-permute-start(bf16[128,1024]{1,0:T(8,128)(2,1)S(1)} %get-tuple-element.13.own_ref.refs_1_), channel_id=1, source_target_pairs={{0,16},{8,24},{16,0},{24,8},{1,17},{9,25},{17,1},{25,9},{2,18},{10... | collective-permute-start | bytes 786440 | tf_op jit(solution)/shard_map/ppermute | solution.py:196
  5.8 2.5 %collective-permute-start.1 = (bf16[64,1024]{1,0:T(8,128)(2,1)S(1)}, bf16[64,1024]{1,0:T(8,128)(2,1)S(1)}, u32[]{:S(2)}, u32[]{:S(2)}) collective-permute-start(bf16[64,1024]{1,0:T(8,128)(2,1)S(1)} %get-tuple-element.15.refs_7_), channel_id=1, source_target_pairs={{0,7},{1,2},{2,1},{3,4},{4,3},{5,6},{6,5},{7,0},{8,15},{9,10},{10,... | collective-permute-start | bytes 393224 | tf_op jit(solution)/shard_map/ppermute | solution.py:190
  8.2 0.0 collective-permute-start.2
  8.3 4.8 %collective-permute-done.1.refs_2_.q_ref = bf16[64,1024]{1,0:T(8,128)(2,1)S(1)} collective-permute-done((bf16[64,1024]{1,0:T(8,128)(2,1)S(1)}, bf16[64,1024]{1,0:T(8,128)(2,1)S(1)}, u32[]{:S(2)}, u32[]{:S(2)}) %collective-permute-start.1) | collective-permute-done | bytes 131104 | tf_op jit(solution)/shard_map/ppermute | solution.py:190
  13.1 0.0 collective-permute-done.2.refs_3_.q_ref
  13.1 0.0 collective-permute-done.3.refs_4_
  13.1 0.0 collective-permute-done.refs_0_
  13.1 0.6 %collective-permute-start.5 = (bf16[132,1024]{1,0:T(8,128)(2,1)S(1)}, bf16[132,1024]{1,0:T(8,128)(2,1)S(1)}, u32[]{:S(2)}, u32[]{:S(2)}) collective-permute-start(bf16[132,1024]{1,0:T(8,128)(2,1)S(1)} %after.6.pair_ref.refs_2_), channel_id=1, source_target_pairs={{0,16},{8,24},{16,0},{24,8},{1,17},{9,25},{17,1},{25,9},{2,18},{10... | collective-permute-start | bytes 811016 | tf_op jit(solution)/shard_map/ppermute | solution.py:196
  13.8 0.1 collective-permute-start.7
  13.9 0.6 %collective-permute-start.6 = (bf16[128,1024]{1,0:T(8,128)(2,1)S(1)}, bf16[128,1024]{1,0:T(8,128)(2,1)S(1)}, u32[]{:S(2)}, u32[]{:S(2)}) collective-permute-start(bf16[128,1024]{1,0:T(8,128)(2,1)S(1)} %collective-permute-done.3.refs_4_), channel_id=1, source_target_pairs={{0,8},{8,0},{16,24},{24,16},{1,9},{9,1},{17,25},{25,17},{2,10},{10... | collective-permute-start | bytes 786440 | tf_op jit(solution)/shard_map/ppermute | solution.py:185
  14.5 1.5 %collective-permute-start.4 = (bf16[128,1024]{1,0:T(8,128)(2,1)S(1)}, bf16[128,1024]{1,0:T(8,128)(2,1)S(1)}, u32[]{:S(2)}, u32[]{:S(2)}) collective-permute-start(bf16[128,1024]{1,0:T(8,128)(2,1)S(1)} %get-tuple-element.13.own_ref.refs_1_), channel_id=1, source_target_pairs={{0,8},{8,0},{16,24},{24,16},{1,9},{9,1},{17,25},{25,17},{2,10},{10... | collective-permute-start | bytes 786440 | tf_op jit(solution)/shard_map/ppermute | solution.py:185
  16.0 0.0 collective-permute-done.7
  16.0 1.5 %collective-permute-start.8 = (bf16[2,2,1024]{2,1,0:T(2,128)(2,1)S(1)}, bf16[2,2,1024]{2,1,0:T(2,128)(2,1)S(1)}, u32[]{:S(2)}, u32[]{:S(2)}) collective-permute-start(bf16[2,2,1024]{2,1,0:T(2,128)(2,1)S(1)} %pad_maximum_fusion.2), channel_id=1, source_target_pairs={{0,2},{1,3},{2,0},{3,1},{4,6},{5,7},{6,4},{7,5},{8,10},{9,11},{10,... | collective-permute-start | bytes 24584 | tf_op jit(solution)/shard_map/ppermute | solution.py:185
  17.6 2.2 %collective-permute-done.8 = bf16[2,2,1024]{2,1,0:T(2,128)(2,1)S(1)} collective-permute-done((bf16[2,2,1024]{2,1,0:T(2,128)(2,1)S(1)}, bf16[2,2,1024]{2,1,0:T(2,128)(2,1)S(1)}, u32[]{:S(2)}, u32[]{:S(2)}) %collective-permute-start.8) | collective-permute-done | bytes 8224 | tf_op jit(solution)/shard_map/ppermute | solution.py:185
  19.8 1.6 %collective-permute-start.9 = (bf16[2,4,1024]{2,1,0:T(4,128)(2,1)S(1)}, bf16[2,4,1024]{2,1,0:T(4,128)(2,1)S(1)}, u32[]{:S(2)}, u32[]{:S(2)}) collective-permute-start(bf16[2,4,1024]{2,1,0:T(4,128)(2,1)S(1)} %pad_maximum_fusion.1), channel_id=1, source_target_pairs={{0,16},{8,24},{16,0},{24,8},{1,17},{9,25},{17,1},{25,9},{2,18},{10... | collective-permute-start | bytes 49160 | tf_op jit(solution)/shard_map/ppermute | solution.py:185
  21.4 0.0 collective-permute-done.5.far_ref.refs_4_
  21.4 0.6 %edge_part.1.refs_1_ = bf16[64,1152]{1,0:T(8,128)(2,1)S(1)} custom-call(bf16[64,1024]{1,0:T(8,128)(2,1)S(1)} %collective-permute-done.1.refs_2_.q_ref, bf16[132,1024]{1,0:T(8,128)(2,1)S(1)} %get-tuple-element.12.own_ref.refs_0_, bf16[132,1024]{1,0:T(8,128)(2,1)S(1)} %after.6.pair_ref.refs_2_, bf16[132,1024]{1,0:T(8,128)(2,1)S(1)} %collective-permute-done.5.far_ref.refs_4_), custom_call_target="tpu_custom_call" | custom-call | flops 50331648 | bytes 1089536 | tf_op jit(solution)/shard_map/edge_part/pallas_call | solution.py:27
  22.0 0.9 %collective-permute-start.10 = (bf16[64,1152]{1,0:T(8,128)(2,1)S(1)}, bf16[64,1152]{1,0:T(8,128)(2,1)S(1)}, u32[]{:S(2)}, u32[]{:S(2)}) collective-permute-start(bf16[64,1152]{1,0:T(8,128)(2,1)S(1)} %edge_part.1.refs_1_), channel_id=1, source_target_pairs={{0,7},{1,2},{2,1},{3,4},{4,3},{5,6},{6,5},{7,0},{8,15},{9,10},{10,... | collective-permute-start | bytes 442376 | tf_op jit(solution)/shard_map/ppermute | solution.py:190
  22.9 0.1 collective-permute-done.6.refs_0_
  23.0 0.0 copy-start
  23.0 5.2 %collective-permute-done.4.pair_ref.refs_3_ = bf16[128,1024]{1,0:T(8,128)(2,1)S(1)} collective-permute-done((bf16[128,1024]{1,0:T(8,128)(2,1)S(1)}, bf16[128,1024]{1,0:T(8,128)(2,1)S(1)}, u32[]{:S(2)}, u32[]{:S(2)}) %collective-permute-start.4) | collective-permute-done | bytes 262176 | tf_op jit(solution)/shard_map/ppermute | solution.py:185
  28.2 0.6 %inner_part.1.refs_1_ = bf16[64,1152]{1,0:T(8,128)(2,1)S(1)} custom-call(bf16[64,1024]{1,0:T(8,128)(2,1)S(1)} %collective-permute-done.2.refs_3_.q_ref, bf16[128,1024]{1,0:T(8,128)(2,1)S(1)} %get-tuple-element.13.own_ref.refs_1_, bf16[128,1024]{1,0:T(8,128)(2,1)S(1)} %collective-permute-done.4.pair_ref.refs_3_, bf16[128,1024]{1,0:T(8,128)(2,1)S(1)} %after.7.far_ref.refs_5_), custom_call_target="tpu_custom_call" | custom-call | flops 50331648 | bytes 1064960 | tf_op jit(solution)/shard_map/inner_part/pallas_call | solution.py:27
  28.8 0.1 collective-permute-start.11
  28.9 0.0 collective-permute-done.9
  28.9 0.1 fusion.6.refs_0_
  29.0 1.3 %own_part.1 = (f32[128,1024]{1,0:T(8,128)S(1)}, f32[128,128]{1,0:T(8,128)S(1)}) custom-call(bf16[132,1024]{1,0:T(8,128)(2,1)S(1)} %get-tuple-element.12.own_ref.refs_0_, bf16[128,1024]{1,0:T(8,128)(2,1)S(1)} %get-tuple-element.13.own_ref.refs_1_, bf16[132,1024]{1,0:T(8,128)(2,1)S(1)} %after.6.pair_ref.refs_2_, ...), custom_call_target="tpu_custom_call" | custom-call | flops 201326592 | bytes 2514944 | tf_op jit(solution)/shard_map/own_part/pallas_call | solution.py:27
  30.3 0.0 collective-permute-done.10.refs_0_
  30.3 0.0 collective-permute-done.11.inner_ref
  30.3 0.0 copy-done
  30.3 1.5 %merge.1 = bf16[8,16,1024]{2,1,0:T(8,128)(2,1)} custom-call(f32[128,1024]{1,0:T(8,128)S(1)} %get-tuple-element.17.refs_1_.own_ref, f32[128,128]{1,0:T(8,128)S(1)} %get-tuple-element.18.lse_ref, bf16[64,1152]{1,0:T(8,128)(2,1)S(1)} %after.9.edge_ref, bf16[64,1152]{1,0:T(8,128)(2,1)S(1)} %collective-permute-done.11.inner_ref, bf16[1024,1024]{1,0:T(8,128)(2,1)S(1)} %copy-done), custom_call_target="tpu_custom_call" | custom-call | flops 268435456 | bytes 3244032 | tf_op jit(solution)/shard_map/merge/pallas_call | solution.py:27
  (14 shorter events, 0.2 us)
Async XLA Ops:
  1.2 11.9 %collective-permute-start = (bf16[132,1024]{1,0:T(8,128)(2,1)S(1)}, bf16[132,1024]{1,0:T(8,128)(2,1)S(1)}, u32[]{:S(2)}, u32[]{:S(2)}) collective-permute-start(bf16[132,1024]{1,0:T(8,128)(2,1)S(1)} %get-tuple-element.12.own_ref.refs_0_), channel_id=1, source_target_pairs={{0,8},{8,0},{16,24},{24,16},{1,9},{9,1},{17,25},{25,17},{2,10},{10... | collective-permute-start | bytes 811016 | tf_op jit(solution)/shard_map/ppermute | solution.py:185
  4.2 8.9 %collective-permute-start.3 = (bf16[128,1024]{1,0:T(8,128)(2,1)S(1)}, bf16[128,1024]{1,0:T(8,128)(2,1)S(1)}, u32[]{:S(2)}, u32[]{:S(2)}) collective-permute-start(bf16[128,1024]{1,0:T(8,128)(2,1)S(1)} %get-tuple-element.13.own_ref.refs_1_), channel_id=1, source_target_pairs={{0,16},{8,24},{16,0},{24,8},{1,17},{9,25},{17,1},{25,9},{2,18},{10... | collective-permute-start | bytes 786440 | tf_op jit(solution)/shard_map/ppermute | solution.py:196
  5.8 7.3 %collective-permute-start.1 = (bf16[64,1024]{1,0:T(8,128)(2,1)S(1)}, bf16[64,1024]{1,0:T(8,128)(2,1)S(1)}, u32[]{:S(2)}, u32[]{:S(2)}) collective-permute-start(bf16[64,1024]{1,0:T(8,128)(2,1)S(1)} %get-tuple-element.15.refs_7_), channel_id=1, source_target_pairs={{0,7},{1,2},{2,1},{3,4},{4,3},{5,6},{6,5},{7,0},{8,15},{9,10},{10,... | collective-permute-start | bytes 393224 | tf_op jit(solution)/shard_map/ppermute | solution.py:190
  8.2 4.9 %collective-permute-start.2 = (bf16[64,1024]{1,0:T(8,128)(2,1)S(1)}, bf16[64,1024]{1,0:T(8,128)(2,1)S(1)}, u32[]{:S(2)}, u32[]{:S(2)}) collective-permute-start(bf16[64,1024]{1,0:T(8,128)(2,1)S(1)} %get-tuple-element.16.refs_6_), channel_id=1, source_target_pairs={{0,1},{1,0},{2,3},{3,2},{4,5},{5,4},{6,7},{7,6},{8,9},{9,8},{10,11... | collective-permute-start | bytes 393224 | tf_op jit(solution)/shard_map/ppermute | solution.py:185
  13.1 8.2 %collective-permute-start.5 = (bf16[132,1024]{1,0:T(8,128)(2,1)S(1)}, bf16[132,1024]{1,0:T(8,128)(2,1)S(1)}, u32[]{:S(2)}, u32[]{:S(2)}) collective-permute-start(bf16[132,1024]{1,0:T(8,128)(2,1)S(1)} %after.6.pair_ref.refs_2_), channel_id=1, source_target_pairs={{0,16},{8,24},{16,0},{24,8},{1,17},{9,25},{17,1},{25,9},{2,18},{10... | collective-permute-start | bytes 811016 | tf_op jit(solution)/shard_map/ppermute | solution.py:196
  13.8 2.2 %collective-permute-start.7 = (bf16[2,5,1024]{2,1,0:T(8,128)(2,1)S(1)}, bf16[2,5,1024]{2,1,0:T(8,128)(2,1)S(1)}, u32[]{:S(2)}, u32[]{:S(2)}) collective-permute-start(bf16[2,5,1024]{2,1,0:T(8,128)(2,1)S(1)} %pad_maximum_fusion), channel_id=1, source_target_pairs={{0,1},{1,0},{2,3},{3,2},{4,5},{5,4},{6,7},{7,6},{8,9},{9,8},{10,11... | collective-permute-start | bytes 61448 | tf_op jit(solution)/shard_map/ppermute | solution.py:185
  13.9 9.2 %collective-permute-start.6 = (bf16[128,1024]{1,0:T(8,128)(2,1)S(1)}, bf16[128,1024]{1,0:T(8,128)(2,1)S(1)}, u32[]{:S(2)}, u32[]{:S(2)}) collective-permute-start(bf16[128,1024]{1,0:T(8,128)(2,1)S(1)} %collective-permute-done.3.refs_4_), channel_id=1, source_target_pairs={{0,8},{8,0},{16,24},{24,16},{1,9},{9,1},{17,25},{25,17},{2,10},{10... | collective-permute-start | bytes 786440 | tf_op jit(solution)/shard_map/ppermute | solution.py:185
  14.5 13.8 %collective-permute-start.4 = (bf16[128,1024]{1,0:T(8,128)(2,1)S(1)}, bf16[128,1024]{1,0:T(8,128)(2,1)S(1)}, u32[]{:S(2)}, u32[]{:S(2)}) collective-permute-start(bf16[128,1024]{1,0:T(8,128)(2,1)S(1)} %get-tuple-element.13.own_ref.refs_1_), channel_id=1, source_target_pairs={{0,8},{8,0},{16,24},{24,16},{1,9},{9,1},{17,25},{25,17},{2,10},{10... | collective-permute-start | bytes 786440 | tf_op jit(solution)/shard_map/ppermute | solution.py:185
  16.0 3.7 %collective-permute-start.8 = (bf16[2,2,1024]{2,1,0:T(2,128)(2,1)S(1)}, bf16[2,2,1024]{2,1,0:T(2,128)(2,1)S(1)}, u32[]{:S(2)}, u32[]{:S(2)}) collective-permute-start(bf16[2,2,1024]{2,1,0:T(2,128)(2,1)S(1)} %pad_maximum_fusion.2), channel_id=1, source_target_pairs={{0,2},{1,3},{2,0},{3,1},{4,6},{5,7},{6,4},{7,5},{8,10},{9,11},{10,... | collective-permute-start | bytes 24584 | tf_op jit(solution)/shard_map/ppermute | solution.py:185
  19.8 9.2 %collective-permute-start.9 = (bf16[2,4,1024]{2,1,0:T(4,128)(2,1)S(1)}, bf16[2,4,1024]{2,1,0:T(4,128)(2,1)S(1)}, u32[]{:S(2)}, u32[]{:S(2)}) collective-permute-start(bf16[2,4,1024]{2,1,0:T(4,128)(2,1)S(1)} %pad_maximum_fusion.1), channel_id=1, source_target_pairs={{0,16},{8,24},{16,0},{24,8},{1,17},{9,25},{17,1},{25,9},{2,18},{10... | collective-permute-start | bytes 49160 | tf_op jit(solution)/shard_map/ppermute | solution.py:185
  22.0 8.3 %collective-permute-start.10 = (bf16[64,1152]{1,0:T(8,128)(2,1)S(1)}, bf16[64,1152]{1,0:T(8,128)(2,1)S(1)}, u32[]{:S(2)}, u32[]{:S(2)}) collective-permute-start(bf16[64,1152]{1,0:T(8,128)(2,1)S(1)} %edge_part.1.refs_1_), channel_id=1, source_target_pairs={{0,7},{1,2},{2,1},{3,4},{4,3},{5,6},{6,5},{7,0},{8,15},{9,10},{10,... | collective-permute-start | bytes 442376 | tf_op jit(solution)/shard_map/ppermute | solution.py:190
  23.0 7.3 %copy-start = (bf16[1024,1024]{1,0:T(8,128)(2,1)S(1)}, bf16[1024,1024]{1,0:T(8,128)(2,1)}, u32[]{:S(2)}) copy-start(bf16[1024,1024]{1,0:T(8,128)(2,1)} %weight_ref.1) | copy-start | bytes 6291460
  28.8 1.4 %collective-permute-start.11 = (bf16[64,1152]{1,0:T(8,128)(2,1)S(1)}, bf16[64,1152]{1,0:T(8,128)(2,1)S(1)}, u32[]{:S(2)}, u32[]{:S(2)}) collective-permute-start(bf16[64,1152]{1,0:T(8,128)(2,1)S(1)} %inner_part.1.refs_1_), channel_id=1, source_target_pairs={{0,1},{1,0},{2,3},{3,2},{4,5},{5,4},{6,7},{7,6},{8,9},{9,8},{10,11... | collective-permute-start | bytes 442376 | tf_op jit(solution)/shard_map/ppermute | solution.py:185

commit v11 on v4

--- a/solution.py
+++ b/solution.py
@@ -251,7 +251,7 @@
     inner_pair = swap(inner_own, "lat", 1)
     inner_hop = stride(inner_own, "lat", -2)
     pooled = after(pooled, weight=4 * WEIGHT)
-    edge_pair = after(edge_pair, pooled, far_q_edge, far_q_inner, inner_hop)
+    edge_pair = after(edge_pair, pooled, far_q_edge, inner_hop)
     edge_far = stride(edge_pair, "lat", 2)
     inner_far = swap(inner_hop, "lat", 1)
     level0 = pooled.reshape(2, 2, width)
@@ -261,7 +261,7 @@
     group = jnp.concatenate([mine, beside[:, 4:5]], axis=1)
     group_lon = swap(group, "lon", 2)
     group_both = jnp.concatenate([group, group_lon], axis=1)
-    group_lat = swap(after(group_both, inner_pair), "lat", 2)
+    group_lat = swap(after(group_both, inner_pair, far_q_inner), "lat", 2)
     coarse = jnp.concatenate([level0_lat, beside[:, 0:4], group_lon, group_lat], axis=1)
     count = coarse.shape[1] // 2
     coarse = jnp.pad(coarse, ((0, 0), (0, 16 - 2 * count), (0, 0)))

time: 30.7 us -> 30.7 us (level)
  starting transfers between devices: 14.5 us -> 14.9 us
  waiting for transfers between devices: 10.4 us -> 10 us
    ppermute x2, starting transfers between devices: 4.32 us -> 4.68 us  [outward(): lax.ppermute(x, axis, [(i, (i + (1 if i % 2 else -1)) % count) for i in r...]
    ppermute x2, waiting for transfers between devices: 8.26 us -> 7.93 us  [outward(): lax.ppermute(x, axis, [(i, (i + (1 if i % 2 else -1)) % count) for i in r...]
where the time goes in v11:
time: 30.7 us; the launch traced here: 30.6 us
  starting transfers between devices  14.9 us (49%)
  waiting for transfers between devices  10 us (33%)
  Pallas kernels  5.27 us (17%)
    ppermute x2, waiting for transfers between devices, outward(): lax.ppermute(x, axis, [(i, (i + (1 if i % 2 else -1)) % count) for i in r...  7.93 us
    ppermute x8, starting transfers between devices, swap(): return lax.ppermute(x, axis, [(i, i ^ distance) for i in range(count)])  7.9 us
    ppermute x2, starting transfers between devices, outward(): lax.ppermute(x, axis, [(i, (i + (1 if i % 2 else -1)) % count) for i in r...  4.68 us
    pallas_call x4, Pallas kernels, call(): pl.pallas_call(kernel, out_shape=outs, in_specs=[VMEM] * len(args), out_s...  4.04 us
    ppermute x2, starting transfers between devices, stride(): return lax.ppermute(x, axis, route)  2.29 us
    ppermute x8, waiting for transfers between devices, swap(): return lax.ppermute(x, axis, [(i, i ^ distance) for i in range(count)])  2.09 us
    pallas_call x1, Pallas kernels, shards(): pl.pallas_call(split_kernel, out_shape=[like(SPAN, width), like(SPAN, wid...  1.23 us
  transfers between devices with their start and end apart: 12, of which 3 were waited for; matrix products, arithmetic and copies ran while one was open for 1% of the time, Pallas kernels for 8%

profile of v11, /device:TPU:0, one launch (start us, length us, event | category | flops | bytes accessed | tf_op | source)
XLA Modules:
  0.0 30.6 jit_solution(9578134367102338349)
XLA Ops:
  0.0 1.2 %split.1 = (bf16[64,1024]{1,0:T(8,128)(2,1)S(1)}, bf16[64,1024]{1,0:T(8,128)(2,1)S(1)}, bf16[132,1024]{1,0:T(8,128)(2,1)S(1)}, bf16[128,1024]{1,0:T(8,128)(2,1)S(1)}, bf16[4,1024]{1,0:T(4,128)(2,1)S(1)}) custom-call(bf16[8,16,1024]{2,1,0:T(8,128)(2,1)} %q_hbm.1, bf16[2,8,16,1024]{3,2,1,0:T(8,128)(2,1)} %kv_hbm.1), custom_call_target="tpu_custom_call" | custom-call | bytes 2097152 | tf_op jit(solution)/shard_map/split/pallas_call | solution.py:228
  1.2 3.0 %collective-permute-start = (bf16[132,1024]{1,0:T(8,128)(2,1)S(1)}, bf16[132,1024]{1,0:T(8,128)(2,1)S(1)}, u32[]{:S(2)}, u32[]{:S(2)}) collective-permute-start(bf16[132,1024]{1,0:T(8,128)(2,1)S(1)} %get-tuple-element.12.own_ref.refs_0_), channel_id=1, source_target_pairs={{0,8},{8,0},{16,24},{24,16},{1,9},{9,1},{17,25},{25,17},{2,10},{10... | collective-permute-start | bytes 811016 | tf_op jit(solution)/shard_map/ppermute | solution.py:185
  4.2 1.5 %collective-permute-start.2 = (bf16[128,1024]{1,0:T(8,128)(2,1)S(1)}, bf16[128,1024]{1,0:T(8,128)(2,1)S(1)}, u32[]{:S(2)}, u32[]{:S(2)}) collective-permute-start(bf16[128,1024]{1,0:T(8,128)(2,1)S(1)} %get-tuple-element.13.own_ref.refs_1_), channel_id=1, source_target_pairs={{0,16},{8,24},{16,0},{24,8},{1,17},{9,25},{17,1},{25,9},{2,18},{10... | collective-permute-start | bytes 786440 | tf_op jit(solution)/shard_map/ppermute | solution.py:196
  5.8 2.5 %collective-permute-start.1 = (bf16[64,1024]{1,0:T(8,128)(2,1)S(1)}, bf16[64,1024]{1,0:T(8,128)(2,1)S(1)}, u32[]{:S(2)}, u32[]{:S(2)}) collective-permute-start(bf16[64,1024]{1,0:T(8,128)(2,1)S(1)} %get-tuple-element.15.refs_7_), channel_id=1, source_target_pairs={{0,7},{1,2},{2,1},{3,4},{4,3},{5,6},{6,5},{7,0},{8,15},{9,10},{10,... | collective-permute-start | bytes 393224 | tf_op jit(solution)/shard_map/ppermute | solution.py:190
  8.2 0.5 %collective-permute-start.3 = (bf16[128,1024]{1,0:T(8,128)(2,1)S(1)}, bf16[128,1024]{1,0:T(8,128)(2,1)S(1)}, u32[]{:S(2)}, u32[]{:S(2)}) collective-permute-start(bf16[128,1024]{1,0:T(8,128)(2,1)S(1)} %get-tuple-element.13.own_ref.refs_1_), channel_id=1, source_target_pairs={{0,8},{8,0},{16,24},{24,16},{1,9},{9,1},{17,25},{25,17},{2,10},{10... | collective-permute-start | bytes 786440 | tf_op jit(solution)/shard_map/ppermute | solution.py:185
  8.8 4.3 %collective-permute-done.1.refs_2_.q_ref = bf16[64,1024]{1,0:T(8,128)(2,1)S(1)} collective-permute-done((bf16[64,1024]{1,0:T(8,128)(2,1)S(1)}, bf16[64,1024]{1,0:T(8,128)(2,1)S(1)}, u32[]{:S(2)}, u32[]{:S(2)}) %collective-permute-start.1) | collective-permute-done | bytes 131104 | tf_op jit(solution)/shard_map/ppermute | solution.py:190
  13.1 0.0 collective-permute-done.2.refs_3_
  13.1 0.0 collective-permute-done.refs_0_
  13.1 0.8 %collective-permute-start.4 = (bf16[132,1024]{1,0:T(8,128)(2,1)S(1)}, bf16[132,1024]{1,0:T(8,128)(2,1)S(1)}, u32[]{:S(2)}, u32[]{:S(2)}) collective-permute-start(bf16[132,1024]{1,0:T(8,128)(2,1)S(1)} %after.7.pair_ref.refs_2_), channel_id=1, source_target_pairs={{0,16},{8,24},{16,0},{24,8},{1,17},{9,25},{17,1},{25,9},{2,18},{10... | collective-permute-start | bytes 811016 | tf_op jit(solution)/shard_map/ppermute | solution.py:196
  14.0 0.1 collective-permute-start.6
  14.0 1.6 %collective-permute-start.5 = (bf16[128,1024]{1,0:T(8,128)(2,1)S(1)}, bf16[128,1024]{1,0:T(8,128)(2,1)S(1)}, u32[]{:S(2)}, u32[]{:S(2)}) collective-permute-start(bf16[128,1024]{1,0:T(8,128)(2,1)S(1)} %collective-permute-done.2.refs_3_), channel_id=1, source_target_pairs={{0,8},{8,0},{16,24},{24,16},{1,9},{9,1},{17,25},{25,17},{2,10},{10... | collective-permute-start | bytes 786440 | tf_op jit(solution)/shard_map/ppermute | solution.py:185
  15.6 0.2 collective-permute-start.8
  15.8 0.0 collective-permute-done.6
  15.8 1.6 %collective-permute-start.7 = (bf16[2,2,1024]{2,1,0:T(2,128)(2,1)S(1)}, bf16[2,2,1024]{2,1,0:T(2,128)(2,1)S(1)}, u32[]{:S(2)}, u32[]{:S(2)}) collective-permute-start(bf16[2,2,1024]{2,1,0:T(2,128)(2,1)S(1)} %pad_maximum_fusion.2), channel_id=1, source_target_pairs={{0,2},{1,3},{2,0},{3,1},{4,6},{5,7},{6,4},{7,5},{8,10},{9,11},{10,... | collective-permute-start | bytes 24584 | tf_op jit(solution)/shard_map/ppermute | solution.py:185
  17.5 2.1 %collective-permute-done.7 = bf16[2,2,1024]{2,1,0:T(2,128)(2,1)S(1)} collective-permute-done((bf16[2,2,1024]{2,1,0:T(2,128)(2,1)S(1)}, bf16[2,2,1024]{2,1,0:T(2,128)(2,1)S(1)}, u32[]{:S(2)}, u32[]{:S(2)}) %collective-permute-start.7) | collective-permute-done | bytes 8224 | tf_op jit(solution)/shard_map/ppermute | solution.py:185
  19.6 0.0 collective-permute-done.8.refs_2_.q_ref
  19.6 0.0 collective-permute-done.3.refs_1_.pair_ref.refs_3_
  19.6 0.9 %collective-permute-start.9 = (bf16[2,4,1024]{2,1,0:T(4,128)(2,1)S(1)}, bf16[2,4,1024]{2,1,0:T(4,128)(2,1)S(1)}, u32[]{:S(2)}, u32[]{:S(2)}) collective-permute-start(bf16[2,4,1024]{2,1,0:T(4,128)(2,1)S(1)} %after.9), channel_id=1, source_target_pairs={{0,16},{8,24},{16,0},{24,8},{1,17},{9,25},{17,1},{25,9},{2,18},{10... | collective-permute-start | bytes 49160 | tf_op jit(solution)/shard_map/ppermute | solution.py:185
  20.5 0.0 collective-permute-done.4.far_ref.refs_4_
  20.5 0.6 %edge_part.1.refs_1_ = bf16[64,1152]{1,0:T(8,128)(2,1)S(1)} custom-call(bf16[64,1024]{1,0:T(8,128)(2,1)S(1)} %collective-permute-done.1.refs_2_.q_ref, bf16[132,1024]{1,0:T(8,128)(2,1)S(1)} %get-tuple-element.12.own_ref.refs_0_, bf16[132,1024]{1,0:T(8,128)(2,1)S(1)} %after.7.pair_ref.refs_2_, bf16[132,1024]{1,0:T(8,128)(2,1)S(1)} %collective-permute-done.4.far_ref.refs_4_), custom_call_target="tpu_custom_call" | custom-call | flops 50331648 | bytes 1089536 | tf_op jit(solution)/shard_map/edge_part/pallas_call | solution.py:27
  21.1 2.2 %collective-permute-start.10 = (bf16[64,1152]{1,0:T(8,128)(2,1)S(1)}, bf16[64,1152]{1,0:T(8,128)(2,1)S(1)}, u32[]{:S(2)}, u32[]{:S(2)}) collective-permute-start(bf16[64,1152]{1,0:T(8,128)(2,1)S(1)} %edge_part.1.refs_1_), channel_id=1, source_target_pairs={{0,7},{1,2},{2,1},{3,4},{4,3},{5,6},{6,5},{7,0},{8,15},{9,10},{10,... | collective-permute-start | bytes 442376 | tf_op jit(solution)/shard_map/ppermute | solution.py:190
  23.3 0.0 collective-permute-done.5.refs_0_
  23.3 0.0 copy-start
  23.3 0.6 %inner_part.1.refs_1_ = bf16[64,1152]{1,0:T(8,128)(2,1)S(1)} custom-call(bf16[64,1024]{1,0:T(8,128)(2,1)S(1)} %collective-permute-done.8.refs_2_.q_ref, bf16[128,1024]{1,0:T(8,128)(2,1)S(1)} %get-tuple-element.13.own_ref.refs_1_, bf16[128,1024]{1,0:T(8,128)(2,1)S(1)} %collective-permute-done.3.refs_1_.pair_ref.refs_3_, ...), custom_call_target="tpu_custom_call" | custom-call | flops 50331648 | bytes 1064960 | tf_op jit(solution)/shard_map/inner_part/pallas_call | solution.py:27
  24.0 0.1 collective-permute-start.11
  24.1 0.0 collective-permute-done.9
  24.1 0.1 fusion.6.refs_0_
  24.1 1.3 %own_part.1 = (f32[128,1024]{1,0:T(8,128)S(1)}, f32[128,128]{1,0:T(8,128)S(1)}) custom-call(bf16[132,1024]{1,0:T(8,128)(2,1)S(1)} %get-tuple-element.12.own_ref.refs_0_, bf16[128,1024]{1,0:T(8,128)(2,1)S(1)} %get-tuple-element.13.own_ref.refs_1_, bf16[132,1024]{1,0:T(8,128)(2,1)S(1)} %after.7.pair_ref.refs_2_, ...), custom_call_target="tpu_custom_call" | custom-call | flops 201326592 | bytes 2514944 | tf_op jit(solution)/shard_map/own_part/pallas_call | solution.py:27
  25.4 3.6 %collective-permute-done.10.refs_0_ = bf16[64,1152]{1,0:T(8,128)(2,1)S(1)} collective-permute-done((bf16[64,1152]{1,0:T(8,128)(2,1)S(1)}, bf16[64,1152]{1,0:T(8,128)(2,1)S(1)}, u32[]{:S(2)}, u32[]{:S(2)}) %collective-permute-start.10) | collective-permute-done | bytes 147488 | tf_op jit(solution)/shard_map/ppermute | solution.py:190
  29.0 0.0 collective-permute-done.11.inner_ref
  29.0 0.0 copy-done
  29.0 1.5 %merge.1 = bf16[8,16,1024]{2,1,0:T(8,128)(2,1)} custom-call(f32[128,1024]{1,0:T(8,128)S(1)} %get-tuple-element.17.refs_1_.own_ref, f32[128,128]{1,0:T(8,128)S(1)} %get-tuple-element.18.lse_ref, bf16[64,1152]{1,0:T(8,128)(2,1)S(1)} %after.11.edge_ref, bf16[64,1152]{1,0:T(8,128)(2,1)S(1)} %collective-permute-done.11.inner_ref, bf16[1024,1024]{1,0:T(8,128)(2,1)S(1)} %copy-done), custom_call_target="tpu_custom_call" | custom-call | flops 268435456 | bytes 3244032 | tf_op jit(solution)/shard_map/merge/pallas_call | solution.py:27
  (15 shorter events, 0.2 us)
Async XLA Ops:
  1.2 11.9 %collective-permute-start = (bf16[132,1024]{1,0:T(8,128)(2,1)S(1)}, bf16[132,1024]{1,0:T(8,128)(2,1)S(1)}, u32[]{:S(2)}, u32[]{:S(2)}) collective-permute-start(bf16[132,1024]{1,0:T(8,128)(2,1)S(1)} %get-tuple-element.12.own_ref.refs_0_), channel_id=1, source_target_pairs={{0,8},{8,0},{16,24},{24,16},{1,9},{9,1},{17,25},{25,17},{2,10},{10... | collective-permute-start | bytes 811016 | tf_op jit(solution)/shard_map/ppermute | solution.py:185
  4.2 8.9 %collective-permute-start.2 = (bf16[128,1024]{1,0:T(8,128)(2,1)S(1)}, bf16[128,1024]{1,0:T(8,128)(2,1)S(1)}, u32[]{:S(2)}, u32[]{:S(2)}) collective-permute-start(bf16[128,1024]{1,0:T(8,128)(2,1)S(1)} %get-tuple-element.13.own_ref.refs_1_), channel_id=1, source_target_pairs={{0,16},{8,24},{16,0},{24,8},{1,17},{9,25},{17,1},{25,9},{2,18},{10... | collective-permute-start | bytes 786440 | tf_op jit(solution)/shard_map/ppermute | solution.py:196
  5.8 7.3 %collective-permute-start.1 = (bf16[64,1024]{1,0:T(8,128)(2,1)S(1)}, bf16[64,1024]{1,0:T(8,128)(2,1)S(1)}, u32[]{:S(2)}, u32[]{:S(2)}) collective-permute-start(bf16[64,1024]{1,0:T(8,128)(2,1)S(1)} %get-tuple-element.15.refs_7_), channel_id=1, source_target_pairs={{0,7},{1,2},{2,1},{3,4},{4,3},{5,6},{6,5},{7,0},{8,15},{9,10},{10,... | collective-permute-start | bytes 393224 | tf_op jit(solution)/shard_map/ppermute | solution.py:190
  8.2 11.3 %collective-permute-start.3 = (bf16[128,1024]{1,0:T(8,128)(2,1)S(1)}, bf16[128,1024]{1,0:T(8,128)(2,1)S(1)}, u32[]{:S(2)}, u32[]{:S(2)}) collective-permute-start(bf16[128,1024]{1,0:T(8,128)(2,1)S(1)} %get-tuple-element.13.own_ref.refs_1_), channel_id=1, source_target_pairs={{0,8},{8,0},{16,24},{24,16},{1,9},{9,1},{17,25},{25,17},{2,10},{10... | collective-permute-start | bytes 786440 | tf_op jit(solution)/shard_map/ppermute | solution.py:185
  13.1 7.4 %collective-permute-start.4 = (bf16[132,1024]{1,0:T(8,128)(2,1)S(1)}, bf16[132,1024]{1,0:T(8,128)(2,1)S(1)}, u32[]{:S(2)}, u32[]{:S(2)}) collective-permute-start(bf16[132,1024]{1,0:T(8,128)(2,1)S(1)} %after.7.pair_ref.refs_2_), channel_id=1, source_target_pairs={{0,16},{8,24},{16,0},{24,8},{1,17},{9,25},{17,1},{25,9},{2,18},{10... | collective-permute-start | bytes 811016 | tf_op jit(solution)/shard_map/ppermute | solution.py:196
  14.0 1.8 %collective-permute-start.6 = (bf16[2,5,1024]{2,1,0:T(8,128)(2,1)S(1)}, bf16[2,5,1024]{2,1,0:T(8,128)(2,1)S(1)}, u32[]{:S(2)}, u32[]{:S(2)}) collective-permute-start(bf16[2,5,1024]{2,1,0:T(8,128)(2,1)S(1)} %pad_maximum_fusion), channel_id=1, source_target_pairs={{0,1},{1,0},{2,3},{3,2},{4,5},{5,4},{6,7},{7,6},{8,9},{9,8},{10,11... | collective-permute-start | bytes 61448 | tf_op jit(solution)/shard_map/ppermute | solution.py:185
  14.0 9.3 %collective-permute-start.5 = (bf16[128,1024]{1,0:T(8,128)(2,1)S(1)}, bf16[128,1024]{1,0:T(8,128)(2,1)S(1)}, u32[]{:S(2)}, u32[]{:S(2)}) collective-permute-start(bf16[128,1024]{1,0:T(8,128)(2,1)S(1)} %collective-permute-done.2.refs_3_), channel_id=1, source_target_pairs={{0,8},{8,0},{16,24},{24,16},{1,9},{9,1},{17,25},{25,17},{2,10},{10... | collective-permute-start | bytes 786440 | tf_op jit(solution)/shard_map/ppermute | solution.py:185
  15.6 4.0 %collective-permute-start.8 = (bf16[64,1024]{1,0:T(8,128)(2,1)S(1)}, bf16[64,1024]{1,0:T(8,128)(2,1)S(1)}, u32[]{:S(2)}, u32[]{:S(2)}) collective-permute-start(bf16[64,1024]{1,0:T(8,128)(2,1)S(1)} %get-tuple-element.16.refs_6_), channel_id=1, source_target_pairs={{0,1},{1,0},{2,3},{3,2},{4,5},{5,4},{6,7},{7,6},{8,9},{9,8},{10,11... | collective-permute-start | bytes 393224 | tf_op jit(solution)/shard_map/ppermute | solution.py:185
  15.8 3.7 %collective-permute-start.7 = (bf16[2,2,1024]{2,1,0:T(2,128)(2,1)S(1)}, bf16[2,2,1024]{2,1,0:T(2,128)(2,1)S(1)}, u32[]{:S(2)}, u32[]{:S(2)}) collective-permute-start(bf16[2,2,1024]{2,1,0:T(2,128)(2,1)S(1)} %pad_maximum_fusion.2), channel_id=1, source_target_pairs={{0,2},{1,3},{2,0},{3,1},{4,6},{5,7},{6,4},{7,5},{8,10},{9,11},{10,... | collective-permute-start | bytes 24584 | tf_op jit(solution)/shard_map/ppermute | solution.py:185
  19.6 4.5 %collective-permute-start.9 = (bf16[2,4,1024]{2,1,0:T(4,128)(2,1)S(1)}, bf16[2,4,1024]{2,1,0:T(4,128)(2,1)S(1)}, u32[]{:S(2)}, u32[]{:S(2)}) collective-permute-start(bf16[2,4,1024]{2,1,0:T(4,128)(2,1)S(1)} %after.9), channel_id=1, source_target_pairs={{0,16},{8,24},{16,0},{24,8},{1,17},{9,25},{17,1},{25,9},{2,18},{10... | collective-permute-start | bytes 49160 | tf_op jit(solution)/shard_map/ppermute | solution.py:185
  21.1 7.9 %collective-permute-start.10 = (bf16[64,1152]{1,0:T(8,128)(2,1)S(1)}, bf16[64,1152]{1,0:T(8,128)(2,1)S(1)}, u32[]{:S(2)}, u32[]{:S(2)}) collective-permute-start(bf16[64,1152]{1,0:T(8,128)(2,1)S(1)} %edge_part.1.refs_1_), channel_id=1, source_target_pairs={{0,7},{1,2},{2,1},{3,4},{4,3},{5,6},{6,5},{7,0},{8,15},{9,10},{10,... | collective-permute-start | bytes 442376 | tf_op jit(solution)/shard_map/ppermute | solution.py:190
  23.3 5.7 %copy-start = (bf16[1024,1024]{1,0:T(8,128)(2,1)S(1)}, bf16[1024,1024]{1,0:T(8,128)(2,1)}, u32[]{:S(2)}) copy-start(bf16[1024,1024]{1,0:T(8,128)(2,1)} %weight_ref.1) | copy-start | bytes 6291460
  24.0 5.1 %collective-permute-start.11 = (bf16[64,1152]{1,0:T(8,128)(2,1)S(1)}, bf16[64,1152]{1,0:T(8,128)(2,1)S(1)}, u32[]{:S(2)}, u32[]{:S(2)}) collective-permute-start(bf16[64,1152]{1,0:T(8,128)(2,1)S(1)} %inner_part.1.refs_1_), channel_id=1, source_target_pairs={{0,1},{1,0},{2,3},{3,2},{4,5},{5,4},{6,7},{7,6},{8,9},{9,8},{10,11... | collective-permute-start | bytes 442376 | tf_op jit(solution)/shard_map/ppermute | solution.py:185

commit v12 on v11

--- a/solution.py
+++ b/solution.py
@@ -251,7 +251,7 @@
     inner_pair = swap(inner_own, "lat", 1)
     inner_hop = stride(inner_own, "lat", -2)
     pooled = after(pooled, weight=4 * WEIGHT)
-    edge_pair = after(edge_pair, pooled, far_q_edge, inner_hop)
+    edge_pair = after(edge_pair, pooled, inner_hop)
     edge_far = stride(edge_pair, "lat", 2)
     inner_far = swap(inner_hop, "lat", 1)
     level0 = pooled.reshape(2, 2, width)
@@ -261,7 +261,7 @@
     group = jnp.concatenate([mine, beside[:, 4:5]], axis=1)
     group_lon = swap(group, "lon", 2)
     group_both = jnp.concatenate([group, group_lon], axis=1)
-    group_lat = swap(after(group_both, inner_pair, far_q_inner), "lat", 2)
+    group_lat = swap(after(group_both, inner_pair, far_q_edge, far_q_inner), "lat", 2)
     coarse = jnp.concatenate([level0_lat, beside[:, 0:4], group_lon, group_lat], axis=1)
     count = coarse.shape[1] // 2
     coarse = jnp.pad(coarse, ((0, 0), (0, 16 - 2 * count), (0, 0)))

time: 30.7 us -> 34.1 us (1.11)
  waiting for transfers between devices: 10 us -> 16.3 us
  starting transfers between devices: 14.9 us -> 12.1 us
    ppermute x2, waiting for transfers between devices: 0.01 us -> 6.24 us  [stride(): return lax.ppermute(x, axis, route)]
    ppermute x2, starting transfers between devices: 4.68 us -> 1.61 us  [outward(): lax.ppermute(x, axis, [(i, (i + (1 if i % 2 else -1)) % count) for i in r...]
    ppermute x2, starting transfers between devices: 2.29 us -> 3.1 us  [stride(): return lax.ppermute(x, axis, route)]
    ppermute x8, starting transfers between devices: 7.9 us -> 7.38 us  [swap(): return lax.ppermute(x, axis, [(i, i ^ distance) for i in range(count)])]
  transfers between devices with their start and end apart: 12 -> 12, of which waited for: 3 -> 6; matrix products, arithmetic and copies ran while one was open for 1% -> 0% of each run, Pallas kernels for 8% -> 7%
where the time goes in v12:
time: 34.1 us; the launch traced here: 34 us
  waiting for transfers between devices  16.3 us (48%)
  starting transfers between devices  12.1 us (35%)
  Pallas kernels  5.27 us (15%)
    ppermute x2, waiting for transfers between devices, outward(): lax.ppermute(x, axis, [(i, (i + (1 if i % 2 else -1)) % count) for i in r...  7.72 us
    ppermute x8, starting transfers between devices, swap(): return lax.ppermute(x, axis, [(i, i ^ distance) for i in range(count)])  7.38 us
    ppermute x2, waiting for transfers between devices, stride(): return lax.ppermute(x, axis, route)  6.24 us
    pallas_call x4, Pallas kernels, call(): pl.pallas_call(kernel, out_shape=outs, in_specs=[VMEM] * len(args), out_s...  4.03 us
    ppermute x2, starting transfers between devices, stride(): return lax.ppermute(x, axis, route)  3.1 us
    ppermute x8, waiting for transfers between devices, swap(): return lax.ppermute(x, axis, [(i, i ^ distance) for i in range(count)])  2.34 us
    ppermute x2, starting transfers between devices, outward(): lax.ppermute(x, axis, [(i, (i + (1 if i % 2 else -1)) % count) for i in r...  1.61 us
    pallas_call x1, Pallas kernels, shards(): pl.pallas_call(split_kernel, out_shape=[like(SPAN, width), like(SPAN, wid...  1.23 us
  transfers between devices with their start and end apart: 12, of which 6 were waited for; matrix products, arithmetic and copies ran while one was open for 0% of the time, Pallas kernels for 7%

profile of v12, /device:TPU:0, one launch (start us, length us, event | category | flops | bytes accessed | tf_op | source)
XLA Modules:
  0.0 34.0 jit_solution(10550655805834787388)
XLA Ops:
  0.0 1.2 %split.1 = (bf16[64,1024]{1,0:T(8,128)(2,1)S(1)}, bf16[64,1024]{1,0:T(8,128)(2,1)S(1)}, bf16[132,1024]{1,0:T(8,128)(2,1)S(1)}, bf16[128,1024]{1,0:T(8,128)(2,1)S(1)}, bf16[4,1024]{1,0:T(4,128)(2,1)S(1)}) custom-call(bf16[8,16,1024]{2,1,0:T(8,128)(2,1)} %q_hbm.1, bf16[2,8,16,1024]{3,2,1,0:T(8,128)(2,1)} %kv_hbm.1), custom_call_target="tpu_custom_call" | custom-call | bytes 2097152 | tf_op jit(solution)/shard_map/split/pallas_call | solution.py:228
  1.2 3.0 %collective-permute-start = (bf16[132,1024]{1,0:T(8,128)(2,1)S(1)}, bf16[132,1024]{1,0:T(8,128)(2,1)S(1)}, u32[]{:S(2)}, u32[]{:S(2)}) collective-permute-start(bf16[132,1024]{1,0:T(8,128)(2,1)S(1)} %get-tuple-element.12.own_ref.refs_0_), channel_id=1, source_target_pairs={{0,8},{8,0},{16,24},{24,16},{1,9},{9,1},{17,25},{25,17},{2,10},{10... | collective-permute-start | bytes 811016 | tf_op jit(solution)/shard_map/ppermute | solution.py:185
  4.2 1.5 %collective-permute-start.1 = (bf16[128,1024]{1,0:T(8,128)(2,1)S(1)}, bf16[128,1024]{1,0:T(8,128)(2,1)S(1)}, u32[]{:S(2)}, u32[]{:S(2)}) collective-permute-start(bf16[128,1024]{1,0:T(8,128)(2,1)S(1)} %get-tuple-element.13.own_ref.refs_1_), channel_id=1, source_target_pairs={{0,16},{8,24},{16,0},{24,8},{1,17},{9,25},{17,1},{25,9},{2,18},{10... | collective-permute-start | bytes 786440 | tf_op jit(solution)/shard_map/ppermute | solution.py:196
  5.8 6.2 %collective-permute-done.1.refs_2_ = bf16[128,1024]{1,0:T(8,128)(2,1)S(1)} collective-permute-done((bf16[128,1024]{1,0:T(8,128)(2,1)S(1)}, bf16[128,1024]{1,0:T(8,128)(2,1)S(1)}, u32[]{:S(2)}, u32[]{:S(2)}) %collective-permute-start.1) | collective-permute-done | bytes 262176 | tf_op jit(solution)/shard_map/ppermute | solution.py:196
  12.0 0.0 collective-permute-done.refs_0_
  12.1 0.1 collective-permute-start.6
  12.2 1.6 %collective-permute-start.3 = (bf16[132,1024]{1,0:T(8,128)(2,1)S(1)}, bf16[132,1024]{1,0:T(8,128)(2,1)S(1)}, u32[]{:S(2)}, u32[]{:S(2)}) collective-permute-start(bf16[132,1024]{1,0:T(8,128)(2,1)S(1)} %after.7.pair_ref.refs_2_), channel_id=1, source_target_pairs={{0,16},{8,24},{16,0},{24,8},{1,17},{9,25},{17,1},{25,9},{2,18},{10... | collective-permute-start | bytes 811016 | tf_op jit(solution)/shard_map/ppermute | solution.py:196
  13.8 0.6 %collective-permute-start.2 = (bf16[128,1024]{1,0:T(8,128)(2,1)S(1)}, bf16[128,1024]{1,0:T(8,128)(2,1)S(1)}, u32[]{:S(2)}, u32[]{:S(2)}) collective-permute-start(bf16[128,1024]{1,0:T(8,128)(2,1)S(1)} %get-tuple-element.13.own_ref.refs_1_), channel_id=1, source_target_pairs={{0,8},{8,0},{16,24},{24,16},{1,9},{9,1},{17,25},{25,17},{2,10},{10... | collective-permute-start | bytes 786440 | tf_op jit(solution)/shard_map/ppermute | solution.py:185
  14.4 1.4 %collective-permute-start.4 = (bf16[128,1024]{1,0:T(8,128)(2,1)S(1)}, bf16[128,1024]{1,0:T(8,128)(2,1)S(1)}, u32[]{:S(2)}, u32[]{:S(2)}) collective-permute-start(bf16[128,1024]{1,0:T(8,128)(2,1)S(1)} %collective-permute-done.1.refs_2_), channel_id=1, source_target_pairs={{0,8},{8,0},{16,24},{24,16},{1,9},{9,1},{17,25},{25,17},{2,10},{10... | collective-permute-start | bytes 786440 | tf_op jit(solution)/shard_map/ppermute | solution.py:185
  15.8 0.0 collective-permute-done.6
  15.9 1.6 %collective-permute-start.7 = (bf16[2,2,1024]{2,1,0:T(2,128)(2,1)S(1)}, bf16[2,2,1024]{2,1,0:T(2,128)(2,1)S(1)}, u32[]{:S(2)}, u32[]{:S(2)}) collective-permute-start(bf16[2,2,1024]{2,1,0:T(2,128)(2,1)S(1)} %pad_maximum_fusion.2), channel_id=1, source_target_pairs={{0,2},{1,3},{2,0},{3,1},{4,6},{5,7},{6,4},{7,5},{8,10},{9,11},{10,... | collective-permute-start | bytes 24584 | tf_op jit(solution)/shard_map/ppermute | solution.py:185
  17.5 1.4 %collective-permute-start.5 = (bf16[64,1024]{1,0:T(8,128)(2,1)S(1)}, bf16[64,1024]{1,0:T(8,128)(2,1)S(1)}, u32[]{:S(2)}, u32[]{:S(2)}) collective-permute-start(bf16[64,1024]{1,0:T(8,128)(2,1)S(1)} %get-tuple-element.15.refs_7_), channel_id=1, source_target_pairs={{0,7},{1,2},{2,1},{3,4},{4,3},{5,6},{6,5},{7,0},{8,15},{9,10},{10,... | collective-permute-start | bytes 393224 | tf_op jit(solution)/shard_map/ppermute | solution.py:190
  18.9 0.7 %collective-permute-done.7 = bf16[2,2,1024]{2,1,0:T(2,128)(2,1)S(1)} collective-permute-done((bf16[2,2,1024]{2,1,0:T(2,128)(2,1)S(1)}, bf16[2,2,1024]{2,1,0:T(2,128)(2,1)S(1)}, u32[]{:S(2)}, u32[]{:S(2)}) %collective-permute-start.7) | collective-permute-done | bytes 8224 | tf_op jit(solution)/shard_map/ppermute | solution.py:185
  19.6 0.0 collective-permute-start.8
  19.6 5.2 %collective-permute-done.5.q_ref.refs_2_ = bf16[64,1024]{1,0:T(8,128)(2,1)S(1)} collective-permute-done((bf16[64,1024]{1,0:T(8,128)(2,1)S(1)}, bf16[64,1024]{1,0:T(8,128)(2,1)S(1)}, u32[]{:S(2)}, u32[]{:S(2)}) %collective-permute-start.5) | collective-permute-done | bytes 131104 | tf_op jit(solution)/shard_map/ppermute | solution.py:190
  24.8 0.0 collective-permute-done.8.refs_3_.q_ref
  24.8 0.0 collective-permute-done.2.refs_1_.pair_ref.refs_3_
  24.8 0.6 %collective-permute-start.9 = (bf16[2,4,1024]{2,1,0:T(4,128)(2,1)S(1)}, bf16[2,4,1024]{2,1,0:T(4,128)(2,1)S(1)}, u32[]{:S(2)}, u32[]{:S(2)}) collective-permute-start(bf16[2,4,1024]{2,1,0:T(4,128)(2,1)S(1)} %after.9), channel_id=1, source_target_pairs={{0,16},{8,24},{16,0},{24,8},{1,17},{9,25},{17,1},{25,9},{2,18},{10... | collective-permute-start | bytes 49160 | tf_op jit(solution)/shard_map/ppermute | solution.py:185
  25.4 0.0 collective-permute-done.3.far_ref.refs_4_
  25.4 0.6 %edge_part.1.refs_1_ = bf16[64,1152]{1,0:T(8,128)(2,1)S(1)} custom-call(bf16[64,1024]{1,0:T(8,128)(2,1)S(1)} %collective-permute-done.5.q_ref.refs_2_, bf16[132,1024]{1,0:T(8,128)(2,1)S(1)} %get-tuple-element.12.own_ref.refs_0_, bf16[132,1024]{1,0:T(8,128)(2,1)S(1)} %after.7.pair_ref.refs_2_, bf16[132,1024]{1,0:T(8,128)(2,1)S(1)} %collective-permute-done.3.far_ref.refs_4_), custom_call_target="tpu_custom_call" | custom-call | flops 50331648 | bytes 1089536 | tf_op jit(solution)/shard_map/edge_part/pallas_call | solution.py:27
  26.0 0.2 collective-permute-start.10
  26.3 1.5 %collective-permute-done.4.refs_0_ = bf16[128,1024]{1,0:T(8,128)(2,1)S(1)} collective-permute-done((bf16[128,1024]{1,0:T(8,128)(2,1)S(1)}, bf16[128,1024]{1,0:T(8,128)(2,1)S(1)}, u32[]{:S(2)}, u32[]{:S(2)}) %collective-permute-start.4) | collective-permute-done | bytes 262176 | tf_op jit(solution)/shard_map/ppermute | solution.py:185
  27.8 0.0 copy-start
  27.8 0.6 %inner_part.1.refs_1_ = bf16[64,1152]{1,0:T(8,128)(2,1)S(1)} custom-call(bf16[64,1024]{1,0:T(8,128)(2,1)S(1)} %collective-permute-done.8.refs_3_.q_ref, bf16[128,1024]{1,0:T(8,128)(2,1)S(1)} %get-tuple-element.13.own_ref.refs_1_, bf16[128,1024]{1,0:T(8,128)(2,1)S(1)} %collective-permute-done.2.refs_1_.pair_ref.refs_3_, ...), custom_call_target="tpu_custom_call" | custom-call | flops 50331648 | bytes 1064960 | tf_op jit(solution)/shard_map/inner_part/pallas_call | solution.py:27
  28.4 0.1 collective-permute-start.11
  28.5 0.1 collective-permute-done.9
  28.6 0.1 fusion.6.refs_0_
  28.7 1.3 %own_part.1 = (f32[128,1024]{1,0:T(8,128)S(1)}, f32[128,128]{1,0:T(8,128)S(1)}) custom-call(bf16[132,1024]{1,0:T(8,128)(2,1)S(1)} %get-tuple-element.12.own_ref.refs_0_, bf16[128,1024]{1,0:T(8,128)(2,1)S(1)} %get-tuple-element.13.own_ref.refs_1_, bf16[132,1024]{1,0:T(8,128)(2,1)S(1)} %after.7.pair_ref.refs_2_, ...), custom_call_target="tpu_custom_call" | custom-call | flops 201326592 | bytes 2514944 | tf_op jit(solution)/shard_map/own_part/pallas_call | solution.py:27
  30.0 2.5 %collective-permute-done.10.refs_0_ = bf16[64,1152]{1,0:T(8,128)(2,1)S(1)} collective-permute-done((bf16[64,1152]{1,0:T(8,128)(2,1)S(1)}, bf16[64,1152]{1,0:T(8,128)(2,1)S(1)}, u32[]{:S(2)}, u32[]{:S(2)}) %collective-permute-start.10) | collective-permute-done | bytes 147488 | tf_op jit(solution)/shard_map/ppermute | solution.py:190
  32.5 0.0 collective-permute-done.11.inner_ref
  32.5 0.0 copy-done
  32.5 1.5 %merge.1 = bf16[8,16,1024]{2,1,0:T(8,128)(2,1)} custom-call(f32[128,1024]{1,0:T(8,128)S(1)} %get-tuple-element.17.refs_1_.own_ref, f32[128,128]{1,0:T(8,128)S(1)} %get-tuple-element.18.lse_ref, bf16[64,1152]{1,0:T(8,128)(2,1)S(1)} %after.11.edge_ref, bf16[64,1152]{1,0:T(8,128)(2,1)S(1)} %collective-permute-done.11.inner_ref, bf16[1024,1024]{1,0:T(8,128)(2,1)S(1)} %copy-done), custom_call_target="tpu_custom_call" | custom-call | flops 268435456 | bytes 3244032 | tf_op jit(solution)/shard_map/merge/pallas_call | solution.py:27
  (15 shorter events, 0.2 us)
Async XLA Ops:
  1.2 10.8 %collective-permute-start = (bf16[132,1024]{1,0:T(8,128)(2,1)S(1)}, bf16[132,1024]{1,0:T(8,128)(2,1)S(1)}, u32[]{:S(2)}, u32[]{:S(2)}) collective-permute-start(bf16[132,1024]{1,0:T(8,128)(2,1)S(1)} %get-tuple-element.12.own_ref.refs_0_), channel_id=1, source_target_pairs={{0,8},{8,0},{16,24},{24,16},{1,9},{9,1},{17,25},{25,17},{2,10},{10... | collective-permute-start | bytes 811016 | tf_op jit(solution)/shard_map/ppermute | solution.py:185
  4.2 7.8 %collective-permute-start.1 = (bf16[128,1024]{1,0:T(8,128)(2,1)S(1)}, bf16[128,1024]{1,0:T(8,128)(2,1)S(1)}, u32[]{:S(2)}, u32[]{:S(2)}) collective-permute-start(bf16[128,1024]{1,0:T(8,128)(2,1)S(1)} %get-tuple-element.13.own_ref.refs_1_), channel_id=1, source_target_pairs={{0,16},{8,24},{16,0},{24,8},{1,17},{9,25},{17,1},{25,9},{2,18},{10... | collective-permute-start | bytes 786440 | tf_op jit(solution)/shard_map/ppermute | solution.py:196
  12.1 3.7 %collective-permute-start.6 = (bf16[2,5,1024]{2,1,0:T(8,128)(2,1)S(1)}, bf16[2,5,1024]{2,1,0:T(8,128)(2,1)S(1)}, u32[]{:S(2)}, u32[]{:S(2)}) collective-permute-start(bf16[2,5,1024]{2,1,0:T(8,128)(2,1)S(1)} %pad_maximum_fusion), channel_id=1, source_target_pairs={{0,1},{1,0},{2,3},{3,2},{4,5},{5,4},{6,7},{7,6},{8,9},{9,8},{10,11... | collective-permute-start | bytes 61448 | tf_op jit(solution)/shard_map/ppermute | solution.py:185
  12.2 13.2 %collective-permute-start.3 = (bf16[132,1024]{1,0:T(8,128)(2,1)S(1)}, bf16[132,1024]{1,0:T(8,128)(2,1)S(1)}, u32[]{:S(2)}, u32[]{:S(2)}) collective-permute-start(bf16[132,1024]{1,0:T(8,128)(2,1)S(1)} %after.7.pair_ref.refs_2_), channel_id=1, source_target_pairs={{0,16},{8,24},{16,0},{24,8},{1,17},{9,25},{17,1},{25,9},{2,18},{10... | collective-permute-start | bytes 811016 | tf_op jit(solution)/shard_map/ppermute | solution.py:196
  13.8 11.1 %collective-permute-start.2 = (bf16[128,1024]{1,0:T(8,128)(2,1)S(1)}, bf16[128,1024]{1,0:T(8,128)(2,1)S(1)}, u32[]{:S(2)}, u32[]{:S(2)}) collective-permute-start(bf16[128,1024]{1,0:T(8,128)(2,1)S(1)} %get-tuple-element.13.own_ref.refs_1_), channel_id=1, source_target_pairs={{0,8},{8,0},{16,24},{24,16},{1,9},{9,1},{17,25},{25,17},{2,10},{10... | collective-permute-start | bytes 786440 | tf_op jit(solution)/shard_map/ppermute | solution.py:185
  14.4 13.4 %collective-permute-start.4 = (bf16[128,1024]{1,0:T(8,128)(2,1)S(1)}, bf16[128,1024]{1,0:T(8,128)(2,1)S(1)}, u32[]{:S(2)}, u32[]{:S(2)}) collective-permute-start(bf16[128,1024]{1,0:T(8,128)(2,1)S(1)} %collective-permute-done.1.refs_2_), channel_id=1, source_target_pairs={{0,8},{8,0},{16,24},{24,16},{1,9},{9,1},{17,25},{25,17},{2,10},{10... | collective-permute-start | bytes 786440 | tf_op jit(solution)/shard_map/ppermute | solution.py:185
  15.9 3.7 %collective-permute-start.7 = (bf16[2,2,1024]{2,1,0:T(2,128)(2,1)S(1)}, bf16[2,2,1024]{2,1,0:T(2,128)(2,1)S(1)}, u32[]{:S(2)}, u32[]{:S(2)}) collective-permute-start(bf16[2,2,1024]{2,1,0:T(2,128)(2,1)S(1)} %pad_maximum_fusion.2), channel_id=1, source_target_pairs={{0,2},{1,3},{2,0},{3,1},{4,6},{5,7},{6,4},{7,5},{8,10},{9,11},{10,... | collective-permute-start | bytes 24584 | tf_op jit(solution)/shard_map/ppermute | solution.py:185
  17.5 7.3 %collective-permute-start.5 = (bf16[64,1024]{1,0:T(8,128)(2,1)S(1)}, bf16[64,1024]{1,0:T(8,128)(2,1)S(1)}, u32[]{:S(2)}, u32[]{:S(2)}) collective-permute-start(bf16[64,1024]{1,0:T(8,128)(2,1)S(1)} %get-tuple-element.15.refs_7_), channel_id=1, source_target_pairs={{0,7},{1,2},{2,1},{3,4},{4,3},{5,6},{6,5},{7,0},{8,15},{9,10},{10,... | collective-permute-start | bytes 393224 | tf_op jit(solution)/shard_map/ppermute | solution.py:190
  19.6 5.3 %collective-permute-start.8 = (bf16[64,1024]{1,0:T(8,128)(2,1)S(1)}, bf16[64,1024]{1,0:T(8,128)(2,1)S(1)}, u32[]{:S(2)}, u32[]{:S(2)}) collective-permute-start(bf16[64,1024]{1,0:T(8,128)(2,1)S(1)} %get-tuple-element.16.refs_6_), channel_id=1, source_target_pairs={{0,1},{1,0},{2,3},{3,2},{4,5},{5,4},{6,7},{7,6},{8,9},{9,8},{10,11... | collective-permute-start | bytes 393224 | tf_op jit(solution)/shard_map/ppermute | solution.py:185
  24.8 3.8 %collective-permute-start.9 = (bf16[2,4,1024]{2,1,0:T(4,128)(2,1)S(1)}, bf16[2,4,1024]{2,1,0:T(4,128)(2,1)S(1)}, u32[]{:S(2)}, u32[]{:S(2)}) collective-permute-start(bf16[2,4,1024]{2,1,0:T(4,128)(2,1)S(1)} %after.9), channel_id=1, source_target_pairs={{0,16},{8,24},{16,0},{24,8},{1,17},{9,25},{17,1},{25,9},{2,18},{10... | collective-permute-start | bytes 49160 | tf_op jit(solution)/shard_map/ppermute | solution.py:185
  26.0 6.4 %collective-permute-start.10 = (bf16[64,1152]{1,0:T(8,128)(2,1)S(1)}, bf16[64,1152]{1,0:T(8,128)(2,1)S(1)}, u32[]{:S(2)}, u32[]{:S(2)}) collective-permute-start(bf16[64,1152]{1,0:T(8,128)(2,1)S(1)} %edge_part.1.refs_1_), channel_id=1, source_target_pairs={{0,7},{1,2},{2,1},{3,4},{4,3},{5,6},{6,5},{7,0},{8,15},{9,10},{10,... | collective-permute-start | bytes 442376 | tf_op jit(solution)/shard_map/ppermute | solution.py:190
  27.8 4.7 %copy-start = (bf16[1024,1024]{1,0:T(8,128)(2,1)S(1)}, bf16[1024,1024]{1,0:T(8,128)(2,1)}, u32[]{:S(2)}) copy-start(bf16[1024,1024]{1,0:T(8,128)(2,1)} %weight_ref.1) | copy-start | bytes 6291460
  28.4 4.1 %collective-permute-start.11 = (bf16[64,1152]{1,0:T(8,128)(2,1)S(1)}, bf16[64,1152]{1,0:T(8,128)(2,1)S(1)}, u32[]{:S(2)}, u32[]{:S(2)}) collective-permute-start(bf16[64,1152]{1,0:T(8,128)(2,1)S(1)} %inner_part.1.refs_1_), channel_id=1, source_target_pairs={{0,1},{1,0},{2,3},{3,2},{4,5},{5,4},{6,7},{7,6},{8,9},{9,8},{10,11... | collective-permute-start | bytes 442376 | tf_op jit(solution)/shard_map/ppermute | solution.py:185

commit v13 on v11

--- a/solution.py
+++ b/solution.py
@@ -155,7 +155,7 @@
     lse_ref[...] = stats
 
 
-def merge_kernel(own_ref, lse_ref, edge_ref, inner_ref, weight_ref, out_ref):
+def merge_kernel(own_ref, lse_ref, edge_ref, inner_ref, weight_ref, out_ref, held_ref, sems):
     width = HEADS * HEAD_DIM
     odd = odd_column()
     merged = []
@@ -176,8 +176,17 @@
     left = jnp.where(odd, inner, edge)
     right = jnp.where(odd, edge, inner)
     attended = jnp.stack([left, right], axis=1).reshape(2 * SPAN, width).astype(BF16)
-    mixed = jnp.dot(attended, weight_ref[...], preferred_element_type=F32)
-    out_ref[...] = mixed.reshape(TILE, 2 * TILE, width).astype(BF16)
+    copies = []
+    for part in range(4):
+        cols = slice(part * width // 4, (part + 1) * width // 4)
+        mixed = jnp.dot(attended, weight_ref[:, cols], preferred_element_type=F32)
+        held_ref[:, :, cols] = mixed.reshape(TILE, 2 * TILE, width // 4).astype(BF16)
+        copies.append(
+            pltpu.make_async_copy(held_ref.at[:, :, cols], out_ref.at[:, :, cols], sems.at[part])
+        )
+        copies[-1].start()
+    for copy in copies:
+        copy.wait()
 
 
 def swap(x, axis, distance):
@@ -311,17 +320,18 @@
         coarse,
     )
     edge_back = after(edge_back, own, weight=WEIGHT)
-    return call(
+    return pl.pallas_call(
         merge_kernel,
-        [jax.ShapeDtypeStruct(queries.shape, BF16)],
-        "merge",
-        4 * SPAN * width * width,
-        own,
-        lse,
-        edge_back,
-        inner_back,
-        out_weight,
-    )[0]
+        out_shape=jax.ShapeDtypeStruct(queries.shape, BF16),
+        in_specs=[VMEM] * 5,
+        out_specs=pl.BlockSpec(memory_space=pl.ANY),
+        scratch_shapes=[pltpu.VMEM(queries.shape, BF16), pltpu.SemaphoreType.DMA((4,))],
+        name="merge",
+        compiler_params=pltpu.CompilerParams(vmem_limit_bytes=LIMIT),
+        cost_estimate=pl.CostEstimate(
+            flops=4 * SPAN * width * width, bytes_accessed=3 << 20, transcendentals=0
+        ),
+    )(own, lse, edge_back, inner_back, out_weight)
 
 
 def solution(mesh):

time: 30.7 us -> 30.7 us (level)
    pallas_call x4 -> x3, Pallas kernels: 4.04 us -> 2.51 us  [call(): pl.pallas_call(kernel, out_shape=outs, in_specs=[VMEM] * len(args), out_s...]
    pallas_call x0 -> x1, Pallas kernels: none -> 1.5 us  [shards(): pl.pallas_call(merge_kernel, out_shape=jax.ShapeDtypeStruct(queries.shape...]
where the time goes in v13:
time: 30.7 us; the launch traced here: 30.5 us
  starting transfers between devices  14.9 us (49%)
  waiting for transfers between devices  10 us (33%)
  Pallas kernels  5.25 us (17%)
    ppermute x2, waiting for transfers between devices, outward(): lax.ppermute(x, axis, [(i, (i + (1 if i % 2 else -1)) % count) for i in r...  7.93 us
    ppermute x8, starting transfers between devices, swap(): return lax.ppermute(x, axis, [(i, i ^ distance) for i in range(count)])  7.9 us
    ppermute x2, starting transfers between devices, outward(): lax.ppermute(x, axis, [(i, (i + (1 if i % 2 else -1)) % count) for i in r...  4.68 us
    pallas_call x3, Pallas kernels, call(): pl.pallas_call(kernel, out_shape=outs, in_specs=[VMEM] * len(args), out_s...  2.51 us
    ppermute x2, starting transfers between devices, stride(): return lax.ppermute(x, axis, route)  2.29 us
    ppermute x8, waiting for transfers between devices, swap(): return lax.ppermute(x, axis, [(i, i ^ distance) for i in range(count)])  2.09 us
    pallas_call x1, Pallas kernels, shards(): pl.pallas_call(merge_kernel, out_shape=jax.ShapeDtypeStruct(queries.shape...  1.5 us
    pallas_call x1, Pallas kernels, shards(): pl.pallas_call(split_kernel, out_shape=[like(SPAN, width), like(SPAN, wid...  1.23 us
  transfers between devices with their start and end apart: 12, of which 3 were waited for; matrix products, arithmetic and copies ran while one was open for 1% of the time, Pallas kernels for 8%

profile of v13, /device:TPU:0, one launch (start us, length us, event | category | flops | bytes accessed | tf_op | source)
XLA Modules:
  0.0 30.5 jit_solution(18405701799889388220)
XLA Ops:
  0.0 1.2 %split.1 = (bf16[64,1024]{1,0:T(8,128)(2,1)S(1)}, bf16[64,1024]{1,0:T(8,128)(2,1)S(1)}, bf16[132,1024]{1,0:T(8,128)(2,1)S(1)}, bf16[128,1024]{1,0:T(8,128)(2,1)S(1)}, bf16[4,1024]{1,0:T(4,128)(2,1)S(1)}) custom-call(bf16[8,16,1024]{2,1,0:T(8,128)(2,1)} %q_hbm.1, bf16[2,8,16,1024]{3,2,1,0:T(8,128)(2,1)} %kv_hbm.1), custom_call_target="tpu_custom_call" | custom-call | bytes 2097152 | tf_op jit(solution)/shard_map/split/pallas_call | solution.py:237
  1.2 3.0 %collective-permute-start = (bf16[132,1024]{1,0:T(8,128)(2,1)S(1)}, bf16[132,1024]{1,0:T(8,128)(2,1)S(1)}, u32[]{:S(2)}, u32[]{:S(2)}) collective-permute-start(bf16[132,1024]{1,0:T(8,128)(2,1)S(1)} %get-tuple-element.12.own_ref.refs_0_), channel_id=1, source_target_pairs={{0,8},{8,0},{16,24},{24,16},{1,9},{9,1},{17,25},{25,17},{2,10},{10... | collective-permute-start | bytes 811016 | tf_op jit(solution)/shard_map/ppermute | solution.py:194
  4.2 1.5 %collective-permute-start.2 = (bf16[128,1024]{1,0:T(8,128)(2,1)S(1)}, bf16[128,1024]{1,0:T(8,128)(2,1)S(1)}, u32[]{:S(2)}, u32[]{:S(2)}) collective-permute-start(bf16[128,1024]{1,0:T(8,128)(2,1)S(1)} %get-tuple-element.13.own_ref.refs_1_), channel_id=1, source_target_pairs={{0,16},{8,24},{16,0},{24,8},{1,17},{9,25},{17,1},{25,9},{2,18},{10... | collective-permute-start | bytes 786440 | tf_op jit(solution)/shard_map/ppermute | solution.py:205
  5.8 2.5 %collective-permute-start.1 = (bf16[64,1024]{1,0:T(8,128)(2,1)S(1)}, bf16[64,1024]{1,0:T(8,128)(2,1)S(1)}, u32[]{:S(2)}, u32[]{:S(2)}) collective-permute-start(bf16[64,1024]{1,0:T(8,128)(2,1)S(1)} %get-tuple-element.15.refs_7_), channel_id=1, source_target_pairs={{0,7},{1,2},{2,1},{3,4},{4,3},{5,6},{6,5},{7,0},{8,15},{9,10},{10,... | collective-permute-start | bytes 393224 | tf_op jit(solution)/shard_map/ppermute | solution.py:199
  8.2 0.5 %collective-permute-start.3 = (bf16[128,1024]{1,0:T(8,128)(2,1)S(1)}, bf16[128,1024]{1,0:T(8,128)(2,1)S(1)}, u32[]{:S(2)}, u32[]{:S(2)}) collective-permute-start(bf16[128,1024]{1,0:T(8,128)(2,1)S(1)} %get-tuple-element.13.own_ref.refs_1_), channel_id=1, source_target_pairs={{0,8},{8,0},{16,24},{24,16},{1,9},{9,1},{17,25},{25,17},{2,10},{10... | collective-permute-start | bytes 786440 | tf_op jit(solution)/shard_map/ppermute | solution.py:194
  8.8 4.3 %collective-permute-done.1.refs_2_.q_ref = bf16[64,1024]{1,0:T(8,128)(2,1)S(1)} collective-permute-done((bf16[64,1024]{1,0:T(8,128)(2,1)S(1)}, bf16[64,1024]{1,0:T(8,128)(2,1)S(1)}, u32[]{:S(2)}, u32[]{:S(2)}) %collective-permute-start.1) | collective-permute-done | bytes 131104 | tf_op jit(solution)/shard_map/ppermute | solution.py:199
  13.1 0.0 collective-permute-done.2.refs_3_
  13.1 0.0 collective-permute-done.refs_0_
  13.1 0.8 %collective-permute-start.4 = (bf16[132,1024]{1,0:T(8,128)(2,1)S(1)}, bf16[132,1024]{1,0:T(8,128)(2,1)S(1)}, u32[]{:S(2)}, u32[]{:S(2)}) collective-permute-start(bf16[132,1024]{1,0:T(8,128)(2,1)S(1)} %after.7.pair_ref.refs_2_), channel_id=1, source_target_pairs={{0,16},{8,24},{16,0},{24,8},{1,17},{9,25},{17,1},{25,9},{2,18},{10... | collective-permute-start | bytes 811016 | tf_op jit(solution)/shard_map/ppermute | solution.py:205
  14.0 0.1 collective-permute-start.6
  14.0 1.6 %collective-permute-start.5 = (bf16[128,1024]{1,0:T(8,128)(2,1)S(1)}, bf16[128,1024]{1,0:T(8,128)(2,1)S(1)}, u32[]{:S(2)}, u32[]{:S(2)}) collective-permute-start(bf16[128,1024]{1,0:T(8,128)(2,1)S(1)} %collective-permute-done.2.refs_3_), channel_id=1, source_target_pairs={{0,8},{8,0},{16,24},{24,16},{1,9},{9,1},{17,25},{25,17},{2,10},{10... | collective-permute-start | bytes 786440 | tf_op jit(solution)/shard_map/ppermute | solution.py:194
  15.6 0.2 collective-permute-start.8
  15.8 0.0 collective-permute-done.6
  15.8 1.6 %collective-permute-start.7 = (bf16[2,2,1024]{2,1,0:T(2,128)(2,1)S(1)}, bf16[2,2,1024]{2,1,0:T(2,128)(2,1)S(1)}, u32[]{:S(2)}, u32[]{:S(2)}) collective-permute-start(bf16[2,2,1024]{2,1,0:T(2,128)(2,1)S(1)} %pad_maximum_fusion.2), channel_id=1, source_target_pairs={{0,2},{1,3},{2,0},{3,1},{4,6},{5,7},{6,4},{7,5},{8,10},{9,11},{10,... | collective-permute-start | bytes 24584 | tf_op jit(solution)/shard_map/ppermute | solution.py:194
  17.5 2.1 %collective-permute-done.7 = bf16[2,2,1024]{2,1,0:T(2,128)(2,1)S(1)} collective-permute-done((bf16[2,2,1024]{2,1,0:T(2,128)(2,1)S(1)}, bf16[2,2,1024]{2,1,0:T(2,128)(2,1)S(1)}, u32[]{:S(2)}, u32[]{:S(2)}) %collective-permute-start.7) | collective-permute-done | bytes 8224 | tf_op jit(solution)/shard_map/ppermute | solution.py:194
  19.6 0.0 collective-permute-done.8.refs_2_.q_ref
  19.6 0.0 collective-permute-done.3.refs_1_.pair_ref.refs_3_
  19.6 0.9 %collective-permute-start.9 = (bf16[2,4,1024]{2,1,0:T(4,128)(2,1)S(1)}, bf16[2,4,1024]{2,1,0:T(4,128)(2,1)S(1)}, u32[]{:S(2)}, u32[]{:S(2)}) collective-permute-start(bf16[2,4,1024]{2,1,0:T(4,128)(2,1)S(1)} %after.9), channel_id=1, source_target_pairs={{0,16},{8,24},{16,0},{24,8},{1,17},{9,25},{17,1},{25,9},{2,18},{10... | collective-permute-start | bytes 49160 | tf_op jit(solution)/shard_map/ppermute | solution.py:194
  20.5 0.0 collective-permute-done.4.far_ref.refs_4_
  20.5 0.6 %edge_part.1.refs_1_ = bf16[64,1152]{1,0:T(8,128)(2,1)S(1)} custom-call(bf16[64,1024]{1,0:T(8,128)(2,1)S(1)} %collective-permute-done.1.refs_2_.q_ref, bf16[132,1024]{1,0:T(8,128)(2,1)S(1)} %get-tuple-element.12.own_ref.refs_0_, bf16[132,1024]{1,0:T(8,128)(2,1)S(1)} %after.7.pair_ref.refs_2_, bf16[132,1024]{1,0:T(8,128)(2,1)S(1)} %collective-permute-done.4.far_ref.refs_4_), custom_call_target="tpu_custom_call" | custom-call | flops 50331648 | bytes 1089536 | tf_op jit(solution)/shard_map/edge_part/pallas_call | solution.py:27
  21.1 2.2 %collective-permute-start.10 = (bf16[64,1152]{1,0:T(8,128)(2,1)S(1)}, bf16[64,1152]{1,0:T(8,128)(2,1)S(1)}, u32[]{:S(2)}, u32[]{:S(2)}) collective-permute-start(bf16[64,1152]{1,0:T(8,128)(2,1)S(1)} %edge_part.1.refs_1_), channel_id=1, source_target_pairs={{0,7},{1,2},{2,1},{3,4},{4,3},{5,6},{6,5},{7,0},{8,15},{9,10},{10,... | collective-permute-start | bytes 442376 | tf_op jit(solution)/shard_map/ppermute | solution.py:199
  23.3 0.0 collective-permute-done.5.refs_0_
  23.3 0.0 copy-start
  23.3 0.6 %inner_part.1.refs_1_ = bf16[64,1152]{1,0:T(8,128)(2,1)S(1)} custom-call(bf16[64,1024]{1,0:T(8,128)(2,1)S(1)} %collective-permute-done.8.refs_2_.q_ref, bf16[128,1024]{1,0:T(8,128)(2,1)S(1)} %get-tuple-element.13.own_ref.refs_1_, bf16[128,1024]{1,0:T(8,128)(2,1)S(1)} %collective-permute-done.3.refs_1_.pair_ref.refs_3_, ...), custom_call_target="tpu_custom_call" | custom-call | flops 50331648 | bytes 1064960 | tf_op jit(solution)/shard_map/inner_part/pallas_call | solution.py:27
  24.0 0.1 collective-permute-start.11
  24.1 0.0 collective-permute-done.9
  24.1 0.1 fusion.6.refs_0_
  24.1 1.3 %own_part.1 = (f32[128,1024]{1,0:T(8,128)S(1)}, f32[128,128]{1,0:T(8,128)S(1)}) custom-call(bf16[132,1024]{1,0:T(8,128)(2,1)S(1)} %get-tuple-element.12.own_ref.refs_0_, bf16[128,1024]{1,0:T(8,128)(2,1)S(1)} %get-tuple-element.13.own_ref.refs_1_, bf16[132,1024]{1,0:T(8,128)(2,1)S(1)} %after.7.pair_ref.refs_2_, ...), custom_call_target="tpu_custom_call" | custom-call | flops 201326592 | bytes 2514944 | tf_op jit(solution)/shard_map/own_part/pallas_call | solution.py:27
  25.4 3.6 %collective-permute-done.10.refs_0_ = bf16[64,1152]{1,0:T(8,128)(2,1)S(1)} collective-permute-done((bf16[64,1152]{1,0:T(8,128)(2,1)S(1)}, bf16[64,1152]{1,0:T(8,128)(2,1)S(1)}, u32[]{:S(2)}, u32[]{:S(2)}) %collective-permute-start.10) | collective-permute-done | bytes 147488 | tf_op jit(solution)/shard_map/ppermute | solution.py:199
  29.0 0.0 collective-permute-done.11.inner_ref
  29.0 0.0 copy-done
  29.0 1.5 %merge.1 = bf16[8,16,1024]{2,1,0:T(8,128)(2,1)} custom-call(f32[128,1024]{1,0:T(8,128)S(1)} %get-tuple-element.17.refs_1_.own_ref, f32[128,128]{1,0:T(8,128)S(1)} %get-tuple-element.18.lse_ref, bf16[64,1152]{1,0:T(8,128)(2,1)S(1)} %after.11.edge_ref, bf16[64,1152]{1,0:T(8,128)(2,1)S(1)} %collective-permute-done.11.inner_ref, bf16[1024,1024]{1,0:T(8,128)(2,1)S(1)} %copy-done), custom_call_target="tpu_custom_call" | custom-call | flops 268435456 | bytes 3145728 | tf_op jit(solution)/shard_map/merge/pallas_call | solution.py:323
  (15 shorter events, 0.2 us)
Async XLA Ops:
  1.2 11.9 %collective-permute-start = (bf16[132,1024]{1,0:T(8,128)(2,1)S(1)}, bf16[132,1024]{1,0:T(8,128)(2,1)S(1)}, u32[]{:S(2)}, u32[]{:S(2)}) collective-permute-start(bf16[132,1024]{1,0:T(8,128)(2,1)S(1)} %get-tuple-element.12.own_ref.refs_0_), channel_id=1, source_target_pairs={{0,8},{8,0},{16,24},{24,16},{1,9},{9,1},{17,25},{25,17},{2,10},{10... | collective-permute-start | bytes 811016 | tf_op jit(solution)/shard_map/ppermute | solution.py:194
  4.2 8.9 %collective-permute-start.2 = (bf16[128,1024]{1,0:T(8,128)(2,1)S(1)}, bf16[128,1024]{1,0:T(8,128)(2,1)S(1)}, u32[]{:S(2)}, u32[]{:S(2)}) collective-permute-start(bf16[128,1024]{1,0:T(8,128)(2,1)S(1)} %get-tuple-element.13.own_ref.refs_1_), channel_id=1, source_target_pairs={{0,16},{8,24},{16,0},{24,8},{1,17},{9,25},{17,1},{25,9},{2,18},{10... | collective-permute-start | bytes 786440 | tf_op jit(solution)/shard_map/ppermute | solution.py:205
  5.8 7.3 %collective-permute-start.1 = (bf16[64,1024]{1,0:T(8,128)(2,1)S(1)}, bf16[64,1024]{1,0:T(8,128)(2,1)S(1)}, u32[]{:S(2)}, u32[]{:S(2)}) collective-permute-start(bf16[64,1024]{1,0:T(8,128)(2,1)S(1)} %get-tuple-element.15.refs_7_), channel_id=1, source_target_pairs={{0,7},{1,2},{2,1},{3,4},{4,3},{5,6},{6,5},{7,0},{8,15},{9,10},{10,... | collective-permute-start | bytes 393224 | tf_op jit(solution)/shard_map/ppermute | solution.py:199
  8.2 11.3 %collective-permute-start.3 = (bf16[128,1024]{1,0:T(8,128)(2,1)S(1)}, bf16[128,1024]{1,0:T(8,128)(2,1)S(1)}, u32[]{:S(2)}, u32[]{:S(2)}) collective-permute-start(bf16[128,1024]{1,0:T(8,128)(2,1)S(1)} %get-tuple-element.13.own_ref.refs_1_), channel_id=1, source_target_pairs={{0,8},{8,0},{16,24},{24,16},{1,9},{9,1},{17,25},{25,17},{2,10},{10... | collective-permute-start | bytes 786440 | tf_op jit(solution)/shard_map/ppermute | solution.py:194
  13.1 7.4 %collective-permute-start.4 = (bf16[132,1024]{1,0:T(8,128)(2,1)S(1)}, bf16[132,1024]{1,0:T(8,128)(2,1)S(1)}, u32[]{:S(2)}, u32[]{:S(2)}) collective-permute-start(bf16[132,1024]{1,0:T(8,128)(2,1)S(1)} %after.7.pair_ref.refs_2_), channel_id=1, source_target_pairs={{0,16},{8,24},{16,0},{24,8},{1,17},{9,25},{17,1},{25,9},{2,18},{10... | collective-permute-start | bytes 811016 | tf_op jit(solution)/shard_map/ppermute | solution.py:205
  14.0 1.8 %collective-permute-start.6 = (bf16[2,5,1024]{2,1,0:T(8,128)(2,1)S(1)}, bf16[2,5,1024]{2,1,0:T(8,128)(2,1)S(1)}, u32[]{:S(2)}, u32[]{:S(2)}) collective-permute-start(bf16[2,5,1024]{2,1,0:T(8,128)(2,1)S(1)} %pad_maximum_fusion), channel_id=1, source_target_pairs={{0,1},{1,0},{2,3},{3,2},{4,5},{5,4},{6,7},{7,6},{8,9},{9,8},{10,11... | collective-permute-start | bytes 61448 | tf_op jit(solution)/shard_map/ppermute | solution.py:194
  14.0 9.3 %collective-permute-start.5 = (bf16[128,1024]{1,0:T(8,128)(2,1)S(1)}, bf16[128,1024]{1,0:T(8,128)(2,1)S(1)}, u32[]{:S(2)}, u32[]{:S(2)}) collective-permute-start(bf16[128,1024]{1,0:T(8,128)(2,1)S(1)} %collective-permute-done.2.refs_3_), channel_id=1, source_target_pairs={{0,8},{8,0},{16,24},{24,16},{1,9},{9,1},{17,25},{25,17},{2,10},{10... | collective-permute-start | bytes 786440 | tf_op jit(solution)/shard_map/ppermute | solution.py:194
  15.6 4.0 %collective-permute-start.8 = (bf16[64,1024]{1,0:T(8,128)(2,1)S(1)}, bf16[64,1024]{1,0:T(8,128)(2,1)S(1)}, u32[]{:S(2)}, u32[]{:S(2)}) collective-permute-start(bf16[64,1024]{1,0:T(8,128)(2,1)S(1)} %get-tuple-element.16.refs_6_), channel_id=1, source_target_pairs={{0,1},{1,0},{2,3},{3,2},{4,5},{5,4},{6,7},{7,6},{8,9},{9,8},{10,11... | collective-permute-start | bytes 393224 | tf_op jit(solution)/shard_map/ppermute | solution.py:194
  15.8 3.7 %collective-permute-start.7 = (bf16[2,2,1024]{2,1,0:T(2,128)(2,1)S(1)}, bf16[2,2,1024]{2,1,0:T(2,128)(2,1)S(1)}, u32[]{:S(2)}, u32[]{:S(2)}) collective-permute-start(bf16[2,2,1024]{2,1,0:T(2,128)(2,1)S(1)} %pad_maximum_fusion.2), channel_id=1, source_target_pairs={{0,2},{1,3},{2,0},{3,1},{4,6},{5,7},{6,4},{7,5},{8,10},{9,11},{10,... | collective-permute-start | bytes 24584 | tf_op jit(solution)/shard_map/ppermute | solution.py:194
  19.6 4.5 %collective-permute-start.9 = (bf16[2,4,1024]{2,1,0:T(4,128)(2,1)S(1)}, bf16[2,4,1024]{2,1,0:T(4,128)(2,1)S(1)}, u32[]{:S(2)}, u32[]{:S(2)}) collective-permute-start(bf16[2,4,1024]{2,1,0:T(4,128)(2,1)S(1)} %after.9), channel_id=1, source_target_pairs={{0,16},{8,24},{16,0},{24,8},{1,17},{9,25},{17,1},{25,9},{2,18},{10... | collective-permute-start | bytes 49160 | tf_op jit(solution)/shard_map/ppermute | solution.py:194
  21.1 7.9 %collective-permute-start.10 = (bf16[64,1152]{1,0:T(8,128)(2,1)S(1)}, bf16[64,1152]{1,0:T(8,128)(2,1)S(1)}, u32[]{:S(2)}, u32[]{:S(2)}) collective-permute-start(bf16[64,1152]{1,0:T(8,128)(2,1)S(1)} %edge_part.1.refs_1_), channel_id=1, source_target_pairs={{0,7},{1,2},{2,1},{3,4},{4,3},{5,6},{6,5},{7,0},{8,15},{9,10},{10,... | collective-permute-start | bytes 442376 | tf_op jit(solution)/shard_map/ppermute | solution.py:199
  23.3 5.7 %copy-start = (bf16[1024,1024]{1,0:T(8,128)(2,1)S(1)}, bf16[1024,1024]{1,0:T(8,128)(2,1)}, u32[]{:S(2)}) copy-start(bf16[1024,1024]{1,0:T(8,128)(2,1)} %weight_ref.1) | copy-start | bytes 6291460
  24.0 5.1 %collective-permute-start.11 = (bf16[64,1152]{1,0:T(8,128)(2,1)S(1)}, bf16[64,1152]{1,0:T(8,128)(2,1)S(1)}, u32[]{:S(2)}, u32[]{:S(2)}) collective-permute-start(bf16[64,1152]{1,0:T(8,128)(2,1)S(1)} %inner_part.1.refs_1_), channel_id=1, source_target_pairs={{0,1},{1,0},{2,3},{3,2},{4,5},{5,4},{6,7},{7,6},{8,9},{9,8},{10,11... | collective-permute-start | bytes 442376 | tf_op jit(solution)/shard_map/ppermute | solution.py:194

commit v14 on v11

--- a/solution.py
+++ b/solution.py
@@ -261,10 +261,8 @@
     group = jnp.concatenate([mine, beside[:, 4:5]], axis=1)
     group_lon = swap(group, "lon", 2)
     group_both = jnp.concatenate([group, group_lon], axis=1)
-    group_lat = swap(after(group_both, inner_pair, far_q_inner), "lat", 2)
-    coarse = jnp.concatenate([level0_lat, beside[:, 0:4], group_lon, group_lat], axis=1)
-    count = coarse.shape[1] // 2
-    coarse = jnp.pad(coarse, ((0, 0), (0, 16 - 2 * count), (0, 0)))
+    group_both = after(group_both, inner_pair, far_q_inner)
+    edge_far = after(edge_far, group_both)
 
     back = jax.ShapeDtypeStruct((SPAN, width + HEAD_DIM), BF16)
     flops = 4 * SPAN * 3 * SPAN * width
@@ -279,6 +277,10 @@
         edge_far,
     )[0]
     edge_back = outward(edge_part, "lon")
+    group_lat = swap(after(group_both, edge_part), "lat", 2)
+    coarse = jnp.concatenate([level0_lat, beside[:, 0:4], group_lon, group_lat], axis=1)
+    count = coarse.shape[1] // 2
+    coarse = jnp.pad(coarse, ((0, 0), (0, 16 - 2 * count), (0, 0)))
     inner_far = after(inner_far, edge_part)
     inner_part = call(
         functools.partial(partial_kernel, n_lat),
@@ -310,7 +312,7 @@
         q_edge,
         coarse,
     )
-    edge_back = after(edge_back, own, weight=WEIGHT)
+    edge_back = after(edge_back, own, weight=4 * WEIGHT)
     return call(
         merge_kernel,
         [jax.ShapeDtypeStruct(queries.shape, BF16)],

time: 30.7 us -> 30.9 us (level)
  waiting for transfers between devices: 10 us -> 10.4 us
    ppermute x2, starting transfers between devices: 4.68 us -> 4.22 us  [outward(): lax.ppermute(x, axis, [(i, (i + (1 if i % 2 else -1)) % count) for i in r...]
  transfers between devices with their start and end apart: 12 -> 12, of which waited for: 3 -> 5; matrix products, arithmetic and copies ran while one was open for 1% -> 1% of each run, Pallas kernels for 8% -> 8%
where the time goes in v14:
time: 30.9 us; the launch traced here: 30.7 us
  starting transfers between devices  14.7 us (48%)
  waiting for transfers between devices  10.4 us (34%)
  Pallas kernels  5.27 us (17%)
    ppermute x8, starting transfers between devices, swap(): return lax.ppermute(x, axis, [(i, i ^ distance) for i in range(count)])  8.2 us
    ppermute x2, waiting for transfers between devices, outward(): lax.ppermute(x, axis, [(i, (i + (1 if i % 2 else -1)) % count) for i in r...  8 us
    ppermute x2, starting transfers between devices, outward(): lax.ppermute(x, axis, [(i, (i + (1 if i % 2 else -1)) % count) for i in r...  4.22 us
    pallas_call x4, Pallas kernels, call(): pl.pallas_call(kernel, out_shape=outs, in_specs=[VMEM] * len(args), out_s...  4.03 us
    ppermute x2, starting transfers between devices, stride(): return lax.ppermute(x, axis, route)  2.29 us
    ppermute x8, waiting for transfers between devices, swap(): return lax.ppermute(x, axis, [(i, i ^ distance) for i in range(count)])  2.26 us
    pallas_call x1, Pallas kernels, shards(): pl.pallas_call(split_kernel, out_shape=[like(SPAN, width), like(SPAN, wid...  1.23 us
  transfers between devices with their start and end apart: 12, of which 5 were waited for; matrix products, arithmetic and copies ran while one was open for 1% of the time, Pallas kernels for 8%

profile of v14, /device:TPU:0, one launch (start us, length us, event | category | flops | bytes accessed | tf_op | source)
XLA Modules:
  0.0 30.7 jit_solution(9980443290796646018)
XLA Ops:
  0.0 1.2 %split.1 = (bf16[64,1024]{1,0:T(8,128)(2,1)S(1)}, bf16[64,1024]{1,0:T(8,128)(2,1)S(1)}, bf16[132,1024]{1,0:T(8,128)(2,1)S(1)}, bf16[128,1024]{1,0:T(8,128)(2,1)S(1)}, bf16[4,1024]{1,0:T(4,128)(2,1)S(1)}) custom-call(bf16[8,16,1024]{2,1,0:T(8,128)(2,1)} %q_hbm.1, bf16[2,8,16,1024]{3,2,1,0:T(8,128)(2,1)} %kv_hbm.1), custom_call_target="tpu_custom_call" | custom-call | bytes 2097152 | tf_op jit(solution)/shard_map/split/pallas_call | solution.py:228
  1.2 3.0 %collective-permute-start = (bf16[132,1024]{1,0:T(8,128)(2,1)S(1)}, bf16[132,1024]{1,0:T(8,128)(2,1)S(1)}, u32[]{:S(2)}, u32[]{:S(2)}) collective-permute-start(bf16[132,1024]{1,0:T(8,128)(2,1)S(1)} %get-tuple-element.12.own_ref.refs_0_), channel_id=1, source_target_pairs={{0,8},{8,0},{16,24},{24,16},{1,9},{9,1},{17,25},{25,17},{2,10},{10... | collective-permute-start | bytes 811016 | tf_op jit(solution)/shard_map/ppermute | solution.py:185
  4.2 1.5 %collective-permute-start.2 = (bf16[128,1024]{1,0:T(8,128)(2,1)S(1)}, bf16[128,1024]{1,0:T(8,128)(2,1)S(1)}, u32[]{:S(2)}, u32[]{:S(2)}) collective-permute-start(bf16[128,1024]{1,0:T(8,128)(2,1)S(1)} %get-tuple-element.13.own_ref.refs_1_), channel_id=1, source_target_pairs={{0,16},{8,24},{16,0},{24,8},{1,17},{9,25},{17,1},{25,9},{2,18},{10... | collective-permute-start | bytes 786440 | tf_op jit(solution)/shard_map/ppermute | solution.py:196
  5.8 2.5 %collective-permute-start.1 = (bf16[64,1024]{1,0:T(8,128)(2,1)S(1)}, bf16[64,1024]{1,0:T(8,128)(2,1)S(1)}, u32[]{:S(2)}, u32[]{:S(2)}) collective-permute-start(bf16[64,1024]{1,0:T(8,128)(2,1)S(1)} %get-tuple-element.15.refs_7_), channel_id=1, source_target_pairs={{0,7},{1,2},{2,1},{3,4},{4,3},{5,6},{6,5},{7,0},{8,15},{9,10},{10,... | collective-permute-start | bytes 393224 | tf_op jit(solution)/shard_map/ppermute | solution.py:190
  8.2 0.5 %collective-permute-start.3 = (bf16[128,1024]{1,0:T(8,128)(2,1)S(1)}, bf16[128,1024]{1,0:T(8,128)(2,1)S(1)}, u32[]{:S(2)}, u32[]{:S(2)}) collective-permute-start(bf16[128,1024]{1,0:T(8,128)(2,1)S(1)} %get-tuple-element.13.own_ref.refs_1_), channel_id=1, source_target_pairs={{0,8},{8,0},{16,24},{24,16},{1,9},{9,1},{17,25},{25,17},{2,10},{10... | collective-permute-start | bytes 786440 | tf_op jit(solution)/shard_map/ppermute | solution.py:185
  8.8 4.3 %collective-permute-done.1.refs_2_.q_ref = bf16[64,1024]{1,0:T(8,128)(2,1)S(1)} collective-permute-done((bf16[64,1024]{1,0:T(8,128)(2,1)S(1)}, bf16[64,1024]{1,0:T(8,128)(2,1)S(1)}, u32[]{:S(2)}, u32[]{:S(2)}) %collective-permute-start.1) | collective-permute-done | bytes 131104 | tf_op jit(solution)/shard_map/ppermute | solution.py:190
  13.1 0.0 collective-permute-done.2.refs_3_
  13.1 0.0 collective-permute-done.refs_0_
  13.1 0.8 %collective-permute-start.4 = (bf16[132,1024]{1,0:T(8,128)(2,1)S(1)}, bf16[132,1024]{1,0:T(8,128)(2,1)S(1)}, u32[]{:S(2)}, u32[]{:S(2)}) collective-permute-start(bf16[132,1024]{1,0:T(8,128)(2,1)S(1)} %after.9.pair_ref.refs_2_), channel_id=1, source_target_pairs={{0,16},{8,24},{16,0},{24,8},{1,17},{9,25},{17,1},{25,9},{2,18},{10... | collective-permute-start | bytes 811016 | tf_op jit(solution)/shard_map/ppermute | solution.py:196
  14.0 0.1 collective-permute-start.5
  14.0 1.6 %collective-permute-start.8 = (bf16[128,1024]{1,0:T(8,128)(2,1)S(1)}, bf16[128,1024]{1,0:T(8,128)(2,1)S(1)}, u32[]{:S(2)}, u32[]{:S(2)}) collective-permute-start(bf16[128,1024]{1,0:T(8,128)(2,1)S(1)} %collective-permute-done.2.refs_3_), channel_id=1, source_target_pairs={{0,8},{8,0},{16,24},{24,16},{1,9},{9,1},{17,25},{25,17},{2,10},{10... | collective-permute-start | bytes 786440 | tf_op jit(solution)/shard_map/ppermute | solution.py:185
  15.6 0.2 collective-permute-start.7
  15.8 0.0 collective-permute-done.5
  15.8 1.6 %collective-permute-start.6 = (bf16[2,2,1024]{2,1,0:T(2,128)(2,1)S(1)}, bf16[2,2,1024]{2,1,0:T(2,128)(2,1)S(1)}, u32[]{:S(2)}, u32[]{:S(2)}) collective-permute-start(bf16[2,2,1024]{2,1,0:T(2,128)(2,1)S(1)} %pad_maximum_fusion.2), channel_id=1, source_target_pairs={{0,2},{1,3},{2,0},{3,1},{4,6},{5,7},{6,4},{7,5},{8,10},{9,11},{10,... | collective-permute-start | bytes 24584 | tf_op jit(solution)/shard_map/ppermute | solution.py:185
  17.5 2.1 %collective-permute-done.6 = bf16[2,2,1024]{2,1,0:T(2,128)(2,1)S(1)} collective-permute-done((bf16[2,2,1024]{2,1,0:T(2,128)(2,1)S(1)}, bf16[2,2,1024]{2,1,0:T(2,128)(2,1)S(1)}, u32[]{:S(2)}, u32[]{:S(2)}) %collective-permute-start.6) | collective-permute-done | bytes 8224 | tf_op jit(solution)/shard_map/ppermute | solution.py:185
  19.6 0.0 collective-permute-done.7.refs_2_.q_ref
  19.6 0.0 collective-permute-done.3.refs_1_.pair_ref.refs_3_
  19.6 0.1 collective-permute-done.4.refs_0_
  19.7 0.6 %edge_part.1.refs_1_ = bf16[64,1152]{1,0:T(8,128)(2,1)S(1)} custom-call(bf16[64,1024]{1,0:T(8,128)(2,1)S(1)} %collective-permute-done.1.refs_2_.q_ref, bf16[132,1024]{1,0:T(8,128)(2,1)S(1)} %get-tuple-element.12.own_ref.refs_0_, bf16[132,1024]{1,0:T(8,128)(2,1)S(1)} %after.9.pair_ref.refs_2_, bf16[132,1024]{1,0:T(8,128)(2,1)S(1)} %after.11.far_ref.refs_4_), custom_call_target="tpu_custom_call" | custom-call | flops 50331648 | bytes 1089536 | tf_op jit(solution)/shard_map/edge_part/pallas_call | solution.py:27
  20.4 1.2 %collective-permute-start.9 = (bf16[2,4,1024]{2,1,0:T(4,128)(2,1)S(1)}, bf16[2,4,1024]{2,1,0:T(4,128)(2,1)S(1)}, u32[]{:S(2)}, u32[]{:S(2)}) collective-permute-start(bf16[2,4,1024]{2,1,0:T(4,128)(2,1)S(1)} %after.13), channel_id=1, source_target_pairs={{0,16},{8,24},{16,0},{24,8},{1,17},{9,25},{17,1},{25,9},{2,18},{10... | collective-permute-start | bytes 49160 | tf_op jit(solution)/shard_map/ppermute | solution.py:185
  21.5 1.7 %collective-permute-start.10 = (bf16[64,1152]{1,0:T(8,128)(2,1)S(1)}, bf16[64,1152]{1,0:T(8,128)(2,1)S(1)}, u32[]{:S(2)}, u32[]{:S(2)}) collective-permute-start(bf16[64,1152]{1,0:T(8,128)(2,1)S(1)} %edge_part.1.refs_1_), channel_id=1, source_target_pairs={{0,7},{1,2},{2,1},{3,4},{4,3},{5,6},{6,5},{7,0},{8,15},{9,10},{10,... | collective-permute-start | bytes 442376 | tf_op jit(solution)/shard_map/ppermute | solution.py:190
  23.3 0.0 collective-permute-done.8.refs_0_
  23.3 0.6 %inner_part.1.refs_1_ = bf16[64,1152]{1,0:T(8,128)(2,1)S(1)} custom-call(bf16[64,1024]{1,0:T(8,128)(2,1)S(1)} %collective-permute-done.7.refs_2_.q_ref, bf16[128,1024]{1,0:T(8,128)(2,1)S(1)} %get-tuple-element.13.own_ref.refs_1_, bf16[128,1024]{1,0:T(8,128)(2,1)S(1)} %collective-permute-done.3.refs_1_.pair_ref.refs_3_, ...), custom_call_target="tpu_custom_call" | custom-call | flops 50331648 | bytes 1064960 | tf_op jit(solution)/shard_map/inner_part/pallas_call | solution.py:27
  23.9 0.1 collective-permute-start.11
  24.0 0.2 collective-permute-done.9
  24.2 0.1 fusion.6.refs_0_
  24.2 0.0 copy-start
  24.3 1.2 %own_part.1 = (f32[128,1024]{1,0:T(8,128)S(1)}, f32[128,128]{1,0:T(8,128)S(1)}) custom-call(bf16[132,1024]{1,0:T(8,128)(2,1)S(1)} %get-tuple-element.12.own_ref.refs_0_, bf16[128,1024]{1,0:T(8,128)(2,1)S(1)} %get-tuple-element.13.own_ref.refs_1_, bf16[132,1024]{1,0:T(8,128)(2,1)S(1)} %after.9.pair_ref.refs_2_, ...), custom_call_target="tpu_custom_call" | custom-call | flops 201326592 | bytes 2514944 | tf_op jit(solution)/shard_map/own_part/pallas_call | solution.py:27
  25.5 3.7 %collective-permute-done.10.refs_0_ = bf16[64,1152]{1,0:T(8,128)(2,1)S(1)} collective-permute-done((bf16[64,1152]{1,0:T(8,128)(2,1)S(1)}, bf16[64,1152]{1,0:T(8,128)(2,1)S(1)}, u32[]{:S(2)}, u32[]{:S(2)}) %collective-permute-start.10) | collective-permute-done | bytes 147488 | tf_op jit(solution)/shard_map/ppermute | solution.py:190
  29.2 0.0 collective-permute-done.11.inner_ref
  29.2 0.0 copy-done
  29.2 1.5 %merge.1 = bf16[8,16,1024]{2,1,0:T(8,128)(2,1)} custom-call(f32[128,1024]{1,0:T(8,128)S(1)} %get-tuple-element.17.refs_1_.own_ref, f32[128,128]{1,0:T(8,128)S(1)} %get-tuple-element.18.lse_ref, bf16[64,1152]{1,0:T(8,128)(2,1)S(1)} %after.15.edge_ref, bf16[64,1152]{1,0:T(8,128)(2,1)S(1)} %collective-permute-done.11.inner_ref, bf16[1024,1024]{1,0:T(8,128)(2,1)S(1)} %copy-done), custom_call_target="tpu_custom_call" | custom-call | flops 268435456 | bytes 3244032 | tf_op jit(solution)/shard_map/merge/pallas_call | solution.py:27
  (17 shorter events, 0.2 us)
Async XLA Ops:
  1.2 11.9 %collective-permute-start = (bf16[132,1024]{1,0:T(8,128)(2,1)S(1)}, bf16[132,1024]{1,0:T(8,128)(2,1)S(1)}, u32[]{:S(2)}, u32[]{:S(2)}) collective-permute-start(bf16[132,1024]{1,0:T(8,128)(2,1)S(1)} %get-tuple-element.12.own_ref.refs_0_), channel_id=1, source_target_pairs={{0,8},{8,0},{16,24},{24,16},{1,9},{9,1},{17,25},{25,17},{2,10},{10... | collective-permute-start | bytes 811016 | tf_op jit(solution)/shard_map/ppermute | solution.py:185
  4.2 8.9 %collective-permute-start.2 = (bf16[128,1024]{1,0:T(8,128)(2,1)S(1)}, bf16[128,1024]{1,0:T(8,128)(2,1)S(1)}, u32[]{:S(2)}, u32[]{:S(2)}) collective-permute-start(bf16[128,1024]{1,0:T(8,128)(2,1)S(1)} %get-tuple-element.13.own_ref.refs_1_), channel_id=1, source_target_pairs={{0,16},{8,24},{16,0},{24,8},{1,17},{9,25},{17,1},{25,9},{2,18},{10... | collective-permute-start | bytes 786440 | tf_op jit(solution)/shard_map/ppermute | solution.py:196
  5.8 7.3 %collective-permute-start.1 = (bf16[64,1024]{1,0:T(8,128)(2,1)S(1)}, bf16[64,1024]{1,0:T(8,128)(2,1)S(1)}, u32[]{:S(2)}, u32[]{:S(2)}) collective-permute-start(bf16[64,1024]{1,0:T(8,128)(2,1)S(1)} %get-tuple-element.15.refs_7_), channel_id=1, source_target_pairs={{0,7},{1,2},{2,1},{3,4},{4,3},{5,6},{6,5},{7,0},{8,15},{9,10},{10,... | collective-permute-start | bytes 393224 | tf_op jit(solution)/shard_map/ppermute | solution.py:190
  8.2 11.3 %collective-permute-start.3 = (bf16[128,1024]{1,0:T(8,128)(2,1)S(1)}, bf16[128,1024]{1,0:T(8,128)(2,1)S(1)}, u32[]{:S(2)}, u32[]{:S(2)}) collective-permute-start(bf16[128,1024]{1,0:T(8,128)(2,1)S(1)} %get-tuple-element.13.own_ref.refs_1_), channel_id=1, source_target_pairs={{0,8},{8,0},{16,24},{24,16},{1,9},{9,1},{17,25},{25,17},{2,10},{10... | collective-permute-start | bytes 786440 | tf_op jit(solution)/shard_map/ppermute | solution.py:185
  13.1 6.6 %collective-permute-start.4 = (bf16[132,1024]{1,0:T(8,128)(2,1)S(1)}, bf16[132,1024]{1,0:T(8,128)(2,1)S(1)}, u32[]{:S(2)}, u32[]{:S(2)}) collective-permute-start(bf16[132,1024]{1,0:T(8,128)(2,1)S(1)} %after.9.pair_ref.refs_2_), channel_id=1, source_target_pairs={{0,16},{8,24},{16,0},{24,8},{1,17},{9,25},{17,1},{25,9},{2,18},{10... | collective-permute-start | bytes 811016 | tf_op jit(solution)/shard_map/ppermute | solution.py:196
  14.0 1.8 %collective-permute-start.5 = (bf16[2,5,1024]{2,1,0:T(8,128)(2,1)S(1)}, bf16[2,5,1024]{2,1,0:T(8,128)(2,1)S(1)}, u32[]{:S(2)}, u32[]{:S(2)}) collective-permute-start(bf16[2,5,1024]{2,1,0:T(8,128)(2,1)S(1)} %pad_maximum_fusion), channel_id=1, source_target_pairs={{0,1},{1,0},{2,3},{3,2},{4,5},{5,4},{6,7},{7,6},{8,9},{9,8},{10,11... | collective-permute-start | bytes 61448 | tf_op jit(solution)/shard_map/ppermute | solution.py:185
  14.0 9.2 %collective-permute-start.8 = (bf16[128,1024]{1,0:T(8,128)(2,1)S(1)}, bf16[128,1024]{1,0:T(8,128)(2,1)S(1)}, u32[]{:S(2)}, u32[]{:S(2)}) collective-permute-start(bf16[128,1024]{1,0:T(8,128)(2,1)S(1)} %collective-permute-done.2.refs_3_), channel_id=1, source_target_pairs={{0,8},{8,0},{16,24},{24,16},{1,9},{9,1},{17,25},{25,17},{2,10},{10... | collective-permute-start | bytes 786440 | tf_op jit(solution)/shard_map/ppermute | solution.py:185
  15.6 4.0 %collective-permute-start.7 = (bf16[64,1024]{1,0:T(8,128)(2,1)S(1)}, bf16[64,1024]{1,0:T(8,128)(2,1)S(1)}, u32[]{:S(2)}, u32[]{:S(2)}) collective-permute-start(bf16[64,1024]{1,0:T(8,128)(2,1)S(1)} %get-tuple-element.16.refs_6_), channel_id=1, source_target_pairs={{0,1},{1,0},{2,3},{3,2},{4,5},{5,4},{6,7},{7,6},{8,9},{9,8},{10,11... | collective-permute-start | bytes 393224 | tf_op jit(solution)/shard_map/ppermute | solution.py:185
  15.8 3.7 %collective-permute-start.6 = (bf16[2,2,1024]{2,1,0:T(2,128)(2,1)S(1)}, bf16[2,2,1024]{2,1,0:T(2,128)(2,1)S(1)}, u32[]{:S(2)}, u32[]{:S(2)}) collective-permute-start(bf16[2,2,1024]{2,1,0:T(2,128)(2,1)S(1)} %pad_maximum_fusion.2), channel_id=1, source_target_pairs={{0,2},{1,3},{2,0},{3,1},{4,6},{5,7},{6,4},{7,5},{8,10},{9,11},{10,... | collective-permute-start | bytes 24584 | tf_op jit(solution)/shard_map/ppermute | solution.py:185
  20.4 3.8 %collective-permute-start.9 = (bf16[2,4,1024]{2,1,0:T(4,128)(2,1)S(1)}, bf16[2,4,1024]{2,1,0:T(4,128)(2,1)S(1)}, u32[]{:S(2)}, u32[]{:S(2)}) collective-permute-start(bf16[2,4,1024]{2,1,0:T(4,128)(2,1)S(1)} %after.13), channel_id=1, source_target_pairs={{0,16},{8,24},{16,0},{24,8},{1,17},{9,25},{17,1},{25,9},{2,18},{10... | collective-permute-start | bytes 49160 | tf_op jit(solution)/shard_map/ppermute | solution.py:185
  21.5 7.7 %collective-permute-start.10 = (bf16[64,1152]{1,0:T(8,128)(2,1)S(1)}, bf16[64,1152]{1,0:T(8,128)(2,1)S(1)}, u32[]{:S(2)}, u32[]{:S(2)}) collective-permute-start(bf16[64,1152]{1,0:T(8,128)(2,1)S(1)} %edge_part.1.refs_1_), channel_id=1, source_target_pairs={{0,7},{1,2},{2,1},{3,4},{4,3},{5,6},{6,5},{7,0},{8,15},{9,10},{10,... | collective-permute-start | bytes 442376 | tf_op jit(solution)/shard_map/ppermute | solution.py:190
  23.9 5.3 %collective-permute-start.11 = (bf16[64,1152]{1,0:T(8,128)(2,1)S(1)}, bf16[64,1152]{1,0:T(8,128)(2,1)S(1)}, u32[]{:S(2)}, u32[]{:S(2)}) collective-permute-start(bf16[64,1152]{1,0:T(8,128)(2,1)S(1)} %inner_part.1.refs_1_), channel_id=1, source_target_pairs={{0,1},{1,0},{2,3},{3,2},{4,5},{5,4},{6,7},{7,6},{8,9},{9,8},{10,11... | collective-permute-start | bytes 442376 | tf_op jit(solution)/shard_map/ppermute | solution.py:185
  24.2 5.0 %copy-start = (bf16[1024,1024]{1,0:T(8,128)(2,1)S(1)}, bf16[1024,1024]{1,0:T(8,128)(2,1)}, u32[]{:S(2)}) copy-start(bf16[1024,1024]{1,0:T(8,128)(2,1)} %weight_ref.1) | copy-start | bytes 6291460
